TPU v7x, 512 devices: a whole 4x8x8 slice. The times are simulated.
512 devices in a mesh: chan: 32 (over z_lo, y, core), row: 16 (over x, z_hi).
Axes of the slice: x: 4, y: 8, z: 8 (z_hi: 4, z_lo: 2; z = z_hi * 2 + z_lo), core: 2. Of those that a mesh axis runs over, the one named last changes fastest.
Arguments:
- pair_acts: bfloat16 [1280, 1280, 128], P('row', 'chan'), may hold values from -6 to 6
- residue_valid: int32 [1280], replicated, may hold values 0 or 1
- chain_index: int32 [1280], replicated, may hold values from 0 to 3, never falling along the last dimension, each value on 1 to 640 neighbouring positions
- norm_gain: float32 [2, 128], replicated, may hold values from 0.5 to 1.5
- norm_bias: float32 [2, 128], replicated, may hold values from -3 to 3
- projection: bfloat16 [2, 128, 256], replicated, may hold values from -0.5 to 0.5
- gate_weight: bfloat16 [2, 128, 128], replicated, may hold values from -0.5 to 0.5
- chain_bias: float32 [2, 128], replicated, may hold values from -4 to 4
- out_gain: float32 [2, 64], replicated, may hold values from 0.5 to 1.5
- out_weight: bfloat16 [2, 64, 128], replicated, may hold values from -0.75 to 0.75
Outputs:
- updated: bfloat16 [1280, 1280, 128], P('row', 'chan')
Inputs may be any that keep to these rules, and one draw needn't show every extreme that they name: `chain_index`: chain numbers never fall along the residues, and no chain is longer than 640 residues.
All inputs are finite; a program needn't handle non-finite values.
Results may differ from a plain program's by a relative error of at most 0.0065.
Values may be sent and summed in bfloat16 or wider, within the bound.
No kernel may reach another device: no remote copies, remote signals or barrier semaphores. Data moves between devices by JAX's collectives and lax.ppermute only.
A program may use at most 64 MiB of HBM per device.

v0:
```python
import functools

import jax
import jax.numpy as jnp
from jax import lax
from jax.experimental import pallas as pl
from jax.experimental.pallas import tpu as pltpu
from jax.sharding import Mesh
from jax.sharding import PartitionSpec as P

AXES = ("zl", "y", "core", "x", "zh")
SIZES = (2, 8, 2, 4, 4)
PLANE = ("zl", "y", "zh")
ROWS = 80
COLUMNS = 40
WIDTH = 128
HIDDEN = 64
X = 4
ZH = 4
SPAN = 16
EPS = 1e-05
DEPTH = 32
LANES = 128
GROUPS = ((0, 32), (32, 32), (64, 16))
STRIDE = 40
CHUNKS = jax.ShapeDtypeStruct((HIDDEN, DEPTH, LANES), jnp.bfloat16)
VMEM = pl.BlockSpec(memory_space=pltpu.VMEM)
SMEM = pl.BlockSpec(memory_space=pltpu.SMEM)


def call(kernel, out_shape, in_specs, scratch_shapes=(), flops=10**8, moved=4 * 10**6):
    outs = jax.tree.map(lambda _: VMEM, out_shape)
    return pl.pallas_call(
        kernel,
        out_shape=out_shape,
        in_specs=in_specs,
        out_specs=outs,
        scratch_shapes=scratch_shapes,
        compiler_params=pltpu.CompilerParams(vmem_limit_bytes=40 * 2**20),
        cost_estimate=pl.CostEstimate(flops=flops, bytes_accessed=moved, transcendentals=0),
    )


def normalize(values, gain, bias):
    average = jnp.mean(values, axis=-1, keepdims=True)
    centred = values - average
    spread = jnp.mean(centred * centred, axis=-1, keepdims=True)
    return (centred * lax.rsqrt(spread + EPS) * gain + bias).astype(jnp.bfloat16)


def block_rows(step, count):
    return [step + DEPTH * group for group in range(count)]


def spread_columns(place_ref, valid_ref):
    lane = lax.broadcasted_iota(jnp.int32, (1, LANES), 1)
    inside = lane % COLUMNS
    found = jnp.zeros((1, LANES), jnp.float32)
    for column in range(COLUMNS):
        value = valid_ref[place_ref[1] + column].astype(jnp.float32)
        found = jnp.where(inside == column, value, found)
    return jnp.where(lane < 3 * COLUMNS, found, 0.0)


def mask_of(step, count, place_ref, valid_ref, columns):
    lane = lax.broadcasted_iota(jnp.int32, (1, LANES), 1)
    mask = jnp.zeros((1, LANES), jnp.float32)
    for group, row in enumerate(block_rows(step, count)):
        value = valid_ref[place_ref[0] + row].astype(jnp.float32)
        inside = (lane >= group * COLUMNS) & (lane < (group + 1) * COLUMNS)
        mask = jnp.where(inside, value, mask)
    return mask * columns


def project_rows(step, count, normed, weight_ref, mask, left_scratch, right_scratch):
    rows = count * COLUMNS
    padded = jnp.concatenate([normed, jnp.zeros((LANES - rows, WIDTH), jnp.bfloat16)], axis=0)
    proj = lax.dot_general(
        weight_ref[...], padded, (((1,), (1,)), ((), ())), preferred_element_type=jnp.float32
    )
    parts = [proj[HIDDEN * n : HIDDEN * (n + 1)] for n in range(4)]
    place = pl.ds(step, HIDDEN, stride=STRIDE)
    left_scratch[place, :] = jax.nn.sigmoid(parts[1]) * parts[0] * mask
    right_scratch[place, :] = jax.nn.sigmoid(parts[3]) * parts[2] * mask


def put_chunks(scratch, out_ref):
    for channel in range(HIDDEN):
        out_ref[channel] = scratch[pl.ds(channel * STRIDE, DEPTH), :].astype(jnp.bfloat16)


def project_kernel(
    place_ref, valid_ref, pair_ref, gain_ref, bias_ref, weight_ref, left_ref, right_ref, left_s, right_s
):
    columns = spread_columns(place_ref, valid_ref)

    def one(step, count):
        values = jnp.concatenate(
            [pair_ref[row].astype(jnp.float32) for row in block_rows(step, count)], axis=0
        )
        normed = normalize(values, gain_ref[...], bias_ref[...])
        mask = mask_of(step, count, place_ref, valid_ref, columns)
        project_rows(step, count, normed, weight_ref, mask, left_s, right_s)

    pl.loop(0, 16)(functools.partial(one, count=3))
    pl.loop(16, DEPTH)(functools.partial(one, count=2))
    put_chunks(left_s, left_ref)
    put_chunks(right_s, right_ref)


SCRATCH = pltpu.VMEM(((HIDDEN + 1) * STRIDE, LANES), jnp.float32)


def project(place, valid, pair, gain, bias, weight):
    return call(
        project_kernel,
        [CHUNKS, CHUNKS],
        [SMEM, SMEM, VMEM, VMEM, VMEM, VMEM],
        [SCRATCH, SCRATCH],
    )(place, valid, pair, gain, bias, weight)


def finish_kernel(
    then,
    place_ref,
    valid_ref,
    chain_ref,
    out_gain_ref,
    pair_ref,
    product_ref,
    gain_ref,
    bias_ref,
    gate_ref,
    chain_bias_ref,
    out_weight_ref,
    *rest,
):
    if then:
        next_gain_ref, next_bias_ref, weight_ref, out_ref, left_ref, right_ref = rest[:6]
        hidden_s, left_s, right_s = rest[6:]
        columns = spread_columns(place_ref, valid_ref)
    else:
        out_ref, hidden_s = rest
    row = lax.broadcasted_iota(jnp.int32, (COLUMNS, WIDTH), 0)
    chain_columns = jnp.full((COLUMNS, WIDTH), -1, jnp.int32)
    for column in range(COLUMNS):
        chain_columns = jnp.where(row == column, chain_ref[place_ref[1] + column], chain_columns)

    def channel(n):
        return product_ref[n].astype(jnp.float32)

    average = jnp.zeros((DEPTH, LANES), jnp.float32)
    for n in range(HIDDEN):
        average = average + channel(n)
    average = average / HIDDEN
    spread = jnp.zeros((DEPTH, LANES), jnp.float32)
    for n in range(HIDDEN):
        centred = channel(n) - average
        spread = spread + centred * centred
    scale = lax.rsqrt(spread / HIDDEN + EPS)
    for n in range(HIDDEN):
        hidden_s[pl.ds(n * STRIDE, DEPTH), :] = (channel(n) - average) * scale * out_gain_ref[n]

    def one(step, count):
        rows = block_rows(step, count)
        values = jnp.concatenate([pair_ref[row].astype(jnp.float32) for row in rows], axis=0)
        normed = normalize(values, gain_ref[...], bias_ref[...])
        gate = jnp.dot(normed, gate_ref[...], preferred_element_type=jnp.float32)
        same = jnp.concatenate(
            [
                jnp.where(chain_columns == chain_ref[place_ref[0] + row], chain_bias_ref[...], 0.0)
                for row in rows
            ],
            axis=0,
        )
        hidden = hidden_s[pl.ds(step, HIDDEN, stride=STRIDE), :].astype(jnp.bfloat16)
        branch = lax.dot_general(
            hidden,
            out_weight_ref[...],
            (((0,), (0,)), ((), ())),
            preferred_element_type=jnp.float32,
        )[: count * COLUMNS]
        new = (values + jax.nn.sigmoid(gate + same) * branch).astype(jnp.bfloat16)
        for group, row in enumerate(rows):
            out_ref[row] = new[group * COLUMNS : (group + 1) * COLUMNS]
        if then:
            normed = normalize(
                new.astype(jnp.float32), next_gain_ref[...], next_bias_ref[...]
            )
            mask = mask_of(step, count, place_ref, valid_ref, columns)
            project_rows(step, count, normed, weight_ref, mask, left_s, right_s)

    pl.loop(0, 16)(functools.partial(one, count=3))
    pl.loop(16, DEPTH)(functools.partial(one, count=2))
    if then:
        put_chunks(left_s, left_ref)
        put_chunks(right_s, right_ref)


def finish(place, valid, chain, out_gain, pair, product, gain, bias, gate, chain_bias, out_weight, then=()):
    out = jax.ShapeDtypeStruct(pair.shape, pair.dtype)
    return call(
        functools.partial(finish_kernel, bool(then)),
        [out, CHUNKS, CHUNKS] if then else [out],
        [SMEM] * 4 + [VMEM] * (7 + len(then)),
        [SCRATCH] * (3 if then else 1),
    )(place, valid, chain, out_gain, pair, product, gain, bias, gate, chain_bias, out_weight, *then)


def gather_block(chunks_ref, zh, group, size):
    lanes = slice(group * COLUMNS, (group + 1) * COLUMNS)
    return jnp.concatenate(
        [chunks_ref[span * ZH + zh, :size, :][:, lanes] for span in range(SPAN)], axis=1
    )


def assemble_kernel(chunks_ref, out_ref):
    for zh in range(ZH):
        for group, (start, size) in enumerate(GROUPS):
            out_ref[pl.ds(zh * ROWS + start, size), :] = gather_block(chunks_ref, zh, group, size)


def assemble(chunks):
    out = jax.ShapeDtypeStruct((ZH * ROWS, SPAN * COLUMNS), jnp.bfloat16)
    return call(assemble_kernel, out, [VMEM])(chunks)


def assemble_turned_kernel(chunks_ref, out_ref, whole):
    for zh in range(ZH):
        for group, (start, size) in enumerate(GROUPS):
            whole[pl.ds(zh * ROWS + start, size), :] = gather_block(
                chunks_ref, zh, group, size
            ).astype(jnp.float32)
    whole[pl.ds(ZH * ROWS, 64), :] = jnp.zeros((64, SPAN * COLUMNS), jnp.float32)
    for part in range(SPAN * COLUMNS // 128):
        turned = whole[:, part * 128 : (part + 1) * 128].T
        out_ref[pl.ds(part * 128, 128), :] = turned[:, : ZH * ROWS].astype(jnp.bfloat16)


def assemble_turned(chunks):
    out = jax.ShapeDtypeStruct((SPAN * COLUMNS, ZH * ROWS), jnp.bfloat16)
    scratch = [pltpu.VMEM((ZH * ROWS + 64, SPAN * COLUMNS), jnp.float32)]
    return call(assemble_turned_kernel, out, [VMEM], scratch)(chunks)


def chunk_of(total, zh, start):
    pieces = []
    for first, size in GROUPS:
        piece = total[pl.ds(zh * ROWS + first, size), :][:, start : start + COLUMNS]
        if size < DEPTH:
            piece = jnp.concatenate(
                [piece, jnp.zeros((DEPTH - size, COLUMNS), jnp.float32)], axis=0
            )
        pieces.append(piece)
    pieces.append(jnp.zeros((DEPTH, LANES - 3 * COLUMNS), jnp.float32))
    return jnp.concatenate(pieces, axis=1).astype(jnp.bfloat16)


def outgoing_kernel(core_ref, left_ref, right_ref, out_ref, left_s, total):
    assemble_kernel(left_ref, left_s)
    for x in range(X):
        total[:, x * ZH * ROWS : (x + 1) * ZH * ROWS] = lax.dot_general(
            left_s[...],
            right_ref[pl.ds(x * ZH * ROWS, ZH * ROWS), :],
            (((1,), (1,)), ((), ())),
            preferred_element_type=jnp.float32,
        )
    for half in range(2):
        slot = lax.rem(core_ref[0] + half, 2)
        for span in range(SPAN):
            for zh in range(ZH):
                out_ref[slot, span * ZH + zh] = chunk_of(total, zh, (2 * span + half) * COLUMNS)


def outgoing(core, left, right):
    out = jax.ShapeDtypeStruct((2,) + CHUNKS.shape, jnp.bfloat16)
    scratch = [
        pltpu.VMEM((ZH * ROWS, SPAN * COLUMNS), jnp.bfloat16),
        pltpu.VMEM((ZH * ROWS, X * ZH * ROWS), jnp.float32),
    ]
    return call(outgoing_kernel, out, [SMEM, VMEM, VMEM], scratch, 6 * 10**8)(core, left, right)


def incoming_kernel(core_ref, own_ref, other_ref, right_ref, out_ref, total):
    for n, left_ref in enumerate((own_ref, other_ref)):
        side = lax.rem(core_ref[0] + n, 2)
        product = jnp.zeros((ZH * COLUMNS, SPAN * COLUMNS), jnp.float32)
        for x in range(X):
            product = product + jnp.dot(
                left_ref[x],
                right_ref[pl.ds(x * ZH * ROWS, ZH * ROWS), :],
                preferred_element_type=jnp.float32,
            )
        for zh in range(ZH):
            start = pl.multiple_of(zh * ROWS + side * COLUMNS, 8)
            total[pl.ds(start, COLUMNS), :] = product[zh * COLUMNS : (zh + 1) * COLUMNS]
    for span in range(SPAN):
        for zh in range(ZH):
            out_ref[span * ZH + zh] = chunk_of(total, zh, span * COLUMNS)


def incoming(core, own, other, right):
    scratch = [pltpu.VMEM((ZH * ROWS, SPAN * COLUMNS), jnp.float32)]
    return call(incoming_kernel, CHUNKS, [SMEM, VMEM, VMEM, VMEM], scratch, 6 * 10**8)(
        core, own, other, right
    )


def exchange(values, axes):
    return lax.all_to_all(values, axes, split_axis=0, concat_axis=0, tiled=True)


def swap_cores(values):
    return lax.ppermute(values, "core", [(0, 1), (1, 0)])


def body(
    pair_acts,
    residue_valid,
    chain_index,
    norm_gain,
    norm_bias,
    projection,
    gate_weight,
    chain_bias,
    out_gain,
    out_weight,
):
    row_start = (lax.axis_index("x") * ZH + lax.axis_index("zh")) * ROWS
    core_index = lax.axis_index("core")
    column_block = (lax.axis_index("zl") * 8 + lax.axis_index("y")) * 2 + core_index
    place = jnp.stack([row_start, column_block * COLUMNS]).astype(jnp.int32)
    core = core_index.reshape(1).astype(jnp.int32)
    turned = projection.transpose(0, 2, 1)

    left, right = project(
        place, residue_valid, pair_acts, norm_gain[:1], norm_bias[:1], turned[0]
    )
    right = assemble(exchange(right, PLANE))
    right = lax.all_gather(right, "x", axis=0, tiled=True)
    halves = outgoing(core, exchange(left, PLANE), right)
    total = halves[0].astype(jnp.float32) + swap_cores(halves[1]).astype(jnp.float32)
    product = exchange(total.astype(jnp.bfloat16), PLANE)
    middle, left, right = finish(
        place,
        residue_valid,
        chain_index,
        out_gain[0],
        pair_acts,
        product,
        norm_gain[:1],
        norm_bias[:1],
        gate_weight[0],
        chain_bias[:1],
        out_weight[0],
        (norm_gain[1:], norm_bias[1:], turned[1]),
    )
    right = assemble(exchange(right, PLANE))
    right = lax.all_gather(right, "x", axis=0, tiled=True)
    left = assemble_turned(exchange(left, PLANE)).reshape(X, ZH * COLUMNS, ZH * ROWS)
    left = exchange(left, "x")
    product = exchange(incoming(core, left, swap_cores(left), right), PLANE)
    return finish(
        place,
        residue_valid,
        chain_index,
        out_gain[1],
        middle,
        product,
        norm_gain[1:],
        norm_bias[1:],
        gate_weight[1],
        chain_bias[1:],
        out_weight[1],
    )[0]


def solution(mesh):
    fine = Mesh(mesh.devices.reshape(SIZES), AXES)
    pairs = P(("x", "zh"), ("zl", "y", "core"), None)
    placed = (pairs, P(), P(), P(), P(), P(), P(), P(), P(), P())
    return jax.shard_map(body, mesh=fine, in_specs=placed, out_specs=pairs, check_vma=False)
```

profile of v0, /device:TPU:6, one launch (start us, length us, event | category | flops | bytes accessed | tf_op | source)
XLA Modules:
  0.0 260.3 jit_solution(12984294335147481183)
XLA Ops:
  6.5 1.0 copy.11
  8.4 1.1 copy-done
  10.3 11.9 %shard_map.100 = (bf16[64,32,128]{2,1,0:T(8,128)(2,1)S(1)}, bf16[64,32,128]{2,1,0:T(8,128)(2,1)S(1)}) custom-call(s32[2]{0:T(128)S(1)} %pad_add_fusion.place_ref, s32[1280]{0:T(1024)S(1)} %copy-done.4, bf16[80,40,128]{2,1,0:T(8,128)(2,1)S(1)} %copy-done, f32[1,128]{1,0:T(1,128)S(1)} %get-tuple-element.29.gain_ref, f32[1,128]{1,0:T(1,128)S(1)} %get-tuple-element.24.bias_ref, ...), custom_call_target="tpu_custom_call" | custom-call | flops 100000000 | bytes 4000000 | tf_op jit(solution)/shard_map/pallas_call | solution.py:115
  22.2 34.8 %all_to_all.35.chunks_ref = bf16[64,32,128]{2,1,0:T(8,128)(2,1)S(1)} all-to-all(bf16[64,32,128]{2,1,0:T(8,128)(2,1)S(1)} %get-tuple-element.11), channel_id=1, replica_groups=mesh['zl'=2,'y'=8,'core'=2,'x'=4,'zh'=4] {'zl','y','zh'}, dimensions={0} | all-to-all | bytes 1048576 | tf_op jit(solution)/shard_map/all_to_all | solution.py:310
  57.1 1.1 shard_map.101
  58.2 24.3 %all_to_all.36.left_ref = bf16[64,32,128]{2,1,0:T(8,128)(2,1)S(1)} all-to-all(bf16[64,32,128]{2,1,0:T(8,128)(2,1)S(1)} %get-tuple-element.10), channel_id=1, replica_groups=mesh['zl'=2,'y'=8,'core'=2,'x'=4,'zh'=4] {'zl','y','zh'}, dimensions={0} | all-to-all | bytes 1048576 | tf_op jit(solution)/shard_map/all_to_all | solution.py:310
  82.6 1.1 all-gather.3.cloned.1.call-done.right_ref
  83.7 1.4 copy-done.3
  85.1 1.9 shard_map.102
  87.2 2.1 collective-permute-start
  89.3 1.9 collective-permute-done
  92.1 13.3 %all-to-all-start.2 = ((bf16[64,32,128]{2,1,0:T(8,128)(2,1)}), bf16[64,32,128]{2,1,0:T(8,128)(2,1)S(1)}, u32[]{:S(2)}, u32[]{:S(2)}) async-start(bf16[64,32,128]{2,1,0:T(8,128)(2,1)} %fusion), calls=%async_computation.2 | async-start | bytes 1048576 | tf_op jit(solution)/shard_map/all_to_all | solution.py:310
  105.5 18.5 %all-to-all-done.2.product_ref = bf16[64,32,128]{2,1,0:T(8,128)(2,1)S(1)} async-done(((bf16[64,32,128]{2,1,0:T(8,128)(2,1)}), bf16[64,32,128]{2,1,0:T(8,128)(2,1)S(1)}, u32[]{:S(2)}, u32[]{:S(2)}) %all-to-all-start.2) | async-done | bytes 524320 | tf_op jit(solution)/shard_map/all_to_all | solution.py:310
  124.1 22.3 %shard_map.103 = (bf16[80,40,128]{2,1,0:T(8,128)(2,1)S(1)}, bf16[64,32,128]{2,1,0:T(8,128)(2,1)S(1)}, bf16[64,32,128]{2,1,0:T(8,128)(2,1)S(1)}) custom-call(s32[2]{0:T(128)S(1)} %pad_add_fusion.place_ref, s32[1280]{0:T(1024)S(1)} %copy-done.5, s32[1280]{0:T(1024)S(1)} %copy-done.6, f32[64]{0:T(128)S(1)} %get-tuple-element.27.out_gain_ref, ...), custom_call_target="tpu_custom_call" | custom-call | flops 100000000 | bytes 4000000 | tf_op jit(solution)/shard_map/pallas_call | solution.py:202
  146.4 24.6 %all_to_all.37.chunks_ref = bf16[64,32,128]{2,1,0:T(8,128)(2,1)S(1)} all-to-all(bf16[64,32,128]{2,1,0:T(8,128)(2,1)S(1)} %get-tuple-element.14), channel_id=1, replica_groups=mesh['zl'=2,'y'=8,'core'=2,'x'=4,'zh'=4] {'zl','y','zh'}, dimensions={0} | all-to-all | bytes 1048576 | tf_op jit(solution)/shard_map/all_to_all | solution.py:310
  171.0 1.1 shard_map.105
  172.1 24.1 %all_to_all.38.chunks_ref = bf16[64,32,128]{2,1,0:T(8,128)(2,1)S(1)} all-to-all(bf16[64,32,128]{2,1,0:T(8,128)(2,1)S(1)} %get-tuple-element.13), channel_id=1, replica_groups=mesh['zl'=2,'y'=8,'core'=2,'x'=4,'zh'=4] {'zl','y','zh'}, dimensions={0} | all-to-all | bytes 1048576 | tf_op jit(solution)/shard_map/all_to_all | solution.py:310
  196.8 10.3 %all_to_all.39.own_ref = bf16[4,160,320]{2,1,0:T(8,128)(2,1)S(1)} all-to-all(bf16[4,160,320]{2,1,0:T(8,128)(2,1)S(1)} %bitcast.28), channel_id=1, replica_groups=mesh['zl'=2,'y'=8,'core'=2,'x'=4,'zh'=4] {'x'}, dimensions={0} | all-to-all | bytes 819200 | tf_op jit(solution)/shard_map/all_to_all | solution.py:310
  207.1 1.9 collective-permute-start.1
  209.0 1.8 collective-permute-done.1.other_ref
  210.8 1.4 copy-done.2
  212.3 1.6 shard_map.106
  213.9 27.0 %all_to_all.40.product_ref = bf16[64,32,128]{2,1,0:T(8,128)(2,1)S(1)} all-to-all(bf16[64,32,128]{2,1,0:T(8,128)(2,1)S(1)} %shard_map.106), channel_id=1, replica_groups=mesh['zl'=2,'y'=8,'core'=2,'x'=4,'zh'=4] {'zl','y','zh'}, dimensions={0} | all-to-all | bytes 1048576 | tf_op jit(solution)/shard_map/all_to_all | solution.py:310
  240.9 12.5 %shard_map.107 = bf16[80,40,128]{2,1,0:T(8,128)(2,1)} custom-call(s32[2]{0:T(128)S(1)} %pad_add_fusion.place_ref, s32[1280]{0:T(1024)S(1)} %copy-done.5, s32[1280]{0:T(1024)S(1)} %copy-done.6, f32[64]{0:T(128)S(1)} %get-tuple-element.28.out_gain_ref, bf16[80,40,128]{2,1,0:T(8,128)(2,1)S(1)} %get-tuple-element.12.pair_ref, ...), custom_call_target="tpu_custom_call" | custom-call | flops 100000000 | bytes 4000000 | tf_op jit(solution)/shard_map/pallas_call | solution.py:202
  (34 shorter events, 3.2 us)
Async XLA Ops:
  6.5 77.2 %all-gather.3.cloned.1.call-start = ((), (), s32[]{:S(2)}) async-start(), calls=%async_computation.7 | async-start | bytes 2048000 | tf_op jit(solution)/shard_map/all_gather | solution.py:340
  8.4 1.1 copy-start
  9.6 0.7 copy-start.4
  83.7 1.4 copy-start.3
  87.1 18.3 %copy-start.9 = (f32[2,128]{1,0:T(2,128)S(1)}, f32[2,128]{1,0:T(2,128)}, u32[]{:S(2)}) copy-start(f32[2,128]{1,0:T(2,128)} %param.17) | copy-start | bytes 3076
  87.1 18.3 %copy-start.10 = (f32[2,64]{1,0:T(2,128)S(1)}, f32[2,64]{1,0:T(2,128)}, u32[]{:S(2)}) copy-start(f32[2,64]{1,0:T(2,128)} %param.18) | copy-start | bytes 1540
  87.1 18.4 %copy-start.8 = (bf16[2,64,128]{2,1,0:T(8,128)(2,1)S(1)}, bf16[2,64,128]{2,1,0:T(8,128)(2,1)}, u32[]{:S(2)}) copy-start(bf16[2,64,128]{2,1,0:T(8,128)(2,1)} %param.19) | copy-start | bytes 98308
  87.1 18.4 %copy-start.7 = (bf16[2,128,128]{2,1,0:T(8,128)(2,1)S(1)}, bf16[2,128,128]{2,1,0:T(8,128)(2,1)}, u32[]{:S(2)}) copy-start(bf16[2,128,128]{2,1,0:T(8,128)(2,1)} %param.16) | copy-start | bytes 196612
  87.2 36.9 %copy-start.1 = (bf16[80,40,128]{2,1,0:T(8,128)(2,1)S(1)}, bf16[80,40,128]{2,1,0:T(8,128)(2,1)}, u32[]{:S(2)}) copy-start(bf16[80,40,128]{2,1,0:T(8,128)(2,1)} %pair_ref.3) | copy-start | bytes 2457604
  87.2 36.9 %copy-start.5 = (s32[1280]{0:T(1024)S(1)}, s32[1280]{0:T(1024)}, u32[]{:S(2)}) copy-start(s32[1280]{0:T(1024)} %valid_ref.5) | copy-start | bytes 15364
  87.2 36.8 %copy-start.6 = (s32[1280]{0:T(1024)S(1)}, s32[1280]{0:T(1024)}, u32[]{:S(2)}) copy-start(s32[1280]{0:T(1024)} %chain_ref.3) | copy-start | bytes 15364
  87.2 3.9 %collective-permute-start = (bf16[64,32,128]{2,1,0:T(8,128)(2,1)S(1)}, bf16[64,32,128]{2,1,0:T(8,128)(2,1)S(1)}, u32[]{:S(2)}, u32[]{:S(2)}) collective-permute-start(bf16[64,32,128]{2,1,0:T(8,128)(2,1)S(1)} %slice_bitcast_fusion), channel_id=1, source_target_pairs={{0,16},{16,0},{1,17},{17,1},{2,18},{18,2},{3,19},{19,3},{4,20},{20... | collective-permute-start | bytes 1572872 | tf_op jit(solution)/shard_map/ppermute | solution.py:314
  92.1 32.0 %all-to-all-start.2 = ((bf16[64,32,128]{2,1,0:T(8,128)(2,1)}), bf16[64,32,128]{2,1,0:T(8,128)(2,1)S(1)}, u32[]{:S(2)}, u32[]{:S(2)}) async-start(bf16[64,32,128]{2,1,0:T(8,128)(2,1)} %fusion), calls=%async_computation.2 | async-start | bytes 1048576 | tf_op jit(solution)/shard_map/all_to_all | solution.py:310
  105.4 105.5 %all-gather.5.cloned.1.call-start = ((), (), s32[]{:S(2)}) async-start(), calls=%async_computation.8 | async-start | bytes 2048000 | tf_op jit(solution)/shard_map/all_gather | solution.py:359
  207.1 3.7 %collective-permute-start.1 = (bf16[4,160,320]{2,1,0:T(8,128)(2,1)S(1)}, bf16[4,160,320]{2,1,0:T(8,128)(2,1)S(1)}, u32[]{:S(2)}, u32[]{:S(2)}) collective-permute-start(bf16[4,160,320]{2,1,0:T(8,128)(2,1)S(1)} %all_to_all.39.own_ref), channel_id=1, source_target_pairs={{0,16},{16,0},{1,17},{17,1},{2,18},{18,2},{3,19},{19,3},{4,20},{20... | collective-permute-start | bytes 1228808 | tf_op jit(solution)/shard_map/ppermute | solution.py:314
  210.8 1.4 copy-start.2
Sparse Core Ops, SparseCore 0:
  58.4 25.3 all-gather.2
  172.2 25.0 all-gather.4
where the time goes:
time: 263 us; the launch traced here: 260 us
  blocking collectives  145 us (55%)
  Pallas kernels  53.2 us (20%)
  waiting for transfers between devices  23.4 us (9%)
  starting transfers between devices  17.3 us (7%)
  between operations  13.6 us (5%)
  local copies, waits for them, and re-layouts  6.6 us (3%)
    all_to_all x6, blocking collectives, exchange(): return lax.all_to_all(values, axes, split_axis=0, concat_axis=0, tiled=True)  145 us
    pallas_call x2, Pallas kernels, finish(): call(functools.partial(finish_kernel, bool(then)), [out, CHUNKS, CHUNKS]...  34.8 us
    all_to_all x1, waiting for transfers between devices, exchange(): return lax.all_to_all(values, axes, split_axis=0, concat_axis=0, tiled=True)  18.5 us
    all_to_all x1, starting transfers between devices, exchange(): return lax.all_to_all(values, axes, split_axis=0, concat_axis=0, tiled=True)  13.3 us
    pallas_call x1, Pallas kernels, project(): call(project_kernel, [CHUNKS, CHUNKS], [SMEM, SMEM, VMEM, VMEM, VMEM, VME...  11.9 us
    unnamed x23, local copies, waits for them, and re-layouts  5.77 us
  transfers between devices with their start and end apart: 5, of which 4 were waited for; matrix products, arithmetic and copies ran while one was open for 0% of the time, Pallas kernels for 0%

commit v1 on v0

v1 whole, which is shorter than its diff:
```python
import functools

import jax
import jax.numpy as jnp
from jax import lax
from jax.experimental import pallas as pl
from jax.experimental.pallas import tpu as pltpu
from jax.sharding import Mesh
from jax.sharding import PartitionSpec as P

AXES = ("zl", "y", "core", "x", "zh")
SIZES = (2, 8, 2, 4, 4)
PLANE = ("zl", "y", "zh")
ROWS = 80
COLUMNS = 40
WIDTH = 128
HIDDEN = 64
X = 4
ZH = 4
SPAN = 16
EPS = 1e-05
DEPTH = 32
LANES = 128
SUB = 8
GROUPS = ((0, 32), (32, 32), (64, 16))
STRIDE = 40
BATCH = 8
CHUNKS = jax.ShapeDtypeStruct((HIDDEN, SUB, DEPTH // SUB * LANES), jnp.bfloat16)
NORMED = jax.ShapeDtypeStruct((DEPTH, LANES, WIDTH), jnp.bfloat16)
GATES = jax.ShapeDtypeStruct((DEPTH, LANES, WIDTH), jnp.float32)
VMEM = pl.BlockSpec(memory_space=pltpu.VMEM)
SMEM = pl.BlockSpec(memory_space=pltpu.SMEM)


def call(kernel, out_shape, in_specs, scratch_shapes=(), flops=10**8, moved=4 * 10**6):
    outs = jax.tree.map(lambda _: VMEM, out_shape)
    return pl.pallas_call(
        kernel,
        out_shape=out_shape,
        in_specs=in_specs,
        out_specs=outs,
        scratch_shapes=scratch_shapes,
        compiler_params=pltpu.CompilerParams(vmem_limit_bytes=40 * 2**20),
        cost_estimate=pl.CostEstimate(flops=flops, bytes_accessed=moved, transcendentals=0),
    )


def normalize(values, gain, bias):
    average = jnp.mean(values, axis=-1, keepdims=True)
    centred = values - average
    spread = jnp.mean(centred * centred, axis=-1, keepdims=True)
    return centred * lax.rsqrt(spread + EPS) * gain + bias


def batches(work):
    half = DEPTH // 2 // BATCH
    pl.loop(0, half)(lambda step: work(step * BATCH, 3))
    pl.loop(half, 2 * half)(lambda step: work(step * BATCH, 2))


def block_rows(first, count):
    return [[first + n + DEPTH * group for group in range(count)] for n in range(BATCH)]


def load_pairs(pair_ref, first, count):
    rows = [row for rows in block_rows(first, count) for row in rows]
    return jnp.concatenate([pair_ref[row].astype(jnp.float32) for row in rows], axis=0)


def pad_rows(values, count):
    size = count * COLUMNS
    empty = jnp.zeros((LANES - size, WIDTH), jnp.float32)
    return [
        jnp.concatenate([values[n * size : (n + 1) * size], empty], axis=0).astype(jnp.bfloat16)
        for n in range(BATCH)
    ]


def spread_columns(place_ref, valid_ref):
    lane = lax.broadcasted_iota(jnp.int32, (1, LANES), 1)
    inside = lane % COLUMNS
    found = jnp.zeros((1, LANES), jnp.float32)
    for column in range(COLUMNS):
        value = valid_ref[place_ref[1] + column].astype(jnp.float32)
        found = jnp.where(inside == column, value, found)
    return jnp.where(lane < 3 * COLUMNS, found, 0.0)


def mask_of(first, count, place_ref, valid_ref, columns):
    lane = lax.broadcasted_iota(jnp.int32, (1, LANES), 1)
    masks = []
    for rows in block_rows(first, count):
        mask = jnp.zeros((1, LANES), jnp.float32)
        for group, row in enumerate(rows):
            value = valid_ref[place_ref[0] + row].astype(jnp.float32)
            inside = (lane >= group * COLUMNS) & (lane < (group + 1) * COLUMNS)
            mask = jnp.where(inside, value, mask)
        masks.append(mask * columns)
    return jnp.concatenate(masks, axis=1)


def factor_rows(first, normed, weight_ref, mask, scratch):
    proj = lax.dot_general(
        weight_ref[...], normed, (((1,), (1,)), ((), ())), preferred_element_type=jnp.float32
    )
    factor = jax.nn.sigmoid(proj[HIDDEN:]) * proj[:HIDDEN] * mask
    for n in range(BATCH):
        place = pl.ds(first + n, HIDDEN, stride=STRIDE)
        scratch[place, :] = factor[:, n * LANES : (n + 1) * LANES]


def flat_chunk(values):
    return jnp.concatenate([values[n : n + SUB] for n in range(0, DEPTH, SUB)], axis=1)


def put_chunks(scratch, out_ref):
    for channel in range(HIDDEN):
        rows = scratch[pl.ds(channel * STRIDE, DEPTH), :]
        out_ref[channel] = flat_chunk(rows).astype(jnp.bfloat16)


SCRATCH = pltpu.VMEM(((HIDDEN + 1) * STRIDE, LANES), jnp.float32)


def right_kernel(
    place_ref, valid_ref, pair_ref, gain_ref, bias_ref, weight_ref, normed_ref, right_ref, right_s
):
    columns = spread_columns(place_ref, valid_ref)

    def work(first, count):
        values = load_pairs(pair_ref, first, count)
        pieces = pad_rows(normalize(values, gain_ref[...], bias_ref[...]), count)
        for n in range(BATCH):
            normed_ref[first + n] = pieces[n]
        mask = mask_of(first, count, place_ref, valid_ref, columns)
        factor_rows(first, jnp.concatenate(pieces, axis=0), weight_ref, mask, right_s)

    batches(work)
    put_chunks(right_s, right_ref)


def project_right(place, valid, pair, gain, bias, weight):
    return call(
        right_kernel, [NORMED, CHUNKS], [SMEM, SMEM, VMEM, VMEM, VMEM, VMEM], [SCRATCH]
    )(place, valid, pair, gain, bias, weight)


def load_normed(normed_ref, first):
    return normed_ref[pl.ds(first, BATCH)].reshape(BATCH * LANES, WIDTH)


def left_kernel(place_ref, valid_ref, normed_ref, weight_ref, left_ref, left_s):
    columns = spread_columns(place_ref, valid_ref)

    def work(first, count):
        mask = mask_of(first, count, place_ref, valid_ref, columns)
        factor_rows(first, load_normed(normed_ref, first), weight_ref, mask, left_s)

    batches(work)
    put_chunks(left_s, left_ref)


def project_left(place, valid, normed, weight):
    return call(left_kernel, CHUNKS, [SMEM, SMEM, VMEM, VMEM], [SCRATCH])(
        place, valid, normed, weight
    )


def gate_kernel(place_ref, chain_ref, normed_ref, gate_ref, chain_bias_ref, out_ref):
    row = lax.broadcasted_iota(jnp.int32, (COLUMNS, WIDTH), 0)
    chain_columns = jnp.full((COLUMNS, WIDTH), -1, jnp.int32)
    for column in range(COLUMNS):
        chain_columns = jnp.where(row == column, chain_ref[place_ref[1] + column], chain_columns)

    def work(first, count):
        logit = jnp.dot(
            load_normed(normed_ref, first), gate_ref[...], preferred_element_type=jnp.float32
        )
        for n, rows in enumerate(block_rows(first, count)):
            for group, row in enumerate(rows):
                same = chain_columns == chain_ref[place_ref[0] + row]
                start = n * LANES + group * COLUMNS
                out_ref[first + n, pl.ds(group * COLUMNS, COLUMNS)] = jax.nn.sigmoid(
                    logit[start : start + COLUMNS] + jnp.where(same, chain_bias_ref[...], 0.0)
                )

    batches(work)


def gates(place, chain, normed, gate, chain_bias):
    return call(gate_kernel, GATES, [SMEM, SMEM, VMEM, VMEM, VMEM])(
        place, chain, normed, gate, chain_bias
    )


def finish_kernel(
    then,
    place_ref,
    valid_ref,
    out_gain_ref,
    pair_ref,
    gates_ref,
    product_ref,
    out_weight_ref,
    *rest,
):
    if then:
        gain_ref, bias_ref, weight_ref, out_ref, normed_ref, right_ref, hidden_s, right_s = rest
        columns = spread_columns(place_ref, valid_ref)
    else:
        out_ref, hidden_s = rest

    def channel(n):
        return product_ref[n].astype(jnp.float32)

    average = channel(0)
    for n in range(1, HIDDEN):
        average = average + channel(n)
    average = average / HIDDEN
    spread = jnp.zeros_like(average)
    for n in range(HIDDEN):
        centred = channel(n) - average
        spread = spread + centred * centred
    scale = lax.rsqrt(spread / HIDDEN + EPS)
    for n in range(HIDDEN):
        hidden = (channel(n) - average) * scale * out_gain_ref[n]
        for part in range(DEPTH // SUB):
            place = pl.ds(n * STRIDE + part * SUB, SUB)
            hidden_s[place, :] = hidden[:, part * LANES : (part + 1) * LANES]

    def work(first, count):
        size = count * COLUMNS
        values = load_pairs(pair_ref, first, count)
        hidden = jnp.concatenate(
            [hidden_s[pl.ds(first + n, HIDDEN, stride=STRIDE), :] for n in range(BATCH)], axis=1
        ).astype(jnp.bfloat16)
        branch = lax.dot_general(
            hidden,
            out_weight_ref[...],
            (((0,), (0,)), ((), ())),
            preferred_element_type=jnp.float32,
        )
        branch = jnp.concatenate(
            [
                branch[n * LANES : n * LANES + size] * gates_ref[first + n, pl.ds(0, size)]
                for n in range(BATCH)
            ],
            axis=0,
        )
        new = values + branch
        places = [row for rows in block_rows(first, count) for row in rows]
        for n, row in enumerate(places):
            out_ref[row] = new[n * COLUMNS : (n + 1) * COLUMNS].astype(jnp.bfloat16)
        if then:
            new = new.astype(jnp.bfloat16).astype(jnp.float32)
            pieces = pad_rows(normalize(new, gain_ref[...], bias_ref[...]), count)
            for n in range(BATCH):
                normed_ref[first + n] = pieces[n]
            mask = mask_of(first, count, place_ref, valid_ref, columns)
            factor_rows(first, jnp.concatenate(pieces, axis=0), weight_ref, mask, right_s)

    batches(work)
    if then:
        put_chunks(right_s, right_ref)


def finish(place, valid, out_gain, pair, gate, product, out_weight, then=()):
    out = jax.ShapeDtypeStruct(pair.shape, pair.dtype)
    return call(
        functools.partial(finish_kernel, bool(then)),
        [out, NORMED, CHUNKS] if then else [out],
        [SMEM] * 3 + [VMEM] * (4 + len(then)),
        [SCRATCH] * (2 if then else 1),
    )(place, valid, out_gain, pair, gate, product, out_weight, *then)


def gather_rows(chunks_ref, zh, group, part):
    start = part * LANES + group * COLUMNS
    return jnp.concatenate(
        [
            chunks_ref[span * ZH + zh].astype(jnp.float32)[:, start : start + COLUMNS]
            for span in range(SPAN)
        ],
        axis=1,
    )


def assemble_into(chunks_ref, put):
    for zh in range(ZH):
        for group, (start, size) in enumerate(GROUPS):
            for part in range(0, size // SUB, 2):
                rows = [gather_rows(chunks_ref, zh, group, part + n) for n in range(2)]
                put(zh * ROWS + start + part * SUB, jnp.concatenate(rows, axis=0))


def assemble_kernel(chunks_ref, out_ref):
    def put(start, values):
        out_ref[pl.ds(start, 2 * SUB), :] = values.astype(jnp.bfloat16)

    assemble_into(chunks_ref, put)


def assemble(chunks):
    out = jax.ShapeDtypeStruct((ZH * ROWS, SPAN * COLUMNS), jnp.bfloat16)
    return call(assemble_kernel, out, [VMEM])(chunks)


def assemble_turned_kernel(chunks_ref, out_ref, whole):
    def put(start, values):
        whole[pl.ds(start, 2 * SUB), :] = values

    assemble_into(chunks_ref, put)
    whole[pl.ds(ZH * ROWS, 64), :] = jnp.zeros((64, SPAN * COLUMNS), jnp.float32)
    for part in range(SPAN * COLUMNS // 128):
        turned = whole[:, part * 128 : (part + 1) * 128].T
        out_ref[pl.ds(part * 128, 128), :] = turned[:, : ZH * ROWS].astype(jnp.bfloat16)


def assemble_turned(chunks):
    out = jax.ShapeDtypeStruct((SPAN * COLUMNS, ZH * ROWS), jnp.bfloat16)
    scratch = [pltpu.VMEM((ZH * ROWS + 64, SPAN * COLUMNS), jnp.float32)]
    return call(assemble_turned_kernel, out, [VMEM], scratch)(chunks)


def chunk_of(total, zh, start):
    pieces = []
    for first, size in GROUPS:
        piece = total[pl.ds(zh * ROWS + first, size), :][:, start : start + COLUMNS]
        if size < DEPTH:
            piece = jnp.concatenate(
                [piece, jnp.zeros((DEPTH - size, COLUMNS), jnp.float32)], axis=0
            )
        pieces.append(piece)
    pieces.append(jnp.zeros((DEPTH, LANES - 3 * COLUMNS), jnp.float32))
    return flat_chunk(jnp.concatenate(pieces, axis=1)).astype(jnp.bfloat16)


def outgoing_kernel(core_ref, left_ref, right_ref, out_ref, left_s, total):
    assemble_kernel(left_ref, left_s)
    for x in range(X):
        total[:, x * ZH * ROWS : (x + 1) * ZH * ROWS] = lax.dot_general(
            left_s[...],
            right_ref[pl.ds(x * ZH * ROWS, ZH * ROWS), :],
            (((1,), (1,)), ((), ())),
            preferred_element_type=jnp.float32,
        )
    for half in range(2):
        slot = lax.rem(core_ref[0] + half, 2)
        for span in range(SPAN):
            for zh in range(ZH):
                out_ref[slot, span * ZH + zh] = chunk_of(total, zh, (2 * span + half) * COLUMNS)


def outgoing(core, left, right):
    out = jax.ShapeDtypeStruct((2,) + CHUNKS.shape, jnp.bfloat16)
    scratch = [
        pltpu.VMEM((ZH * ROWS, SPAN * COLUMNS), jnp.bfloat16),
        pltpu.VMEM((ZH * ROWS, X * ZH * ROWS), jnp.float32),
    ]
    return call(outgoing_kernel, out, [SMEM, VMEM, VMEM], scratch, 6 * 10**8)(core, left, right)


def incoming_kernel(core_ref, own_ref, other_ref, right_ref, out_ref, total):
    for n, left_ref in enumerate((own_ref, other_ref)):
        side = lax.rem(core_ref[0] + n, 2)
        product = jnp.zeros((ZH * COLUMNS, SPAN * COLUMNS), jnp.float32)
        for x in range(X):
            product = product + jnp.dot(
                left_ref[x],
                right_ref[pl.ds(x * ZH * ROWS, ZH * ROWS), :],
                preferred_element_type=jnp.float32,
            )
        for zh in range(ZH):
            start = pl.multiple_of(zh * ROWS + side * COLUMNS, 8)
            total[pl.ds(start, COLUMNS), :] = product[zh * COLUMNS : (zh + 1) * COLUMNS]
    for span in range(SPAN):
        for zh in range(ZH):
            out_ref[span * ZH + zh] = chunk_of(total, zh, span * COLUMNS)


def incoming(core, own, other, right):
    scratch = [pltpu.VMEM((ZH * ROWS, SPAN * COLUMNS), jnp.float32)]
    return call(incoming_kernel, CHUNKS, [SMEM, VMEM, VMEM, VMEM], scratch, 6 * 10**8)(
        core, own, other, right
    )


def exchange(values, axes):
    return lax.all_to_all(values, axes, split_axis=0, concat_axis=0, tiled=True)


def swap_cores(values):
    return lax.ppermute(values, "core", [(0, 1), (1, 0)])


def body(
    pair_acts,
    residue_valid,
    chain_index,
    norm_gain,
    norm_bias,
    projection,
    gate_weight,
    chain_bias,
    out_gain,
    out_weight,
):
    row_start = (lax.axis_index("x") * ZH + lax.axis_index("zh")) * ROWS
    core_index = lax.axis_index("core")
    column_block = (lax.axis_index("zl") * 8 + lax.axis_index("y")) * 2 + core_index
    place = jnp.stack([row_start, column_block * COLUMNS]).astype(jnp.int32)
    core = core_index.reshape(1).astype(jnp.int32)
    turned = projection.transpose(0, 2, 1)

    normed, right = project_right(
        place, residue_valid, pair_acts, norm_gain[:1], norm_bias[:1], turned[0, 2 * HIDDEN :]
    )
    right = assemble(exchange(right, PLANE))
    right = lax.all_gather(right, "x", axis=0, tiled=True)
    left = project_left(place, residue_valid, normed, turned[0, : 2 * HIDDEN])
    gate = gates(place, chain_index, normed, gate_weight[0], chain_bias[:1])
    halves = outgoing(core, exchange(left, PLANE), right)
    total = halves[0].astype(jnp.float32) + swap_cores(halves[1]).astype(jnp.float32)
    product = exchange(total.astype(jnp.bfloat16), PLANE)
    middle, normed, right = finish(
        place,
        residue_valid,
        out_gain[0],
        pair_acts,
        gate,
        product,
        out_weight[0],
        (norm_gain[1:], norm_bias[1:], turned[1, 2 * HIDDEN :]),
    )
    right = assemble(exchange(right, PLANE))
    right = lax.all_gather(right, "x", axis=0, tiled=True)
    left = project_left(place, residue_valid, normed, turned[1, : 2 * HIDDEN])
    gate = gates(place, chain_index, normed, gate_weight[1], chain_bias[1:])
    left = assemble_turned(exchange(left, PLANE)).reshape(X, ZH * COLUMNS, ZH * ROWS)
    left = exchange(left, "x")
    product = exchange(incoming(core, left, swap_cores(left), right), PLANE)
    return finish(
        place, residue_valid, out_gain[1], middle, gate, product, out_weight[1]
    )[0]


def solution(mesh):
    fine = Mesh(mesh.devices.reshape(SIZES), AXES)
    pairs = P(("x", "zh"), ("zl", "y", "core"), None)
    placed = (pairs, P(), P(), P(), P(), P(), P(), P(), P(), P())
    return jax.shard_map(body, mesh=fine, in_specs=placed, out_specs=pairs, check_vma=False)
```

time: 263 us -> 232 us (0.88)
  Pallas kernels: 53.2 us -> 24.5 us
  blocking collectives: 145 us -> 118 us
  waiting for transfers between devices: 23.4 us -> 37.6 us
  starting transfers between devices: 17.3 us -> 24.1 us
  local copies, waits for them, and re-layouts: 6.6 us -> 9.77 us
    pallas_call x3 -> x7, Pallas kernels: 46.8 us -> 17.3 us  [the longest x2 8.07 us: finish(): call(functools.partial(finish_kernel, bool(then)), [out, NORMED, CHUNKS]...]
    all_to_all x6 -> x5, blocking collectives: 145 us -> 118 us  [exchange(): return lax.all_to_all(values, axes, split_axis=0, concat_axis=0, tiled=True)]
    all_to_all x1 -> x2, waiting for transfers between devices: 18.5 us -> 33.8 us  [exchange(): return lax.all_to_all(values, axes, split_axis=0, concat_axis=0, tiled=True)]
    all_to_all x1 -> x2, starting transfers between devices: 13.3 us -> 20.3 us  [exchange(): return lax.all_to_all(values, axes, split_axis=0, concat_axis=0, tiled=True)]
    unnamed x23 -> x27, local copies, waits for them, and re-layouts: 5.77 us -> 8.94 us
  transfers between devices with their start and end apart: 5 -> 6, of which waited for: 4 -> 4; matrix products, arithmetic and copies ran while one was open for 0% -> 0% of each run, Pallas kernels for 0% -> 3%
where the time goes in v1:
time: 232 us; the launch traced here: 229 us
  blocking collectives  118 us (51%)
  waiting for transfers between devices  37.6 us (16%)
  Pallas kernels  24.5 us (11%)
  starting transfers between devices  24.1 us (10%)
  between operations  13.7 us (6%)
  local copies, waits for them, and re-layouts  9.77 us (4%)
    all_to_all x5, blocking collectives, exchange(): return lax.all_to_all(values, axes, split_axis=0, concat_axis=0, tiled=True)  118 us
    all_to_all x2, waiting for transfers between devices, exchange(): return lax.all_to_all(values, axes, split_axis=0, concat_axis=0, tiled=True)  33.8 us
    all_to_all x2, starting transfers between devices, exchange(): return lax.all_to_all(values, axes, split_axis=0, concat_axis=0, tiled=True)  20.3 us
    unnamed x27, local copies, waits for them, and re-layouts  8.94 us
    pallas_call x2, Pallas kernels, finish(): call(functools.partial(finish_kernel, bool(then)), [out, NORMED, CHUNKS]...  8.07 us
  transfers between devices with their start and end apart: 6, of which 4 were waited for; matrix products, arithmetic and copies ran while one was open for 0% of the time, Pallas kernels for 3%

profile of v1, /device:TPU:6, one launch (start us, length us, event | category | flops | bytes accessed | tf_op | source)
XLA Modules:
  0.0 228.8 jit_solution(2204387685995750254)
XLA Ops:
  10.3 2.8 %shard_map.100 = (bf16[32,128,128]{2,1,0:T(8,128)(2,1)S(1)}, bf16[64,8,512]{2,1,0:T(8,128)(2,1)S(1)}) custom-call(s32[2]{0:T(128)S(1)} %pad_add_fusion.place_ref, s32[1280]{0:T(1024)S(1)} %copy-done.6, bf16[80,40,128]{2,1,0:T(8,128)(2,1)S(1)} %copy-done, f32[1,128]{1,0:T(1,128)S(1)} %get-tuple-element.31.gain_ref, f32[1,128]{1,0:T(1,128)S(1)} %get-tuple-element.26.bias_ref, ...), custom_call_target="tpu_custom_call" | custom-call | flops 100000000 | bytes 4000000 | tf_op jit(solution)/shard_map/pallas_call | solution.py:143
  13.1 34.8 %all_to_all.35.chunks_ref = bf16[64,8,512]{2,1,0:T(8,128)(2,1)S(1)} all-to-all(bf16[64,8,512]{2,1,0:T(8,128)(2,1)S(1)} %get-tuple-element.11), channel_id=1, replica_groups=mesh['zl'=2,'y'=8,'core'=2,'x'=4,'zh'=4] {'zl','y','zh'}, dimensions={0} | all-to-all | bytes 1048576 | tf_op jit(solution)/shard_map/all_to_all | solution.py:389
  49.1 1.7 shard_map.102
  50.8 24.3 %all_to_all.36.left_ref = bf16[64,8,512]{2,1,0:T(8,128)(2,1)S(1)} all-to-all(bf16[64,8,512]{2,1,0:T(8,128)(2,1)S(1)} %shard_map.102), channel_id=1, replica_groups=mesh['zl'=2,'y'=8,'core'=2,'x'=4,'zh'=4] {'zl','y','zh'}, dimensions={0} | all-to-all | bytes 1048576 | tf_op jit(solution)/shard_map/all_to_all | solution.py:389
  75.2 1.4 copy-done.3
  76.6 1.9 shard_map.104
  78.6 1.9 collective-permute-start
  80.5 1.9 collective-permute-done
  83.3 13.1 %all-to-all-start.2 = ((bf16[64,8,512]{2,1,0:T(8,128)(2,1)}), bf16[64,8,512]{2,1,0:T(8,128)(2,1)}, u32[]{:S(2)}, u32[]{:S(2)}) async-start(bf16[64,8,512]{2,1,0:T(8,128)(2,1)} %fusion), calls=%async_computation.2 | async-start | bytes 1048576 | tf_op jit(solution)/shard_map/all_to_all | solution.py:389
  96.6 1.5 shard_map.101.gates_ref
  98.1 16.8 %all-to-all-done.2.product_ref = bf16[64,8,512]{2,1,0:T(8,128)(2,1)} async-done(((bf16[64,8,512]{2,1,0:T(8,128)(2,1)}), bf16[64,8,512]{2,1,0:T(8,128)(2,1)}, u32[]{:S(2)}, u32[]{:S(2)}) %all-to-all-start.2) | async-done | bytes 524320 | tf_op jit(solution)/shard_map/all_to_all | solution.py:389
  116.1 4.6 %shard_map.105 = (bf16[80,40,128]{2,1,0:T(8,128)(2,1)S(1)}, bf16[32,128,128]{2,1,0:T(8,128)(2,1)S(1)}, bf16[64,8,512]{2,1,0:T(8,128)(2,1)S(1)}) custom-call(s32[2]{0:T(128)S(1)} %pad_add_fusion.place_ref, s32[1280]{0:T(1024)S(1)} %copy-done.7, f32[64]{0:T(128)S(1)} %get-tuple-element.29.out_gain_ref, bf16[80,40,128]{2,1,0:T(8,128)(2,1)S(1)} %copy-done.1, ...), custom_call_target="tpu_custom_call" | custom-call | flops 100000000 | bytes 4000000 | tf_op jit(solution)/shard_map/pallas_call | solution.py:269
  121.6 24.6 %all_to_all.37.chunks_ref = bf16[64,8,512]{2,1,0:T(8,128)(2,1)S(1)} all-to-all(bf16[64,8,512]{2,1,0:T(8,128)(2,1)S(1)} %get-tuple-element.14), channel_id=1, replica_groups=mesh['zl'=2,'y'=8,'core'=2,'x'=4,'zh'=4] {'zl','y','zh'}, dimensions={0} | all-to-all | bytes 1048576 | tf_op jit(solution)/shard_map/all_to_all | solution.py:389
  147.4 1.7 shard_map.107
  149.1 24.1 %all_to_all.38.chunks_ref = bf16[64,8,512]{2,1,0:T(8,128)(2,1)S(1)} all-to-all(bf16[64,8,512]{2,1,0:T(8,128)(2,1)S(1)} %shard_map.107), channel_id=1, replica_groups=mesh['zl'=2,'y'=8,'core'=2,'x'=4,'zh'=4] {'zl','y','zh'}, dimensions={0} | all-to-all | bytes 1048576 | tf_op jit(solution)/shard_map/all_to_all | solution.py:389
  173.7 10.3 %all_to_all.39.own_ref = bf16[4,160,320]{2,1,0:T(8,128)(2,1)S(1)} all-to-all(bf16[4,160,320]{2,1,0:T(8,128)(2,1)S(1)} %bitcast.32), channel_id=1, replica_groups=mesh['zl'=2,'y'=8,'core'=2,'x'=4,'zh'=4] {'x'}, dimensions={0} | all-to-all | bytes 819200 | tf_op jit(solution)/shard_map/all_to_all | solution.py:389
  184.0 1.9 collective-permute-start.1
  186.0 1.8 collective-permute-done.1.other_ref
  187.8 1.4 copy-done.2
  189.2 2.4 %shard_map.110 = bf16[64,8,512]{2,1,0:T(8,128)(2,1)} custom-call(s32[1]{0:T(128)} %bitcast.7.core_ref, bf16[4,160,320]{2,1,0:T(8,128)(2,1)S(1)} %all_to_all.39.own_ref, bf16[4,160,320]{2,1,0:T(8,128)(2,1)S(1)} %collective-permute-done.1.other_ref, bf16[1280,640]{1,0:T(8,128)(2,1)S(1)} %copy-done.2), custom_call_target="tpu_custom_call" | custom-call | flops 600000000 | bytes 4000000 | tf_op jit(solution)/shard_map/pallas_call | solution.py:383
  191.6 7.2 %all-to-all-start.6 = ((bf16[64,8,512]{2,1,0:T(8,128)(2,1)}), bf16[64,8,512]{2,1,0:T(8,128)(2,1)}, u32[]{:S(2)}, u32[]{:S(2)}) async-start(bf16[64,8,512]{2,1,0:T(8,128)(2,1)} %shard_map.110), calls=%async_computation.6 | async-start | bytes 1048576 | tf_op jit(solution)/shard_map/all_to_all | solution.py:389
  198.8 1.5 shard_map.106.gates_ref
  200.3 17.0 %all-to-all-done.6.product_ref = bf16[64,8,512]{2,1,0:T(8,128)(2,1)} async-done(((bf16[64,8,512]{2,1,0:T(8,128)(2,1)}), bf16[64,8,512]{2,1,0:T(8,128)(2,1)}, u32[]{:S(2)}, u32[]{:S(2)}) %all-to-all-start.6) | async-done | bytes 524320 | tf_op jit(solution)/shard_map/all_to_all | solution.py:389
  218.5 3.4 %shard_map.111 = bf16[80,40,128]{2,1,0:T(8,128)(2,1)} custom-call(s32[2]{0:T(128)S(1)} %pad_add_fusion.place_ref, s32[1280]{0:T(1024)S(1)} %copy-done.7, f32[64]{0:T(128)S(1)} %get-tuple-element.30.out_gain_ref, bf16[80,40,128]{2,1,0:T(8,128)(2,1)S(1)} %copy-done.5, f32[32,128,128]{2,1,0:T(8,128)S(1)} %shard_map.106.gates_ref, ...), custom_call_target="tpu_custom_call" | custom-call | flops 100000000 | bytes 4000000 | tf_op jit(solution)/shard_map/pallas_call | solution.py:269
  (43 shorter events, 10.8 us)
Async XLA Ops:
  6.5 42.6 %copy-start.7 = (s32[1280]{0:T(1024)S(1)}, s32[1280]{0:T(1024)}, u32[]{:S(2)}) copy-start(s32[1280]{0:T(1024)} %valid_ref.9) | copy-start | bytes 15364
  6.5 68.6 %all-gather.3.cloned.1.call-start = ((), (), s32[]{:S(2)}) async-start(), calls=%async_computation.7 | async-start | bytes 2048000 | tf_op jit(solution)/shard_map/all_gather | solution.py:419
  8.5 1.1 copy-start
  9.6 0.7 copy-start.6
  75.2 1.4 copy-start.3
  78.5 18.0 %copy-start.11 = (f32[2,128]{1,0:T(2,128)S(1)}, f32[2,128]{1,0:T(2,128)}, u32[]{:S(2)}) copy-start(f32[2,128]{1,0:T(2,128)} %param.17) | copy-start | bytes 3076
  78.5 18.0 %copy-start.9 = (bf16[2,128,128]{2,1,0:T(8,128)(2,1)S(1)}, bf16[2,128,128]{2,1,0:T(8,128)(2,1)}, u32[]{:S(2)}) copy-start(bf16[2,128,128]{2,1,0:T(8,128)(2,1)} %param.16) | copy-start | bytes 196612
  78.5 18.0 %copy-start.8 = (s32[1280]{0:T(1024)S(1)}, s32[1280]{0:T(1024)}, u32[]{:S(2)}) copy-start(s32[1280]{0:T(1024)} %chain_ref.3) | copy-start | bytes 15364
  78.6 3.8 %collective-permute-start = (bf16[64,8,512]{2,1,0:T(8,128)(2,1)S(1)}, bf16[64,8,512]{2,1,0:T(8,128)(2,1)S(1)}, u32[]{:S(2)}, u32[]{:S(2)}) collective-permute-start(bf16[64,8,512]{2,1,0:T(8,128)(2,1)S(1)} %slice_bitcast_fusion), channel_id=1, source_target_pairs={{0,16},{16,0},{1,17},{17,1},{2,18},{18,2},{3,19},{19,3},{4,20},{20... | collective-permute-start | bytes 1572872 | tf_op jit(solution)/shard_map/ppermute | solution.py:393
  83.3 14.8 %copy-start.12 = (f32[2,64]{1,0:T(2,128)S(1)}, f32[2,64]{1,0:T(2,128)}, u32[]{:S(2)}) copy-start(f32[2,64]{1,0:T(2,128)} %param.18) | copy-start | bytes 1540
  83.3 14.8 %copy-start.10 = (bf16[2,64,128]{2,1,0:T(8,128)(2,1)S(1)}, bf16[2,64,128]{2,1,0:T(8,128)(2,1)}, u32[]{:S(2)}) copy-start(bf16[2,64,128]{2,1,0:T(8,128)(2,1)} %param.19) | copy-start | bytes 98308
  83.3 31.6 %all-to-all-start.2 = ((bf16[64,8,512]{2,1,0:T(8,128)(2,1)}), bf16[64,8,512]{2,1,0:T(8,128)(2,1)}, u32[]{:S(2)}, u32[]{:S(2)}) async-start(bf16[64,8,512]{2,1,0:T(8,128)(2,1)} %fusion), calls=%async_computation.2 | async-start | bytes 1048576 | tf_op jit(solution)/shard_map/all_to_all | solution.py:389
  96.4 91.3 %all-gather.5.cloned.1.call-start = ((), (), s32[]{:S(2)}) async-start(), calls=%async_computation.8 | async-start | bytes 2048000 | tf_op jit(solution)/shard_map/all_gather | solution.py:436
  115.0 1.1 copy-start.1
  120.7 0.9 copy-start.4
  184.0 3.7 %collective-permute-start.1 = (bf16[4,160,320]{2,1,0:T(8,128)(2,1)S(1)}, bf16[4,160,320]{2,1,0:T(8,128)(2,1)S(1)}, u32[]{:S(2)}, u32[]{:S(2)}) collective-permute-start(bf16[4,160,320]{2,1,0:T(8,128)(2,1)S(1)} %all_to_all.39.own_ref), channel_id=1, source_target_pairs={{0,16},{16,0},{1,17},{17,1},{2,18},{18,2},{3,19},{19,3},{4,20},{20... | collective-permute-start | bytes 1228808 | tf_op jit(solution)/shard_map/ppermute | solution.py:393
  187.8 1.4 copy-start.2
  191.6 25.7 %all-to-all-start.6 = ((bf16[64,8,512]{2,1,0:T(8,128)(2,1)}), bf16[64,8,512]{2,1,0:T(8,128)(2,1)}, u32[]{:S(2)}, u32[]{:S(2)}) async-start(bf16[64,8,512]{2,1,0:T(8,128)(2,1)} %shard_map.110), calls=%async_computation.6 | async-start | bytes 1048576 | tf_op jit(solution)/shard_map/all_to_all | solution.py:389
  217.3 1.1 copy-start.5
Sparse Core Ops, SparseCore 0:
  49.2 25.3 all-gather.2
  147.5 25.0 all-gather.4

commit v2 on v1

--- a/solution.py
+++ b/solution.py
@@ -10,7 +10,7 @@
 
 AXES = ("zl", "y", "core", "x", "zh")
 SIZES = (2, 8, 2, 4, 4)
-PLANE = ("zl", "y", "zh")
+PLANE = ("y", "zh", "zl")
 ROWS = 80
 COLUMNS = 40
 WIDTH = 128
@@ -29,11 +29,18 @@
 NORMED = jax.ShapeDtypeStruct((DEPTH, LANES, WIDTH), jnp.bfloat16)
 GATES = jax.ShapeDtypeStruct((DEPTH, LANES, WIDTH), jnp.float32)
 VMEM = pl.BlockSpec(memory_space=pltpu.VMEM)
+ANY = pl.BlockSpec(memory_space=pl.ANY)
 SMEM = pl.BlockSpec(memory_space=pltpu.SMEM)
 
 
-def call(kernel, out_shape, in_specs, scratch_shapes=(), flops=10**8, moved=4 * 10**6):
-    outs = jax.tree.map(lambda _: VMEM, out_shape)
+def spot(span, zh):
+    zl, y = divmod(span, 8)
+    return (y * ZH + zh) * 2 + zl
+
+
+def call(kernel, out_shape, in_specs, scratch_shapes=(), flops=10**8, outs=None):
+    outs = outs or jax.tree.map(lambda _: VMEM, out_shape)
+    moved = 4 * 10**6
     return pl.pallas_call(
         kernel,
         out_shape=out_shape,
@@ -99,9 +106,14 @@
     return jnp.concatenate(masks, axis=1)
 
 
-def factor_rows(first, normed, weight_ref, mask, scratch):
+def weight_of(weight_ref, which, start):
+    columns = weight_ref[which][:, start : start + 2 * HIDDEN]
+    return columns.astype(jnp.float32).T.astype(jnp.bfloat16)
+
+
+def factor_rows(first, normed, weight, mask, scratch):
     proj = lax.dot_general(
-        weight_ref[...], normed, (((1,), (1,)), ((), ())), preferred_element_type=jnp.float32
+        weight, normed, (((1,), (1,)), ((), ())), preferred_element_type=jnp.float32
     )
     factor = jax.nn.sigmoid(proj[HIDDEN:]) * proj[:HIDDEN] * mask
     for n in range(BATCH):
@@ -126,14 +138,15 @@
     place_ref, valid_ref, pair_ref, gain_ref, bias_ref, weight_ref, normed_ref, right_ref, right_s
 ):
     columns = spread_columns(place_ref, valid_ref)
+    weight = weight_of(weight_ref, 0, 2 * HIDDEN)
 
     def work(first, count):
         values = load_pairs(pair_ref, first, count)
-        pieces = pad_rows(normalize(values, gain_ref[...], bias_ref[...]), count)
+        pieces = pad_rows(normalize(values, gain_ref[0:1], bias_ref[0:1]), count)
         for n in range(BATCH):
             normed_ref[first + n] = pieces[n]
         mask = mask_of(first, count, place_ref, valid_ref, columns)
-        factor_rows(first, jnp.concatenate(pieces, axis=0), weight_ref, mask, right_s)
+        factor_rows(first, jnp.concatenate(pieces, axis=0), weight, mask, right_s)
 
     batches(work)
     put_chunks(right_s, right_ref)
@@ -149,52 +162,112 @@
     return normed_ref[pl.ds(first, BATCH)].reshape(BATCH * LANES, WIDTH)
 
 
-def left_kernel(place_ref, valid_ref, normed_ref, weight_ref, left_ref, left_s):
+def left_work(which, place_ref, valid_ref, normed_ref, weight_ref, left_s):
     columns = spread_columns(place_ref, valid_ref)
+    weight = weight_of(weight_ref, which, 0)
 
     def work(first, count):
         mask = mask_of(first, count, place_ref, valid_ref, columns)
-        factor_rows(first, load_normed(normed_ref, first), weight_ref, mask, left_s)
-
-    batches(work)
-    put_chunks(left_s, left_ref)
-
-
-def project_left(place, valid, normed, weight):
-    return call(left_kernel, CHUNKS, [SMEM, SMEM, VMEM, VMEM], [SCRATCH])(
-        place, valid, normed, weight
-    )
-
-
-def gate_kernel(place_ref, chain_ref, normed_ref, gate_ref, chain_bias_ref, out_ref):
+        factor_rows(first, load_normed(normed_ref, first), weight, mask, left_s)
+
+    return work
+
+
+def gate_work(which, place_ref, chain_ref, normed_ref, gate_ref, chain_bias_ref, out_ref):
     row = lax.broadcasted_iota(jnp.int32, (COLUMNS, WIDTH), 0)
     chain_columns = jnp.full((COLUMNS, WIDTH), -1, jnp.int32)
     for column in range(COLUMNS):
         chain_columns = jnp.where(row == column, chain_ref[place_ref[1] + column], chain_columns)
+    offset = chain_bias_ref[which : which + 1]
 
     def work(first, count):
         logit = jnp.dot(
-            load_normed(normed_ref, first), gate_ref[...], preferred_element_type=jnp.float32
+            load_normed(normed_ref, first), gate_ref[which], preferred_element_type=jnp.float32
         )
         for n, rows in enumerate(block_rows(first, count)):
             for group, row in enumerate(rows):
                 same = chain_columns == chain_ref[place_ref[0] + row]
                 start = n * LANES + group * COLUMNS
                 out_ref[first + n, pl.ds(group * COLUMNS, COLUMNS)] = jax.nn.sigmoid(
-                    logit[start : start + COLUMNS] + jnp.where(same, chain_bias_ref[...], 0.0)
+                    logit[start : start + COLUMNS] + jnp.where(same, offset, 0.0)
                 )
 
+    return work
+
+
+def left_kernel(which, place_ref, valid_ref, normed_ref, weight_ref, left_ref, left_s):
+    batches(left_work(which, place_ref, valid_ref, normed_ref, weight_ref, left_s))
+    put_chunks(left_s, left_ref)
+
+
+def project_left(which, place, valid, normed, weight):
+    kernel = functools.partial(left_kernel, which)
+    return call(kernel, CHUNKS, [SMEM, SMEM, VMEM, VMEM], [SCRATCH])(place, valid, normed, weight)
+
+
+def gate_kernel(
+    which,
+    place_ref,
+    chain_ref,
+    normed_ref,
+    gate_ref,
+    chain_bias_ref,
+    pair_ref,
+    out_ref,
+    kept_ref,
+    sem,
+):
+    keep = pltpu.make_async_copy(pair_ref, kept_ref, sem)
+    keep.start()
+    batches(
+        gate_work(which, place_ref, chain_ref, normed_ref, gate_ref, chain_bias_ref, out_ref)
+    )
+    keep.wait()
+
+
+def gates(which, place, chain, normed, gate, chain_bias, pair):
+    kernel = functools.partial(gate_kernel, which)
+    return call(
+        kernel,
+        [GATES, jax.ShapeDtypeStruct(pair.shape, pair.dtype)],
+        [SMEM, SMEM, VMEM, VMEM, VMEM, ANY],
+        [pltpu.SemaphoreType.DMA],
+    )(place, chain, normed, gate, chain_bias, pair)
+
+
+def left_and_gate_kernel(
+    which,
+    place_ref,
+    valid_ref,
+    chain_ref,
+    normed_ref,
+    weight_ref,
+    gate_ref,
+    chain_bias_ref,
+    left_ref,
+    out_ref,
+    left_s,
+):
+    left = left_work(which, place_ref, valid_ref, normed_ref, weight_ref, left_s)
+    gate = gate_work(which, place_ref, chain_ref, normed_ref, gate_ref, chain_bias_ref, out_ref)
+
+    def work(first, count):
+        left(first, count)
+        gate(first, count)
+
     batches(work)
-
-
-def gates(place, chain, normed, gate, chain_bias):
-    return call(gate_kernel, GATES, [SMEM, SMEM, VMEM, VMEM, VMEM])(
-        place, chain, normed, gate, chain_bias
+    put_chunks(left_s, left_ref)
+
+
+def left_and_gates(which, place, valid, chain, normed, weight, gate, chain_bias):
+    kernel = functools.partial(left_and_gate_kernel, which)
+    return call(kernel, [CHUNKS, GATES], [SMEM] * 3 + [VMEM] * 4, [SCRATCH])(
+        place, valid, chain, normed, weight, gate, chain_bias
     )
 
 
 def finish_kernel(
-    then,
+    which,
     place_ref,
     valid_ref,
     out_gain_ref,
@@ -204,11 +277,15 @@
     out_weight_ref,
     *rest,
 ):
+    then = which == 0
     if then:
-        gain_ref, bias_ref, weight_ref, out_ref, normed_ref, right_ref, hidden_s, right_s = rest
+        gain_ref, bias_ref, weight_ref, out_ref, normed_ref, right_ref = rest[:6]
+        hidden_s, right_s = rest[6:]
+        new_s = out_ref
         columns = spread_columns(place_ref, valid_ref)
+        weight = weight_of(weight_ref, 1, 2 * HIDDEN)
     else:
-        out_ref, hidden_s = rest
+        out_ref, hidden_s, new_s, out_sem = rest
 
     def channel(n):
         return product_ref[n].astype(jnp.float32)
@@ -223,7 +300,7 @@
         spread = spread + centred * centred
     scale = lax.rsqrt(spread / HIDDEN + EPS)
     for n in range(HIDDEN):
-        hidden = (channel(n) - average) * scale * out_gain_ref[n]
+        hidden = (channel(n) - average) * scale * out_gain_ref[which, n]
         for part in range(DEPTH // SUB):
             place = pl.ds(n * STRIDE + part * SUB, SUB)
             hidden_s[place, :] = hidden[:, part * LANES : (part + 1) * LANES]
@@ -236,7 +313,7 @@
         ).astype(jnp.bfloat16)
         branch = lax.dot_general(
             hidden,
-            out_weight_ref[...],
+            out_weight_ref[which],
             (((0,), (0,)), ((), ())),
             preferred_element_type=jnp.float32,
         )
@@ -250,27 +327,35 @@
         new = values + branch
         places = [row for rows in block_rows(first, count) for row in rows]
         for n, row in enumerate(places):
-            out_ref[row] = new[n * COLUMNS : (n + 1) * COLUMNS].astype(jnp.bfloat16)
+            new_s[row] = new[n * COLUMNS : (n + 1) * COLUMNS].astype(jnp.bfloat16)
+        if not then:
+            for group in range(count):
+                span = pl.ds(first + DEPTH * group, BATCH)
+                pltpu.make_async_copy(new_s.at[span], out_ref.at[span], out_sem).start()
         if then:
             new = new.astype(jnp.bfloat16).astype(jnp.float32)
-            pieces = pad_rows(normalize(new, gain_ref[...], bias_ref[...]), count)
+            pieces = pad_rows(normalize(new, gain_ref[1:2], bias_ref[1:2]), count)
             for n in range(BATCH):
                 normed_ref[first + n] = pieces[n]
             mask = mask_of(first, count, place_ref, valid_ref, columns)
-            factor_rows(first, jnp.concatenate(pieces, axis=0), weight_ref, mask, right_s)
+            factor_rows(first, jnp.concatenate(pieces, axis=0), weight, mask, right_s)
 
     batches(work)
     if then:
         put_chunks(right_s, right_ref)
-
-
-def finish(place, valid, out_gain, pair, gate, product, out_weight, then=()):
+    else:
+        pltpu.make_async_copy(new_s, out_ref, out_sem).wait()
+
+
+def finish(which, place, valid, out_gain, pair, gate, product, out_weight, then=()):
     out = jax.ShapeDtypeStruct(pair.shape, pair.dtype)
+    last = [pltpu.VMEM(pair.shape, pair.dtype), pltpu.SemaphoreType.DMA]
     return call(
-        functools.partial(finish_kernel, bool(then)),
+        functools.partial(finish_kernel, which),
         [out, NORMED, CHUNKS] if then else [out],
         [SMEM] * 3 + [VMEM] * (4 + len(then)),
-        [SCRATCH] * (2 if then else 1),
+        [SCRATCH] + ([SCRATCH] if then else last),
+        outs=None if then else [ANY],
     )(place, valid, out_gain, pair, gate, product, out_weight, *then)
 
 
@@ -278,7 +363,7 @@
     start = part * LANES + group * COLUMNS
     return jnp.concatenate(
         [
-            chunks_ref[span * ZH + zh].astype(jnp.float32)[:, start : start + COLUMNS]
+            chunks_ref[spot(span, zh)].astype(jnp.float32)[:, start : start + COLUMNS]
             for span in range(SPAN)
         ],
         axis=1,
@@ -348,7 +433,7 @@
         slot = lax.rem(core_ref[0] + half, 2)
         for span in range(SPAN):
             for zh in range(ZH):
-                out_ref[slot, span * ZH + zh] = chunk_of(total, zh, (2 * span + half) * COLUMNS)
+                out_ref[slot, spot(span, zh)] = chunk_of(total, zh, (2 * span + half) * COLUMNS)
 
 
 def outgoing(core, left, right):
@@ -375,7 +460,7 @@
             total[pl.ds(start, COLUMNS), :] = product[zh * COLUMNS : (zh + 1) * COLUMNS]
     for span in range(SPAN):
         for zh in range(ZH):
-            out_ref[span * ZH + zh] = chunk_of(total, zh, span * COLUMNS)
+            out_ref[spot(span, zh)] = chunk_of(total, zh, span * COLUMNS)
 
 
 def incoming(core, own, other, right):
@@ -410,38 +495,37 @@
     column_block = (lax.axis_index("zl") * 8 + lax.axis_index("y")) * 2 + core_index
     place = jnp.stack([row_start, column_block * COLUMNS]).astype(jnp.int32)
     core = core_index.reshape(1).astype(jnp.int32)
-    turned = projection.transpose(0, 2, 1)
 
     normed, right = project_right(
-        place, residue_valid, pair_acts, norm_gain[:1], norm_bias[:1], turned[0, 2 * HIDDEN :]
+        place, residue_valid, pair_acts, norm_gain, norm_bias, projection
     )
     right = assemble(exchange(right, PLANE))
     right = lax.all_gather(right, "x", axis=0, tiled=True)
-    left = project_left(place, residue_valid, normed, turned[0, : 2 * HIDDEN])
-    gate = gates(place, chain_index, normed, gate_weight[0], chain_bias[:1])
+    left, gate = left_and_gates(
+        0, place, residue_valid, chain_index, normed, projection, gate_weight, chain_bias
+    )
     halves = outgoing(core, exchange(left, PLANE), right)
     total = halves[0].astype(jnp.float32) + swap_cores(halves[1]).astype(jnp.float32)
     product = exchange(total.astype(jnp.bfloat16), PLANE)
     middle, normed, right = finish(
+        0,
         place,
         residue_valid,
-        out_gain[0],
+        out_gain,
         pair_acts,
         gate,
         product,
-        out_weight[0],
-        (norm_gain[1:], norm_bias[1:], turned[1, 2 * HIDDEN :]),
+        out_weight,
+        (norm_gain, norm_bias, projection),
     )
     right = assemble(exchange(right, PLANE))
     right = lax.all_gather(right, "x", axis=0, tiled=True)
-    left = project_left(place, residue_valid, normed, turned[1, : 2 * HIDDEN])
-    gate = gates(place, chain_index, normed, gate_weight[1], chain_bias[1:])
+    left = project_left(1, place, residue_valid, normed, projection)
+    gate, middle = gates(1, place, chain_index, normed, gate_weight, chain_bias, middle)
     left = assemble_turned(exchange(left, PLANE)).reshape(X, ZH * COLUMNS, ZH * ROWS)
     left = exchange(left, "x")
     product = exchange(incoming(core, left, swap_cores(left), right), PLANE)
-    return finish(
-        place, residue_valid, out_gain[1], middle, gate, product, out_weight[1]
-    )[0]
+    return finish(1, place, residue_valid, out_gain, middle, gate, product, out_weight)[0]
 
 
 def solution(mesh):

time: 232 us -> 229 us (0.987)
  blocking collectives: 118 us -> 149 us
  waiting for transfers between devices: 37.6 us -> 19.2 us
  starting transfers between devices: 24.1 us -> 10.9 us
    all_to_all x5 -> x6, blocking collectives: 118 us -> 149 us  [exchange(): return lax.all_to_all(values, axes, split_axis=0, concat_axis=0, tiled=True)]
    all_to_all x2 -> x1, waiting for transfers between devices: 33.8 us -> 15.4 us  [exchange(): return lax.all_to_all(values, axes, split_axis=0, concat_axis=0, tiled=True)]
    all_to_all x2 -> x1, starting transfers between devices: 20.3 us -> 6.86 us  [exchange(): return lax.all_to_all(values, axes, split_axis=0, concat_axis=0, tiled=True)]
    unnamed x27 -> x42, local copies, waits for them, and re-layouts: 8.94 us -> 11.1 us
    pallas_call x6 -> x5, Pallas kernels: 14.5 us -> 12.9 us  [the longest x2 7.44 us: finish(): call(functools.partial(finish_kernel, which), [out, NORMED, CHUNKS] if th...]
  transfers between devices with their start and end apart: 6 -> 5, of which waited for: 4 -> 3; matrix products, arithmetic and copies ran while one was open for 0% -> 0% of each run, Pallas kernels for 3% -> 3%
where the time goes in v2:
time: 229 us; the launch traced here: 227 us
  blocking collectives  149 us (65%)
  Pallas kernels  23 us (10%)
  waiting for transfers between devices  19.2 us (8%)
  between operations  13.6 us (6%)
  local copies, waits for them, and re-layouts  11.1 us (5%)
  starting transfers between devices  10.9 us (5%)
    all_to_all x6, blocking collectives, exchange(): return lax.all_to_all(values, axes, split_axis=0, concat_axis=0, tiled=True)  149 us
    all_to_all x1, waiting for transfers between devices, exchange(): return lax.all_to_all(values, axes, split_axis=0, concat_axis=0, tiled=True)  15.4 us
    unnamed x42, local copies, waits for them, and re-layouts  11.1 us
    pallas_call x2, Pallas kernels, finish(): call(functools.partial(finish_kernel, which), [out, NORMED, CHUNKS] if th...  7.44 us
    all_to_all x1, starting transfers between devices, exchange(): return lax.all_to_all(values, axes, split_axis=0, concat_axis=0, tiled=True)  6.86 us
  transfers between devices with their start and end apart: 5, of which 3 were waited for; matrix products, arithmetic and copies ran while one was open for 0% of the time, Pallas kernels for 3%

profile of v2, /device:TPU:6, one launch (start us, length us, event | category | flops | bytes accessed | tf_op | source)
XLA Modules:
  0.0 227.0 jit_solution(10889134195050968739)
XLA Ops:
  6.6 1.1 copy-done
  10.7 2.9 %shard_map.100 = (bf16[32,128,128]{2,1,0:T(8,128)(2,1)S(1)}, bf16[64,8,512]{2,1,0:T(8,128)(2,1)S(1)}) custom-call(s32[2]{0:T(128)S(1)} %pad_add_fusion.place_ref, s32[1280]{0:T(1024)S(1)} %copy-done.11, bf16[80,40,128]{2,1,0:T(8,128)(2,1)S(1)} %copy-done, f32[2,128]{1,0:T(2,128)S(1)} %copy-done.16, f32[2,128]{1,0:T(2,128)S(1)} %copy-done.18, ...), custom_call_target="tpu_custom_call" | custom-call | flops 100000000 | bytes 4000000 | tf_op jit(solution)/shard_map/pallas_call | solution.py:156
  13.6 35.7 %all_to_all.35.chunks_ref = bf16[64,8,512]{2,1,0:T(8,128)(2,1)S(1)} all-to-all(bf16[64,8,512]{2,1,0:T(8,128)(2,1)S(1)} %get-tuple-element.17), channel_id=1, replica_groups=mesh['zl'=2,'y'=8,'core'=2,'x'=4,'zh'=4] {'y','zh','zl'}, dimensions={0} | all-to-all | bytes 1048576 | tf_op jit(solution)/shard_map/all_to_all | solution.py:474
  50.5 2.1 shard_map.101
  52.6 23.9 %all_to_all.36.left_ref = bf16[64,8,512]{2,1,0:T(8,128)(2,1)S(1)} all-to-all(bf16[64,8,512]{2,1,0:T(8,128)(2,1)S(1)} %get-tuple-element.16), channel_id=1, replica_groups=mesh['zl'=2,'y'=8,'core'=2,'x'=4,'zh'=4] {'y','zh','zl'}, dimensions={0} | all-to-all | bytes 1048576 | tf_op jit(solution)/shard_map/all_to_all | solution.py:474
  76.6 1.4 copy-done.5
  78.0 1.9 shard_map.103
  80.0 2.1 collective-permute-start
  82.1 1.9 collective-permute-done
  84.1 30.9 %all_to_all.37.product_ref = bf16[64,8,512]{2,1,0:T(8,128)(2,1)S(1)} all-to-all(bf16[64,8,512]{2,1,0:T(8,128)(2,1)S(1)} %fusion), channel_id=1, replica_groups=mesh['zl'=2,'y'=8,'core'=2,'x'=4,'zh'=4] {'y','zh','zl'}, dimensions={0} | all-to-all | bytes 1048576 | tf_op jit(solution)/shard_map/all_to_all | solution.py:474
  115.0 4.2 %shard_map.104 = (bf16[80,40,128]{2,1,0:T(8,128)(2,1)S(1)}, bf16[32,128,128]{2,1,0:T(8,128)(2,1)S(1)}, bf16[64,8,512]{2,1,0:T(8,128)(2,1)S(1)}) custom-call(s32[2]{0:T(128)S(1)} %pad_add_fusion.place_ref, s32[1280]{0:T(1024)S(1)} %copy-done.12, f32[2,64]{1,0:T(2,128)S(1)} %copy-done.20, bf16[80,40,128]{2,1,0:T(8,128)(2,1)S(1)} %copy-done.1, ...), custom_call_target="tpu_custom_call" | custom-call | flops 100000000 | bytes 4000000 | tf_op jit(solution)/shard_map/pallas_call | solution.py:353
  120.1 24.4 %all_to_all.38.chunks_ref = bf16[64,8,512]{2,1,0:T(8,128)(2,1)S(1)} all-to-all(bf16[64,8,512]{2,1,0:T(8,128)(2,1)S(1)} %get-tuple-element.22), channel_id=1, replica_groups=mesh['zl'=2,'y'=8,'core'=2,'x'=4,'zh'=4] {'y','zh','zl'}, dimensions={0} | all-to-all | bytes 1048576 | tf_op jit(solution)/shard_map/all_to_all | solution.py:474
  145.7 1.8 shard_map.106
  147.5 23.8 %all_to_all.39.chunks_ref = bf16[64,8,512]{2,1,0:T(8,128)(2,1)S(1)} all-to-all(bf16[64,8,512]{2,1,0:T(8,128)(2,1)S(1)} %shard_map.106), channel_id=1, replica_groups=mesh['zl'=2,'y'=8,'core'=2,'x'=4,'zh'=4] {'y','zh','zl'}, dimensions={0} | all-to-all | bytes 1048576 | tf_op jit(solution)/shard_map/all_to_all | solution.py:474
  171.8 10.3 %all_to_all.40.own_ref = bf16[4,160,320]{2,1,0:T(8,128)(2,1)S(1)} all-to-all(bf16[4,160,320]{2,1,0:T(8,128)(2,1)S(1)} %bitcast.11), channel_id=1, replica_groups=mesh['zl'=2,'y'=8,'core'=2,'x'=4,'zh'=4] {'x'}, dimensions={0} | all-to-all | bytes 819200 | tf_op jit(solution)/shard_map/all_to_all | solution.py:474
  182.2 1.9 collective-permute-start.1
  184.1 1.8 collective-permute-done.1.other_ref
  185.9 1.4 copy-done.4
  187.4 2.4 %shard_map.109 = bf16[64,8,512]{2,1,0:T(8,128)(2,1)} custom-call(s32[1]{0:T(128)} %bitcast.2.core_ref, bf16[4,160,320]{2,1,0:T(8,128)(2,1)S(1)} %all_to_all.40.own_ref, bf16[4,160,320]{2,1,0:T(8,128)(2,1)S(1)} %collective-permute-done.1.other_ref, bf16[1280,640]{1,0:T(8,128)(2,1)S(1)} %copy-done.4), custom_call_target="tpu_custom_call" | custom-call | flops 600000000 | bytes 4000000 | tf_op jit(solution)/shard_map/pallas_call | solution.py:468
  189.8 6.9 %all-to-all-start.6 = ((bf16[64,8,512]{2,1,0:T(8,128)(2,1)}), bf16[64,8,512]{2,1,0:T(8,128)(2,1)}, u32[]{:S(2)}, u32[]{:S(2)}) async-start(bf16[64,8,512]{2,1,0:T(8,128)(2,1)} %shard_map.109), calls=%async_computation.6 | async-start | bytes 1048576 | tf_op jit(solution)/shard_map/all_to_all | solution.py:474
  197.8 1.6 shard_map.105
  200.3 15.4 %all-to-all-done.6.product_ref = bf16[64,8,512]{2,1,0:T(8,128)(2,1)} async-done(((bf16[64,8,512]{2,1,0:T(8,128)(2,1)}), bf16[64,8,512]{2,1,0:T(8,128)(2,1)}, u32[]{:S(2)}, u32[]{:S(2)}) %all-to-all-start.6) | async-done | bytes 524320 | tf_op jit(solution)/shard_map/all_to_all | solution.py:474
  215.7 1.1 copy-done.7
  216.9 3.2 %shard_map.110 = bf16[80,40,128]{2,1,0:T(8,128)(2,1)} custom-call(s32[2]{0:T(128)S(1)} %pad_add_fusion.place_ref, s32[1280]{0:T(1024)S(1)} %copy-done.12, f32[2,64]{1,0:T(2,128)S(1)} %copy-done.20, bf16[80,40,128]{2,1,0:T(8,128)(2,1)S(1)} %copy-done.7, f32[32,128,128]{2,1,0:T(8,128)S(1)} %get-tuple-element.21.gates_ref, ...), custom_call_target="tpu_custom_call" | custom-call | flops 100000000 | bytes 4000000 | tf_op jit(solution)/shard_map/pallas_call | solution.py:353
  (50 shorter events, 9.1 us)
Async XLA Ops:
  6.5 43.9 %copy-start.12 = (s32[1280]{0:T(1024)S(1)}, s32[1280]{0:T(1024)}, u32[]{:S(2)}) copy-start(s32[1280]{0:T(1024)} %valid_ref.9) | copy-start | bytes 15364
  6.5 44.0 %copy-start.15 = (f32[2,128]{1,0:T(2,128)S(1)}, f32[2,128]{1,0:T(2,128)}, u32[]{:S(2)}) copy-start(f32[2,128]{1,0:T(2,128)} %chain_bias_ref.3) | copy-start | bytes 3076
  6.5 44.0 %copy-start.14 = (s32[1280]{0:T(1024)S(1)}, s32[1280]{0:T(1024)}, u32[]{:S(2)}) copy-start(s32[1280]{0:T(1024)} %chain_ref.3) | copy-start | bytes 15364
  6.5 70.0 %all-gather.3.cloned.1.call-start = ((), (), s32[]{:S(2)}) async-start(), calls=%async_computation.7 | async-start | bytes 2048000 | tf_op jit(solution)/shard_map/all_gather | solution.py:503
  6.6 1.1 copy-start
  7.8 0.9 copy-start.2
  8.7 0.7 copy-start.11
  10.7 39.8 %copy-start.3 = (bf16[2,128,256]{2,1,0:T(8,128)(2,1)S(1)}, bf16[2,128,256]{2,1,0:T(8,128)(2,1)}, u32[]{:S(2)}) copy-start(bf16[2,128,256]{2,1,0:T(8,128)(2,1)} %weight_ref.5) | copy-start | bytes 393220
  10.7 39.8 %copy-start.10 = (bf16[2,128,128]{2,1,0:T(8,128)(2,1)S(1)}, bf16[2,128,128]{2,1,0:T(8,128)(2,1)}, u32[]{:S(2)}) copy-start(bf16[2,128,128]{2,1,0:T(8,128)(2,1)} %gate_ref.3) | copy-start | bytes 196612
  50.4 135.5 %all-gather.5.cloned.1.call-start = ((), (), s32[]{:S(2)}) async-start(), calls=%async_computation.8 | async-start | bytes 2048000 | tf_op jit(solution)/shard_map/all_gather | solution.py:522
  76.6 1.4 copy-start.5
  79.9 35.1 %copy-start.1 = (bf16[80,40,128]{2,1,0:T(8,128)(2,1)S(1)}, bf16[80,40,128]{2,1,0:T(8,128)(2,1)}, u32[]{:S(2)}) copy-start(bf16[80,40,128]{2,1,0:T(8,128)(2,1)} %pair_ref.3) | copy-start | bytes 2457604
  79.9 35.1 %copy-start.13 = (bf16[2,64,128]{2,1,0:T(8,128)(2,1)S(1)}, bf16[2,64,128]{2,1,0:T(8,128)(2,1)}, u32[]{:S(2)}) copy-start(bf16[2,64,128]{2,1,0:T(8,128)(2,1)} %out_weight_ref.3) | copy-start | bytes 98308
  79.9 35.0 %copy-start.17 = (f32[2,128]{1,0:T(2,128)S(1)}, f32[2,128]{1,0:T(2,128)}, u32[]{:S(2)}) copy-start(f32[2,128]{1,0:T(2,128)} %rest_0_.1) | copy-start | bytes 3076
  79.9 35.0 %copy-start.19 = (f32[2,128]{1,0:T(2,128)S(1)}, f32[2,128]{1,0:T(2,128)}, u32[]{:S(2)}) copy-start(f32[2,128]{1,0:T(2,128)} %rest_1_.1) | copy-start | bytes 3076
  80.0 35.0 %copy-start.20 = (f32[2,64]{1,0:T(2,128)S(1)}, f32[2,64]{1,0:T(2,128)}, u32[]{:S(2)}) copy-start(f32[2,64]{1,0:T(2,128)} %out_gain_ref.3) | copy-start | bytes 1540
  80.0 3.9 %collective-permute-start = (bf16[64,8,512]{2,1,0:T(8,128)(2,1)S(1)}, bf16[64,8,512]{2,1,0:T(8,128)(2,1)S(1)}, u32[]{:S(2)}, u32[]{:S(2)}) collective-permute-start(bf16[64,8,512]{2,1,0:T(8,128)(2,1)S(1)} %slice_bitcast_fusion), channel_id=1, source_target_pairs={{0,16},{16,0},{1,17},{17,1},{2,18},{18,2},{3,19},{19,3},{4,20},{20... | collective-permute-start | bytes 1572872 | tf_op jit(solution)/shard_map/ppermute | solution.py:478
  119.2 0.9 copy-start.8
  182.2 3.7 %collective-permute-start.1 = (bf16[4,160,320]{2,1,0:T(8,128)(2,1)S(1)}, bf16[4,160,320]{2,1,0:T(8,128)(2,1)S(1)}, u32[]{:S(2)}, u32[]{:S(2)}) collective-permute-start(bf16[4,160,320]{2,1,0:T(8,128)(2,1)S(1)} %all_to_all.40.own_ref), channel_id=1, source_target_pairs={{0,16},{16,0},{1,17},{17,1},{2,18},{18,2},{3,19},{19,3},{4,20},{20... | collective-permute-start | bytes 1228808 | tf_op jit(solution)/shard_map/ppermute | solution.py:478
  185.9 1.4 copy-start.4
  189.8 26.0 %all-to-all-start.6 = ((bf16[64,8,512]{2,1,0:T(8,128)(2,1)}), bf16[64,8,512]{2,1,0:T(8,128)(2,1)}, u32[]{:S(2)}, u32[]{:S(2)}) async-start(bf16[64,8,512]{2,1,0:T(8,128)(2,1)} %shard_map.109), calls=%async_computation.6 | async-start | bytes 1048576 | tf_op jit(solution)/shard_map/all_to_all | solution.py:474
  196.6 1.1 copy-start.9
  199.4 0.9 copy-start.6
  215.7 1.1 copy-start.7
  (2 other events, 1.4 us)
Sparse Core Ops, SparseCore 0:
  50.5 24.5 all-gather.2
  145.8 24.5 all-gather.4

commit v3 on v2

v3 whole, which is shorter than its diff:
```python
import functools

import jax
import jax.numpy as jnp
from jax import lax
from jax.experimental import pallas as pl
from jax.experimental.pallas import tpu as pltpu
from jax.sharding import Mesh
from jax.sharding import PartitionSpec as P

AXES = ("zl", "y", "core", "x", "zh")
SIZES = (2, 8, 2, 4, 4)
PLANE = ("y", "zh", "zl")
ROWS = 80
COLUMNS = 40
WIDTH = 128
HIDDEN = 64
X = 4
ZH = 4
SPAN = 16
EPS = 1e-05
DEPTH = 32
LANES = 128
SUB = 8
WHOLE = 3
TAIL = 8 * 9
STRIDE = 40
BOTH = 56
BATCH = 8
CHUNKS = jax.ShapeDtypeStruct((HIDDEN, SUB, DEPTH // SUB * LANES), jnp.bfloat16)
BOTH_CHUNKS = jax.ShapeDtypeStruct((HIDDEN, SUB, BOTH // SUB * LANES), jnp.bfloat16)
NORMED = jax.ShapeDtypeStruct((DEPTH, LANES, WIDTH), jnp.bfloat16)
GATES = jax.ShapeDtypeStruct((2, DEPTH, LANES, WIDTH), jnp.float32)
VMEM = pl.BlockSpec(memory_space=pltpu.VMEM)
ANY = pl.BlockSpec(memory_space=pl.ANY)
SMEM = pl.BlockSpec(memory_space=pltpu.SMEM)


def spot(span, zh):
    zl, y = divmod(span, 8)
    return (y * ZH + zh) * 2 + zl


def call(kernel, out_shape, in_specs, scratch_shapes=(), flops=10**8, outs=None, grant=40):
    outs = outs or jax.tree.map(lambda _: VMEM, out_shape)
    moved = 4 * 10**6
    return pl.pallas_call(
        kernel,
        out_shape=out_shape,
        in_specs=in_specs,
        out_specs=outs,
        scratch_shapes=scratch_shapes,
        compiler_params=pltpu.CompilerParams(vmem_limit_bytes=grant * 2**20),
        cost_estimate=pl.CostEstimate(flops=flops, bytes_accessed=moved, transcendentals=0),
    )


def normalize(values, gain, bias):
    average = jnp.mean(values, axis=-1, keepdims=True)
    centred = values - average
    spread = jnp.mean(centred * centred, axis=-1, keepdims=True)
    return centred * lax.rsqrt(spread + EPS) * gain + bias


def batches(work):
    pl.loop(0, WHOLE)(lambda step: work(step * BATCH, 3))
    work(WHOLE * BATCH, 1)


def block_rows(first, count):
    if count == 1:
        return [[TAIL + n] for n in range(BATCH)]
    return [[first + n + WHOLE * SUB * group for group in range(count)] for n in range(BATCH)]


def load_pairs(pair_ref, first, count):
    rows = [row for rows in block_rows(first, count) for row in rows]
    return jnp.concatenate([pair_ref[row].astype(jnp.float32) for row in rows], axis=0)


def pad_rows(values, count):
    size = count * COLUMNS
    empty = jnp.zeros((LANES - size, WIDTH), jnp.float32)
    return [
        jnp.concatenate([values[n * size : (n + 1) * size], empty], axis=0).astype(jnp.bfloat16)
        for n in range(BATCH)
    ]


def spread_columns(place_ref, valid_ref):
    lane = lax.broadcasted_iota(jnp.int32, (1, LANES), 1)
    inside = lane % COLUMNS
    found = jnp.zeros((1, LANES), jnp.float32)
    for column in range(COLUMNS):
        value = valid_ref[place_ref[1] + column].astype(jnp.float32)
        found = jnp.where(inside == column, value, found)
    return jnp.where(lane < 3 * COLUMNS, found, 0.0)


def mask_of(first, count, place_ref, valid_ref, columns, shift=0):
    lane = lax.broadcasted_iota(jnp.int32, (1, LANES), 1)
    masks = []
    for rows in block_rows(first, count):
        mask = jnp.zeros((1, LANES), jnp.float32)
        for group, row in enumerate(rows):
            value = valid_ref[place_ref[0] + row].astype(jnp.float32)
            start = (group + shift) * COLUMNS
            inside = (lane >= start) & (lane < start + COLUMNS)
            mask = jnp.where(inside, value, mask)
        masks.append(mask * columns)
    return jnp.concatenate(masks, axis=1)


def weight_of(weight_ref, which, start):
    columns = weight_ref[which][:, start : start + 2 * HIDDEN]
    return columns.astype(jnp.float32).T.astype(jnp.bfloat16)


def factor_of(normed, weight, mask):
    proj = lax.dot_general(
        weight, normed, (((1,), (1,)), ((), ())), preferred_element_type=jnp.float32
    )
    return jax.nn.sigmoid(proj[HIDDEN:]) * proj[:HIDDEN] * mask


def keep_rows(factor, scratch, first, stride):
    for n in range(BATCH):
        place = pl.ds(first + n, HIDDEN, stride=stride)
        scratch[place, :] = factor[:, n * LANES : (n + 1) * LANES]


def put_chunks(scratch, out_ref, stride, depth):
    for channel in range(HIDDEN):
        rows = scratch[pl.ds(channel * stride, depth), :]
        tiles = [rows[n : n + SUB] for n in range(0, depth, SUB)]
        out_ref[channel] = jnp.concatenate(tiles, axis=1).astype(jnp.bfloat16)


SCRATCH = pltpu.VMEM(((HIDDEN + 1) * STRIDE, LANES), jnp.float32)


def right_kernel(
    place_ref,
    valid_ref,
    pair_any,
    gain_any,
    bias_any,
    weight_any,
    normed_ref,
    right_ref,
    right_s,
    pair_ref,
    gain_ref,
    bias_ref,
    weight_ref,
    sems,
):
    moves = ((pair_any, pair_ref), (gain_any, gain_ref), (bias_any, bias_ref), (weight_any, weight_ref))
    copies = [pltpu.make_async_copy(a, b, sems.at[n]) for n, (a, b) in enumerate(moves)]
    for copy in copies:
        copy.start()
    columns = spread_columns(place_ref, valid_ref)
    for copy in copies:
        copy.wait()
    weight = weight_of(weight_ref, 0, 2 * HIDDEN)

    def work(first, count):
        values = load_pairs(pair_ref, first, count)
        pieces = pad_rows(normalize(values, gain_ref[0:1], bias_ref[0:1]), count)
        for n in range(BATCH):
            normed_ref[first + n] = pieces[n]
        mask = mask_of(first, count, place_ref, valid_ref, columns)
        factor = factor_of(jnp.concatenate(pieces, axis=0), weight, mask)
        keep_rows(factor, right_s, first, STRIDE)

    batches(work)
    put_chunks(right_s, right_ref, STRIDE, DEPTH)


def project_right(place, valid, *operands):
    scratch = [pltpu.VMEM(each.shape, each.dtype) for each in operands]
    return call(
        right_kernel,
        [NORMED, CHUNKS],
        [SMEM, SMEM] + [ANY] * 4,
        [SCRATCH] + scratch + [pltpu.SemaphoreType.DMA((4,))],
        grant=60,
    )(place, valid, *operands)


def load_normed(normed_ref, first):
    return normed_ref[pl.ds(first, BATCH)].reshape(BATCH * LANES, WIDTH)


def gate_work(
    which, place_ref, chain_ref, normed_ref, gate_ref, chain_bias_ref, pair_ref, out_ref
):
    row = lax.broadcasted_iota(jnp.int32, (COLUMNS, WIDTH), 0)
    chain_columns = jnp.full((COLUMNS, WIDTH), -1, jnp.int32)
    for column in range(COLUMNS):
        chain_columns = jnp.where(row == column, chain_ref[place_ref[1] + column], chain_columns)
    offset = chain_bias_ref[which : which + 1]

    def work(first, count):
        logit = jnp.dot(
            load_normed(normed_ref, first), gate_ref[which], preferred_element_type=jnp.float32
        )
        for n, rows in enumerate(block_rows(first, count)):
            for group, row in enumerate(rows):
                same = chain_columns == chain_ref[place_ref[0] + row]
                start = n * LANES + group * COLUMNS
                place = pl.ds(group * COLUMNS, COLUMNS)
                out_ref[0, first + n, place] = jax.nn.sigmoid(
                    logit[start : start + COLUMNS] + jnp.where(same, offset, 0.0)
                )
                out_ref[1, first + n, place] = pair_ref[row].astype(jnp.float32)

    return work


def gate_kernel(which, *refs):
    batches(gate_work(which, *refs))


def gates(which, place, chain, normed, gate, chain_bias, pair):
    kernel = functools.partial(gate_kernel, which)
    return call(kernel, GATES, [SMEM, SMEM, VMEM, VMEM, VMEM, VMEM])(
        place, chain, normed, gate, chain_bias, pair
    )


def left_and_gate_kernel(
    place_ref,
    valid_ref,
    chain_ref,
    normed_ref,
    weight_ref,
    gate_ref,
    chain_bias_ref,
    pair_ref,
    left_ref,
    out_ref,
    left_s,
):
    columns = spread_columns(place_ref, valid_ref)
    weight = weight_of(weight_ref, 0, 0)
    gate = gate_work(
        0, place_ref, chain_ref, normed_ref, gate_ref, chain_bias_ref, pair_ref, out_ref
    )

    def work(first, count):
        mask = mask_of(first, count, place_ref, valid_ref, columns)
        keep_rows(factor_of(load_normed(normed_ref, first), weight, mask), left_s, first, STRIDE)
        gate(first, count)

    batches(work)
    put_chunks(left_s, left_ref, STRIDE, DEPTH)


def left_and_gates(place, valid, chain, normed, weight, gate, chain_bias, pair):
    return call(left_and_gate_kernel, [CHUNKS, GATES], [SMEM] * 3 + [VMEM] * 5, [SCRATCH])(
        place, valid, chain, normed, weight, gate, chain_bias, pair
    )


def finish_kernel(which, place_ref, valid_ref, out_gain_ref, gates_ref, product_ref, out_weight_ref, *rest):
    then = which == 0
    if then:
        gain_ref, bias_ref, weight_ref, out_ref, normed_ref, both_ref, hidden_s, both_s = rest
        new_s = out_ref
        columns = spread_columns(place_ref, valid_ref)
        left_weight = weight_of(weight_ref, 1, 0)
        right_weight = weight_of(weight_ref, 1, 2 * HIDDEN)
    else:
        out_ref, hidden_s, new_s, out_sem = rest

    def channel(n):
        return product_ref[n].astype(jnp.float32)

    average = channel(0)
    for n in range(1, HIDDEN):
        average = average + channel(n)
    average = average / HIDDEN
    spread = jnp.zeros_like(average)
    for n in range(HIDDEN):
        centred = channel(n) - average
        spread = spread + centred * centred
    scale = lax.rsqrt(spread / HIDDEN + EPS)
    for n in range(HIDDEN):
        hidden = (channel(n) - average) * scale * out_gain_ref[which, n]
        for part in range(DEPTH // SUB):
            place = pl.ds(n * STRIDE + part * SUB, SUB)
            hidden_s[place, :] = hidden[:, part * LANES : (part + 1) * LANES]

    def work(first, count):
        size = count * COLUMNS
        hidden = jnp.concatenate(
            [hidden_s[pl.ds(first + n, HIDDEN, stride=STRIDE), :] for n in range(BATCH)], axis=1
        ).astype(jnp.bfloat16)
        branch = lax.dot_general(
            hidden,
            out_weight_ref[which],
            (((0,), (0,)), ((), ())),
            preferred_element_type=jnp.float32,
        )
        new = jnp.concatenate(
            [
                gates_ref[1, first + n, pl.ds(0, size)]
                + gates_ref[0, first + n, pl.ds(0, size)] * branch[n * LANES : n * LANES + size]
                for n in range(BATCH)
            ],
            axis=0,
        )
        places = [row for rows in block_rows(first, count) for row in rows]
        for n, row in enumerate(places):
            new_s[row] = new[n * COLUMNS : (n + 1) * COLUMNS].astype(jnp.bfloat16)
        if not then:
            for group in range(count):
                span = pl.ds(block_rows(first, count)[0][group], BATCH)
                pltpu.make_async_copy(new_s.at[span], out_ref.at[span], out_sem).start()
            return
        new = new.astype(jnp.bfloat16).astype(jnp.float32)
        values = normalize(new, gain_ref[1:2], bias_ref[1:2])
        pieces = pad_rows(values, count)
        for n in range(BATCH):
            normed_ref[first + n] = pieces[n]
        mask = mask_of(first, count, place_ref, valid_ref, columns)
        if count == 3:
            normed = jnp.concatenate(pieces, axis=0)
            keep_rows(factor_of(normed, left_weight, mask), both_s, first, BOTH)
            right_first = first + WHOLE * SUB
            keep_rows(factor_of(normed, right_weight, mask), both_s, right_first, BOTH)
        else:
            twice = [values[n * size : (n + 1) * size] for n in range(BATCH) for _ in range(2)]
            normed = jnp.concatenate(
                [
                    each
                    for n in range(BATCH)
                    for each in twice[2 * n : 2 * n + 2]
                    + [jnp.zeros((LANES - 2 * size, WIDTH), jnp.float32)]
                ],
                axis=0,
            ).astype(jnp.bfloat16)
            other = mask_of(first, count, place_ref, valid_ref, columns, 1)
            factor = factor_of(normed, left_weight, mask) + factor_of(normed, right_weight, other)
            keep_rows(factor, both_s, 2 * WHOLE * SUB, BOTH)

    batches(work)
    if then:
        put_chunks(both_s, both_ref, BOTH, BOTH)
    else:
        pltpu.make_async_copy(new_s, out_ref, out_sem).wait()


def finish(which, place, valid, out_gain, gate, product, out_weight, *then):
    shape = (ROWS, COLUMNS, WIDTH)
    out = jax.ShapeDtypeStruct(shape, jnp.bfloat16)
    both = [pltpu.VMEM(((HIDDEN + 1) * BOTH, LANES), jnp.float32)]
    last = [pltpu.VMEM(shape, jnp.bfloat16), pltpu.SemaphoreType.DMA]
    return call(
        functools.partial(finish_kernel, which),
        [out, NORMED, BOTH_CHUNKS] if then else [out],
        [SMEM] * 3 + [VMEM] * (3 + len(then)),
        [SCRATCH] + (both if then else last),
        outs=None if then else [ANY],
    )(place, valid, out_gain, gate, product, out_weight, *then)


ALONE = (0, 3, 0)
LEFT = (0, 6, 0)
RIGHT = (3, 6, COLUMNS)


def gather_rows(chunks_ref, zh, block, layout):
    tile, last_tile, last_lane = layout
    start = last_tile * LANES + last_lane
    if block < 9:
        start = (tile + block % 3) * LANES + block // 3 * COLUMNS
    return jnp.concatenate(
        [
            chunks_ref[spot(span, zh)].astype(jnp.float32)[:, start : start + COLUMNS]
            for span in range(SPAN)
        ],
        axis=1,
    )


def assemble_into(chunks_ref, layout, put):
    for zh in range(ZH):
        for block in range(0, ROWS // SUB, 2):
            rows = [gather_rows(chunks_ref, zh, block + n, layout) for n in range(2)]
            put(zh * ROWS + block * SUB, jnp.concatenate(rows, axis=0))


def assemble_kernel(layout, chunks_ref, out_ref):
    def put(start, values):
        out_ref[pl.ds(start, 2 * SUB), :] = values.astype(jnp.bfloat16)

    assemble_into(chunks_ref, layout, put)


def assemble(chunks, layout):
    out = jax.ShapeDtypeStruct((ZH * ROWS, SPAN * COLUMNS), jnp.bfloat16)
    return call(functools.partial(assemble_kernel, layout), out, [VMEM])(chunks)


def assemble_turned_kernel(layout, chunks_ref, out_ref, whole):
    def put(start, values):
        whole[pl.ds(start, 2 * SUB), :] = values

    assemble_into(chunks_ref, layout, put)
    whole[pl.ds(ZH * ROWS, 64), :] = jnp.zeros((64, SPAN * COLUMNS), jnp.float32)
    for part in range(SPAN * COLUMNS // 128):
        turned = whole[:, part * 128 : (part + 1) * 128].T
        out_ref[pl.ds(part * 128, 128), :] = turned[:, : ZH * ROWS].astype(jnp.bfloat16)


def assemble_turned(chunks, layout):
    out = jax.ShapeDtypeStruct((SPAN * COLUMNS, ZH * ROWS), jnp.bfloat16)
    scratch = [pltpu.VMEM((ZH * ROWS + 64, SPAN * COLUMNS), jnp.float32)]
    kernel = functools.partial(assemble_turned_kernel, layout)
    return call(kernel, out, [VMEM], scratch)(chunks)


def chunk_of(total, zh, start):
    pieces = [
        total[pl.ds(zh * ROWS + block * SUB, SUB), :][:, start : start + COLUMNS]
        for block in range(ROWS // SUB)
    ]
    lanes = []
    for tile in range(WHOLE):
        lanes += pieces[tile:9:3] + [jnp.zeros((SUB, LANES - 3 * COLUMNS), jnp.float32)]
    lanes += [pieces[9], jnp.zeros((SUB, LANES - COLUMNS), jnp.float32)]
    return jnp.concatenate(lanes, axis=1).astype(jnp.bfloat16)


def outgoing_kernel(core_ref, left_ref, right_ref, out_ref, left_s, total):
    assemble_kernel(ALONE, left_ref, left_s)
    for x in range(X):
        total[:, x * ZH * ROWS : (x + 1) * ZH * ROWS] = lax.dot_general(
            left_s[...],
            right_ref[pl.ds(x * ZH * ROWS, ZH * ROWS), :],
            (((1,), (1,)), ((), ())),
            preferred_element_type=jnp.float32,
        )
    for half in range(2):
        slot = lax.rem(core_ref[0] + half, 2)
        for span in range(SPAN):
            for zh in range(ZH):
                out_ref[slot, spot(span, zh)] = chunk_of(total, zh, (2 * span + half) * COLUMNS)


def outgoing(core, left, right):
    out = jax.ShapeDtypeStruct((2,) + CHUNKS.shape, jnp.bfloat16)
    scratch = [
        pltpu.VMEM((ZH * ROWS, SPAN * COLUMNS), jnp.bfloat16),
        pltpu.VMEM((ZH * ROWS, X * ZH * ROWS), jnp.float32),
    ]
    return call(outgoing_kernel, out, [SMEM, VMEM, VMEM], scratch, 6 * 10**8)(core, left, right)


def incoming_kernel(core_ref, own_ref, other_ref, right_ref, out_ref, total):
    for n, left_ref in enumerate((own_ref, other_ref)):
        side = lax.rem(core_ref[0] + n, 2)
        product = jnp.zeros((ZH * COLUMNS, SPAN * COLUMNS), jnp.float32)
        for x in range(X):
            product = product + jnp.dot(
                left_ref[x],
                right_ref[pl.ds(x * ZH * ROWS, ZH * ROWS), :],
                preferred_element_type=jnp.float32,
            )
        for zh in range(ZH):
            start = pl.multiple_of(zh * ROWS + side * COLUMNS, 8)
            total[pl.ds(start, COLUMNS), :] = product[zh * COLUMNS : (zh + 1) * COLUMNS]
    for span in range(SPAN):
        for zh in range(ZH):
            out_ref[spot(span, zh)] = chunk_of(total, zh, span * COLUMNS)


def incoming(core, own, other, right):
    scratch = [pltpu.VMEM((ZH * ROWS, SPAN * COLUMNS), jnp.float32)]
    return call(incoming_kernel, CHUNKS, [SMEM, VMEM, VMEM, VMEM], scratch, 6 * 10**8)(
        core, own, other, right
    )


def exchange(values, axes):
    return lax.all_to_all(values, axes, split_axis=0, concat_axis=0, tiled=True)


def swap_cores(values):
    return lax.ppermute(values, "core", [(0, 1), (1, 0)])


def body(
    pair_acts,
    residue_valid,
    chain_index,
    norm_gain,
    norm_bias,
    projection,
    gate_weight,
    chain_bias,
    out_gain,
    out_weight,
):
    row_start = (lax.axis_index("x") * ZH + lax.axis_index("zh")) * ROWS
    core_index = lax.axis_index("core")
    column_block = (lax.axis_index("zl") * 8 + lax.axis_index("y")) * 2 + core_index
    place = jnp.stack([row_start, column_block * COLUMNS]).astype(jnp.int32)
    core = core_index.reshape(1).astype(jnp.int32)

    normed, right = project_right(
        place, residue_valid, pair_acts, norm_gain, norm_bias, projection
    )
    right = assemble(exchange(right, PLANE), ALONE)
    right = lax.all_gather(right, "x", axis=0, tiled=True)
    left, gate = left_and_gates(
        place,
        residue_valid,
        chain_index,
        normed,
        projection,
        gate_weight,
        chain_bias,
        pair_acts,
    )
    halves = outgoing(core, exchange(left, PLANE), right)
    total = halves[0].astype(jnp.float32) + swap_cores(halves[1]).astype(jnp.float32)
    product = exchange(total.astype(jnp.bfloat16), PLANE)
    middle, normed, both = finish(
        0,
        place,
        residue_valid,
        out_gain,
        gate,
        product,
        out_weight,
        norm_gain,
        norm_bias,
        projection,
    )
    both = exchange(both, PLANE)
    right = assemble(both, RIGHT)
    right = lax.all_gather(right, "x", axis=0, tiled=True)
    left = assemble_turned(both, LEFT).reshape(X, ZH * COLUMNS, ZH * ROWS)
    left = exchange(left, "x")
    product = exchange(incoming(core, left, swap_cores(left), right), PLANE)
    gate = gates(1, place, chain_index, normed, gate_weight, chain_bias, middle)
    return finish(1, place, residue_valid, out_gain, gate, product, out_weight)[0]


def solution(mesh):
    fine = Mesh(mesh.devices.reshape(SIZES), AXES)
    pairs = P(("x", "zh"), ("zl", "y", "core"), None)
    placed = (pairs, P(), P(), P(), P(), P(), P(), P(), P(), P())
    return jax.shard_map(body, mesh=fine, in_specs=placed, out_specs=pairs, check_vma=False)
```

time: 229 us -> 230 us (level)
  blocking collectives: 149 us -> 127 us
  waiting for transfers between devices: 19.2 us -> 29.9 us
  starting transfers between devices: 10.9 us -> 17.3 us
  local copies, waits for them, and re-layouts: 11.1 us -> 16 us
    all_to_all x6 -> x5, blocking collectives: 149 us -> 127 us  [exchange(): return lax.all_to_all(values, axes, split_axis=0, concat_axis=0, tiled=True)]
    all_gather x2, waiting for transfers between devices: 0.01 us -> 10.9 us  [body(): right = lax.all_gather(right, 'x', axis=0, tiled=True)]
    all_to_all x1, starting transfers between devices: 6.86 us -> 13.3 us  [exchange(): return lax.all_to_all(values, axes, split_axis=0, concat_axis=0, tiled=True)]
    unnamed x42 -> x48, local copies, waits for them, and re-layouts: 11.1 us -> 16 us
    pallas_call x9 -> x8, Pallas kernels: 18.7 us -> 19 us  [the longest x2 7.34 us: finish(): call(functools.partial(finish_kernel, which), [out, NORMED, BOTH_CHUNKS]...]
  transfers between devices with their start and end apart: 5 -> 5, of which waited for: 3 -> 4; matrix products, arithmetic and copies ran while one was open for 0% -> 0% of each run, Pallas kernels for 3% -> 2%
where the time goes in v3:
time: 230 us; the launch traced here: 228 us
  blocking collectives  127 us (55%)
  waiting for transfers between devices  29.9 us (13%)
  Pallas kernels  23.3 us (10%)
  starting transfers between devices  17.3 us (8%)
  local copies, waits for them, and re-layouts  16 us (7%)
  between operations  13.6 us (6%)
    all_to_all x5, blocking collectives, exchange(): return lax.all_to_all(values, axes, split_axis=0, concat_axis=0, tiled=True)  127 us
    unnamed x48, local copies, waits for them, and re-layouts  16 us
    all_to_all x1, waiting for transfers between devices, exchange(): return lax.all_to_all(values, axes, split_axis=0, concat_axis=0, tiled=True)  15.4 us
    all_to_all x1, starting transfers between devices, exchange(): return lax.all_to_all(values, axes, split_axis=0, concat_axis=0, tiled=True)  13.3 us
    all_gather x2, waiting for transfers between devices, body(): right = lax.all_gather(right, 'x', axis=0, tiled=True)  10.9 us
    pallas_call x2, Pallas kernels, finish(): call(functools.partial(finish_kernel, which), [out, NORMED, BOTH_CHUNKS]...  7.34 us
    pallas_call x1, Pallas kernels, project_right(): call(right_kernel, [NORMED, CHUNKS], [SMEM, SMEM] + [ANY] * 4, [SCRATCH]...  5.11 us
  transfers between devices with their start and end apart: 5, of which 4 were waited for; matrix products, arithmetic and copies ran while one was open for 0% of the time, Pallas kernels for 2%

profile of v3, /device:TPU:6, one launch (start us, length us, event | category | flops | bytes accessed | tf_op | source)
XLA Modules:
  0.0 227.8 jit_solution(3859810283682103763)
XLA Ops:
  7.1 5.1 %shard_map.100 = (bf16[32,128,128]{2,1,0:T(8,128)(2,1)}, bf16[64,8,512]{2,1,0:T(8,128)(2,1)}) custom-call(s32[2]{0:T(128)} %pad_add_fusion.place_ref.refs_0_, s32[1280]{0:T(1024)} %valid_ref.7, bf16[80,40,128]{2,1,0:T(8,128)(2,1)} %pair_ref.1, f32[2,128]{1,0:T(2,128)} %rest_0_.1, f32[2,128]{1,0:T(2,128)} %rest_1_.1, bf16[2,128,256]{2,1,0:T(8,128)(2,1)} %rest_2_.1), custom_call_target="tpu_custom_call" | custom-call | flops 100000000 | bytes 4000000 | tf_op jit(solution)/shard_map/pallas_call | solution.py:182
  12.3 35.9 %all_to_all.30.chunks_ref = bf16[64,8,512]{2,1,0:T(8,128)(2,1)S(1)} all-to-all(bf16[64,8,512]{2,1,0:T(8,128)(2,1)} %get-tuple-element.15), channel_id=1, replica_groups=mesh['zl'=2,'y'=8,'core'=2,'x'=4,'zh'=4] {'y','zh','zl'}, dimensions={0} | all-to-all | bytes 1048576 | tf_op jit(solution)/shard_map/all_to_all | solution.py:488
  56.1 2.1 shard_map.101
  58.3 2.0 copy-done.2
  60.3 24.0 %all_to_all.31.left_ref = bf16[64,8,512]{2,1,0:T(8,128)(2,1)S(1)} all-to-all(bf16[64,8,512]{2,1,0:T(8,128)(2,1)S(1)} %get-tuple-element.14), channel_id=1, replica_groups=mesh['zl'=2,'y'=8,'core'=2,'x'=4,'zh'=4] {'y','zh','zl'}, dimensions={0} | all-to-all | bytes 1048576 | tf_op jit(solution)/shard_map/all_to_all | solution.py:488
  84.3 1.6 copy-done.6
  85.9 1.9 shard_map.103
  87.9 1.9 collective-permute-start
  89.8 1.9 collective-permute-done
  91.8 24.5 %all_to_all.32.product_ref = bf16[64,8,512]{2,1,0:T(8,128)(2,1)S(1)} all-to-all(bf16[64,8,512]{2,1,0:T(8,128)(2,1)S(1)} %fusion), channel_id=1, replica_groups=mesh['zl'=2,'y'=8,'core'=2,'x'=4,'zh'=4] {'y','zh','zl'}, dimensions={0} | all-to-all | bytes 1048576 | tf_op jit(solution)/shard_map/all_to_all | solution.py:488
  116.4 4.6 %shard_map.104 = (bf16[80,40,128]{2,1,0:T(8,128)(2,1)S(1)}, bf16[32,128,128]{2,1,0:T(8,128)(2,1)S(1)}, bf16[64,8,896]{2,1,0:T(8,128)(2,1)S(1)}) custom-call(s32[2]{0:T(128)S(1)} %copy-done.18, s32[1280]{0:T(1024)S(1)} %copy-done.14, f32[2,64]{1,0:T(2,128)S(1)} %copy-done.23, f32[2,32,128,128]{3,2,1,0:T(8,128)S(1)} %copy-done.3, ...), custom_call_target="tpu_custom_call" | custom-call | flops 100000000 | bytes 4000000 | tf_op jit(solution)/shard_map/pallas_call | solution.py:360
  120.9 32.1 %all_to_all.33.chunks_ref = bf16[64,8,896]{2,1,0:T(8,128)(2,1)S(1)} all-to-all(bf16[64,8,896]{2,1,0:T(8,128)(2,1)S(1)} %get-tuple-element.18), channel_id=1, replica_groups=mesh['zl'=2,'y'=8,'core'=2,'x'=4,'zh'=4] {'y','zh','zl'}, dimensions={0} | all-to-all | bytes 1835008 | tf_op jit(solution)/shard_map/all_to_all | solution.py:488
  154.8 10.4 %all_to_all.34.own_ref = bf16[4,160,320]{2,1,0:T(8,128)(2,1)S(1)} all-to-all(bf16[4,160,320]{2,1,0:T(8,128)(2,1)S(1)} %bitcast.11), channel_id=1, replica_groups=mesh['zl'=2,'y'=8,'core'=2,'x'=4,'zh'=4] {'x'}, dimensions={0} | all-to-all | bytes 819200 | tf_op jit(solution)/shard_map/all_to_all | solution.py:488
  165.2 2.1 collective-permute-start.1
  167.3 1.6 collective-permute-done.1.other_ref
  169.0 10.9 %all-gather.5.cloned.1.call-done.right_ref = bf16[1280,640]{1,0:T(8,128)(2,1)} async-done(((bf16[320,640]{1,0:T(8,128)(2,1)}), bf16[1280,640]{1,0:T(8,128)(2,1)}) %all-gather.5.cloned.1.call-update) | async-done | bytes 1638416 | tf_op jit(solution)/shard_map/all_gather | solution.py:545
  179.9 1.4 copy-done.5
  181.3 2.4 %shard_map.108 = bf16[64,8,512]{2,1,0:T(8,128)(2,1)} custom-call(s32[1]{0:T(128)} %bitcast.2.core_ref, bf16[4,160,320]{2,1,0:T(8,128)(2,1)S(1)} %all_to_all.34.own_ref, bf16[4,160,320]{2,1,0:T(8,128)(2,1)S(1)} %collective-permute-done.1.other_ref, bf16[1280,640]{1,0:T(8,128)(2,1)S(1)} %copy-done.5), custom_call_target="tpu_custom_call" | custom-call | flops 600000000 | bytes 4000000 | tf_op jit(solution)/shard_map/pallas_call | solution.py:482
  183.7 13.3 %all-to-all-start.5 = ((bf16[64,8,512]{2,1,0:T(8,128)(2,1)}), bf16[64,8,512]{2,1,0:T(8,128)(2,1)S(1)}, u32[]{:S(2)}, u32[]{:S(2)}) async-start(bf16[64,8,512]{2,1,0:T(8,128)(2,1)} %shard_map.108), calls=%async_computation.5 | async-start | bytes 1048576 | tf_op jit(solution)/shard_map/all_to_all | solution.py:488
  197.1 1.5 shard_map.105.gates_ref
  198.6 2.0 copy-done
  200.6 15.4 %all-to-all-done.5.product_ref = bf16[64,8,512]{2,1,0:T(8,128)(2,1)S(1)} async-done(((bf16[64,8,512]{2,1,0:T(8,128)(2,1)}), bf16[64,8,512]{2,1,0:T(8,128)(2,1)S(1)}, u32[]{:S(2)}, u32[]{:S(2)}) %all-to-all-start.5) | async-done | bytes 524320 | tf_op jit(solution)/shard_map/all_to_all | solution.py:488
  216.0 2.2 copy-done.1
  218.2 2.8 %shard_map.109 = bf16[80,40,128]{2,1,0:T(8,128)(2,1)} custom-call(s32[2]{0:T(128)S(1)} %copy-done.18, s32[1280]{0:T(1024)S(1)} %copy-done.14, f32[2,64]{1,0:T(2,128)S(1)} %copy-done.23, f32[2,32,128,128]{3,2,1,0:T(8,128)S(1)} %copy-done.1, bf16[64,8,512]{2,1,0:T(8,128)(2,1)S(1)} %all-to-all-done.5.product_ref, bf16[2,64,128]{2,1,0:T(8,128)(2,1)S(1)} %copy-done.12), custom_call_target="tpu_custom_call" | custom-call | flops 100000000 | bytes 4000000 | tf_op jit(solution)/shard_map/pallas_call | solution.py:360
  (54 shorter events, 10.6 us)
Async XLA Ops:
  6.5 77.8 %all-gather.3.cloned.1.call-start = ((), (), s32[]{:S(2)}) async-start(), calls=%async_computation.6 | async-start | bytes 2048000 | tf_op jit(solution)/shard_map/all_gather | solution.py:517
  49.3 130.6 %all-gather.5.cloned.1.call-start = ((), (), s32[]{:S(2)}) async-start(), calls=%async_computation.7 | async-start | bytes 2048000 | tf_op jit(solution)/shard_map/all_gather | solution.py:545
  49.3 1.1 copy-start.4
  50.5 0.9 copy-start.7
  51.4 1.2 copy-start.9
  58.3 2.0 copy-start.2
  60.2 56.1 %copy-start.8 = (bf16[2,128,256]{2,1,0:T(8,128)(2,1)S(1)}, bf16[2,128,256]{2,1,0:T(8,128)(2,1)}, u32[]{:S(2)}) copy-start(bf16[2,128,256]{2,1,0:T(8,128)(2,1)} %rest_2_.1) | copy-start | bytes 393220
  60.2 56.1 %copy-start.12 = (bf16[2,64,128]{2,1,0:T(8,128)(2,1)S(1)}, bf16[2,64,128]{2,1,0:T(8,128)(2,1)}, u32[]{:S(2)}) copy-start(bf16[2,64,128]{2,1,0:T(8,128)(2,1)} %out_weight_ref.3) | copy-start | bytes 98308
  60.3 56.1 %copy-start.14 = (s32[1280]{0:T(1024)S(1)}, s32[1280]{0:T(1024)}, u32[]{:S(2)}) copy-start(s32[1280]{0:T(1024)} %valid_ref.7) | copy-start | bytes 15364
  60.3 56.1 %copy-start.18 = (s32[2]{0:T(128)S(1)}, s32[2]{0:T(128)}, u32[]{:S(2)}) copy-start(s32[2]{0:T(128)} %pad_add_fusion.place_ref.refs_0_) | copy-start | bytes 28
  60.3 56.1 %copy-start.19 = (f32[2,128]{1,0:T(2,128)S(1)}, f32[2,128]{1,0:T(2,128)}, u32[]{:S(2)}) copy-start(f32[2,128]{1,0:T(2,128)} %rest_0_.1) | copy-start | bytes 3076
  60.3 56.1 %copy-start.20 = (f32[2,128]{1,0:T(2,128)S(1)}, f32[2,128]{1,0:T(2,128)}, u32[]{:S(2)}) copy-start(f32[2,128]{1,0:T(2,128)} %rest_1_.1) | copy-start | bytes 3076
  60.3 56.1 %copy-start.23 = (f32[2,64]{1,0:T(2,128)S(1)}, f32[2,64]{1,0:T(2,128)}, u32[]{:S(2)}) copy-start(f32[2,64]{1,0:T(2,128)} %out_gain_ref.3) | copy-start | bytes 1540
  84.3 32.0 %copy-start.3 = (f32[2,32,128,128]{3,2,1,0:T(8,128)S(1)}, f32[2,32,128,128]{3,2,1,0:T(8,128)}, u32[]{:S(2)}) copy-start(f32[2,32,128,128]{3,2,1,0:T(8,128)} %copy-done.2) | copy-start | bytes 12582916
  84.3 1.6 copy-start.6
  87.9 3.8 %collective-permute-start = (bf16[64,8,512]{2,1,0:T(8,128)(2,1)S(1)}, bf16[64,8,512]{2,1,0:T(8,128)(2,1)S(1)}, u32[]{:S(2)}, u32[]{:S(2)}) collective-permute-start(bf16[64,8,512]{2,1,0:T(8,128)(2,1)S(1)} %slice_bitcast_fusion), channel_id=1, source_target_pairs={{0,16},{16,0},{1,17},{17,1},{2,18},{18,2},{3,19},{19,3},{4,20},{20... | collective-permute-start | bytes 1572872 | tf_op jit(solution)/shard_map/ppermute | solution.py:492
  153.1 44.0 %copy-start.11 = (bf16[2,128,128]{2,1,0:T(8,128)(2,1)S(1)}, bf16[2,128,128]{2,1,0:T(8,128)(2,1)}, u32[]{:S(2)}) copy-start(bf16[2,128,128]{2,1,0:T(8,128)(2,1)} %refs_3_.1) | copy-start | bytes 196612
  153.1 44.0 %copy-start.16 = (s32[1280]{0:T(1024)S(1)}, s32[1280]{0:T(1024)}, u32[]{:S(2)}) copy-start(s32[1280]{0:T(1024)} %refs_1_.1) | copy-start | bytes 15364
  153.1 44.0 %copy-start.22 = (f32[2,128]{1,0:T(2,128)S(1)}, f32[2,128]{1,0:T(2,128)}, u32[]{:S(2)}) copy-start(f32[2,128]{1,0:T(2,128)} %refs_4_.1) | copy-start | bytes 3076
  165.2 3.7 %collective-permute-start.1 = (bf16[4,160,320]{2,1,0:T(8,128)(2,1)S(1)}, bf16[4,160,320]{2,1,0:T(8,128)(2,1)S(1)}, u32[]{:S(2)}, u32[]{:S(2)}) collective-permute-start(bf16[4,160,320]{2,1,0:T(8,128)(2,1)S(1)} %all_to_all.34.own_ref), channel_id=1, source_target_pairs={{0,16},{16,0},{1,17},{17,1},{2,18},{18,2},{3,19},{19,3},{4,20},{20... | collective-permute-start | bytes 1228808 | tf_op jit(solution)/shard_map/ppermute | solution.py:492
  179.9 1.4 copy-start.5
  183.7 32.2 %all-to-all-start.5 = ((bf16[64,8,512]{2,1,0:T(8,128)(2,1)}), bf16[64,8,512]{2,1,0:T(8,128)(2,1)S(1)}, u32[]{:S(2)}, u32[]{:S(2)}) async-start(bf16[64,8,512]{2,1,0:T(8,128)(2,1)} %shard_map.108), calls=%async_computation.5 | async-start | bytes 1048576 | tf_op jit(solution)/shard_map/all_to_all | solution.py:488
  198.6 2.0 copy-start
  216.0 2.2 copy-start.1
  (5 other events, 3.5 us)
Sparse Core Ops, SparseCore 0:
  49.4 24.5 all-gather.2
  154.4 25.4 all-gather.4

commit v4 on v3

--- a/solution.py
+++ b/solution.py
@@ -41,7 +41,7 @@
     return (y * ZH + zh) * 2 + zl
 
 
-def call(kernel, out_shape, in_specs, scratch_shapes=(), flops=10**8, outs=None, grant=40):
+def call(kernel, out_shape, in_specs, scratch_shapes=(), flops=10**8, outs=None):
     outs = outs or jax.tree.map(lambda _: VMEM, out_shape)
     moved = 4 * 10**6
     return pl.pallas_call(
@@ -50,7 +50,7 @@
         in_specs=in_specs,
         out_specs=outs,
         scratch_shapes=scratch_shapes,
-        compiler_params=pltpu.CompilerParams(vmem_limit_bytes=grant * 2**20),
+        compiler_params=pltpu.CompilerParams(vmem_limit_bytes=40 * 2**20),
         cost_estimate=pl.CostEstimate(flops=flops, bytes_accessed=moved, transcendentals=0),
     )
 
@@ -140,33 +140,14 @@
 
 
 def right_kernel(
-    place_ref,
-    valid_ref,
-    pair_any,
-    gain_any,
-    bias_any,
-    weight_any,
-    normed_ref,
-    right_ref,
-    right_s,
-    pair_ref,
-    gain_ref,
-    bias_ref,
-    weight_ref,
-    sems,
+    place_ref, valid_ref, pair_ref, vectors_ref, weight_ref, normed_ref, right_ref, right_s
 ):
-    moves = ((pair_any, pair_ref), (gain_any, gain_ref), (bias_any, bias_ref), (weight_any, weight_ref))
-    copies = [pltpu.make_async_copy(a, b, sems.at[n]) for n, (a, b) in enumerate(moves)]
-    for copy in copies:
-        copy.start()
     columns = spread_columns(place_ref, valid_ref)
-    for copy in copies:
-        copy.wait()
     weight = weight_of(weight_ref, 0, 2 * HIDDEN)
 
     def work(first, count):
         values = load_pairs(pair_ref, first, count)
-        pieces = pad_rows(normalize(values, gain_ref[0:1], bias_ref[0:1]), count)
+        pieces = pad_rows(normalize(values, vectors_ref[0:1], vectors_ref[2:3]), count)
         for n in range(BATCH):
             normed_ref[first + n] = pieces[n]
         mask = mask_of(first, count, place_ref, valid_ref, columns)
@@ -177,15 +158,10 @@
     put_chunks(right_s, right_ref, STRIDE, DEPTH)
 
 
-def project_right(place, valid, *operands):
-    scratch = [pltpu.VMEM(each.shape, each.dtype) for each in operands]
-    return call(
-        right_kernel,
-        [NORMED, CHUNKS],
-        [SMEM, SMEM] + [ANY] * 4,
-        [SCRATCH] + scratch + [pltpu.SemaphoreType.DMA((4,))],
-        grant=60,
-    )(place, valid, *operands)
+def project_right(place, valid, pair, vectors, weight):
+    return call(right_kernel, [NORMED, CHUNKS], [SMEM, SMEM, VMEM, VMEM, VMEM], [SCRATCH])(
+        place, valid, pair, vectors, weight
+    )
 
 
 def load_normed(normed_ref, first):
@@ -193,13 +169,13 @@
 
 
 def gate_work(
-    which, place_ref, chain_ref, normed_ref, gate_ref, chain_bias_ref, pair_ref, out_ref
+    which, place_ref, chain_ref, normed_ref, gate_ref, vectors_ref, pair_ref, out_ref
 ):
     row = lax.broadcasted_iota(jnp.int32, (COLUMNS, WIDTH), 0)
     chain_columns = jnp.full((COLUMNS, WIDTH), -1, jnp.int32)
     for column in range(COLUMNS):
         chain_columns = jnp.where(row == column, chain_ref[place_ref[1] + column], chain_columns)
-    offset = chain_bias_ref[which : which + 1]
+    offset = vectors_ref[4 + which : 5 + which]
 
     def work(first, count):
         logit = jnp.dot(
@@ -222,10 +198,10 @@
     batches(gate_work(which, *refs))
 
 
-def gates(which, place, chain, normed, gate, chain_bias, pair):
+def gates(which, place, chain, normed, gate, vectors, pair):
     kernel = functools.partial(gate_kernel, which)
     return call(kernel, GATES, [SMEM, SMEM, VMEM, VMEM, VMEM, VMEM])(
-        place, chain, normed, gate, chain_bias, pair
+        place, chain, normed, gate, vectors, pair
     )
 
 
@@ -236,7 +212,7 @@
     normed_ref,
     weight_ref,
     gate_ref,
-    chain_bias_ref,
+    vectors_ref,
     pair_ref,
     left_ref,
     out_ref,
@@ -245,7 +221,7 @@
     columns = spread_columns(place_ref, valid_ref)
     weight = weight_of(weight_ref, 0, 0)
     gate = gate_work(
-        0, place_ref, chain_ref, normed_ref, gate_ref, chain_bias_ref, pair_ref, out_ref
+        0, place_ref, chain_ref, normed_ref, gate_ref, vectors_ref, pair_ref, out_ref
     )
 
     def work(first, count):
@@ -257,16 +233,16 @@
     put_chunks(left_s, left_ref, STRIDE, DEPTH)
 
 
-def left_and_gates(place, valid, chain, normed, weight, gate, chain_bias, pair):
+def left_and_gates(place, valid, chain, normed, weight, gate, vectors, pair):
     return call(left_and_gate_kernel, [CHUNKS, GATES], [SMEM] * 3 + [VMEM] * 5, [SCRATCH])(
-        place, valid, chain, normed, weight, gate, chain_bias, pair
+        place, valid, chain, normed, weight, gate, vectors, pair
     )
 
 
 def finish_kernel(which, place_ref, valid_ref, out_gain_ref, gates_ref, product_ref, out_weight_ref, *rest):
     then = which == 0
     if then:
-        gain_ref, bias_ref, weight_ref, out_ref, normed_ref, both_ref, hidden_s, both_s = rest
+        vectors_ref, weight_ref, out_ref, normed_ref, both_ref, hidden_s, both_s = rest
         new_s = out_ref
         columns = spread_columns(place_ref, valid_ref)
         left_weight = weight_of(weight_ref, 1, 0)
@@ -320,7 +296,7 @@
                 pltpu.make_async_copy(new_s.at[span], out_ref.at[span], out_sem).start()
             return
         new = new.astype(jnp.bfloat16).astype(jnp.float32)
-        values = normalize(new, gain_ref[1:2], bias_ref[1:2])
+        values = normalize(new, vectors_ref[1:2], vectors_ref[3:4])
         pieces = pad_rows(values, count)
         for n in range(BATCH):
             normed_ref[first + n] = pieces[n]
@@ -434,39 +410,47 @@
     return jnp.concatenate(lanes, axis=1).astype(jnp.bfloat16)
 
 
-def outgoing_kernel(core_ref, left_ref, right_ref, out_ref, left_s, total):
+def outgoing_kernel(core_ref, left_ref, *rest):
+    rights, (out_ref, left_s, total) = rest[:X], rest[X:]
     assemble_kernel(ALONE, left_ref, left_s)
-    for x in range(X):
-        total[:, x * ZH * ROWS : (x + 1) * ZH * ROWS] = lax.dot_general(
+    for n, right_ref in enumerate(rights):
+        total[:, n * ZH * ROWS : (n + 1) * ZH * ROWS] = lax.dot_general(
             left_s[...],
-            right_ref[pl.ds(x * ZH * ROWS, ZH * ROWS), :],
+            right_ref[...],
             (((1,), (1,)), ((), ())),
             preferred_element_type=jnp.float32,
         )
     for half in range(2):
         slot = lax.rem(core_ref[0] + half, 2)
-        for span in range(SPAN):
-            for zh in range(ZH):
-                out_ref[slot, spot(span, zh)] = chunk_of(total, zh, (2 * span + half) * COLUMNS)
-
-
-def outgoing(core, left, right):
+        for n in range(X):
+            x = lax.rem(core_ref[1] + n, X)
+            for low in range(ZH):
+                span = ((lax.rem(x, 2) * ZH + low) * ZH) * 2 + x // 2
+                for zh in range(ZH):
+                    start = ((n * ZH + low) * 2 + half) * COLUMNS
+                    out_ref[slot, span + zh * 2] = chunk_of(total, zh, start)
+
+
+def outgoing(core, left, rights):
     out = jax.ShapeDtypeStruct((2,) + CHUNKS.shape, jnp.bfloat16)
     scratch = [
         pltpu.VMEM((ZH * ROWS, SPAN * COLUMNS), jnp.bfloat16),
         pltpu.VMEM((ZH * ROWS, X * ZH * ROWS), jnp.float32),
     ]
-    return call(outgoing_kernel, out, [SMEM, VMEM, VMEM], scratch, 6 * 10**8)(core, left, right)
-
-
-def incoming_kernel(core_ref, own_ref, other_ref, right_ref, out_ref, total):
+    return call(outgoing_kernel, out, [SMEM] + [VMEM] * (1 + X), scratch, 6 * 10**8)(
+        core, left, *rights
+    )
+
+
+def incoming_kernel(core_ref, own_ref, other_ref, *rest):
+    rights, (_, out_ref, total) = rest[:X], rest[X:]
     for n, left_ref in enumerate((own_ref, other_ref)):
         side = lax.rem(core_ref[0] + n, 2)
         product = jnp.zeros((ZH * COLUMNS, SPAN * COLUMNS), jnp.float32)
-        for x in range(X):
+        for m, right_ref in enumerate(rights):
             product = product + jnp.dot(
-                left_ref[x],
-                right_ref[pl.ds(x * ZH * ROWS, ZH * ROWS), :],
+                left_ref[lax.rem(core_ref[1] + m, X)],
+                right_ref[...],
                 preferred_element_type=jnp.float32,
             )
         for zh in range(ZH):
@@ -477,11 +461,18 @@
             out_ref[spot(span, zh)] = chunk_of(total, zh, span * COLUMNS)
 
 
-def incoming(core, own, other, right):
+def incoming(core, own, other, rights, gate):
     scratch = [pltpu.VMEM((ZH * ROWS, SPAN * COLUMNS), jnp.float32)]
-    return call(incoming_kernel, CHUNKS, [SMEM, VMEM, VMEM, VMEM], scratch, 6 * 10**8)(
-        core, own, other, right
-    )
+    return call(
+        incoming_kernel, CHUNKS, [SMEM] + [VMEM] * (2 + X) + [ANY], scratch, 6 * 10**8
+    )(core, own, other, *rights, gate)
+
+
+def gather_x(block):
+    def shift(by):
+        return lax.ppermute(block, "x", [(x, (x + by) % X) for x in range(X)])
+
+    return [block] + [shift(-n) for n in range(1, X)]
 
 
 def exchange(values, axes):
@@ -508,45 +499,26 @@
     core_index = lax.axis_index("core")
     column_block = (lax.axis_index("zl") * 8 + lax.axis_index("y")) * 2 + core_index
     place = jnp.stack([row_start, column_block * COLUMNS]).astype(jnp.int32)
-    core = core_index.reshape(1).astype(jnp.int32)
-
-    normed, right = project_right(
-        place, residue_valid, pair_acts, norm_gain, norm_bias, projection
-    )
-    right = assemble(exchange(right, PLANE), ALONE)
-    right = lax.all_gather(right, "x", axis=0, tiled=True)
+    core = jnp.stack([core_index, lax.axis_index("x")]).astype(jnp.int32)
+
+    vectors = jnp.concatenate([norm_gain, norm_bias, chain_bias], axis=0)
+    normed, right = project_right(place, residue_valid, pair_acts, vectors, projection)
+    rights = gather_x(assemble(exchange(right, PLANE), ALONE))
     left, gate = left_and_gates(
-        place,
-        residue_valid,
-        chain_index,
-        normed,
-        projection,
-        gate_weight,
-        chain_bias,
-        pair_acts,
-    )
-    halves = outgoing(core, exchange(left, PLANE), right)
+        place, residue_valid, chain_index, normed, projection, gate_weight, vectors, pair_acts
+    )
+    halves = outgoing(core, exchange(left, PLANE), rights)
     total = halves[0].astype(jnp.float32) + swap_cores(halves[1]).astype(jnp.float32)
     product = exchange(total.astype(jnp.bfloat16), PLANE)
     middle, normed, both = finish(
-        0,
-        place,
-        residue_valid,
-        out_gain,
-        gate,
-        product,
-        out_weight,
-        norm_gain,
-        norm_bias,
-        projection,
+        0, place, residue_valid, out_gain, gate, product, out_weight, vectors, projection
     )
     both = exchange(both, PLANE)
-    right = assemble(both, RIGHT)
-    right = lax.all_gather(right, "x", axis=0, tiled=True)
+    rights = gather_x(assemble(both, RIGHT))
+    gate = gates(1, place, chain_index, normed, gate_weight, vectors, middle)
     left = assemble_turned(both, LEFT).reshape(X, ZH * COLUMNS, ZH * ROWS)
     left = exchange(left, "x")
-    product = exchange(incoming(core, left, swap_cores(left), right), PLANE)
-    gate = gates(1, place, chain_index, normed, gate_weight, chain_bias, middle)
+    product = exchange(incoming(core, left, swap_cores(left), rights, gate), PLANE)
     return finish(1, place, residue_valid, out_gain, gate, product, out_weight)[0]
 
 

time: 230 us -> 215 us (0.935)
  blocking collectives: 127 us -> 90.8 us
  starting transfers between devices: 17.3 us -> 51.7 us
  between operations: 13.6 us -> 0.4 us
  local copies, waits for them, and re-layouts: 16 us -> 10.2 us
  waiting for transfers between devices: 29.9 us -> 34.8 us
    all_to_all x5 -> x3, blocking collectives: 127 us -> 90.8 us  [exchange(): return lax.all_to_all(values, axes, split_axis=0, concat_axis=0, tiled=True)]
    ppermute x0 -> x6, starting transfers between devices: none -> 19.6 us  [shift(): return lax.ppermute(block, 'x', [(x, (x + by) % X) for x in range(X)])]
    all_to_all x1 -> x3, starting transfers between devices: 13.3 us -> 28.1 us  [exchange(): return lax.all_to_all(values, axes, split_axis=0, concat_axis=0, tiled=True)]
    ppermute x0 -> x6, waiting for transfers between devices: none -> 14.3 us  [shift(): return lax.ppermute(block, 'x', [(x, (x + by) % X) for x in range(X)])]
    all_gather x2 -> x0, waiting for transfers between devices: 10.9 us -> none  [body(): right = lax.all_gather(right, 'x', axis=0, tiled=True)]
    unnamed x48 -> x36, local copies, waits for them, and re-layouts: 16 us -> 10.2 us
    all_to_all x1 -> x3, waiting for transfers between devices: 15.4 us -> 18.6 us  [exchange(): return lax.all_to_all(values, axes, split_axis=0, concat_axis=0, tiled=True)]
  transfers between devices with their start and end apart: 5 -> 11, of which waited for: 4 -> 7; matrix products, arithmetic and copies ran while one was open for 0% -> 0% of each run, Pallas kernels for 2% -> 2%
where the time goes in v4:
time: 215 us; the launch traced here: 211 us
  blocking collectives  90.8 us (42%)
  starting transfers between devices  51.7 us (24%)
  waiting for transfers between devices  34.8 us (16%)
  Pallas kernels  22.1 us (10%)
  local copies, waits for them, and re-layouts  10.2 us (5%)
    all_to_all x3, blocking collectives, exchange(): return lax.all_to_all(values, axes, split_axis=0, concat_axis=0, tiled=True)  90.8 us
    all_to_all x3, starting transfers between devices, exchange(): return lax.all_to_all(values, axes, split_axis=0, concat_axis=0, tiled=True)  28.1 us
    ppermute x6, starting transfers between devices, shift(): return lax.ppermute(block, 'x', [(x, (x + by) % X) for x in range(X)])  19.6 us
    all_to_all x3, waiting for transfers between devices, exchange(): return lax.all_to_all(values, axes, split_axis=0, concat_axis=0, tiled=True)  18.6 us
    ppermute x6, waiting for transfers between devices, shift(): return lax.ppermute(block, 'x', [(x, (x + by) % X) for x in range(X)])  14.3 us
    unnamed x36, local copies, waits for them, and re-layouts  10.2 us
    pallas_call x2, Pallas kernels, finish(): call(functools.partial(finish_kernel, which), [out, NORMED, BOTH_CHUNKS]...  7.33 us
  transfers between devices with their start and end apart: 11, of which 7 were waited for; matrix products, arithmetic and copies ran while one was open for 0% of the time, Pallas kernels for 2%

profile of v4, /device:TPU:6, one launch (start us, length us, event | category | flops | bytes accessed | tf_op | source)
XLA Modules:
  0.0 211.0 jit_solution(13704984681223068145)
XLA Ops:
  3.5 3.6 %shard_map.100 = (bf16[32,128,128]{2,1,0:T(8,128)(2,1)S(1)}, bf16[64,8,512]{2,1,0:T(8,128)(2,1)}) custom-call(s32[2]{0:T(128)S(1)} %pad_add_fusion.place_ref.refs_0_, s32[1280]{0:T(1024)S(1)} %copy-done.12, bf16[80,40,128]{2,1,0:T(8,128)(2,1)S(1)} %copy-done.2, f32[6,128]{1,0:T(8,128)S(1)} %pad_maximum_fusion.vectors_ref.rest_0_.refs_4_, ...), custom_call_target="tpu_custom_call" | custom-call | flops 100000000 | bytes 4000000 | tf_op jit(solution)/shard_map/pallas_call | solution.py:162
  7.2 16.6 %all-to-all-start.1 = ((bf16[64,8,512]{2,1,0:T(8,128)(2,1)}), bf16[64,8,512]{2,1,0:T(8,128)(2,1)S(1)}, u32[]{:S(2)}, u32[]{:S(2)}) async-start(bf16[64,8,512]{2,1,0:T(8,128)(2,1)} %get-tuple-element.15), calls=%async_computation.1 | async-start | bytes 1048576 | tf_op jit(solution)/shard_map/all_to_all | solution.py:479
  28.1 2.9 %shard_map.101 = (bf16[64,8,512]{2,1,0:T(8,128)(2,1)}, f32[2,32,128,128]{3,2,1,0:T(8,128)S(1)}) custom-call(s32[2]{0:T(128)S(1)} %pad_add_fusion.place_ref.refs_0_, s32[1280]{0:T(1024)S(1)} %copy-done.13, s32[1280]{0:T(1024)S(1)} %copy-done.15, bf16[32,128,128]{2,1,0:T(8,128)(2,1)S(1)} %get-tuple-element.12.normed_ref, bf16[2,128,256]{2,1,0:T(8,128)(2,1)S(1)} %copy-done.5, ...), custom_call_target="tpu_custom_call" | custom-call | flops 100000000 | bytes 4000000 | tf_op jit(solution)/shard_map/pallas_call | solution.py:237
  33.0 10.1 %all-to-all-done.1.chunks_ref = bf16[64,8,512]{2,1,0:T(8,128)(2,1)S(1)} async-done(((bf16[64,8,512]{2,1,0:T(8,128)(2,1)}), bf16[64,8,512]{2,1,0:T(8,128)(2,1)S(1)}, u32[]{:S(2)}, u32[]{:S(2)}) %all-to-all-start.1) | async-done | bytes 524320 | tf_op jit(solution)/shard_map/all_to_all | solution.py:479
  43.1 5.5 %all-to-all-start = ((bf16[64,8,512]{2,1,0:T(8,128)(2,1)}), bf16[64,8,512]{2,1,0:T(8,128)(2,1)S(1)}, u32[]{:S(2)}, u32[]{:S(2)}) async-start(bf16[64,8,512]{2,1,0:T(8,128)(2,1)} %get-tuple-element.14), calls=%async_computation | async-start | bytes 1048576 | tf_op jit(solution)/shard_map/all_to_all | solution.py:479
  48.9 2.7 %collective-permute-start = (bf16[320,640]{1,0:T(8,128)(2,1)S(1)}, bf16[320,640]{1,0:T(8,128)(2,1)S(1)}, u32[]{:S(2)}, u32[]{:S(2)}) collective-permute-start(bf16[320,640]{1,0:T(8,128)(2,1)S(1)} %shard_map.102.rest_0_), channel_id=1, source_target_pairs={{0,12},{4,0},{8,4},{12,8},{1,13},{5,1},{9,5},{13,9},{2,14},{6,2},{... | collective-permute-start | bytes 1228808 | tf_op jit(solution)/shard_map/ppermute | solution.py:473
  51.7 3.0 %collective-permute-start.1 = (bf16[320,640]{1,0:T(8,128)(2,1)S(1)}, bf16[320,640]{1,0:T(8,128)(2,1)S(1)}, u32[]{:S(2)}, u32[]{:S(2)}) collective-permute-start(bf16[320,640]{1,0:T(8,128)(2,1)S(1)} %shard_map.102.rest_0_), channel_id=1, source_target_pairs={{0,8},{4,12},{8,0},{12,4},{1,9},{5,13},{9,1},{13,5},{2,10},{6,14},... | collective-permute-start | bytes 1228808 | tf_op jit(solution)/shard_map/ppermute | solution.py:473
  54.7 4.0 %collective-permute-start.2 = (bf16[320,640]{1,0:T(8,128)(2,1)S(1)}, bf16[320,640]{1,0:T(8,128)(2,1)S(1)}, u32[]{:S(2)}, u32[]{:S(2)}) collective-permute-start(bf16[320,640]{1,0:T(8,128)(2,1)S(1)} %shard_map.102.rest_0_), channel_id=1, source_target_pairs={{0,4},{4,8},{8,12},{12,0},{1,5},{5,9},{9,13},{13,1},{2,6},{6,10},{... | collective-permute-start | bytes 1228808 | tf_op jit(solution)/shard_map/ppermute | solution.py:473
  58.8 8.5 %all-to-all-done.left_ref = bf16[64,8,512]{2,1,0:T(8,128)(2,1)S(1)} async-done(((bf16[64,8,512]{2,1,0:T(8,128)(2,1)}), bf16[64,8,512]{2,1,0:T(8,128)(2,1)S(1)}, u32[]{:S(2)}, u32[]{:S(2)}) %all-to-all-start) | async-done | bytes 524320 | tf_op jit(solution)/shard_map/all_to_all | solution.py:479
  67.3 4.0 %collective-permute-done.rest_1_ = bf16[320,640]{1,0:T(8,128)(2,1)S(1)} collective-permute-done((bf16[320,640]{1,0:T(8,128)(2,1)S(1)}, bf16[320,640]{1,0:T(8,128)(2,1)S(1)}, u32[]{:S(2)}, u32[]{:S(2)}) %collective-permute-start) | collective-permute-done | bytes 409632 | tf_op jit(solution)/shard_map/ppermute | solution.py:473
  71.3 2.5 %collective-permute-done.2.rest_3_ = bf16[320,640]{1,0:T(8,128)(2,1)S(1)} collective-permute-done((bf16[320,640]{1,0:T(8,128)(2,1)S(1)}, bf16[320,640]{1,0:T(8,128)(2,1)S(1)}, u32[]{:S(2)}, u32[]{:S(2)}) %collective-permute-start.2) | collective-permute-done | bytes 409632 | tf_op jit(solution)/shard_map/ppermute | solution.py:473
  73.8 2.4 %shard_map.103 = bf16[2,64,8,512]{3,2,1,0:T(8,128)(2,1)S(1)} custom-call(s32[2]{0:T(128)S(1)} %pad_add_fusion.1.core_ref, bf16[64,8,512]{2,1,0:T(8,128)(2,1)S(1)} %all-to-all-done.left_ref, bf16[320,640]{1,0:T(8,128)(2,1)S(1)} %shard_map.102.rest_0_, bf16[320,640]{1,0:T(8,128)(2,1)S(1)} %collective-permute-done.rest_1_, ...), custom_call_target="tpu_custom_call" | custom-call | flops 600000000 | bytes 4000000 | tf_op jit(solution)/shard_map/pallas_call | solution.py:440
  80.3 31.5 %all_to_all.30.product_ref = bf16[64,8,512]{2,1,0:T(8,128)(2,1)S(1)} all-to-all(bf16[64,8,512]{2,1,0:T(8,128)(2,1)S(1)} %fusion), channel_id=1, replica_groups=mesh['zl'=2,'y'=8,'core'=2,'x'=4,'zh'=4] {'y','zh','zl'}, dimensions={0} | all-to-all | bytes 1048576 | tf_op jit(solution)/shard_map/all_to_all | solution.py:479
  111.8 4.6 %shard_map.104 = (bf16[80,40,128]{2,1,0:T(8,128)(2,1)S(1)}, bf16[32,128,128]{2,1,0:T(8,128)(2,1)S(1)}, bf16[64,8,896]{2,1,0:T(8,128)(2,1)S(1)}) custom-call(s32[2]{0:T(128)S(1)} %pad_add_fusion.place_ref.refs_0_, s32[1280]{0:T(1024)S(1)} %copy-done.14, f32[2,64]{1,0:T(2,128)S(1)} %copy-done.17, f32[2,32,128,128]{3,2,1,0:T(8,128)S(1)} %copy-done.1, ...), custom_call_target="tpu_custom_call" | custom-call | flops 100000000 | bytes 4000000 | tf_op jit(solution)/shard_map/pallas_call | solution.py:336
  116.4 32.1 %all_to_all.31.chunks_ref = bf16[64,8,896]{2,1,0:T(8,128)(2,1)S(1)} all-to-all(bf16[64,8,896]{2,1,0:T(8,128)(2,1)S(1)} %get-tuple-element.18), channel_id=1, replica_groups=mesh['zl'=2,'y'=8,'core'=2,'x'=4,'zh'=4] {'y','zh','zl'}, dimensions={0} | all-to-all | bytes 1835008 | tf_op jit(solution)/shard_map/all_to_all | solution.py:479
  149.9 6.1 %all-to-all-start.4 = ((bf16[4,160,320]{2,1,0:T(8,128)(2,1)}), bf16[4,160,320]{2,1,0:T(8,128)(2,1)S(1)}, u32[]{:S(2)}, u32[]{:S(2)}) async-start(bf16[4,160,320]{2,1,0:T(8,128)(2,1)} %bitcast.6), calls=%async_computation.4 | async-start | bytes 983040 | tf_op jit(solution)/shard_map/all_to_all | solution.py:479
  156.3 2.8 %collective-permute-start.5 = (bf16[320,640]{1,0:T(8,128)(2,1)S(1)}, bf16[320,640]{1,0:T(8,128)(2,1)S(1)}, u32[]{:S(2)}, u32[]{:S(2)}) collective-permute-start(bf16[320,640]{1,0:T(8,128)(2,1)S(1)} %shard_map.107.rest_0_), channel_id=1, source_target_pairs={{0,12},{4,0},{8,4},{12,8},{1,13},{5,1},{9,5},{13,9},{2,14},{6,2},{... | collective-permute-start | bytes 1228808 | tf_op jit(solution)/shard_map/ppermute | solution.py:473
  159.1 2.6 %collective-permute-start.6 = (bf16[320,640]{1,0:T(8,128)(2,1)S(1)}, bf16[320,640]{1,0:T(8,128)(2,1)S(1)}, u32[]{:S(2)}, u32[]{:S(2)}) collective-permute-start(bf16[320,640]{1,0:T(8,128)(2,1)S(1)} %shard_map.107.rest_0_), channel_id=1, source_target_pairs={{0,8},{4,12},{8,0},{12,4},{1,9},{5,13},{9,1},{13,5},{2,10},{6,14},... | collective-permute-start | bytes 1228808 | tf_op jit(solution)/shard_map/ppermute | solution.py:473
  161.7 4.5 %collective-permute-start.7 = (bf16[320,640]{1,0:T(8,128)(2,1)S(1)}, bf16[320,640]{1,0:T(8,128)(2,1)S(1)}, u32[]{:S(2)}, u32[]{:S(2)}) collective-permute-start(bf16[320,640]{1,0:T(8,128)(2,1)S(1)} %shard_map.107.rest_0_), channel_id=1, source_target_pairs={{0,4},{4,8},{8,12},{12,0},{1,5},{5,9},{9,13},{13,1},{2,6},{6,10},{... | collective-permute-start | bytes 1228808 | tf_op jit(solution)/shard_map/ppermute | solution.py:473
  166.2 2.1 collective-permute-start.4
  171.0 6.9 %collective-permute-done.5.rest_1_ = bf16[320,640]{1,0:T(8,128)(2,1)S(1)} collective-permute-done((bf16[320,640]{1,0:T(8,128)(2,1)S(1)}, bf16[320,640]{1,0:T(8,128)(2,1)S(1)}, u32[]{:S(2)}, u32[]{:S(2)}) %collective-permute-start.5) | collective-permute-done | bytes 409632 | tf_op jit(solution)/shard_map/ppermute | solution.py:473
  178.8 2.1 %shard_map.108 = bf16[64,8,512]{2,1,0:T(8,128)(2,1)S(1)} custom-call(s32[2]{0:T(128)S(1)} %pad_add_fusion.1.core_ref, bf16[4,160,320]{2,1,0:T(8,128)(2,1)S(1)} %all-to-all-done.4.own_ref, bf16[4,160,320]{2,1,0:T(8,128)(2,1)S(1)} %collective-permute-done.4.other_ref, bf16[320,640]{1,0:T(8,128)(2,1)S(1)} %shard_map.107.rest_0_, ...), custom_call_target="tpu_custom_call" | custom-call | flops 600000000 | bytes 4000000 | tf_op jit(solution)/shard_map/pallas_call | solution.py:466
  180.9 27.2 %all_to_all.32.product_ref = bf16[64,8,512]{2,1,0:T(8,128)(2,1)S(1)} all-to-all(bf16[64,8,512]{2,1,0:T(8,128)(2,1)S(1)} %shard_map.108), channel_id=1, replica_groups=mesh['zl'=2,'y'=8,'core'=2,'x'=4,'zh'=4] {'y','zh','zl'}, dimensions={0} | all-to-all | bytes 1048576 | tf_op jit(solution)/shard_map/all_to_all | solution.py:479
  208.1 2.8 %shard_map.109 = bf16[80,40,128]{2,1,0:T(8,128)(2,1)} custom-call(s32[2]{0:T(128)S(1)} %pad_add_fusion.place_ref.refs_0_, s32[1280]{0:T(1024)S(1)} %copy-done.14, f32[2,64]{1,0:T(2,128)S(1)} %copy-done.17, f32[2,32,128,128]{3,2,1,0:T(8,128)S(1)} %shard_map.105.rest_4_.gates_ref, bf16[64,8,512]{2,1,0:T(8,128)(2,1)S(1)} %all_to_all.32.product_ref, ...), custom_call_target="tpu_custom_call" | custom-call | flops 100000000 | bytes 4000000 | tf_op jit(solution)/shard_map/pallas_call | solution.py:336
  (52 shorter events, 19.5 us)
Async XLA Ops:
  0.8 1.1 copy-start.2
  1.9 0.9 copy-start.4
  7.2 35.9 %all-to-all-start.1 = ((bf16[64,8,512]{2,1,0:T(8,128)(2,1)}), bf16[64,8,512]{2,1,0:T(8,128)(2,1)S(1)}, u32[]{:S(2)}, u32[]{:S(2)}) async-start(bf16[64,8,512]{2,1,0:T(8,128)(2,1)} %get-tuple-element.15), calls=%async_computation.1 | async-start | bytes 1048576 | tf_op jit(solution)/shard_map/all_to_all | solution.py:479
  23.8 1.1 copy-start.3
  31.0 2.0 copy-start
  43.0 68.7 %copy-start.6 = (bf16[2,128,256]{2,1,0:T(8,128)(2,1)S(1)}, bf16[2,128,256]{2,1,0:T(8,128)(2,1)}, u32[]{:S(2)}) copy-start(bf16[2,128,256]{2,1,0:T(8,128)(2,1)} %rest_1_.1) | copy-start | bytes 393220
  43.0 68.7 %copy-start.11 = (bf16[2,64,128]{2,1,0:T(8,128)(2,1)S(1)}, bf16[2,64,128]{2,1,0:T(8,128)(2,1)}, u32[]{:S(2)}) copy-start(bf16[2,64,128]{2,1,0:T(8,128)(2,1)} %out_weight_ref.3) | copy-start | bytes 98308
  43.0 68.7 %copy-start.14 = (s32[1280]{0:T(1024)S(1)}, s32[1280]{0:T(1024)}, u32[]{:S(2)}) copy-start(s32[1280]{0:T(1024)} %valid_ref.7) | copy-start | bytes 15364
  43.0 68.7 %copy-start.17 = (f32[2,64]{1,0:T(2,128)S(1)}, f32[2,64]{1,0:T(2,128)}, u32[]{:S(2)}) copy-start(f32[2,64]{1,0:T(2,128)} %out_gain_ref.3) | copy-start | bytes 1540
  43.1 24.3 %all-to-all-start = ((bf16[64,8,512]{2,1,0:T(8,128)(2,1)}), bf16[64,8,512]{2,1,0:T(8,128)(2,1)S(1)}, u32[]{:S(2)}, u32[]{:S(2)}) async-start(bf16[64,8,512]{2,1,0:T(8,128)(2,1)} %get-tuple-element.14), calls=%async_computation | async-start | bytes 1048576 | tf_op jit(solution)/shard_map/all_to_all | solution.py:479
  48.9 22.3 %collective-permute-start = (bf16[320,640]{1,0:T(8,128)(2,1)S(1)}, bf16[320,640]{1,0:T(8,128)(2,1)S(1)}, u32[]{:S(2)}, u32[]{:S(2)}) collective-permute-start(bf16[320,640]{1,0:T(8,128)(2,1)S(1)} %shard_map.102.rest_0_), channel_id=1, source_target_pairs={{0,12},{4,0},{8,4},{12,8},{1,13},{5,1},{9,5},{13,9},{2,14},{6,2},{... | collective-permute-start | bytes 1228808 | tf_op jit(solution)/shard_map/ppermute | solution.py:473
  51.7 19.6 %collective-permute-start.1 = (bf16[320,640]{1,0:T(8,128)(2,1)S(1)}, bf16[320,640]{1,0:T(8,128)(2,1)S(1)}, u32[]{:S(2)}, u32[]{:S(2)}) collective-permute-start(bf16[320,640]{1,0:T(8,128)(2,1)S(1)} %shard_map.102.rest_0_), channel_id=1, source_target_pairs={{0,8},{4,12},{8,0},{12,4},{1,9},{5,13},{9,1},{13,5},{2,10},{6,14},... | collective-permute-start | bytes 1228808 | tf_op jit(solution)/shard_map/ppermute | solution.py:473
  54.7 19.1 %collective-permute-start.2 = (bf16[320,640]{1,0:T(8,128)(2,1)S(1)}, bf16[320,640]{1,0:T(8,128)(2,1)S(1)}, u32[]{:S(2)}, u32[]{:S(2)}) collective-permute-start(bf16[320,640]{1,0:T(8,128)(2,1)S(1)} %shard_map.102.rest_0_), channel_id=1, source_target_pairs={{0,4},{4,8},{8,12},{12,0},{1,5},{5,9},{9,13},{13,1},{2,6},{6,10},{... | collective-permute-start | bytes 1228808 | tf_op jit(solution)/shard_map/ppermute | solution.py:473
  67.3 44.4 %copy-start.1 = (f32[2,32,128,128]{3,2,1,0:T(8,128)S(1)}, f32[2,32,128,128]{3,2,1,0:T(8,128)}, u32[]{:S(2)}) copy-start(f32[2,32,128,128]{3,2,1,0:T(8,128)} %copy-done) | copy-start | bytes 12582916
  76.3 3.8 %collective-permute-start.3 = (bf16[64,8,512]{2,1,0:T(8,128)(2,1)S(1)}, bf16[64,8,512]{2,1,0:T(8,128)(2,1)S(1)}, u32[]{:S(2)}, u32[]{:S(2)}) collective-permute-start(bf16[64,8,512]{2,1,0:T(8,128)(2,1)S(1)} %slice_bitcast_fusion), channel_id=1, source_target_pairs={{0,16},{16,0},{1,17},{17,1},{2,18},{18,2},{3,19},{19,3},{4,20},{20... | collective-permute-start | bytes 1572872 | tf_op jit(solution)/shard_map/ppermute | solution.py:483
  111.8 56.5 %copy-start.10 = (bf16[2,128,128]{2,1,0:T(8,128)(2,1)S(1)}, bf16[2,128,128]{2,1,0:T(8,128)(2,1)}, u32[]{:S(2)}) copy-start(bf16[2,128,128]{2,1,0:T(8,128)(2,1)} %refs_3_.1) | copy-start | bytes 196612
  111.8 56.5 %copy-start.16 = (s32[1280]{0:T(1024)S(1)}, s32[1280]{0:T(1024)}, u32[]{:S(2)}) copy-start(s32[1280]{0:T(1024)} %refs_1_.1) | copy-start | bytes 15364
  116.4 32.1 %copy-start.7 = (bf16[80,40,128]{2,1,0:T(8,128)(2,1)}, bf16[80,40,128]{2,1,0:T(8,128)(2,1)S(1)}, u32[]{:S(2)}) copy-start(bf16[80,40,128]{2,1,0:T(8,128)(2,1)S(1)} %get-tuple-element.17.refs_5_) | copy-start | bytes 2457604
  149.9 16.3 %all-to-all-start.4 = ((bf16[4,160,320]{2,1,0:T(8,128)(2,1)}), bf16[4,160,320]{2,1,0:T(8,128)(2,1)S(1)}, u32[]{:S(2)}, u32[]{:S(2)}) async-start(bf16[4,160,320]{2,1,0:T(8,128)(2,1)} %bitcast.6), calls=%async_computation.4 | async-start | bytes 983040 | tf_op jit(solution)/shard_map/all_to_all | solution.py:479
  156.3 21.6 %collective-permute-start.5 = (bf16[320,640]{1,0:T(8,128)(2,1)S(1)}, bf16[320,640]{1,0:T(8,128)(2,1)S(1)}, u32[]{:S(2)}, u32[]{:S(2)}) collective-permute-start(bf16[320,640]{1,0:T(8,128)(2,1)S(1)} %shard_map.107.rest_0_), channel_id=1, source_target_pairs={{0,12},{4,0},{8,4},{12,8},{1,13},{5,1},{9,5},{13,9},{2,14},{6,2},{... | collective-permute-start | bytes 1228808 | tf_op jit(solution)/shard_map/ppermute | solution.py:473
  159.1 18.8 %collective-permute-start.6 = (bf16[320,640]{1,0:T(8,128)(2,1)S(1)}, bf16[320,640]{1,0:T(8,128)(2,1)S(1)}, u32[]{:S(2)}, u32[]{:S(2)}) collective-permute-start(bf16[320,640]{1,0:T(8,128)(2,1)S(1)} %shard_map.107.rest_0_), channel_id=1, source_target_pairs={{0,8},{4,12},{8,0},{12,4},{1,9},{5,13},{9,1},{13,5},{2,10},{6,14},... | collective-permute-start | bytes 1228808 | tf_op jit(solution)/shard_map/ppermute | solution.py:473
  161.7 17.1 %collective-permute-start.7 = (bf16[320,640]{1,0:T(8,128)(2,1)S(1)}, bf16[320,640]{1,0:T(8,128)(2,1)S(1)}, u32[]{:S(2)}, u32[]{:S(2)}) collective-permute-start(bf16[320,640]{1,0:T(8,128)(2,1)S(1)} %shard_map.107.rest_0_), channel_id=1, source_target_pairs={{0,4},{4,8},{8,12},{12,0},{1,5},{5,9},{9,13},{13,1},{2,6},{6,10},{... | collective-permute-start | bytes 1228808 | tf_op jit(solution)/shard_map/ppermute | solution.py:473
  166.2 12.6 %collective-permute-start.4 = (bf16[4,160,320]{2,1,0:T(8,128)(2,1)S(1)}, bf16[4,160,320]{2,1,0:T(8,128)(2,1)S(1)}, u32[]{:S(2)}, u32[]{:S(2)}) collective-permute-start(bf16[4,160,320]{2,1,0:T(8,128)(2,1)S(1)} %all-to-all-done.4.own_ref), channel_id=1, source_target_pairs={{0,16},{16,0},{1,17},{17,1},{2,18},{18,2},{3,19},{19,3},{4,20},{20... | collective-permute-start | bytes 1228808 | tf_op jit(solution)/shard_map/ppermute | solution.py:483
  168.3 1.1 copy-start.8
  (5 other events, 3.8 us)

commit v5 on v4

--- a/solution.py
+++ b/solution.py
@@ -41,7 +41,7 @@
     return (y * ZH + zh) * 2 + zl
 
 
-def call(kernel, out_shape, in_specs, scratch_shapes=(), flops=10**8, outs=None):
+def call(kernel, out_shape, in_specs, scratch_shapes=(), flops=10**8, outs=None, grant=40):
     outs = outs or jax.tree.map(lambda _: VMEM, out_shape)
     moved = 4 * 10**6
     return pl.pallas_call(
@@ -50,7 +50,7 @@
         in_specs=in_specs,
         out_specs=outs,
         scratch_shapes=scratch_shapes,
-        compiler_params=pltpu.CompilerParams(vmem_limit_bytes=40 * 2**20),
+        compiler_params=pltpu.CompilerParams(vmem_limit_bytes=grant * 2**20),
         cost_estimate=pl.CostEstimate(flops=flops, bytes_accessed=moved, transcendentals=0),
     )
 
@@ -140,9 +140,26 @@
 
 
 def right_kernel(
-    place_ref, valid_ref, pair_ref, vectors_ref, weight_ref, normed_ref, right_ref, right_s
+    place_ref,
+    valid_ref,
+    pair_any,
+    vectors_any,
+    weight_any,
+    normed_ref,
+    right_ref,
+    right_s,
+    pair_ref,
+    vectors_ref,
+    weight_ref,
+    sems,
 ):
+    moves = ((pair_any, pair_ref), (vectors_any, vectors_ref), (weight_any, weight_ref))
+    copies = [pltpu.make_async_copy(a, b, sems.at[n]) for n, (a, b) in enumerate(moves)]
+    for copy in copies:
+        copy.start()
     columns = spread_columns(place_ref, valid_ref)
+    for copy in copies:
+        copy.wait()
     weight = weight_of(weight_ref, 0, 2 * HIDDEN)
 
     def work(first, count):
@@ -158,10 +175,15 @@
     put_chunks(right_s, right_ref, STRIDE, DEPTH)
 
 
-def project_right(place, valid, pair, vectors, weight):
-    return call(right_kernel, [NORMED, CHUNKS], [SMEM, SMEM, VMEM, VMEM, VMEM], [SCRATCH])(
-        place, valid, pair, vectors, weight
-    )
+def project_right(place, valid, *operands):
+    scratch = [pltpu.VMEM(each.shape, each.dtype) for each in operands]
+    return call(
+        right_kernel,
+        [NORMED, CHUNKS],
+        [SMEM, SMEM] + [ANY] * 3,
+        [SCRATCH] + scratch + [pltpu.SemaphoreType.DMA((3,))],
+        grant=60,
+    )(place, valid, *operands)
 
 
 def load_normed(normed_ref, first):
@@ -380,7 +402,7 @@
     return call(functools.partial(assemble_kernel, layout), out, [VMEM])(chunks)
 
 
-def assemble_turned_kernel(layout, chunks_ref, out_ref, whole):
+def assemble_turned_kernel(layout, chunks_ref, _, out_ref, whole):
     def put(start, values):
         whole[pl.ds(start, 2 * SUB), :] = values
 
@@ -391,11 +413,11 @@
         out_ref[pl.ds(part * 128, 128), :] = turned[:, : ZH * ROWS].astype(jnp.bfloat16)
 
 
-def assemble_turned(chunks, layout):
+def assemble_turned(chunks, layout, after):
     out = jax.ShapeDtypeStruct((SPAN * COLUMNS, ZH * ROWS), jnp.bfloat16)
     scratch = [pltpu.VMEM((ZH * ROWS + 64, SPAN * COLUMNS), jnp.float32)]
     kernel = functools.partial(assemble_turned_kernel, layout)
-    return call(kernel, out, [VMEM], scratch)(chunks)
+    return call(kernel, out, [VMEM, ANY], scratch)(chunks, after)
 
 
 def chunk_of(total, zh, start):
@@ -410,13 +432,18 @@
     return jnp.concatenate(lanes, axis=1).astype(jnp.bfloat16)
 
 
+def blocks_of(refs):
+    whole = [ref[...] for ref in refs]
+    return [whole[0], whole[1], jnp.concatenate(whole[2:4], axis=0), whole[4]]
+
+
 def outgoing_kernel(core_ref, left_ref, *rest):
-    rights, (out_ref, left_s, total) = rest[:X], rest[X:]
+    rights, (out_ref, left_s, total) = rest[: X + 1], rest[X + 1 :]
     assemble_kernel(ALONE, left_ref, left_s)
-    for n, right_ref in enumerate(rights):
+    for n, right in enumerate(blocks_of(rights)):
         total[:, n * ZH * ROWS : (n + 1) * ZH * ROWS] = lax.dot_general(
             left_s[...],
-            right_ref[...],
+            right,
             (((1,), (1,)), ((), ())),
             preferred_element_type=jnp.float32,
         )
@@ -437,20 +464,20 @@
         pltpu.VMEM((ZH * ROWS, SPAN * COLUMNS), jnp.bfloat16),
         pltpu.VMEM((ZH * ROWS, X * ZH * ROWS), jnp.float32),
     ]
-    return call(outgoing_kernel, out, [SMEM] + [VMEM] * (1 + X), scratch, 6 * 10**8)(
+    return call(outgoing_kernel, out, [SMEM] + [VMEM] * (2 + X), scratch, 6 * 10**8)(
         core, left, *rights
     )
 
 
 def incoming_kernel(core_ref, own_ref, other_ref, *rest):
-    rights, (_, out_ref, total) = rest[:X], rest[X:]
+    rights, (_, out_ref, total) = rest[: X + 1], rest[X + 1 :]
     for n, left_ref in enumerate((own_ref, other_ref)):
         side = lax.rem(core_ref[0] + n, 2)
         product = jnp.zeros((ZH * COLUMNS, SPAN * COLUMNS), jnp.float32)
-        for m, right_ref in enumerate(rights):
+        for m, right in enumerate(blocks_of(rights)):
             product = product + jnp.dot(
                 left_ref[lax.rem(core_ref[1] + m, X)],
-                right_ref[...],
+                right,
                 preferred_element_type=jnp.float32,
             )
         for zh in range(ZH):
@@ -464,15 +491,19 @@
 def incoming(core, own, other, rights, gate):
     scratch = [pltpu.VMEM((ZH * ROWS, SPAN * COLUMNS), jnp.float32)]
     return call(
-        incoming_kernel, CHUNKS, [SMEM] + [VMEM] * (2 + X) + [ANY], scratch, 6 * 10**8
+        incoming_kernel, CHUNKS, [SMEM] + [VMEM] * (3 + X) + [ANY], scratch, 6 * 10**8
     )(core, own, other, *rights, gate)
 
 
 def gather_x(block):
-    def shift(by):
-        return lax.ppermute(block, "x", [(x, (x + by) % X) for x in range(X)])
-
-    return [block] + [shift(-n) for n in range(1, X)]
+    def shift(values, by):
+        return lax.ppermute(values, "x", [(x, (x - by) % X) for x in range(X)])
+
+    half = block.shape[0] // 2
+    before = shift(block, 3)
+    after = shift(block, 1)
+    straight = shift(block[:half], 2)
+    return [block, after, straight, shift(after[half:], 1), before]
 
 
 def exchange(values, axes):
@@ -516,7 +547,7 @@
     both = exchange(both, PLANE)
     rights = gather_x(assemble(both, RIGHT))
     gate = gates(1, place, chain_index, normed, gate_weight, vectors, middle)
-    left = assemble_turned(both, LEFT).reshape(X, ZH * COLUMNS, ZH * ROWS)
+    left = assemble_turned(both, LEFT, rights[0]).reshape(X, ZH * COLUMNS, ZH * ROWS)
     left = exchange(left, "x")
     product = exchange(incoming(core, left, swap_cores(left), rights, gate), PLANE)
     return finish(1, place, residue_valid, out_gain, gate, product, out_weight)[0]

time: 215 us -> 215 us (level)
  starting transfers between devices: 51.7 us -> 54.9 us
    all_to_all x3, waiting for transfers between devices: 18.6 us -> 8.97 us  [exchange(): return lax.all_to_all(values, axes, split_axis=0, concat_axis=0, tiled=True)]
    ppermute x6 -> x8, waiting for transfers between devices: 14.3 us -> 22.9 us  [shift(): return lax.ppermute(values, 'x', [(x, (x - by) % X) for x in range(X)])]
    ppermute x6 -> x8, starting transfers between devices: 19.6 us -> 24.4 us  [shift(): return lax.ppermute(values, 'x', [(x, (x - by) % X) for x in range(X)])]
  transfers between devices with their start and end apart: 11 -> 13, of which waited for: 7 -> 7; matrix products, arithmetic and copies ran while one was open for 0% -> 0% of each run, Pallas kernels for 2% -> 2%
where the time goes in v5:
time: 215 us; the launch traced here: 213 us
  blocking collectives  88.8 us (41%)
  starting transfers between devices  54.9 us (26%)
  waiting for transfers between devices  33.8 us (16%)
  Pallas kernels  24 us (11%)
  local copies, waits for them, and re-layouts  8.91 us (4%)
    all_to_all x3, blocking collectives, exchange(): return lax.all_to_all(values, axes, split_axis=0, concat_axis=0, tiled=True)  88.8 us
    all_to_all x3, starting transfers between devices, exchange(): return lax.all_to_all(values, axes, split_axis=0, concat_axis=0, tiled=True)  26.4 us
    ppermute x8, starting transfers between devices, shift(): return lax.ppermute(values, 'x', [(x, (x - by) % X) for x in range(X)])  24.4 us
    ppermute x8, waiting for transfers between devices, shift(): return lax.ppermute(values, 'x', [(x, (x - by) % X) for x in range(X)])  22.9 us
    all_to_all x3, waiting for transfers between devices, exchange(): return lax.all_to_all(values, axes, split_axis=0, concat_axis=0, tiled=True)  8.97 us
    unnamed x36, local copies, waits for them, and re-layouts  8.8 us
    pallas_call x2, Pallas kernels, finish(): call(functools.partial(finish_kernel, which), [out, NORMED, BOTH_CHUNKS]...  7.34 us
    pallas_call x1, Pallas kernels, project_right(): call(right_kernel, [NORMED, CHUNKS], [SMEM, SMEM] + [ANY] * 3, [SCRATCH]...  5.07 us
  transfers between devices with their start and end apart: 13, of which 7 were waited for; matrix products, arithmetic and copies ran while one was open for 0% of the time, Pallas kernels for 2%

profile of v5, /device:TPU:6, one launch (start us, length us, event | category | flops | bytes accessed | tf_op | source)
XLA Modules:
  0.0 213.0 jit_solution(6171873092089281693)
XLA Ops:
  1.9 5.1 %shard_map.100 = (bf16[32,128,128]{2,1,0:T(8,128)(2,1)}, bf16[64,8,512]{2,1,0:T(8,128)(2,1)}) custom-call(s32[2]{0:T(128)} %pad_add_fusion.place_ref.refs_0_, s32[1280]{0:T(1024)} %valid_ref.7, bf16[80,40,128]{2,1,0:T(8,128)(2,1)} %pair_ref.1, f32[6,128]{1,0:T(8,128)} %pad_maximum_fusion.vectors_any.vectors_ref.rest_0_.refs_4_, bf16[2,128,256]{2,1,0:T(8,128)(2,1)} %rest_1_.1), custom_call_target="tpu_custom_call" | custom-call | flops 100000000 | bytes 4000000 | tf_op jit(solution)/shard_map/pallas_call | solution.py:180
  7.0 16.6 %all-to-all-start.1 = ((bf16[64,8,512]{2,1,0:T(8,128)(2,1)}), bf16[64,8,512]{2,1,0:T(8,128)(2,1)S(1)}, u32[]{:S(2)}, u32[]{:S(2)}) async-start(bf16[64,8,512]{2,1,0:T(8,128)(2,1)} %get-tuple-element.15), calls=%async_computation.1 | async-start | bytes 1048576 | tf_op jit(solution)/shard_map/all_to_all | solution.py:510
  30.4 2.9 %shard_map.101 = (bf16[64,8,512]{2,1,0:T(8,128)(2,1)}, f32[2,32,128,128]{3,2,1,0:T(8,128)S(1)}) custom-call(s32[2]{0:T(128)S(1)} %copy-done.15, s32[1280]{0:T(1024)S(1)} %copy-done.9, s32[1280]{0:T(1024)S(1)} %copy-done.13, bf16[32,128,128]{2,1,0:T(8,128)(2,1)S(1)} %copy-done.5, bf16[2,128,256]{2,1,0:T(8,128)(2,1)S(1)} %copy-done.3, ...), custom_call_target="tpu_custom_call" | custom-call | flops 100000000 | bytes 4000000 | tf_op jit(solution)/shard_map/pallas_call | solution.py:259
  35.3 7.6 %all-to-all-done.1.chunks_ref = bf16[64,8,512]{2,1,0:T(8,128)(2,1)S(1)} async-done(((bf16[64,8,512]{2,1,0:T(8,128)(2,1)}), bf16[64,8,512]{2,1,0:T(8,128)(2,1)S(1)}, u32[]{:S(2)}, u32[]{:S(2)}) %all-to-all-start.1) | async-done | bytes 524320 | tf_op jit(solution)/shard_map/all_to_all | solution.py:510
  42.8 5.3 %all-to-all-start = ((bf16[64,8,512]{2,1,0:T(8,128)(2,1)}), bf16[64,8,512]{2,1,0:T(8,128)(2,1)S(1)}, u32[]{:S(2)}, u32[]{:S(2)}) async-start(bf16[64,8,512]{2,1,0:T(8,128)(2,1)} %get-tuple-element.14), calls=%async_computation | async-start | bytes 1048576 | tf_op jit(solution)/shard_map/all_to_all | solution.py:510
  48.7 2.8 %collective-permute-start = (bf16[320,640]{1,0:T(8,128)(2,1)S(1)}, bf16[320,640]{1,0:T(8,128)(2,1)S(1)}, u32[]{:S(2)}, u32[]{:S(2)}) collective-permute-start(bf16[320,640]{1,0:T(8,128)(2,1)S(1)} %shard_map.102.rest_0_), channel_id=1, source_target_pairs={{0,12},{4,0},{8,4},{12,8},{1,13},{5,1},{9,5},{13,9},{2,14},{6,2},{... | collective-permute-start | bytes 1228808 | tf_op jit(solution)/shard_map/ppermute | solution.py:500
  51.4 4.3 %collective-permute-start.3 = (bf16[320,640]{1,0:T(8,128)(2,1)S(1)}, bf16[320,640]{1,0:T(8,128)(2,1)S(1)}, u32[]{:S(2)}, u32[]{:S(2)}) collective-permute-start(bf16[320,640]{1,0:T(8,128)(2,1)S(1)} %shard_map.102.rest_0_), channel_id=1, source_target_pairs={{0,4},{4,8},{8,12},{12,0},{1,5},{5,9},{9,13},{13,1},{2,6},{6,10},{... | collective-permute-start | bytes 1228808 | tf_op jit(solution)/shard_map/ppermute | solution.py:500
  55.8 2.1 collective-permute-start.1
  57.9 8.7 %collective-permute-done.rest_1_ = bf16[320,640]{1,0:T(8,128)(2,1)S(1)} collective-permute-done((bf16[320,640]{1,0:T(8,128)(2,1)S(1)}, bf16[320,640]{1,0:T(8,128)(2,1)S(1)}, u32[]{:S(2)}, u32[]{:S(2)}) %collective-permute-start) | collective-permute-done | bytes 409632 | tf_op jit(solution)/shard_map/ppermute | solution.py:500
  68.6 6.8 %collective-permute-done.2.rest_3_ = bf16[160,640]{1,0:T(8,128)(2,1)S(1)} collective-permute-done((bf16[160,640]{1,0:T(8,128)(2,1)S(1)}, bf16[160,640]{1,0:T(8,128)(2,1)S(1)}, u32[]{:S(2)}, u32[]{:S(2)}) %collective-permute-start.2) | collective-permute-done | bytes 204832 | tf_op jit(solution)/shard_map/ppermute | solution.py:500
  75.5 2.5 %shard_map.103 = bf16[2,64,8,512]{3,2,1,0:T(8,128)(2,1)S(1)} custom-call(s32[2]{0:T(128)S(1)} %pad_add_fusion.1.core_ref, bf16[64,8,512]{2,1,0:T(8,128)(2,1)S(1)} %all-to-all-done.left_ref, bf16[320,640]{1,0:T(8,128)(2,1)S(1)} %shard_map.102.rest_0_, bf16[320,640]{1,0:T(8,128)(2,1)S(1)} %collective-permute-done.rest_1_, ...), custom_call_target="tpu_custom_call" | custom-call | flops 600000000 | bytes 4000000 | tf_op jit(solution)/shard_map/pallas_call | solution.py:467
  81.9 31.0 %all_to_all.30.product_ref = bf16[64,8,512]{2,1,0:T(8,128)(2,1)S(1)} all-to-all(bf16[64,8,512]{2,1,0:T(8,128)(2,1)S(1)} %fusion), channel_id=1, replica_groups=mesh['zl'=2,'y'=8,'core'=2,'x'=4,'zh'=4] {'y','zh','zl'}, dimensions={0} | all-to-all | bytes 1048576 | tf_op jit(solution)/shard_map/all_to_all | solution.py:510
  113.0 4.6 %shard_map.104 = (bf16[80,40,128]{2,1,0:T(8,128)(2,1)S(1)}, bf16[32,128,128]{2,1,0:T(8,128)(2,1)S(1)}, bf16[64,8,896]{2,1,0:T(8,128)(2,1)S(1)}) custom-call(s32[2]{0:T(128)S(1)} %copy-done.16, s32[1280]{0:T(1024)S(1)} %copy-done.10, f32[2,64]{1,0:T(2,128)S(1)} %copy-done.17, f32[2,32,128,128]{3,2,1,0:T(8,128)S(1)} %copy-done.1, ...), custom_call_target="tpu_custom_call" | custom-call | flops 100000000 | bytes 4000000 | tf_op jit(solution)/shard_map/pallas_call | solution.py:358
  117.6 32.3 %all_to_all.31.chunks_ref = bf16[64,8,896]{2,1,0:T(8,128)(2,1)S(1)} all-to-all(bf16[64,8,896]{2,1,0:T(8,128)(2,1)S(1)} %get-tuple-element.18), channel_id=1, replica_groups=mesh['zl'=2,'y'=8,'core'=2,'x'=4,'zh'=4] {'y','zh','zl'}, dimensions={0} | all-to-all | bytes 1835008 | tf_op jit(solution)/shard_map/all_to_all | solution.py:510
  151.6 4.5 %all-to-all-start.4 = ((bf16[4,160,320]{2,1,0:T(8,128)(2,1)}), bf16[4,160,320]{2,1,0:T(8,128)(2,1)S(1)}, u32[]{:S(2)}, u32[]{:S(2)}) async-start(bf16[4,160,320]{2,1,0:T(8,128)(2,1)} %bitcast.6), calls=%async_computation.4 | async-start | bytes 983040 | tf_op jit(solution)/shard_map/all_to_all | solution.py:510
  156.1 2.8 %collective-permute-start.6 = (bf16[320,640]{1,0:T(8,128)(2,1)S(1)}, bf16[320,640]{1,0:T(8,128)(2,1)S(1)}, u32[]{:S(2)}, u32[]{:S(2)}) collective-permute-start(bf16[320,640]{1,0:T(8,128)(2,1)S(1)} %shard_map.106._.rest_0_), channel_id=1, source_target_pairs={{0,12},{4,0},{8,4},{12,8},{1,13},{5,1},{9,5},{13,9},{2,14},{6,2},{... | collective-permute-start | bytes 1228808 | tf_op jit(solution)/shard_map/ppermute | solution.py:500
  158.9 4.3 %collective-permute-start.9 = (bf16[320,640]{1,0:T(8,128)(2,1)S(1)}, bf16[320,640]{1,0:T(8,128)(2,1)}, u32[]{:S(2)}, u32[]{:S(2)}) collective-permute-start(bf16[320,640]{1,0:T(8,128)(2,1)S(1)} %shard_map.106._.rest_0_), channel_id=1, source_target_pairs={{0,4},{4,8},{8,12},{12,0},{1,5},{5,9},{9,13},{13,1},{2,6},{6,10},{... | collective-permute-start | bytes 1228808 | tf_op jit(solution)/shard_map/ppermute | solution.py:500
  166.7 4.0 %collective-permute-start.7 = (bf16[160,640]{1,0:T(8,128)(2,1)S(1)}, bf16[160,640]{1,0:T(8,128)(2,1)S(1)}, u32[]{:S(2)}, u32[]{:S(2)}) collective-permute-start(bf16[160,640]{1,0:T(8,128)(2,1)S(1)} %slice.28), channel_id=1, source_target_pairs={{0,8},{4,12},{8,0},{12,4},{1,9},{5,13},{9,1},{13,5},{2,10},{6,14},... | collective-permute-start | bytes 614408 | tf_op jit(solution)/shard_map/ppermute | solution.py:500
  170.7 2.3 %collective-permute-start.8 = (bf16[160,640]{1,0:T(8,128)(2,1)S(1)}, bf16[160,640]{1,0:T(8,128)(2,1)S(1)}, u32[]{:S(2)}, u32[]{:S(2)}) collective-permute-start(bf16[160,640]{1,0:T(8,128)(2,1)S(1)} %slice.29), channel_id=1, source_target_pairs={{0,12},{4,0},{8,4},{12,8},{1,13},{5,1},{9,5},{13,9},{2,14},{6,2},{... | collective-permute-start | bytes 614408 | tf_op jit(solution)/shard_map/ppermute | solution.py:500
  174.6 3.4 %collective-permute-done.7.rest_2_ = bf16[160,640]{1,0:T(8,128)(2,1)S(1)} collective-permute-done((bf16[160,640]{1,0:T(8,128)(2,1)S(1)}, bf16[160,640]{1,0:T(8,128)(2,1)S(1)}, u32[]{:S(2)}, u32[]{:S(2)}) %collective-permute-start.7) | collective-permute-done | bytes 204832 | tf_op jit(solution)/shard_map/ppermute | solution.py:500
  178.0 4.0 %collective-permute-done.8.rest_3_ = bf16[160,640]{1,0:T(8,128)(2,1)S(1)} collective-permute-done((bf16[160,640]{1,0:T(8,128)(2,1)S(1)}, bf16[160,640]{1,0:T(8,128)(2,1)S(1)}, u32[]{:S(2)}, u32[]{:S(2)}) %collective-permute-start.8) | collective-permute-done | bytes 204832 | tf_op jit(solution)/shard_map/ppermute | solution.py:500
  182.0 2.6 %shard_map.108 = bf16[64,8,512]{2,1,0:T(8,128)(2,1)S(1)} custom-call(s32[2]{0:T(128)S(1)} %pad_add_fusion.1.core_ref, bf16[4,160,320]{2,1,0:T(8,128)(2,1)S(1)} %all-to-all-done.4.own_ref, bf16[4,160,320]{2,1,0:T(8,128)(2,1)S(1)} %collective-permute-done.5.other_ref, bf16[320,640]{1,0:T(8,128)(2,1)S(1)} %shard_map.106._.rest_0_, ...), custom_call_target="tpu_custom_call" | custom-call | flops 600000000 | bytes 4000000 | tf_op jit(solution)/shard_map/pallas_call | solution.py:493
  184.6 25.5 %all_to_all.32.product_ref = bf16[64,8,512]{2,1,0:T(8,128)(2,1)S(1)} all-to-all(bf16[64,8,512]{2,1,0:T(8,128)(2,1)S(1)} %shard_map.108), channel_id=1, replica_groups=mesh['zl'=2,'y'=8,'core'=2,'x'=4,'zh'=4] {'y','zh','zl'}, dimensions={0} | all-to-all | bytes 1048576 | tf_op jit(solution)/shard_map/all_to_all | solution.py:510
  210.1 2.8 %shard_map.109 = bf16[80,40,128]{2,1,0:T(8,128)(2,1)} custom-call(s32[2]{0:T(128)S(1)} %copy-done.16, s32[1280]{0:T(1024)S(1)} %copy-done.10, f32[2,64]{1,0:T(2,128)S(1)} %copy-done.17, f32[2,32,128,128]{3,2,1,0:T(8,128)S(1)} %shard_map.105.rest_5_.gates_ref, bf16[64,8,512]{2,1,0:T(8,128)(2,1)S(1)} %all_to_all.32.product_ref, bf16[2,64,128]{2,1,0:T(8,128)(2,1)S(1)} %copy-done.8), custom_call_target="tpu_custom_call" | custom-call | flops 100000000 | bytes 4000000 | tf_op jit(solution)/shard_map/pallas_call | solution.py:358
  (60 shorter events, 23.9 us)
Async XLA Ops:
  7.0 35.9 %all-to-all-start.1 = ((bf16[64,8,512]{2,1,0:T(8,128)(2,1)}), bf16[64,8,512]{2,1,0:T(8,128)(2,1)S(1)}, u32[]{:S(2)}, u32[]{:S(2)}) async-start(bf16[64,8,512]{2,1,0:T(8,128)(2,1)} %get-tuple-element.15), calls=%async_computation.1 | async-start | bytes 1048576 | tf_op jit(solution)/shard_map/all_to_all | solution.py:510
  25.6 1.2 copy-start.5
  33.3 2.0 copy-start
  42.8 25.8 %all-to-all-start = ((bf16[64,8,512]{2,1,0:T(8,128)(2,1)}), bf16[64,8,512]{2,1,0:T(8,128)(2,1)S(1)}, u32[]{:S(2)}, u32[]{:S(2)}) async-start(bf16[64,8,512]{2,1,0:T(8,128)(2,1)} %get-tuple-element.14), calls=%async_computation | async-start | bytes 1048576 | tf_op jit(solution)/shard_map/all_to_all | solution.py:510
  48.2 64.8 %copy-start.4 = (bf16[2,128,256]{2,1,0:T(8,128)(2,1)S(1)}, bf16[2,128,256]{2,1,0:T(8,128)(2,1)}, u32[]{:S(2)}) copy-start(bf16[2,128,256]{2,1,0:T(8,128)(2,1)} %rest_1_.1) | copy-start | bytes 393220
  48.2 64.8 %copy-start.8 = (bf16[2,64,128]{2,1,0:T(8,128)(2,1)S(1)}, bf16[2,64,128]{2,1,0:T(8,128)(2,1)}, u32[]{:S(2)}) copy-start(bf16[2,64,128]{2,1,0:T(8,128)(2,1)} %out_weight_ref.3) | copy-start | bytes 98308
  48.2 64.7 %copy-start.10 = (s32[1280]{0:T(1024)S(1)}, s32[1280]{0:T(1024)}, u32[]{:S(2)}) copy-start(s32[1280]{0:T(1024)} %valid_ref.7) | copy-start | bytes 15364
  48.2 64.7 %copy-start.12 = (f32[6,128]{1,0:T(8,128)S(1)}, f32[6,128]{1,0:T(8,128)}, u32[]{:S(2)}) copy-start(f32[6,128]{1,0:T(8,128)} %pad_maximum_fusion.vectors_any.vectors_ref.rest_0_.refs_4_) | copy-start | bytes 9220
  48.2 64.7 %copy-start.16 = (s32[2]{0:T(128)S(1)}, s32[2]{0:T(128)}, u32[]{:S(2)}) copy-start(s32[2]{0:T(128)} %pad_add_fusion.place_ref.refs_0_) | copy-start | bytes 28
  48.2 64.7 %copy-start.17 = (f32[2,64]{1,0:T(2,128)S(1)}, f32[2,64]{1,0:T(2,128)}, u32[]{:S(2)}) copy-start(f32[2,64]{1,0:T(2,128)} %out_gain_ref.3) | copy-start | bytes 1540
  48.7 17.9 %collective-permute-start = (bf16[320,640]{1,0:T(8,128)(2,1)S(1)}, bf16[320,640]{1,0:T(8,128)(2,1)S(1)}, u32[]{:S(2)}, u32[]{:S(2)}) collective-permute-start(bf16[320,640]{1,0:T(8,128)(2,1)S(1)} %shard_map.102.rest_0_), channel_id=1, source_target_pairs={{0,12},{4,0},{8,4},{12,8},{1,13},{5,1},{9,5},{13,9},{2,14},{6,2},{... | collective-permute-start | bytes 1228808 | tf_op jit(solution)/shard_map/ppermute | solution.py:500
  51.4 17.2 %collective-permute-start.3 = (bf16[320,640]{1,0:T(8,128)(2,1)S(1)}, bf16[320,640]{1,0:T(8,128)(2,1)S(1)}, u32[]{:S(2)}, u32[]{:S(2)}) collective-permute-start(bf16[320,640]{1,0:T(8,128)(2,1)S(1)} %shard_map.102.rest_0_), channel_id=1, source_target_pairs={{0,4},{4,8},{8,12},{12,0},{1,5},{5,9},{9,13},{13,1},{2,6},{6,10},{... | collective-permute-start | bytes 1228808 | tf_op jit(solution)/shard_map/ppermute | solution.py:500
  55.8 12.9 %collective-permute-start.1 = (bf16[160,640]{1,0:T(8,128)(2,1)S(1)}, bf16[160,640]{1,0:T(8,128)(2,1)S(1)}, u32[]{:S(2)}, u32[]{:S(2)}) collective-permute-start(bf16[160,640]{1,0:T(8,128)(2,1)S(1)} %slice.24), channel_id=1, source_target_pairs={{0,8},{4,12},{8,0},{12,4},{1,9},{5,13},{9,1},{13,5},{2,10},{6,14},... | collective-permute-start | bytes 614408 | tf_op jit(solution)/shard_map/ppermute | solution.py:500
  66.6 8.9 %collective-permute-start.2 = (bf16[160,640]{1,0:T(8,128)(2,1)S(1)}, bf16[160,640]{1,0:T(8,128)(2,1)S(1)}, u32[]{:S(2)}, u32[]{:S(2)}) collective-permute-start(bf16[160,640]{1,0:T(8,128)(2,1)S(1)} %slice.25), channel_id=1, source_target_pairs={{0,12},{4,0},{8,4},{12,8},{1,13},{5,1},{9,5},{13,9},{2,14},{6,2},{... | collective-permute-start | bytes 614408 | tf_op jit(solution)/shard_map/ppermute | solution.py:500
  68.6 44.4 %copy-start.1 = (f32[2,32,128,128]{3,2,1,0:T(8,128)S(1)}, f32[2,32,128,128]{3,2,1,0:T(8,128)}, u32[]{:S(2)}) copy-start(f32[2,32,128,128]{3,2,1,0:T(8,128)} %copy-done) | copy-start | bytes 12582916
  78.0 3.8 %collective-permute-start.4 = (bf16[64,8,512]{2,1,0:T(8,128)(2,1)S(1)}, bf16[64,8,512]{2,1,0:T(8,128)(2,1)S(1)}, u32[]{:S(2)}, u32[]{:S(2)}) collective-permute-start(bf16[64,8,512]{2,1,0:T(8,128)(2,1)S(1)} %slice_bitcast_fusion), channel_id=1, source_target_pairs={{0,16},{16,0},{1,17},{17,1},{2,18},{18,2},{3,19},{19,3},{4,20},{20... | collective-permute-start | bytes 1572872 | tf_op jit(solution)/shard_map/ppermute | solution.py:514
  117.6 55.5 %copy-start.7 = (bf16[2,128,128]{2,1,0:T(8,128)(2,1)S(1)}, bf16[2,128,128]{2,1,0:T(8,128)(2,1)}, u32[]{:S(2)}) copy-start(bf16[2,128,128]{2,1,0:T(8,128)(2,1)} %refs_3_.1) | copy-start | bytes 196612
  117.6 55.5 %copy-start.14 = (s32[1280]{0:T(1024)S(1)}, s32[1280]{0:T(1024)}, u32[]{:S(2)}) copy-start(s32[1280]{0:T(1024)} %refs_1_.1) | copy-start | bytes 15364
  151.6 13.0 %all-to-all-start.4 = ((bf16[4,160,320]{2,1,0:T(8,128)(2,1)}), bf16[4,160,320]{2,1,0:T(8,128)(2,1)S(1)}, u32[]{:S(2)}, u32[]{:S(2)}) async-start(bf16[4,160,320]{2,1,0:T(8,128)(2,1)} %bitcast.6), calls=%async_computation.4 | async-start | bytes 983040 | tf_op jit(solution)/shard_map/all_to_all | solution.py:510
  156.1 14.6 %collective-permute-start.6 = (bf16[320,640]{1,0:T(8,128)(2,1)S(1)}, bf16[320,640]{1,0:T(8,128)(2,1)S(1)}, u32[]{:S(2)}, u32[]{:S(2)}) collective-permute-start(bf16[320,640]{1,0:T(8,128)(2,1)S(1)} %shard_map.106._.rest_0_), channel_id=1, source_target_pairs={{0,12},{4,0},{8,4},{12,8},{1,13},{5,1},{9,5},{13,9},{2,14},{6,2},{... | collective-permute-start | bytes 1228808 | tf_op jit(solution)/shard_map/ppermute | solution.py:500
  158.9 19.1 %collective-permute-start.9 = (bf16[320,640]{1,0:T(8,128)(2,1)S(1)}, bf16[320,640]{1,0:T(8,128)(2,1)}, u32[]{:S(2)}, u32[]{:S(2)}) collective-permute-start(bf16[320,640]{1,0:T(8,128)(2,1)S(1)} %shard_map.106._.rest_0_), channel_id=1, source_target_pairs={{0,4},{4,8},{8,12},{12,0},{1,5},{5,9},{9,13},{13,1},{2,6},{6,10},{... | collective-permute-start | bytes 1228808 | tf_op jit(solution)/shard_map/ppermute | solution.py:500
  164.6 17.4 %collective-permute-start.5 = (bf16[4,160,320]{2,1,0:T(8,128)(2,1)S(1)}, bf16[4,160,320]{2,1,0:T(8,128)(2,1)S(1)}, u32[]{:S(2)}, u32[]{:S(2)}) collective-permute-start(bf16[4,160,320]{2,1,0:T(8,128)(2,1)S(1)} %all-to-all-done.4.own_ref), channel_id=1, source_target_pairs={{0,16},{16,0},{1,17},{17,1},{2,18},{18,2},{3,19},{19,3},{4,20},{20... | collective-permute-start | bytes 1228808 | tf_op jit(solution)/shard_map/ppermute | solution.py:514
  166.7 11.3 %collective-permute-start.7 = (bf16[160,640]{1,0:T(8,128)(2,1)S(1)}, bf16[160,640]{1,0:T(8,128)(2,1)S(1)}, u32[]{:S(2)}, u32[]{:S(2)}) collective-permute-start(bf16[160,640]{1,0:T(8,128)(2,1)S(1)} %slice.28), channel_id=1, source_target_pairs={{0,8},{4,12},{8,0},{12,4},{1,9},{5,13},{9,1},{13,5},{2,10},{6,14},... | collective-permute-start | bytes 614408 | tf_op jit(solution)/shard_map/ppermute | solution.py:500
  170.7 11.2 %collective-permute-start.8 = (bf16[160,640]{1,0:T(8,128)(2,1)S(1)}, bf16[160,640]{1,0:T(8,128)(2,1)S(1)}, u32[]{:S(2)}, u32[]{:S(2)}) collective-permute-start(bf16[160,640]{1,0:T(8,128)(2,1)S(1)} %slice.29), channel_id=1, source_target_pairs={{0,12},{4,0},{8,4},{12,8},{1,13},{5,1},{9,5},{13,9},{2,14},{6,2},{... | collective-permute-start | bytes 614408 | tf_op jit(solution)/shard_map/ppermute | solution.py:500
  (7 other events, 5.6 us)

commit v6 on v3

--- a/solution.py
+++ b/solution.py
@@ -25,10 +25,8 @@
 WHOLE = 3
 TAIL = 8 * 9
 STRIDE = 40
-BOTH = 56
 BATCH = 8
 CHUNKS = jax.ShapeDtypeStruct((HIDDEN, SUB, DEPTH // SUB * LANES), jnp.bfloat16)
-BOTH_CHUNKS = jax.ShapeDtypeStruct((HIDDEN, SUB, BOTH // SUB * LANES), jnp.bfloat16)
 NORMED = jax.ShapeDtypeStruct((DEPTH, LANES, WIDTH), jnp.bfloat16)
 GATES = jax.ShapeDtypeStruct((2, DEPTH, LANES, WIDTH), jnp.float32)
 VMEM = pl.BlockSpec(memory_space=pltpu.VMEM)
@@ -97,14 +95,14 @@
     return jnp.where(lane < 3 * COLUMNS, found, 0.0)
 
 
-def mask_of(first, count, place_ref, valid_ref, columns, shift=0):
+def mask_of(first, count, place_ref, valid_ref, columns):
     lane = lax.broadcasted_iota(jnp.int32, (1, LANES), 1)
     masks = []
     for rows in block_rows(first, count):
         mask = jnp.zeros((1, LANES), jnp.float32)
         for group, row in enumerate(rows):
             value = valid_ref[place_ref[0] + row].astype(jnp.float32)
-            start = (group + shift) * COLUMNS
+            start = group * COLUMNS
             inside = (lane >= start) & (lane < start + COLUMNS)
             mask = jnp.where(inside, value, mask)
         masks.append(mask * columns)
@@ -123,16 +121,16 @@
     return jax.nn.sigmoid(proj[HIDDEN:]) * proj[:HIDDEN] * mask
 
 
-def keep_rows(factor, scratch, first, stride):
+def keep_rows(factor, scratch, first):
     for n in range(BATCH):
-        place = pl.ds(first + n, HIDDEN, stride=stride)
+        place = pl.ds(first + n, HIDDEN, stride=STRIDE)
         scratch[place, :] = factor[:, n * LANES : (n + 1) * LANES]
 
 
-def put_chunks(scratch, out_ref, stride, depth):
+def put_chunks(scratch, out_ref):
     for channel in range(HIDDEN):
-        rows = scratch[pl.ds(channel * stride, depth), :]
-        tiles = [rows[n : n + SUB] for n in range(0, depth, SUB)]
+        rows = scratch[pl.ds(channel * STRIDE, DEPTH), :]
+        tiles = [rows[n : n + SUB] for n in range(0, DEPTH, SUB)]
         out_ref[channel] = jnp.concatenate(tiles, axis=1).astype(jnp.bfloat16)
 
 
@@ -155,7 +153,7 @@
     weight_ref,
     sems,
 ):
-    moves = ((pair_any, pair_ref), (gain_any, gain_ref), (bias_any, bias_ref), (weight_any, weight_ref))
+    moves = ((gain_any, gain_ref), (bias_any, bias_ref), (weight_any, weight_ref), (pair_any, pair_ref))
     copies = [pltpu.make_async_copy(a, b, sems.at[n]) for n, (a, b) in enumerate(moves)]
     for copy in copies:
         copy.start()
@@ -171,10 +169,10 @@
             normed_ref[first + n] = pieces[n]
         mask = mask_of(first, count, place_ref, valid_ref, columns)
         factor = factor_of(jnp.concatenate(pieces, axis=0), weight, mask)
-        keep_rows(factor, right_s, first, STRIDE)
+        keep_rows(factor, right_s, first)
 
     batches(work)
-    put_chunks(right_s, right_ref, STRIDE, DEPTH)
+    put_chunks(right_s, right_ref)
 
 
 def project_right(place, valid, *operands):
@@ -218,18 +216,8 @@
     return work
 
 
-def gate_kernel(which, *refs):
-    batches(gate_work(which, *refs))
-
-
-def gates(which, place, chain, normed, gate, chain_bias, pair):
-    kernel = functools.partial(gate_kernel, which)
-    return call(kernel, GATES, [SMEM, SMEM, VMEM, VMEM, VMEM, VMEM])(
-        place, chain, normed, gate, chain_bias, pair
-    )
-
-
 def left_and_gate_kernel(
+    which,
     place_ref,
     valid_ref,
     chain_ref,
@@ -243,22 +231,23 @@
     left_s,
 ):
     columns = spread_columns(place_ref, valid_ref)
-    weight = weight_of(weight_ref, 0, 0)
+    weight = weight_of(weight_ref, which, 0)
     gate = gate_work(
-        0, place_ref, chain_ref, normed_ref, gate_ref, chain_bias_ref, pair_ref, out_ref
+        which, place_ref, chain_ref, normed_ref, gate_ref, chain_bias_ref, pair_ref, out_ref
     )
 
     def work(first, count):
         mask = mask_of(first, count, place_ref, valid_ref, columns)
-        keep_rows(factor_of(load_normed(normed_ref, first), weight, mask), left_s, first, STRIDE)
+        keep_rows(factor_of(load_normed(normed_ref, first), weight, mask), left_s, first)
         gate(first, count)
 
     batches(work)
-    put_chunks(left_s, left_ref, STRIDE, DEPTH)
-
-
-def left_and_gates(place, valid, chain, normed, weight, gate, chain_bias, pair):
-    return call(left_and_gate_kernel, [CHUNKS, GATES], [SMEM] * 3 + [VMEM] * 5, [SCRATCH])(
+    put_chunks(left_s, left_ref)
+
+
+def left_and_gates(which, place, valid, chain, normed, weight, gate, chain_bias, pair):
+    kernel = functools.partial(left_and_gate_kernel, which)
+    return call(kernel, [CHUNKS, GATES], [SMEM] * 3 + [VMEM] * 5, [SCRATCH])(
         place, valid, chain, normed, weight, gate, chain_bias, pair
     )
 
@@ -266,11 +255,10 @@
 def finish_kernel(which, place_ref, valid_ref, out_gain_ref, gates_ref, product_ref, out_weight_ref, *rest):
     then = which == 0
     if then:
-        gain_ref, bias_ref, weight_ref, out_ref, normed_ref, both_ref, hidden_s, both_s = rest
+        gain_ref, bias_ref, weight_ref, out_ref, normed_ref, right_ref, hidden_s, right_s = rest
         new_s = out_ref
         columns = spread_columns(place_ref, valid_ref)
-        left_weight = weight_of(weight_ref, 1, 0)
-        right_weight = weight_of(weight_ref, 1, 2 * HIDDEN)
+        weight = weight_of(weight_ref, 1, 2 * HIDDEN)
     else:
         out_ref, hidden_s, new_s, out_sem = rest
 
@@ -320,34 +308,16 @@
                 pltpu.make_async_copy(new_s.at[span], out_ref.at[span], out_sem).start()
             return
         new = new.astype(jnp.bfloat16).astype(jnp.float32)
-        values = normalize(new, gain_ref[1:2], bias_ref[1:2])
-        pieces = pad_rows(values, count)
+        pieces = pad_rows(normalize(new, gain_ref[1:2], bias_ref[1:2]), count)
         for n in range(BATCH):
             normed_ref[first + n] = pieces[n]
         mask = mask_of(first, count, place_ref, valid_ref, columns)
-        if count == 3:
-            normed = jnp.concatenate(pieces, axis=0)
-            keep_rows(factor_of(normed, left_weight, mask), both_s, first, BOTH)
-            right_first = first + WHOLE * SUB
-            keep_rows(factor_of(normed, right_weight, mask), both_s, right_first, BOTH)
-        else:
-            twice = [values[n * size : (n + 1) * size] for n in range(BATCH) for _ in range(2)]
-            normed = jnp.concatenate(
-                [
-                    each
-                    for n in range(BATCH)
-                    for each in twice[2 * n : 2 * n + 2]
-                    + [jnp.zeros((LANES - 2 * size, WIDTH), jnp.float32)]
-                ],
-                axis=0,
-            ).astype(jnp.bfloat16)
-            other = mask_of(first, count, place_ref, valid_ref, columns, 1)
-            factor = factor_of(normed, left_weight, mask) + factor_of(normed, right_weight, other)
-            keep_rows(factor, both_s, 2 * WHOLE * SUB, BOTH)
+        factor = factor_of(jnp.concatenate(pieces, axis=0), weight, mask)
+        keep_rows(factor, right_s, first)
 
     batches(work)
     if then:
-        put_chunks(both_s, both_ref, BOTH, BOTH)
+        put_chunks(right_s, right_ref)
     else:
         pltpu.make_async_copy(new_s, out_ref, out_sem).wait()
 
@@ -355,27 +325,20 @@
 def finish(which, place, valid, out_gain, gate, product, out_weight, *then):
     shape = (ROWS, COLUMNS, WIDTH)
     out = jax.ShapeDtypeStruct(shape, jnp.bfloat16)
-    both = [pltpu.VMEM(((HIDDEN + 1) * BOTH, LANES), jnp.float32)]
     last = [pltpu.VMEM(shape, jnp.bfloat16), pltpu.SemaphoreType.DMA]
     return call(
         functools.partial(finish_kernel, which),
-        [out, NORMED, BOTH_CHUNKS] if then else [out],
+        [out, NORMED, CHUNKS] if then else [out],
         [SMEM] * 3 + [VMEM] * (3 + len(then)),
-        [SCRATCH] + (both if then else last),
+        [SCRATCH] + ([SCRATCH] if then else last),
         outs=None if then else [ANY],
     )(place, valid, out_gain, gate, product, out_weight, *then)
 
 
-ALONE = (0, 3, 0)
-LEFT = (0, 6, 0)
-RIGHT = (3, 6, COLUMNS)
-
-
-def gather_rows(chunks_ref, zh, block, layout):
-    tile, last_tile, last_lane = layout
-    start = last_tile * LANES + last_lane
+def gather_rows(chunks_ref, zh, block):
+    start = WHOLE * LANES
     if block < 9:
-        start = (tile + block % 3) * LANES + block // 3 * COLUMNS
+        start = block % 3 * LANES + block // 3 * COLUMNS
     return jnp.concatenate(
         [
             chunks_ref[spot(span, zh)].astype(jnp.float32)[:, start : start + COLUMNS]
@@ -385,41 +348,42 @@
     )
 
 
-def assemble_into(chunks_ref, layout, put):
+def assemble_into(chunks_ref, put):
     for zh in range(ZH):
         for block in range(0, ROWS // SUB, 2):
-            rows = [gather_rows(chunks_ref, zh, block + n, layout) for n in range(2)]
+            rows = [gather_rows(chunks_ref, zh, block + n) for n in range(2)]
             put(zh * ROWS + block * SUB, jnp.concatenate(rows, axis=0))
 
 
-def assemble_kernel(layout, chunks_ref, out_ref):
+def assemble_kernel(chunks_ref, out_ref):
     def put(start, values):
-        out_ref[pl.ds(start, 2 * SUB), :] = values.astype(jnp.bfloat16)
-
-    assemble_into(chunks_ref, layout, put)
-
-
-def assemble(chunks, layout):
-    out = jax.ShapeDtypeStruct((ZH * ROWS, SPAN * COLUMNS), jnp.bfloat16)
-    return call(functools.partial(assemble_kernel, layout), out, [VMEM])(chunks)
-
-
-def assemble_turned_kernel(layout, chunks_ref, out_ref, whole):
+        rows = values.astype(jnp.bfloat16)
+        for x in range(X):
+            out_ref[x, pl.ds(start, 2 * SUB)] = rows
+
+    assemble_into(chunks_ref, put)
+
+
+def assemble(chunks):
+    out = jax.ShapeDtypeStruct((X, ZH * ROWS, SPAN * COLUMNS), jnp.bfloat16)
+    return call(assemble_kernel, out, [VMEM])(chunks)
+
+
+def assemble_turned_kernel(chunks_ref, out_ref, whole):
     def put(start, values):
         whole[pl.ds(start, 2 * SUB), :] = values
 
-    assemble_into(chunks_ref, layout, put)
+    assemble_into(chunks_ref, put)
     whole[pl.ds(ZH * ROWS, 64), :] = jnp.zeros((64, SPAN * COLUMNS), jnp.float32)
     for part in range(SPAN * COLUMNS // 128):
         turned = whole[:, part * 128 : (part + 1) * 128].T
         out_ref[pl.ds(part * 128, 128), :] = turned[:, : ZH * ROWS].astype(jnp.bfloat16)
 
 
-def assemble_turned(chunks, layout):
+def assemble_turned(chunks):
     out = jax.ShapeDtypeStruct((SPAN * COLUMNS, ZH * ROWS), jnp.bfloat16)
     scratch = [pltpu.VMEM((ZH * ROWS + 64, SPAN * COLUMNS), jnp.float32)]
-    kernel = functools.partial(assemble_turned_kernel, layout)
-    return call(kernel, out, [VMEM], scratch)(chunks)
+    return call(assemble_turned_kernel, out, [VMEM], scratch)(chunks)
 
 
 def chunk_of(total, zh, start):
@@ -435,11 +399,14 @@
 
 
 def outgoing_kernel(core_ref, left_ref, right_ref, out_ref, left_s, total):
-    assemble_kernel(ALONE, left_ref, left_s)
+    def put(start, values):
+        left_s[pl.ds(start, 2 * SUB), :] = values.astype(jnp.bfloat16)
+
+    assemble_into(left_ref, put)
     for x in range(X):
         total[:, x * ZH * ROWS : (x + 1) * ZH * ROWS] = lax.dot_general(
             left_s[...],
-            right_ref[pl.ds(x * ZH * ROWS, ZH * ROWS), :],
+            right_ref[x],
             (((1,), (1,)), ((), ())),
             preferred_element_type=jnp.float32,
         )
@@ -466,7 +433,7 @@
         for x in range(X):
             product = product + jnp.dot(
                 left_ref[x],
-                right_ref[pl.ds(x * ZH * ROWS, ZH * ROWS), :],
+                right_ref[x],
                 preferred_element_type=jnp.float32,
             )
         for zh in range(ZH):
@@ -510,25 +477,29 @@
     place = jnp.stack([row_start, column_block * COLUMNS]).astype(jnp.int32)
     core = core_index.reshape(1).astype(jnp.int32)
 
+    def factors(which, normed, right, pair):
+        right = exchange(assemble(exchange(right, PLANE)), "x")
+        left, gate = left_and_gates(
+            which,
+            place,
+            residue_valid,
+            chain_index,
+            normed,
+            projection,
+            gate_weight,
+            chain_bias,
+            pair,
+        )
+        return exchange(left, PLANE), right, gate
+
     normed, right = project_right(
         place, residue_valid, pair_acts, norm_gain, norm_bias, projection
     )
-    right = assemble(exchange(right, PLANE), ALONE)
-    right = lax.all_gather(right, "x", axis=0, tiled=True)
-    left, gate = left_and_gates(
-        place,
-        residue_valid,
-        chain_index,
-        normed,
-        projection,
-        gate_weight,
-        chain_bias,
-        pair_acts,
-    )
-    halves = outgoing(core, exchange(left, PLANE), right)
+    left, right, gate = factors(0, normed, right, pair_acts)
+    halves = outgoing(core, left, right)
     total = halves[0].astype(jnp.float32) + swap_cores(halves[1]).astype(jnp.float32)
     product = exchange(total.astype(jnp.bfloat16), PLANE)
-    middle, normed, both = finish(
+    middle, normed, right = finish(
         0,
         place,
         residue_valid,
@@ -540,13 +511,10 @@
         norm_bias,
         projection,
     )
-    both = exchange(both, PLANE)
-    right = assemble(both, RIGHT)
-    right = lax.all_gather(right, "x", axis=0, tiled=True)
-    left = assemble_turned(both, LEFT).reshape(X, ZH * COLUMNS, ZH * ROWS)
+    left, right, gate = factors(1, normed, right, middle)
+    left = assemble_turned(left).reshape(X, ZH * COLUMNS, ZH * ROWS)
     left = exchange(left, "x")
     product = exchange(incoming(core, left, swap_cores(left), right), PLANE)
-    gate = gates(1, place, chain_index, normed, gate_weight, chain_bias, middle)
     return finish(1, place, residue_valid, out_gain, gate, product, out_weight)[0]
 
 

time: 230 us -> 240 us (1.043)
  waiting for transfers between devices: 29.9 us -> 67.4 us
  blocking collectives: 127 us -> 96.8 us
  starting transfers between devices: 17.3 us -> 42.5 us
  between operations: 13.6 us -> 0.43 us
  local copies, waits for them, and re-layouts: 16 us -> 5.24 us
    all_to_all x1 -> x5, waiting for transfers between devices: 15.4 us -> 63.7 us  [exchange(): return lax.all_to_all(values, axes, split_axis=0, concat_axis=0, tiled=True)]
    all_to_all x5 -> x4, blocking collectives: 127 us -> 96.8 us  [exchange(): return lax.all_to_all(values, axes, split_axis=0, concat_axis=0, tiled=True)]
    all_to_all x1 -> x5, starting transfers between devices: 13.3 us -> 38.7 us  [exchange(): return lax.all_to_all(values, axes, split_axis=0, concat_axis=0, tiled=True)]
    all_gather x2 -> x0, waiting for transfers between devices: 10.9 us -> none  [body(): right = lax.all_gather(right, 'x', axis=0, tiled=True)]
    unnamed x48 -> x32, local copies, waits for them, and re-layouts: 16 us -> 5.2 us
  transfers between devices with their start and end apart: 5 -> 7, of which waited for: 4 -> 7; matrix products, arithmetic and copies ran while one was open for 0% -> 0% of each run, Pallas kernels for 2% -> 3%
where the time goes in v6:
time: 240 us; the launch traced here: 238 us
  blocking collectives  96.8 us (40%)
  waiting for transfers between devices  67.4 us (28%)
  starting transfers between devices  42.5 us (18%)
  Pallas kernels  24.6 us (10%)
  local copies, waits for them, and re-layouts  5.24 us (2%)
    all_to_all x4, blocking collectives, exchange(): return lax.all_to_all(values, axes, split_axis=0, concat_axis=0, tiled=True)  96.8 us
    all_to_all x5, waiting for transfers between devices, exchange(): return lax.all_to_all(values, axes, split_axis=0, concat_axis=0, tiled=True)  63.7 us
    all_to_all x5, starting transfers between devices, exchange(): return lax.all_to_all(values, axes, split_axis=0, concat_axis=0, tiled=True)  38.7 us
    pallas_call x2, Pallas kernels, finish(): call(functools.partial(finish_kernel, which), [out, NORMED, CHUNKS] if th...  7.63 us
    unnamed x32, local copies, waits for them, and re-layouts  5.2 us
    pallas_call x1, Pallas kernels, project_right(): call(right_kernel, [NORMED, CHUNKS], [SMEM, SMEM] + [ANY] * 4, [SCRATCH]...  5.17 us
    pallas_call x2, Pallas kernels, left_and_gates(): call(kernel, [CHUNKS, GATES], [SMEM] * 3 + [VMEM] * 5, [SCRATCH])  5.06 us
  transfers between devices with their start and end apart: 7, of which 7 were waited for; matrix products, arithmetic and copies ran while one was open for 0% of the time, Pallas kernels for 3%

profile of v6, /device:TPU:6, one launch (start us, length us, event | category | flops | bytes accessed | tf_op | source)
XLA Modules:
  0.0 237.8 jit_solution(6426666635405753756)
XLA Ops:
  0.7 5.2 %shard_map.100 = (bf16[32,128,128]{2,1,0:T(8,128)(2,1)}, bf16[64,8,512]{2,1,0:T(8,128)(2,1)}) custom-call(s32[2]{0:T(128)} %pad_add_fusion.place_ref, s32[1280]{0:T(1024)} %valid_ref.9, bf16[80,40,128]{2,1,0:T(8,128)(2,1)} %pair_ref.1, f32[2,128]{1,0:T(2,128)} %rest_0_.1, f32[2,128]{1,0:T(2,128)} %rest_1_.1, bf16[2,128,256]{2,1,0:T(8,128)(2,1)} %weight_ref.3), custom_call_target="tpu_custom_call" | custom-call | flops 100000000 | bytes 4000000 | tf_op jit(solution)/shard_map/pallas_call | solution.py:180
  5.8 16.6 %all-to-all-start.1 = ((bf16[64,8,512]{2,1,0:T(8,128)(2,1)}), bf16[64,8,512]{2,1,0:T(8,128)(2,1)S(1)}, u32[]{:S(2)}, u32[]{:S(2)}) async-start(bf16[64,8,512]{2,1,0:T(8,128)(2,1)} %get-tuple-element.17), calls=%async_computation.1 | async-start | bytes 1048576 | tf_op jit(solution)/shard_map/all_to_all | solution.py:455
  23.7 2.9 %shard_map.101 = (bf16[64,8,512]{2,1,0:T(8,128)(2,1)}, f32[2,32,128,128]{3,2,1,0:T(8,128)S(1)}) custom-call(s32[2]{0:T(128)S(1)} %copy-done.11, s32[1280]{0:T(1024)S(1)} %copy-done.8, s32[1280]{0:T(1024)S(1)} %copy-done.10, bf16[32,128,128]{2,1,0:T(8,128)(2,1)S(1)} %copy-done.6, bf16[2,128,256]{2,1,0:T(8,128)(2,1)S(1)} %copy-done.5, ...), custom_call_target="tpu_custom_call" | custom-call | flops 100000000 | bytes 4000000 | tf_op jit(solution)/shard_map/pallas_call | solution.py:250
  26.7 2.0 copy-done.2
  28.7 13.1 %all-to-all-done.1.chunks_ref = bf16[64,8,512]{2,1,0:T(8,128)(2,1)S(1)} async-done(((bf16[64,8,512]{2,1,0:T(8,128)(2,1)}), bf16[64,8,512]{2,1,0:T(8,128)(2,1)S(1)}, u32[]{:S(2)}, u32[]{:S(2)}) %all-to-all-start.1) | async-done | bytes 524320 | tf_op jit(solution)/shard_map/all_to_all | solution.py:455
  41.7 5.3 %all-to-all-start = ((bf16[64,8,512]{2,1,0:T(8,128)(2,1)}), bf16[64,8,512]{2,1,0:T(8,128)(2,1)S(1)}, u32[]{:S(2)}, u32[]{:S(2)}) async-start(bf16[64,8,512]{2,1,0:T(8,128)(2,1)} %get-tuple-element.16), calls=%async_computation | async-start | bytes 1048576 | tf_op jit(solution)/shard_map/all_to_all | solution.py:455
  47.5 18.4 %all-to-all-done.left_ref = bf16[64,8,512]{2,1,0:T(8,128)(2,1)S(1)} async-done(((bf16[64,8,512]{2,1,0:T(8,128)(2,1)}), bf16[64,8,512]{2,1,0:T(8,128)(2,1)S(1)}, u32[]{:S(2)}, u32[]{:S(2)}) %all-to-all-start) | async-done | bytes 524320 | tf_op jit(solution)/shard_map/all_to_all | solution.py:455
  65.9 20.5 %all_to_all.45.right_ref = bf16[4,320,640]{2,1,0:T(8,128)(2,1)S(1)} all-to-all(bf16[4,320,640]{2,1,0:T(8,128)(2,1)S(1)} %shard_map.102), channel_id=1, replica_groups=mesh['zl'=2,'y'=8,'core'=2,'x'=4,'zh'=4] {'x'}, dimensions={0} | all-to-all | bytes 3276800 | tf_op jit(solution)/shard_map/all_to_all | solution.py:455
  86.3 1.9 shard_map.103
  88.3 1.9 collective-permute-start
  92.3 27.0 %all_to_all.46.product_ref = bf16[64,8,512]{2,1,0:T(8,128)(2,1)S(1)} all-to-all(bf16[64,8,512]{2,1,0:T(8,128)(2,1)S(1)} %fusion), channel_id=1, replica_groups=mesh['zl'=2,'y'=8,'core'=2,'x'=4,'zh'=4] {'y','zh','zl'}, dimensions={0} | all-to-all | bytes 1048576 | tf_op jit(solution)/shard_map/all_to_all | solution.py:455
  119.3 4.9 %shard_map.104 = (bf16[80,40,128]{2,1,0:T(8,128)(2,1)S(1)}, bf16[32,128,128]{2,1,0:T(8,128)(2,1)S(1)}, bf16[64,8,512]{2,1,0:T(8,128)(2,1)}) custom-call(s32[2]{0:T(128)S(1)} %copy-done.11, s32[1280]{0:T(1024)S(1)} %copy-done.8, f32[2,64]{1,0:T(2,128)S(1)} %copy-done.15, f32[2,32,128,128]{3,2,1,0:T(8,128)S(1)} %copy-done.3, ...), custom_call_target="tpu_custom_call" | custom-call | flops 100000000 | bytes 4000000 | tf_op jit(solution)/shard_map/pallas_call | solution.py:329
  124.1 2.1 shard_map.105
  126.3 2.0 copy-done
  128.2 24.4 %all_to_all.47.chunks_ref = bf16[64,8,512]{2,1,0:T(8,128)(2,1)S(1)} all-to-all(bf16[64,8,512]{2,1,0:T(8,128)(2,1)S(1)} %get-tuple-element.21), channel_id=1, replica_groups=mesh['zl'=2,'y'=8,'core'=2,'x'=4,'zh'=4] {'y','zh','zl'}, dimensions={0} | all-to-all | bytes 1048576 | tf_op jit(solution)/shard_map/all_to_all | solution.py:455
  152.7 5.7 %all-to-all-start.6 = ((bf16[64,8,512]{2,1,0:T(8,128)(2,1)}), bf16[64,8,512]{2,1,0:T(8,128)(2,1)S(1)}, u32[]{:S(2)}, u32[]{:S(2)}) async-start(bf16[64,8,512]{2,1,0:T(8,128)(2,1)} %get-tuple-element.22), calls=%async_computation.6 | async-start | bytes 1048576 | tf_op jit(solution)/shard_map/all_to_all | solution.py:455
  159.7 17.0 %all-to-all-done.6.chunks_ref = bf16[64,8,512]{2,1,0:T(8,128)(2,1)S(1)} async-done(((bf16[64,8,512]{2,1,0:T(8,128)(2,1)}), bf16[64,8,512]{2,1,0:T(8,128)(2,1)S(1)}, u32[]{:S(2)}, u32[]{:S(2)}) %all-to-all-start.6) | async-done | bytes 524320 | tf_op jit(solution)/shard_map/all_to_all | solution.py:455
  176.7 5.5 %all-to-all-start.5 = ((bf16[4,160,320]{2,1,0:T(8,128)(2,1)}), bf16[4,160,320]{2,1,0:T(8,128)(2,1)S(1)}, u32[]{:S(2)}, u32[]{:S(2)}) async-start(bf16[4,160,320]{2,1,0:T(8,128)(2,1)} %bitcast.5), calls=%async_computation.5 | async-start | bytes 983040 | tf_op jit(solution)/shard_map/all_to_all | solution.py:455
  183.7 4.3 %all-to-all-done.5.own_ref = bf16[4,160,320]{2,1,0:T(8,128)(2,1)S(1)} async-done(((bf16[4,160,320]{2,1,0:T(8,128)(2,1)}), bf16[4,160,320]{2,1,0:T(8,128)(2,1)S(1)}, u32[]{:S(2)}, u32[]{:S(2)}) %all-to-all-start.5) | async-done | bytes 409632 | tf_op jit(solution)/shard_map/all_to_all | solution.py:455
  188.0 5.6 %all-to-all-start.7 = ((bf16[4,320,640]{2,1,0:T(8,128)(2,1)}), bf16[4,320,640]{2,1,0:T(8,128)(2,1)S(1)}, u32[]{:S(2)}, u32[]{:S(2)}) async-start(bf16[4,320,640]{2,1,0:T(8,128)(2,1)} %shard_map.107), calls=%async_computation.7 | async-start | bytes 3276800 | tf_op jit(solution)/shard_map/all_to_all | solution.py:455
  193.6 1.9 collective-permute-start.1
  197.4 11.0 %all-to-all-done.7.right_ref = bf16[4,320,640]{2,1,0:T(8,128)(2,1)S(1)} async-done(((bf16[4,320,640]{2,1,0:T(8,128)(2,1)}), bf16[4,320,640]{2,1,0:T(8,128)(2,1)S(1)}, u32[]{:S(2)}, u32[]{:S(2)}) %all-to-all-start.7) | async-done | bytes 1638432 | tf_op jit(solution)/shard_map/all_to_all | solution.py:455
  209.9 24.9 %all_to_all.48.product_ref = bf16[64,8,512]{2,1,0:T(8,128)(2,1)S(1)} all-to-all(bf16[64,8,512]{2,1,0:T(8,128)(2,1)S(1)} %shard_map.108), channel_id=1, replica_groups=mesh['zl'=2,'y'=8,'core'=2,'x'=4,'zh'=4] {'y','zh','zl'}, dimensions={0} | all-to-all | bytes 1048576 | tf_op jit(solution)/shard_map/all_to_all | solution.py:455
  234.8 2.8 %shard_map.109 = bf16[80,40,128]{2,1,0:T(8,128)(2,1)} custom-call(s32[2]{0:T(128)S(1)} %copy-done.11, s32[1280]{0:T(1024)S(1)} %copy-done.8, f32[2,64]{1,0:T(2,128)S(1)} %copy-done.15, f32[2,32,128,128]{3,2,1,0:T(8,128)S(1)} %copy-done.1, bf16[64,8,512]{2,1,0:T(8,128)(2,1)S(1)} %all_to_all.48.product_ref, bf16[2,64,128]{2,1,0:T(8,128)(2,1)S(1)} %copy-done.9), custom_call_target="tpu_custom_call" | custom-call | flops 100000000 | bytes 4000000 | tf_op jit(solution)/shard_map/pallas_call | solution.py:329
  (39 shorter events, 10.7 us)
Async XLA Ops:
  0.0 22.5 %copy-start.8 = (s32[1280]{0:T(1024)S(1)}, s32[1280]{0:T(1024)}, u32[]{:S(2)}) copy-start(s32[1280]{0:T(1024)} %valid_ref.9) | copy-start | bytes 15364
  0.0 22.5 %copy-start.5 = (bf16[2,128,256]{2,1,0:T(8,128)(2,1)S(1)}, bf16[2,128,256]{2,1,0:T(8,128)(2,1)}, u32[]{:S(2)}) copy-start(bf16[2,128,256]{2,1,0:T(8,128)(2,1)} %weight_ref.3) | copy-start | bytes 393220
  0.0 22.5 %copy-start.4 = (bf16[80,40,128]{2,1,0:T(8,128)(2,1)S(1)}, bf16[80,40,128]{2,1,0:T(8,128)(2,1)}, u32[]{:S(2)}) copy-start(bf16[80,40,128]{2,1,0:T(8,128)(2,1)} %pair_ref.1) | copy-start | bytes 2457604
  0.0 22.5 %copy-start.12 = (f32[2,128]{1,0:T(2,128)S(1)}, f32[2,128]{1,0:T(2,128)}, u32[]{:S(2)}) copy-start(f32[2,128]{1,0:T(2,128)} %chain_bias_ref.3) | copy-start | bytes 3076
  0.0 22.5 %copy-start.7 = (bf16[2,128,128]{2,1,0:T(8,128)(2,1)S(1)}, bf16[2,128,128]{2,1,0:T(8,128)(2,1)}, u32[]{:S(2)}) copy-start(bf16[2,128,128]{2,1,0:T(8,128)(2,1)} %gate_ref.3) | copy-start | bytes 196612
  0.0 22.5 %copy-start.10 = (s32[1280]{0:T(1024)S(1)}, s32[1280]{0:T(1024)}, u32[]{:S(2)}) copy-start(s32[1280]{0:T(1024)} %chain_ref.3) | copy-start | bytes 15364
  0.7 21.8 %copy-start.11 = (s32[2]{0:T(128)S(1)}, s32[2]{0:T(128)}, u32[]{:S(2)}) copy-start(s32[2]{0:T(128)} %pad_add_fusion.place_ref) | copy-start | bytes 28
  5.8 35.9 %all-to-all-start.1 = ((bf16[64,8,512]{2,1,0:T(8,128)(2,1)}), bf16[64,8,512]{2,1,0:T(8,128)(2,1)S(1)}, u32[]{:S(2)}, u32[]{:S(2)}) async-start(bf16[64,8,512]{2,1,0:T(8,128)(2,1)} %get-tuple-element.17), calls=%async_computation.1 | async-start | bytes 1048576 | tf_op jit(solution)/shard_map/all_to_all | solution.py:455
  22.5 1.2 copy-start.6
  26.7 2.0 copy-start.2
  41.7 24.1 %all-to-all-start = ((bf16[64,8,512]{2,1,0:T(8,128)(2,1)}), bf16[64,8,512]{2,1,0:T(8,128)(2,1)S(1)}, u32[]{:S(2)}, u32[]{:S(2)}) async-start(bf16[64,8,512]{2,1,0:T(8,128)(2,1)} %get-tuple-element.16), calls=%async_computation | async-start | bytes 1048576 | tf_op jit(solution)/shard_map/all_to_all | solution.py:455
  86.3 32.9 %copy-start.3 = (f32[2,32,128,128]{3,2,1,0:T(8,128)S(1)}, f32[2,32,128,128]{3,2,1,0:T(8,128)}, u32[]{:S(2)}) copy-start(f32[2,32,128,128]{3,2,1,0:T(8,128)} %copy-done.2) | copy-start | bytes 12582916
  88.2 31.0 %copy-start.9 = (bf16[2,64,128]{2,1,0:T(8,128)(2,1)S(1)}, bf16[2,64,128]{2,1,0:T(8,128)(2,1)}, u32[]{:S(2)}) copy-start(bf16[2,64,128]{2,1,0:T(8,128)(2,1)} %out_weight_ref.3) | copy-start | bytes 98308
  88.2 31.0 %copy-start.13 = (f32[2,128]{1,0:T(2,128)S(1)}, f32[2,128]{1,0:T(2,128)}, u32[]{:S(2)}) copy-start(f32[2,128]{1,0:T(2,128)} %rest_0_.1) | copy-start | bytes 3076
  88.3 31.0 %copy-start.14 = (f32[2,128]{1,0:T(2,128)S(1)}, f32[2,128]{1,0:T(2,128)}, u32[]{:S(2)}) copy-start(f32[2,128]{1,0:T(2,128)} %rest_1_.1) | copy-start | bytes 3076
  88.3 31.0 %copy-start.15 = (f32[2,64]{1,0:T(2,128)S(1)}, f32[2,64]{1,0:T(2,128)}, u32[]{:S(2)}) copy-start(f32[2,64]{1,0:T(2,128)} %out_gain_ref.3) | copy-start | bytes 1540
  88.3 3.8 %collective-permute-start = (bf16[64,8,512]{2,1,0:T(8,128)(2,1)S(1)}, bf16[64,8,512]{2,1,0:T(8,128)(2,1)S(1)}, u32[]{:S(2)}, u32[]{:S(2)}) collective-permute-start(bf16[64,8,512]{2,1,0:T(8,128)(2,1)S(1)} %slice_bitcast_fusion), channel_id=1, source_target_pairs={{0,16},{16,0},{1,17},{17,1},{2,18},{18,2},{3,19},{19,3},{4,20},{20... | collective-permute-start | bytes 1572872 | tf_op jit(solution)/shard_map/ppermute | solution.py:459
  126.3 2.0 copy-start
  152.7 24.0 %all-to-all-start.6 = ((bf16[64,8,512]{2,1,0:T(8,128)(2,1)}), bf16[64,8,512]{2,1,0:T(8,128)(2,1)S(1)}, u32[]{:S(2)}, u32[]{:S(2)}) async-start(bf16[64,8,512]{2,1,0:T(8,128)(2,1)} %get-tuple-element.22), calls=%async_computation.6 | async-start | bytes 1048576 | tf_op jit(solution)/shard_map/all_to_all | solution.py:455
  176.7 11.3 %all-to-all-start.5 = ((bf16[4,160,320]{2,1,0:T(8,128)(2,1)}), bf16[4,160,320]{2,1,0:T(8,128)(2,1)S(1)}, u32[]{:S(2)}, u32[]{:S(2)}) async-start(bf16[4,160,320]{2,1,0:T(8,128)(2,1)} %bitcast.5), calls=%async_computation.5 | async-start | bytes 983040 | tf_op jit(solution)/shard_map/all_to_all | solution.py:455
  188.0 20.3 %all-to-all-start.7 = ((bf16[4,320,640]{2,1,0:T(8,128)(2,1)}), bf16[4,320,640]{2,1,0:T(8,128)(2,1)S(1)}, u32[]{:S(2)}, u32[]{:S(2)}) async-start(bf16[4,320,640]{2,1,0:T(8,128)(2,1)} %shard_map.107), calls=%async_computation.7 | async-start | bytes 3276800 | tf_op jit(solution)/shard_map/all_to_all | solution.py:455
  193.6 3.7 %collective-permute-start.1 = (bf16[4,160,320]{2,1,0:T(8,128)(2,1)S(1)}, bf16[4,160,320]{2,1,0:T(8,128)(2,1)S(1)}, u32[]{:S(2)}, u32[]{:S(2)}) collective-permute-start(bf16[4,160,320]{2,1,0:T(8,128)(2,1)S(1)} %all-to-all-done.5.own_ref), channel_id=1, source_target_pairs={{0,16},{16,0},{1,17},{17,1},{2,18},{18,2},{3,19},{19,3},{4,20},{20... | collective-permute-start | bytes 1228808 | tf_op jit(solution)/shard_map/ppermute | solution.py:459
  208.3 26.5 %copy-start.1 = (f32[2,32,128,128]{3,2,1,0:T(8,128)S(1)}, f32[2,32,128,128]{3,2,1,0:T(8,128)}, u32[]{:S(2)}) copy-start(f32[2,32,128,128]{3,2,1,0:T(8,128)} %copy-done) | copy-start | bytes 12582916

commit v7 on v4

--- a/solution.py
+++ b/solution.py
@@ -41,7 +41,7 @@
     return (y * ZH + zh) * 2 + zl
 
 
-def call(kernel, out_shape, in_specs, scratch_shapes=(), flops=10**8, outs=None):
+def call(kernel, out_shape, in_specs, scratch_shapes=(), flops=10**8, outs=None, grant=40):
     outs = outs or jax.tree.map(lambda _: VMEM, out_shape)
     moved = 4 * 10**6
     return pl.pallas_call(
@@ -50,7 +50,7 @@
         in_specs=in_specs,
         out_specs=outs,
         scratch_shapes=scratch_shapes,
-        compiler_params=pltpu.CompilerParams(vmem_limit_bytes=40 * 2**20),
+        compiler_params=pltpu.CompilerParams(vmem_limit_bytes=grant * 2**20),
         cost_estimate=pl.CostEstimate(flops=flops, bytes_accessed=moved, transcendentals=0),
     )
 
@@ -63,7 +63,8 @@
 
 
 def batches(work):
-    pl.loop(0, WHOLE)(lambda step: work(step * BATCH, 3))
+    for step in range(WHOLE):
+        work(step * BATCH, 3)
     work(WHOLE * BATCH, 1)
 
 
@@ -140,16 +141,40 @@
 
 
 def right_kernel(
-    place_ref, valid_ref, pair_ref, vectors_ref, weight_ref, normed_ref, right_ref, right_s
+    place_ref,
+    valid_ref,
+    pair_any,
+    gain_any,
+    bias_any,
+    weight_any,
+    right_ref,
+    right_s,
+    pair_ref,
+    gain_ref,
+    bias_ref,
+    weight_ref,
+    sems,
 ):
+    moves = [(gain_any, gain_ref), (bias_any, bias_ref), (weight_any, weight_ref)]
+    parts = []
+    for first in range(0, DEPTH, BATCH):
+        for row in block_rows(first, 3 if first < WHOLE * BATCH else 1)[0]:
+            parts.append(len(moves))
+            rows = pl.ds(row, BATCH)
+            moves.append((pair_any.at[rows], pair_ref.at[rows]))
+    copies = [pltpu.make_async_copy(a, b, sems.at[n]) for n, (a, b) in enumerate(moves)]
+    for copy in copies:
+        copy.start()
     columns = spread_columns(place_ref, valid_ref)
+    for copy in copies[: parts[0]]:
+        copy.wait()
     weight = weight_of(weight_ref, 0, 2 * HIDDEN)
 
     def work(first, count):
+        for part in parts[first // BATCH * 3 :][:count]:
+            copies[part].wait()
         values = load_pairs(pair_ref, first, count)
-        pieces = pad_rows(normalize(values, vectors_ref[0:1], vectors_ref[2:3]), count)
-        for n in range(BATCH):
-            normed_ref[first + n] = pieces[n]
+        pieces = pad_rows(normalize(values, gain_ref[0:1], bias_ref[0:1]), count)
         mask = mask_of(first, count, place_ref, valid_ref, columns)
         factor = factor_of(jnp.concatenate(pieces, axis=0), weight, mask)
         keep_rows(factor, right_s, first, STRIDE)
@@ -158,19 +183,22 @@
     put_chunks(right_s, right_ref, STRIDE, DEPTH)
 
 
-def project_right(place, valid, pair, vectors, weight):
-    return call(right_kernel, [NORMED, CHUNKS], [SMEM, SMEM, VMEM, VMEM, VMEM], [SCRATCH])(
-        place, valid, pair, vectors, weight
-    )
+def project_right(place, valid, *operands):
+    scratch = [pltpu.VMEM(each.shape, each.dtype) for each in operands]
+    return call(
+        right_kernel,
+        CHUNKS,
+        [SMEM, SMEM] + [ANY] * 4,
+        [SCRATCH] + scratch + [pltpu.SemaphoreType.DMA((13,))],
+        grant=60,
+    )(place, valid, *operands)
 
 
 def load_normed(normed_ref, first):
     return normed_ref[pl.ds(first, BATCH)].reshape(BATCH * LANES, WIDTH)
 
 
-def gate_work(
-    which, place_ref, chain_ref, normed_ref, gate_ref, vectors_ref, pair_ref, out_ref
-):
+def gate_work(which, place_ref, chain_ref, normed_of, gate_ref, vectors_ref, pair_ref, out_ref):
     row = lax.broadcasted_iota(jnp.int32, (COLUMNS, WIDTH), 0)
     chain_columns = jnp.full((COLUMNS, WIDTH), -1, jnp.int32)
     for column in range(COLUMNS):
@@ -179,7 +207,7 @@
 
     def work(first, count):
         logit = jnp.dot(
-            load_normed(normed_ref, first), gate_ref[which], preferred_element_type=jnp.float32
+            normed_of(first, count), gate_ref[which], preferred_element_type=jnp.float32
         )
         for n, rows in enumerate(block_rows(first, count)):
             for group, row in enumerate(rows):
@@ -194,8 +222,15 @@
     return work
 
 
-def gate_kernel(which, *refs):
-    batches(gate_work(which, *refs))
+def gate_kernel(
+    which, place_ref, chain_ref, normed_ref, gate_ref, vectors_ref, pair_ref, out_ref
+):
+    def normed_of(first, count):
+        return load_normed(normed_ref, first)
+
+    batches(
+        gate_work(which, place_ref, chain_ref, normed_of, gate_ref, vectors_ref, pair_ref, out_ref)
+    )
 
 
 def gates(which, place, chain, normed, gate, vectors, pair):
@@ -209,7 +244,6 @@
     place_ref,
     valid_ref,
     chain_ref,
-    normed_ref,
     weight_ref,
     gate_ref,
     vectors_ref,
@@ -220,22 +254,27 @@
 ):
     columns = spread_columns(place_ref, valid_ref)
     weight = weight_of(weight_ref, 0, 0)
-    gate = gate_work(
-        0, place_ref, chain_ref, normed_ref, gate_ref, vectors_ref, pair_ref, out_ref
-    )
 
     def work(first, count):
+        values = load_pairs(pair_ref, first, count)
+        pieces = pad_rows(normalize(values, vectors_ref[0:1], vectors_ref[2:3]), count)
+        normed = jnp.concatenate(pieces, axis=0)
         mask = mask_of(first, count, place_ref, valid_ref, columns)
-        keep_rows(factor_of(load_normed(normed_ref, first), weight, mask), left_s, first, STRIDE)
-        gate(first, count)
+        keep_rows(factor_of(normed, weight, mask), left_s, first, STRIDE)
+        gate(lambda *_: normed, first, count)
+
+    def gate(normed_of, first, count):
+        gate_work(
+            0, place_ref, chain_ref, normed_of, gate_ref, vectors_ref, pair_ref, out_ref
+        )(first, count)
 
     batches(work)
     put_chunks(left_s, left_ref, STRIDE, DEPTH)
 
 
-def left_and_gates(place, valid, chain, normed, weight, gate, vectors, pair):
-    return call(left_and_gate_kernel, [CHUNKS, GATES], [SMEM] * 3 + [VMEM] * 5, [SCRATCH])(
-        place, valid, chain, normed, weight, gate, vectors, pair
+def left_and_gates(place, valid, chain, weight, gate, vectors, pair):
+    return call(left_and_gate_kernel, [CHUNKS, GATES], [SMEM] * 3 + [VMEM] * 4, [SCRATCH])(
+        place, valid, chain, weight, gate, vectors, pair
     )
 
 
@@ -502,10 +541,10 @@
     core = jnp.stack([core_index, lax.axis_index("x")]).astype(jnp.int32)
 
     vectors = jnp.concatenate([norm_gain, norm_bias, chain_bias], axis=0)
-    normed, right = project_right(place, residue_valid, pair_acts, vectors, projection)
+    right = project_right(place, residue_valid, pair_acts, norm_gain, norm_bias, projection)
     rights = gather_x(assemble(exchange(right, PLANE), ALONE))
     left, gate = left_and_gates(
-        place, residue_valid, chain_index, normed, projection, gate_weight, vectors, pair_acts
+        place, residue_valid, chain_index, projection, gate_weight, vectors, pair_acts
     )
     halves = outgoing(core, exchange(left, PLANE), rights)
     total = halves[0].astype(jnp.float32) + swap_cores(halves[1]).astype(jnp.float32)

time: 215 us -> 212 us (0.986)
    unnamed x36 -> x34, local copies, waits for them, and re-layouts: 10.2 us -> 8.02 us
  transfers between devices with their start and end apart: 11 -> 11, of which waited for: 7 -> 7; matrix products, arithmetic and copies ran while one was open for 0% -> 0% of each run, Pallas kernels for 2% -> 3%
where the time goes in v7:
time: 212 us; the launch traced here: 208 us
  blocking collectives  90.8 us (43%)
  starting transfers between devices  51.6 us (24%)
  waiting for transfers between devices  33.6 us (16%)
  Pallas kernels  22.2 us (10%)
  local copies, waits for them, and re-layouts  8.05 us (4%)
    all_to_all x3, blocking collectives, exchange(): return lax.all_to_all(values, axes, split_axis=0, concat_axis=0, tiled=True)  90.8 us
    all_to_all x3, starting transfers between devices, exchange(): return lax.all_to_all(values, axes, split_axis=0, concat_axis=0, tiled=True)  28.2 us
    ppermute x6, starting transfers between devices, shift(): return lax.ppermute(block, 'x', [(x, (x + by) % X) for x in range(X)])  19.6 us
    all_to_all x3, waiting for transfers between devices, exchange(): return lax.all_to_all(values, axes, split_axis=0, concat_axis=0, tiled=True)  16.8 us
    ppermute x6, waiting for transfers between devices, shift(): return lax.ppermute(block, 'x', [(x, (x + by) % X) for x in range(X)])  14.9 us
    unnamed x34, local copies, waits for them, and re-layouts  8.02 us
    pallas_call x2, Pallas kernels, finish(): call(functools.partial(finish_kernel, which), [out, NORMED, BOTH_CHUNKS]...  6.07 us
    pallas_call x1, Pallas kernels, project_right(): call(right_kernel, CHUNKS, [SMEM, SMEM] + [ANY] * 4, [SCRATCH] + scratch...  4.86 us
  transfers between devices with their start and end apart: 11, of which 7 were waited for; matrix products, arithmetic and copies ran while one was open for 0% of the time, Pallas kernels for 3%

profile of v7, /device:TPU:6, one launch (start us, length us, event | category | flops | bytes accessed | tf_op | source)
XLA Modules:
  0.0 208.1 jit_solution(440989904276711759)
XLA Ops:
  0.6 4.9 %shard_map.101 = bf16[64,8,512]{2,1,0:T(8,128)(2,1)} custom-call(s32[2]{0:T(128)} %pad_add_fusion.place_ref, s32[1280]{0:T(1024)} %valid_ref.7, bf16[80,40,128]{2,1,0:T(8,128)(2,1)} %pair_any.1, f32[2,128]{1,0:T(2,128)} %gain_any.1, f32[2,128]{1,0:T(2,128)} %bias_any.1, bf16[2,128,256]{2,1,0:T(8,128)(2,1)} %rest_1_.1), custom_call_target="tpu_custom_call" | custom-call | flops 100000000 | bytes 4000000 | tf_op jit(solution)/shard_map/pallas_call | solution.py:188
  5.4 16.6 %all-to-all-start.1 = ((bf16[64,8,512]{2,1,0:T(8,128)(2,1)}), bf16[64,8,512]{2,1,0:T(8,128)(2,1)S(1)}, u32[]{:S(2)}, u32[]{:S(2)}) async-start(bf16[64,8,512]{2,1,0:T(8,128)(2,1)} %shard_map.101), calls=%async_computation.1 | async-start | bytes 1048576 | tf_op jit(solution)/shard_map/all_to_all | solution.py:518
  27.7 3.4 %shard_map.100 = (bf16[64,8,512]{2,1,0:T(8,128)(2,1)}, f32[2,32,128,128]{3,2,1,0:T(8,128)S(1)}) custom-call(s32[2]{0:T(128)S(1)} %copy-done.14, s32[1280]{0:T(1024)S(1)} %copy-done.10, s32[1280]{0:T(1024)S(1)} %copy-done.12, bf16[2,128,256]{2,1,0:T(8,128)(2,1)S(1)} %copy-done.3, bf16[2,128,128]{2,1,0:T(8,128)(2,1)S(1)} %copy-done.7, ...), custom_call_target="tpu_custom_call" | custom-call | flops 100000000 | bytes 4000000 | tf_op jit(solution)/shard_map/pallas_call | solution.py:276
  31.1 2.0 copy-done
  33.0 8.3 %all-to-all-done.1.chunks_ref = bf16[64,8,512]{2,1,0:T(8,128)(2,1)S(1)} async-done(((bf16[64,8,512]{2,1,0:T(8,128)(2,1)}), bf16[64,8,512]{2,1,0:T(8,128)(2,1)S(1)}, u32[]{:S(2)}, u32[]{:S(2)}) %all-to-all-start.1) | async-done | bytes 524320 | tf_op jit(solution)/shard_map/all_to_all | solution.py:518
  41.4 5.5 %all-to-all-start = ((bf16[64,8,512]{2,1,0:T(8,128)(2,1)}), bf16[64,8,512]{2,1,0:T(8,128)(2,1)S(1)}, u32[]{:S(2)}, u32[]{:S(2)}) async-start(bf16[64,8,512]{2,1,0:T(8,128)(2,1)} %get-tuple-element.11), calls=%async_computation | async-start | bytes 1048576 | tf_op jit(solution)/shard_map/all_to_all | solution.py:518
  47.2 2.7 %collective-permute-start = (bf16[320,640]{1,0:T(8,128)(2,1)S(1)}, bf16[320,640]{1,0:T(8,128)(2,1)S(1)}, u32[]{:S(2)}, u32[]{:S(2)}) collective-permute-start(bf16[320,640]{1,0:T(8,128)(2,1)S(1)} %shard_map.102.rest_0_), channel_id=1, source_target_pairs={{0,12},{4,0},{8,4},{12,8},{1,13},{5,1},{9,5},{13,9},{2,14},{6,2},{... | collective-permute-start | bytes 1228808 | tf_op jit(solution)/shard_map/ppermute | solution.py:512
  50.0 3.0 %collective-permute-start.1 = (bf16[320,640]{1,0:T(8,128)(2,1)S(1)}, bf16[320,640]{1,0:T(8,128)(2,1)S(1)}, u32[]{:S(2)}, u32[]{:S(2)}) collective-permute-start(bf16[320,640]{1,0:T(8,128)(2,1)S(1)} %shard_map.102.rest_0_), channel_id=1, source_target_pairs={{0,8},{4,12},{8,0},{12,4},{1,9},{5,13},{9,1},{13,5},{2,10},{6,14},... | collective-permute-start | bytes 1228808 | tf_op jit(solution)/shard_map/ppermute | solution.py:512
  53.0 4.0 %collective-permute-start.2 = (bf16[320,640]{1,0:T(8,128)(2,1)S(1)}, bf16[320,640]{1,0:T(8,128)(2,1)S(1)}, u32[]{:S(2)}, u32[]{:S(2)}) collective-permute-start(bf16[320,640]{1,0:T(8,128)(2,1)S(1)} %shard_map.102.rest_0_), channel_id=1, source_target_pairs={{0,4},{4,8},{8,12},{12,0},{1,5},{5,9},{9,13},{13,1},{2,6},{6,10},{... | collective-permute-start | bytes 1228808 | tf_op jit(solution)/shard_map/ppermute | solution.py:512
  57.1 8.5 %all-to-all-done.left_ref = bf16[64,8,512]{2,1,0:T(8,128)(2,1)S(1)} async-done(((bf16[64,8,512]{2,1,0:T(8,128)(2,1)}), bf16[64,8,512]{2,1,0:T(8,128)(2,1)S(1)}, u32[]{:S(2)}, u32[]{:S(2)}) %all-to-all-start) | async-done | bytes 524320 | tf_op jit(solution)/shard_map/all_to_all | solution.py:518
  65.6 4.0 %collective-permute-done.rest_1_ = bf16[320,640]{1,0:T(8,128)(2,1)S(1)} collective-permute-done((bf16[320,640]{1,0:T(8,128)(2,1)S(1)}, bf16[320,640]{1,0:T(8,128)(2,1)S(1)}, u32[]{:S(2)}, u32[]{:S(2)}) %collective-permute-start) | collective-permute-done | bytes 409632 | tf_op jit(solution)/shard_map/ppermute | solution.py:512
  69.6 2.5 %collective-permute-done.2.rest_3_ = bf16[320,640]{1,0:T(8,128)(2,1)S(1)} collective-permute-done((bf16[320,640]{1,0:T(8,128)(2,1)S(1)}, bf16[320,640]{1,0:T(8,128)(2,1)S(1)}, u32[]{:S(2)}, u32[]{:S(2)}) %collective-permute-start.2) | collective-permute-done | bytes 409632 | tf_op jit(solution)/shard_map/ppermute | solution.py:512
  72.1 2.5 %shard_map.103 = bf16[2,64,8,512]{3,2,1,0:T(8,128)(2,1)S(1)} custom-call(s32[2]{0:T(128)S(1)} %pad_add_fusion.1.core_ref, bf16[64,8,512]{2,1,0:T(8,128)(2,1)S(1)} %all-to-all-done.left_ref, bf16[320,640]{1,0:T(8,128)(2,1)S(1)} %shard_map.102.rest_0_, bf16[320,640]{1,0:T(8,128)(2,1)S(1)} %collective-permute-done.rest_1_, ...), custom_call_target="tpu_custom_call" | custom-call | flops 600000000 | bytes 4000000 | tf_op jit(solution)/shard_map/pallas_call | solution.py:479
  78.6 31.5 %all_to_all.30.product_ref = bf16[64,8,512]{2,1,0:T(8,128)(2,1)S(1)} all-to-all(bf16[64,8,512]{2,1,0:T(8,128)(2,1)S(1)} %fusion), channel_id=1, replica_groups=mesh['zl'=2,'y'=8,'core'=2,'x'=4,'zh'=4] {'y','zh','zl'}, dimensions={0} | all-to-all | bytes 1048576 | tf_op jit(solution)/shard_map/all_to_all | solution.py:518
  110.1 3.8 %shard_map.104 = (bf16[80,40,128]{2,1,0:T(8,128)(2,1)S(1)}, bf16[32,128,128]{2,1,0:T(8,128)(2,1)S(1)}, bf16[64,8,896]{2,1,0:T(8,128)(2,1)S(1)}) custom-call(s32[2]{0:T(128)S(1)} %copy-done.15, s32[1280]{0:T(1024)S(1)} %copy-done.11, f32[2,64]{1,0:T(2,128)S(1)} %copy-done.16, f32[2,32,128,128]{3,2,1,0:T(8,128)S(1)} %copy-done.1, ...), custom_call_target="tpu_custom_call" | custom-call | flops 100000000 | bytes 4000000 | tf_op jit(solution)/shard_map/pallas_call | solution.py:375
  113.9 32.1 %all_to_all.31.chunks_ref = bf16[64,8,896]{2,1,0:T(8,128)(2,1)S(1)} all-to-all(bf16[64,8,896]{2,1,0:T(8,128)(2,1)S(1)} %get-tuple-element.14), channel_id=1, replica_groups=mesh['zl'=2,'y'=8,'core'=2,'x'=4,'zh'=4] {'y','zh','zl'}, dimensions={0} | all-to-all | bytes 1835008 | tf_op jit(solution)/shard_map/all_to_all | solution.py:518
  147.4 6.1 %all-to-all-start.4 = ((bf16[4,160,320]{2,1,0:T(8,128)(2,1)}), bf16[4,160,320]{2,1,0:T(8,128)(2,1)S(1)}, u32[]{:S(2)}, u32[]{:S(2)}) async-start(bf16[4,160,320]{2,1,0:T(8,128)(2,1)} %bitcast.6), calls=%async_computation.4 | async-start | bytes 983040 | tf_op jit(solution)/shard_map/all_to_all | solution.py:518
  153.9 2.8 %collective-permute-start.5 = (bf16[320,640]{1,0:T(8,128)(2,1)S(1)}, bf16[320,640]{1,0:T(8,128)(2,1)S(1)}, u32[]{:S(2)}, u32[]{:S(2)}) collective-permute-start(bf16[320,640]{1,0:T(8,128)(2,1)S(1)} %shard_map.107.rest_0_), channel_id=1, source_target_pairs={{0,12},{4,0},{8,4},{12,8},{1,13},{5,1},{9,5},{13,9},{2,14},{6,2},{... | collective-permute-start | bytes 1228808 | tf_op jit(solution)/shard_map/ppermute | solution.py:512
  156.7 2.6 %collective-permute-start.6 = (bf16[320,640]{1,0:T(8,128)(2,1)S(1)}, bf16[320,640]{1,0:T(8,128)(2,1)S(1)}, u32[]{:S(2)}, u32[]{:S(2)}) collective-permute-start(bf16[320,640]{1,0:T(8,128)(2,1)S(1)} %shard_map.107.rest_0_), channel_id=1, source_target_pairs={{0,8},{4,12},{8,0},{12,4},{1,9},{5,13},{9,1},{13,5},{2,10},{6,14},... | collective-permute-start | bytes 1228808 | tf_op jit(solution)/shard_map/ppermute | solution.py:512
  159.2 4.5 %collective-permute-start.7 = (bf16[320,640]{1,0:T(8,128)(2,1)S(1)}, bf16[320,640]{1,0:T(8,128)(2,1)S(1)}, u32[]{:S(2)}, u32[]{:S(2)}) collective-permute-start(bf16[320,640]{1,0:T(8,128)(2,1)S(1)} %shard_map.107.rest_0_), channel_id=1, source_target_pairs={{0,4},{4,8},{8,12},{12,0},{1,5},{5,9},{9,13},{13,1},{2,6},{6,10},{... | collective-permute-start | bytes 1228808 | tf_op jit(solution)/shard_map/ppermute | solution.py:512
  167.9 7.5 %collective-permute-done.5.rest_1_ = bf16[320,640]{1,0:T(8,128)(2,1)S(1)} collective-permute-done((bf16[320,640]{1,0:T(8,128)(2,1)S(1)}, bf16[320,640]{1,0:T(8,128)(2,1)S(1)}, u32[]{:S(2)}, u32[]{:S(2)}) %collective-permute-start.5) | collective-permute-done | bytes 409632 | tf_op jit(solution)/shard_map/ppermute | solution.py:512
  176.3 2.1 %shard_map.108 = bf16[64,8,512]{2,1,0:T(8,128)(2,1)S(1)} custom-call(s32[2]{0:T(128)S(1)} %pad_add_fusion.1.core_ref, bf16[4,160,320]{2,1,0:T(8,128)(2,1)S(1)} %all-to-all-done.4.own_ref, bf16[4,160,320]{2,1,0:T(8,128)(2,1)S(1)} %collective-permute-done.4.other_ref, bf16[320,640]{1,0:T(8,128)(2,1)S(1)} %shard_map.107.rest_0_, ...), custom_call_target="tpu_custom_call" | custom-call | flops 600000000 | bytes 4000000 | tf_op jit(solution)/shard_map/pallas_call | solution.py:505
  178.5 27.2 %all_to_all.32.product_ref = bf16[64,8,512]{2,1,0:T(8,128)(2,1)S(1)} all-to-all(bf16[64,8,512]{2,1,0:T(8,128)(2,1)S(1)} %shard_map.108), channel_id=1, replica_groups=mesh['zl'=2,'y'=8,'core'=2,'x'=4,'zh'=4] {'y','zh','zl'}, dimensions={0} | all-to-all | bytes 1048576 | tf_op jit(solution)/shard_map/all_to_all | solution.py:518
  205.7 2.3 %shard_map.109 = bf16[80,40,128]{2,1,0:T(8,128)(2,1)} custom-call(s32[2]{0:T(128)S(1)} %copy-done.15, s32[1280]{0:T(1024)S(1)} %copy-done.11, f32[2,64]{1,0:T(2,128)S(1)} %copy-done.16, f32[2,32,128,128]{3,2,1,0:T(8,128)S(1)} %shard_map.105.rest_4_.gates_ref, bf16[64,8,512]{2,1,0:T(8,128)(2,1)S(1)} %all_to_all.32.product_ref, bf16[2,64,128]{2,1,0:T(8,128)(2,1)S(1)} %copy-done.9), custom_call_target="tpu_custom_call" | custom-call | flops 100000000 | bytes 4000000 | tf_op jit(solution)/shard_map/pallas_call | solution.py:375
  (50 shorter events, 17.4 us)
Async XLA Ops:
  5.4 35.9 %all-to-all-start.1 = ((bf16[64,8,512]{2,1,0:T(8,128)(2,1)}), bf16[64,8,512]{2,1,0:T(8,128)(2,1)S(1)}, u32[]{:S(2)}, u32[]{:S(2)}) async-start(bf16[64,8,512]{2,1,0:T(8,128)(2,1)} %shard_map.101), calls=%async_computation.1 | async-start | bytes 1048576 | tf_op jit(solution)/shard_map/all_to_all | solution.py:518
  22.8 1.1 copy-start.2
  23.9 0.9 copy-start.3
  31.1 2.0 copy-start
  41.3 68.7 %copy-start.4 = (bf16[2,128,256]{2,1,0:T(8,128)(2,1)S(1)}, bf16[2,128,256]{2,1,0:T(8,128)(2,1)}, u32[]{:S(2)}) copy-start(bf16[2,128,256]{2,1,0:T(8,128)(2,1)} %rest_1_.1) | copy-start | bytes 393220
  41.3 68.7 %copy-start.9 = (bf16[2,64,128]{2,1,0:T(8,128)(2,1)S(1)}, bf16[2,64,128]{2,1,0:T(8,128)(2,1)}, u32[]{:S(2)}) copy-start(bf16[2,64,128]{2,1,0:T(8,128)(2,1)} %out_weight_ref.3) | copy-start | bytes 98308
  41.3 68.7 %copy-start.11 = (s32[1280]{0:T(1024)S(1)}, s32[1280]{0:T(1024)}, u32[]{:S(2)}) copy-start(s32[1280]{0:T(1024)} %valid_ref.7) | copy-start | bytes 15364
  41.3 68.7 %copy-start.15 = (s32[2]{0:T(128)S(1)}, s32[2]{0:T(128)}, u32[]{:S(2)}) copy-start(s32[2]{0:T(128)} %pad_add_fusion.place_ref) | copy-start | bytes 28
  41.3 68.7 %copy-start.16 = (f32[2,64]{1,0:T(2,128)S(1)}, f32[2,64]{1,0:T(2,128)}, u32[]{:S(2)}) copy-start(f32[2,64]{1,0:T(2,128)} %out_gain_ref.3) | copy-start | bytes 1540
  41.4 24.3 %all-to-all-start = ((bf16[64,8,512]{2,1,0:T(8,128)(2,1)}), bf16[64,8,512]{2,1,0:T(8,128)(2,1)S(1)}, u32[]{:S(2)}, u32[]{:S(2)}) async-start(bf16[64,8,512]{2,1,0:T(8,128)(2,1)} %get-tuple-element.11), calls=%async_computation | async-start | bytes 1048576 | tf_op jit(solution)/shard_map/all_to_all | solution.py:518
  47.2 22.3 %collective-permute-start = (bf16[320,640]{1,0:T(8,128)(2,1)S(1)}, bf16[320,640]{1,0:T(8,128)(2,1)S(1)}, u32[]{:S(2)}, u32[]{:S(2)}) collective-permute-start(bf16[320,640]{1,0:T(8,128)(2,1)S(1)} %shard_map.102.rest_0_), channel_id=1, source_target_pairs={{0,12},{4,0},{8,4},{12,8},{1,13},{5,1},{9,5},{13,9},{2,14},{6,2},{... | collective-permute-start | bytes 1228808 | tf_op jit(solution)/shard_map/ppermute | solution.py:512
  50.0 19.6 %collective-permute-start.1 = (bf16[320,640]{1,0:T(8,128)(2,1)S(1)}, bf16[320,640]{1,0:T(8,128)(2,1)S(1)}, u32[]{:S(2)}, u32[]{:S(2)}) collective-permute-start(bf16[320,640]{1,0:T(8,128)(2,1)S(1)} %shard_map.102.rest_0_), channel_id=1, source_target_pairs={{0,8},{4,12},{8,0},{12,4},{1,9},{5,13},{9,1},{13,5},{2,10},{6,14},... | collective-permute-start | bytes 1228808 | tf_op jit(solution)/shard_map/ppermute | solution.py:512
  53.0 19.1 %collective-permute-start.2 = (bf16[320,640]{1,0:T(8,128)(2,1)S(1)}, bf16[320,640]{1,0:T(8,128)(2,1)S(1)}, u32[]{:S(2)}, u32[]{:S(2)}) collective-permute-start(bf16[320,640]{1,0:T(8,128)(2,1)S(1)} %shard_map.102.rest_0_), channel_id=1, source_target_pairs={{0,4},{4,8},{8,12},{12,0},{1,5},{5,9},{9,13},{13,1},{2,6},{6,10},{... | collective-permute-start | bytes 1228808 | tf_op jit(solution)/shard_map/ppermute | solution.py:512
  65.6 44.5 %copy-start.1 = (f32[2,32,128,128]{3,2,1,0:T(8,128)S(1)}, f32[2,32,128,128]{3,2,1,0:T(8,128)}, u32[]{:S(2)}) copy-start(f32[2,32,128,128]{3,2,1,0:T(8,128)} %copy-done) | copy-start | bytes 12582916
  74.6 3.8 %collective-permute-start.3 = (bf16[64,8,512]{2,1,0:T(8,128)(2,1)S(1)}, bf16[64,8,512]{2,1,0:T(8,128)(2,1)S(1)}, u32[]{:S(2)}, u32[]{:S(2)}) collective-permute-start(bf16[64,8,512]{2,1,0:T(8,128)(2,1)S(1)} %slice_bitcast_fusion), channel_id=1, source_target_pairs={{0,16},{16,0},{1,17},{17,1},{2,18},{18,2},{3,19},{19,3},{4,20},{20... | collective-permute-start | bytes 1572872 | tf_op jit(solution)/shard_map/ppermute | solution.py:522
  110.1 55.6 %copy-start.8 = (bf16[2,128,128]{2,1,0:T(8,128)(2,1)S(1)}, bf16[2,128,128]{2,1,0:T(8,128)(2,1)}, u32[]{:S(2)}) copy-start(bf16[2,128,128]{2,1,0:T(8,128)(2,1)} %gate_ref.3) | copy-start | bytes 196612
  110.1 55.6 %copy-start.13 = (s32[1280]{0:T(1024)S(1)}, s32[1280]{0:T(1024)}, u32[]{:S(2)}) copy-start(s32[1280]{0:T(1024)} %chain_ref.3) | copy-start | bytes 15364
  113.9 32.1 %copy-start.5 = (bf16[80,40,128]{2,1,0:T(8,128)(2,1)}, bf16[80,40,128]{2,1,0:T(8,128)(2,1)S(1)}, u32[]{:S(2)}) copy-start(bf16[80,40,128]{2,1,0:T(8,128)(2,1)S(1)} %get-tuple-element.13.pair_ref) | copy-start | bytes 2457604
  147.4 16.3 %all-to-all-start.4 = ((bf16[4,160,320]{2,1,0:T(8,128)(2,1)}), bf16[4,160,320]{2,1,0:T(8,128)(2,1)S(1)}, u32[]{:S(2)}, u32[]{:S(2)}) async-start(bf16[4,160,320]{2,1,0:T(8,128)(2,1)} %bitcast.6), calls=%async_computation.4 | async-start | bytes 983040 | tf_op jit(solution)/shard_map/all_to_all | solution.py:518
  153.9 21.6 %collective-permute-start.5 = (bf16[320,640]{1,0:T(8,128)(2,1)S(1)}, bf16[320,640]{1,0:T(8,128)(2,1)S(1)}, u32[]{:S(2)}, u32[]{:S(2)}) collective-permute-start(bf16[320,640]{1,0:T(8,128)(2,1)S(1)} %shard_map.107.rest_0_), channel_id=1, source_target_pairs={{0,12},{4,0},{8,4},{12,8},{1,13},{5,1},{9,5},{13,9},{2,14},{6,2},{... | collective-permute-start | bytes 1228808 | tf_op jit(solution)/shard_map/ppermute | solution.py:512
  156.7 18.8 %collective-permute-start.6 = (bf16[320,640]{1,0:T(8,128)(2,1)S(1)}, bf16[320,640]{1,0:T(8,128)(2,1)S(1)}, u32[]{:S(2)}, u32[]{:S(2)}) collective-permute-start(bf16[320,640]{1,0:T(8,128)(2,1)S(1)} %shard_map.107.rest_0_), channel_id=1, source_target_pairs={{0,8},{4,12},{8,0},{12,4},{1,9},{5,13},{9,1},{13,5},{2,10},{6,14},... | collective-permute-start | bytes 1228808 | tf_op jit(solution)/shard_map/ppermute | solution.py:512
  159.2 17.1 %collective-permute-start.7 = (bf16[320,640]{1,0:T(8,128)(2,1)S(1)}, bf16[320,640]{1,0:T(8,128)(2,1)S(1)}, u32[]{:S(2)}, u32[]{:S(2)}) collective-permute-start(bf16[320,640]{1,0:T(8,128)(2,1)S(1)} %shard_map.107.rest_0_), channel_id=1, source_target_pairs={{0,4},{4,8},{8,12},{12,0},{1,5},{5,9},{9,13},{13,1},{2,6},{6,10},{... | collective-permute-start | bytes 1228808 | tf_op jit(solution)/shard_map/ppermute | solution.py:512
  163.7 12.6 %collective-permute-start.4 = (bf16[4,160,320]{2,1,0:T(8,128)(2,1)S(1)}, bf16[4,160,320]{2,1,0:T(8,128)(2,1)S(1)}, u32[]{:S(2)}, u32[]{:S(2)}) collective-permute-start(bf16[4,160,320]{2,1,0:T(8,128)(2,1)S(1)} %all-to-all-done.4.own_ref), channel_id=1, source_target_pairs={{0,16},{16,0},{1,17},{17,1},{2,18},{18,2},{3,19},{19,3},{4,20},{20... | collective-permute-start | bytes 1228808 | tf_op jit(solution)/shard_map/ppermute | solution.py:522
  165.7 1.1 copy-start.6
  (4 other events, 2.8 us)

commit v8 on v7

--- a/solution.py
+++ b/solution.py
@@ -24,6 +24,7 @@
 SUB = 8
 WHOLE = 3
 TAIL = 8 * 9
+ORDER = (0, 2, 1, 3)
 STRIDE = 40
 BOTH = 56
 BATCH = 8
@@ -130,8 +131,8 @@
         scratch[place, :] = factor[:, n * LANES : (n + 1) * LANES]
 
 
-def put_chunks(scratch, out_ref, stride, depth):
-    for channel in range(HIDDEN):
+def put_chunks(scratch, out_ref, stride, depth, channels=range(HIDDEN)):
+    for channel in channels:
         rows = scratch[pl.ds(channel * stride, depth), :]
         tiles = [rows[n : n + SUB] for n in range(0, depth, SUB)]
         out_ref[channel] = jnp.concatenate(tiles, axis=1).astype(jnp.bfloat16)
@@ -147,13 +148,15 @@
     gain_any,
     bias_any,
     weight_any,
+    right_any,
+    right_s,
     right_ref,
-    right_s,
     pair_ref,
     gain_ref,
     bias_ref,
     weight_ref,
     sems,
+    out_sem,
 ):
     moves = [(gain_any, gain_ref), (bias_any, bias_ref), (weight_any, weight_ref)]
     parts = []
@@ -180,16 +183,22 @@
         keep_rows(factor, right_s, first, STRIDE)
 
     batches(work)
-    put_chunks(right_s, right_ref, STRIDE, DEPTH)
+    for part in range(0, HIDDEN, 16):
+        put_chunks(right_s, right_ref, STRIDE, DEPTH, range(part, part + 16))
+        span = pl.ds(part, 16)
+        pltpu.make_async_copy(right_ref.at[span], right_any.at[span], out_sem).start()
+    pltpu.make_async_copy(right_ref, right_any, out_sem).wait()
 
 
 def project_right(place, valid, *operands):
-    scratch = [pltpu.VMEM(each.shape, each.dtype) for each in operands]
+    scratch = [pltpu.VMEM(each.shape, each.dtype) for each in (CHUNKS,) + operands]
+    sems = [pltpu.SemaphoreType.DMA((13,)), pltpu.SemaphoreType.DMA]
     return call(
         right_kernel,
         CHUNKS,
         [SMEM, SMEM] + [ANY] * 4,
-        [SCRATCH] + scratch + [pltpu.SemaphoreType.DMA((13,))],
+        [SCRATCH] + scratch + sems,
+        outs=ANY,
         grant=60,
     )(place, valid, *operands)
 
@@ -461,8 +470,8 @@
         )
     for half in range(2):
         slot = lax.rem(core_ref[0] + half, 2)
-        for n in range(X):
-            x = lax.rem(core_ref[1] + n, X)
+        for n, ahead in enumerate(ORDER):
+            x = lax.rem(core_ref[1] + ahead, X)
             for low in range(ZH):
                 span = ((lax.rem(x, 2) * ZH + low) * ZH) * 2 + x // 2
                 for zh in range(ZH):
@@ -486,9 +495,9 @@
     for n, left_ref in enumerate((own_ref, other_ref)):
         side = lax.rem(core_ref[0] + n, 2)
         product = jnp.zeros((ZH * COLUMNS, SPAN * COLUMNS), jnp.float32)
-        for m, right_ref in enumerate(rights):
+        for ahead, right_ref in zip(ORDER, rights):
             product = product + jnp.dot(
-                left_ref[lax.rem(core_ref[1] + m, X)],
+                left_ref[lax.rem(core_ref[1] + ahead, X)],
                 right_ref[...],
                 preferred_element_type=jnp.float32,
             )
@@ -508,10 +517,10 @@
 
 
 def gather_x(block):
-    def shift(by):
-        return lax.ppermute(block, "x", [(x, (x + by) % X) for x in range(X)])
-
-    return [block] + [shift(-n) for n in range(1, X)]
+    def shift(ahead):
+        return lax.ppermute(block, "x", [(x, (x - ahead) % X) for x in range(X)])
+
+    return [block] + [shift(ahead) for ahead in ORDER[1:]]
 
 
 def exchange(values, axes):

time: 212 us -> 207 us (0.976)
  waiting for transfers between devices: 33.6 us -> 29.9 us
    ppermute x6, waiting for transfers between devices: 14.9 us -> 11.8 us  [shift(): return lax.ppermute(block, 'x', [(x, (x - ahead) % X) for x in range(X)])]
  transfers between devices with their start and end apart: 11 -> 11, of which waited for: 7 -> 6; matrix products, arithmetic and copies ran while one was open for 0% -> 0% of each run, Pallas kernels for 3% -> 3%
where the time goes in v8:
time: 207 us; the launch traced here: 204 us
  blocking collectives  90.8 us (44%)
  starting transfers between devices  51.5 us (25%)
  waiting for transfers between devices  29.9 us (14%)
  Pallas kernels  22.2 us (11%)
  local copies, waits for them, and re-layouts  8.05 us (4%)
    all_to_all x3, blocking collectives, exchange(): return lax.all_to_all(values, axes, split_axis=0, concat_axis=0, tiled=True)  90.8 us
    all_to_all x3, starting transfers between devices, exchange(): return lax.all_to_all(values, axes, split_axis=0, concat_axis=0, tiled=True)  26.9 us
    ppermute x6, starting transfers between devices, shift(): return lax.ppermute(block, 'x', [(x, (x - ahead) % X) for x in range(X)])  20.8 us
    all_to_all x3, waiting for transfers between devices, exchange(): return lax.all_to_all(values, axes, split_axis=0, concat_axis=0, tiled=True)  16.2 us
    ppermute x6, waiting for transfers between devices, shift(): return lax.ppermute(block, 'x', [(x, (x - ahead) % X) for x in range(X)])  11.8 us
    unnamed x34, local copies, waits for them, and re-layouts  8.02 us
    pallas_call x2, Pallas kernels, finish(): call(functools.partial(finish_kernel, which), [out, NORMED, BOTH_CHUNKS]...  6.07 us
    pallas_call x1, Pallas kernels, project_right(): call(right_kernel, CHUNKS, [SMEM, SMEM] + [ANY] * 4, [SCRATCH] + scratch...  4.84 us
  transfers between devices with their start and end apart: 11, of which 6 were waited for; matrix products, arithmetic and copies ran while one was open for 0% of the time, Pallas kernels for 3%

profile of v8, /device:TPU:6, one launch (start us, length us, event | category | flops | bytes accessed | tf_op | source)
XLA Modules:
  0.0 204.3 jit_solution(3637539729709216400)
XLA Ops:
  0.6 4.8 %shard_map.101 = bf16[64,8,512]{2,1,0:T(8,128)(2,1)} custom-call(s32[2]{0:T(128)} %pad_add_fusion.place_ref, s32[1280]{0:T(1024)} %valid_ref.7, bf16[80,40,128]{2,1,0:T(8,128)(2,1)} %pair_any.1, f32[2,128]{1,0:T(2,128)} %gain_any.1, f32[2,128]{1,0:T(2,128)} %bias_any.1, bf16[2,128,256]{2,1,0:T(8,128)(2,1)} %rest_1_.1), custom_call_target="tpu_custom_call" | custom-call | flops 100000000 | bytes 4000000 | tf_op jit(solution)/shard_map/pallas_call | solution.py:196
  5.4 16.6 %all-to-all-start.1 = ((bf16[64,8,512]{2,1,0:T(8,128)(2,1)}), bf16[64,8,512]{2,1,0:T(8,128)(2,1)S(1)}, u32[]{:S(2)}, u32[]{:S(2)}) async-start(bf16[64,8,512]{2,1,0:T(8,128)(2,1)} %shard_map.101), calls=%async_computation.1 | async-start | bytes 1048576 | tf_op jit(solution)/shard_map/all_to_all | solution.py:527
  27.6 3.4 %shard_map.100 = (bf16[64,8,512]{2,1,0:T(8,128)(2,1)}, f32[2,32,128,128]{3,2,1,0:T(8,128)S(1)}) custom-call(s32[2]{0:T(128)S(1)} %copy-done.14, s32[1280]{0:T(1024)S(1)} %copy-done.10, s32[1280]{0:T(1024)S(1)} %copy-done.12, bf16[2,128,256]{2,1,0:T(8,128)(2,1)S(1)} %copy-done.3, bf16[2,128,128]{2,1,0:T(8,128)(2,1)S(1)} %copy-done.7, ...), custom_call_target="tpu_custom_call" | custom-call | flops 100000000 | bytes 4000000 | tf_op jit(solution)/shard_map/pallas_call | solution.py:285
  31.0 2.0 copy-done
  33.0 8.3 %all-to-all-done.1.chunks_ref = bf16[64,8,512]{2,1,0:T(8,128)(2,1)S(1)} async-done(((bf16[64,8,512]{2,1,0:T(8,128)(2,1)}), bf16[64,8,512]{2,1,0:T(8,128)(2,1)S(1)}, u32[]{:S(2)}, u32[]{:S(2)}) %all-to-all-start.1) | async-done | bytes 524320 | tf_op jit(solution)/shard_map/all_to_all | solution.py:527
  41.3 5.5 %all-to-all-start = ((bf16[64,8,512]{2,1,0:T(8,128)(2,1)}), bf16[64,8,512]{2,1,0:T(8,128)(2,1)S(1)}, u32[]{:S(2)}, u32[]{:S(2)}) async-start(bf16[64,8,512]{2,1,0:T(8,128)(2,1)} %get-tuple-element.11), calls=%async_computation | async-start | bytes 1048576 | tf_op jit(solution)/shard_map/all_to_all | solution.py:527
  47.2 3.3 %collective-permute-start = (bf16[320,640]{1,0:T(8,128)(2,1)S(1)}, bf16[320,640]{1,0:T(8,128)(2,1)S(1)}, u32[]{:S(2)}, u32[]{:S(2)}) collective-permute-start(bf16[320,640]{1,0:T(8,128)(2,1)S(1)} %shard_map.102.rest_0_), channel_id=1, source_target_pairs={{0,8},{4,12},{8,0},{12,4},{1,9},{5,13},{9,1},{13,5},{2,10},{6,14},... | collective-permute-start | bytes 1228808 | tf_op jit(solution)/shard_map/ppermute | solution.py:521
  52.5 5.1 %collective-permute-start.2 = (bf16[320,640]{1,0:T(8,128)(2,1)S(1)}, bf16[320,640]{1,0:T(8,128)(2,1)S(1)}, u32[]{:S(2)}, u32[]{:S(2)}) collective-permute-start(bf16[320,640]{1,0:T(8,128)(2,1)S(1)} %shard_map.102.rest_0_), channel_id=1, source_target_pairs={{0,4},{4,8},{8,12},{12,0},{1,5},{5,9},{9,13},{13,1},{2,6},{6,10},{... | collective-permute-start | bytes 1228808 | tf_op jit(solution)/shard_map/ppermute | solution.py:521
  57.7 7.9 %all-to-all-done.left_ref = bf16[64,8,512]{2,1,0:T(8,128)(2,1)S(1)} async-done(((bf16[64,8,512]{2,1,0:T(8,128)(2,1)}), bf16[64,8,512]{2,1,0:T(8,128)(2,1)S(1)}, u32[]{:S(2)}, u32[]{:S(2)}) %all-to-all-start) | async-done | bytes 524320 | tf_op jit(solution)/shard_map/all_to_all | solution.py:527
  65.6 4.3 %collective-permute-done.1.rest_2_ = bf16[320,640]{1,0:T(8,128)(2,1)S(1)} collective-permute-done((bf16[320,640]{1,0:T(8,128)(2,1)S(1)}, bf16[320,640]{1,0:T(8,128)(2,1)S(1)}, u32[]{:S(2)}, u32[]{:S(2)}) %collective-permute-start.1) | collective-permute-done | bytes 409632 | tf_op jit(solution)/shard_map/ppermute | solution.py:521
  69.9 2.5 %shard_map.103 = bf16[2,64,8,512]{3,2,1,0:T(8,128)(2,1)S(1)} custom-call(s32[2]{0:T(128)S(1)} %pad_add_fusion.1.core_ref, bf16[64,8,512]{2,1,0:T(8,128)(2,1)S(1)} %all-to-all-done.left_ref, bf16[320,640]{1,0:T(8,128)(2,1)S(1)} %shard_map.102.rest_0_, bf16[320,640]{1,0:T(8,128)(2,1)S(1)} %collective-permute-done.rest_1_, ...), custom_call_target="tpu_custom_call" | custom-call | flops 600000000 | bytes 4000000 | tf_op jit(solution)/shard_map/pallas_call | solution.py:488
  72.4 1.9 collective-permute-start.3
  76.3 31.5 %all_to_all.30.product_ref = bf16[64,8,512]{2,1,0:T(8,128)(2,1)S(1)} all-to-all(bf16[64,8,512]{2,1,0:T(8,128)(2,1)S(1)} %fusion), channel_id=1, replica_groups=mesh['zl'=2,'y'=8,'core'=2,'x'=4,'zh'=4] {'y','zh','zl'}, dimensions={0} | all-to-all | bytes 1048576 | tf_op jit(solution)/shard_map/all_to_all | solution.py:527
  107.9 3.8 %shard_map.104 = (bf16[80,40,128]{2,1,0:T(8,128)(2,1)S(1)}, bf16[32,128,128]{2,1,0:T(8,128)(2,1)S(1)}, bf16[64,8,896]{2,1,0:T(8,128)(2,1)S(1)}) custom-call(s32[2]{0:T(128)S(1)} %copy-done.15, s32[1280]{0:T(1024)S(1)} %copy-done.11, f32[2,64]{1,0:T(2,128)S(1)} %copy-done.16, f32[2,32,128,128]{3,2,1,0:T(8,128)S(1)} %copy-done.1, ...), custom_call_target="tpu_custom_call" | custom-call | flops 100000000 | bytes 4000000 | tf_op jit(solution)/shard_map/pallas_call | solution.py:384
  111.7 32.1 %all_to_all.31.chunks_ref = bf16[64,8,896]{2,1,0:T(8,128)(2,1)S(1)} all-to-all(bf16[64,8,896]{2,1,0:T(8,128)(2,1)S(1)} %get-tuple-element.14), channel_id=1, replica_groups=mesh['zl'=2,'y'=8,'core'=2,'x'=4,'zh'=4] {'y','zh','zl'}, dimensions={0} | all-to-all | bytes 1835008 | tf_op jit(solution)/shard_map/all_to_all | solution.py:527
  145.2 4.8 %all-to-all-start.4 = ((bf16[4,160,320]{2,1,0:T(8,128)(2,1)}), bf16[4,160,320]{2,1,0:T(8,128)(2,1)S(1)}, u32[]{:S(2)}, u32[]{:S(2)}) async-start(bf16[4,160,320]{2,1,0:T(8,128)(2,1)} %bitcast.6), calls=%async_computation.4 | async-start | bytes 983040 | tf_op jit(solution)/shard_map/all_to_all | solution.py:527
  150.3 3.4 %collective-permute-start.5 = (bf16[320,640]{1,0:T(8,128)(2,1)S(1)}, bf16[320,640]{1,0:T(8,128)(2,1)S(1)}, u32[]{:S(2)}, u32[]{:S(2)}) collective-permute-start(bf16[320,640]{1,0:T(8,128)(2,1)S(1)} %shard_map.107.rest_0_), channel_id=1, source_target_pairs={{0,8},{4,12},{8,0},{12,4},{1,9},{5,13},{9,1},{13,5},{2,10},{6,14},... | collective-permute-start | bytes 1228808 | tf_op jit(solution)/shard_map/ppermute | solution.py:521
  155.6 5.1 %collective-permute-start.7 = (bf16[320,640]{1,0:T(8,128)(2,1)S(1)}, bf16[320,640]{1,0:T(8,128)(2,1)S(1)}, u32[]{:S(2)}, u32[]{:S(2)}) collective-permute-start(bf16[320,640]{1,0:T(8,128)(2,1)S(1)} %shard_map.107.rest_0_), channel_id=1, source_target_pairs={{0,4},{4,8},{8,12},{12,0},{1,5},{5,9},{9,13},{13,1},{2,6},{6,10},{... | collective-permute-start | bytes 1228808 | tf_op jit(solution)/shard_map/ppermute | solution.py:521
  160.8 1.9 collective-permute-start.4
  165.0 2.2 %collective-permute-done.5.rest_1_ = bf16[320,640]{1,0:T(8,128)(2,1)S(1)} collective-permute-done((bf16[320,640]{1,0:T(8,128)(2,1)S(1)}, bf16[320,640]{1,0:T(8,128)(2,1)S(1)}, u32[]{:S(2)}, u32[]{:S(2)}) %collective-permute-start.5) | collective-permute-done | bytes 409632 | tf_op jit(solution)/shard_map/ppermute | solution.py:521
  167.1 5.4 %collective-permute-done.6.rest_2_ = bf16[320,640]{1,0:T(8,128)(2,1)S(1)} collective-permute-done((bf16[320,640]{1,0:T(8,128)(2,1)S(1)}, bf16[320,640]{1,0:T(8,128)(2,1)S(1)}, u32[]{:S(2)}, u32[]{:S(2)}) %collective-permute-start.6) | collective-permute-done | bytes 409632 | tf_op jit(solution)/shard_map/ppermute | solution.py:521
  172.5 2.1 %shard_map.108 = bf16[64,8,512]{2,1,0:T(8,128)(2,1)S(1)} custom-call(s32[2]{0:T(128)S(1)} %pad_add_fusion.1.core_ref, bf16[4,160,320]{2,1,0:T(8,128)(2,1)S(1)} %all-to-all-done.4.own_ref, bf16[4,160,320]{2,1,0:T(8,128)(2,1)S(1)} %collective-permute-done.4.other_ref, bf16[320,640]{1,0:T(8,128)(2,1)S(1)} %shard_map.107.rest_0_, ...), custom_call_target="tpu_custom_call" | custom-call | flops 600000000 | bytes 4000000 | tf_op jit(solution)/shard_map/pallas_call | solution.py:514
  174.7 27.2 %all_to_all.32.product_ref = bf16[64,8,512]{2,1,0:T(8,128)(2,1)S(1)} all-to-all(bf16[64,8,512]{2,1,0:T(8,128)(2,1)S(1)} %shard_map.108), channel_id=1, replica_groups=mesh['zl'=2,'y'=8,'core'=2,'x'=4,'zh'=4] {'y','zh','zl'}, dimensions={0} | all-to-all | bytes 1048576 | tf_op jit(solution)/shard_map/all_to_all | solution.py:527
  201.9 2.3 %shard_map.109 = bf16[80,40,128]{2,1,0:T(8,128)(2,1)} custom-call(s32[2]{0:T(128)S(1)} %copy-done.15, s32[1280]{0:T(1024)S(1)} %copy-done.11, f32[2,64]{1,0:T(2,128)S(1)} %copy-done.16, f32[2,32,128,128]{3,2,1,0:T(8,128)S(1)} %shard_map.105.rest_4_.gates_ref, bf16[64,8,512]{2,1,0:T(8,128)(2,1)S(1)} %all_to_all.32.product_ref, bf16[2,64,128]{2,1,0:T(8,128)(2,1)S(1)} %copy-done.9), custom_call_target="tpu_custom_call" | custom-call | flops 100000000 | bytes 4000000 | tf_op jit(solution)/shard_map/pallas_call | solution.py:384
  (50 shorter events, 16.6 us)
Async XLA Ops:
  5.4 35.9 %all-to-all-start.1 = ((bf16[64,8,512]{2,1,0:T(8,128)(2,1)}), bf16[64,8,512]{2,1,0:T(8,128)(2,1)S(1)}, u32[]{:S(2)}, u32[]{:S(2)}) async-start(bf16[64,8,512]{2,1,0:T(8,128)(2,1)} %shard_map.101), calls=%async_computation.1 | async-start | bytes 1048576 | tf_op jit(solution)/shard_map/all_to_all | solution.py:527
  22.8 1.1 copy-start.2
  23.9 0.9 copy-start.3
  31.0 2.0 copy-start
  41.3 66.5 %copy-start.4 = (bf16[2,128,256]{2,1,0:T(8,128)(2,1)S(1)}, bf16[2,128,256]{2,1,0:T(8,128)(2,1)}, u32[]{:S(2)}) copy-start(bf16[2,128,256]{2,1,0:T(8,128)(2,1)} %rest_1_.1) | copy-start | bytes 393220
  41.3 66.5 %copy-start.9 = (bf16[2,64,128]{2,1,0:T(8,128)(2,1)S(1)}, bf16[2,64,128]{2,1,0:T(8,128)(2,1)}, u32[]{:S(2)}) copy-start(bf16[2,64,128]{2,1,0:T(8,128)(2,1)} %out_weight_ref.3) | copy-start | bytes 98308
  41.3 66.5 %copy-start.11 = (s32[1280]{0:T(1024)S(1)}, s32[1280]{0:T(1024)}, u32[]{:S(2)}) copy-start(s32[1280]{0:T(1024)} %valid_ref.7) | copy-start | bytes 15364
  41.3 66.5 %copy-start.15 = (s32[2]{0:T(128)S(1)}, s32[2]{0:T(128)}, u32[]{:S(2)}) copy-start(s32[2]{0:T(128)} %pad_add_fusion.place_ref) | copy-start | bytes 28
  41.3 66.5 %copy-start.16 = (f32[2,64]{1,0:T(2,128)S(1)}, f32[2,64]{1,0:T(2,128)}, u32[]{:S(2)}) copy-start(f32[2,64]{1,0:T(2,128)} %out_gain_ref.3) | copy-start | bytes 1540
  41.3 24.3 %all-to-all-start = ((bf16[64,8,512]{2,1,0:T(8,128)(2,1)}), bf16[64,8,512]{2,1,0:T(8,128)(2,1)S(1)}, u32[]{:S(2)}, u32[]{:S(2)}) async-start(bf16[64,8,512]{2,1,0:T(8,128)(2,1)} %get-tuple-element.11), calls=%async_computation | async-start | bytes 1048576 | tf_op jit(solution)/shard_map/all_to_all | solution.py:527
  47.2 18.4 %collective-permute-start = (bf16[320,640]{1,0:T(8,128)(2,1)S(1)}, bf16[320,640]{1,0:T(8,128)(2,1)S(1)}, u32[]{:S(2)}, u32[]{:S(2)}) collective-permute-start(bf16[320,640]{1,0:T(8,128)(2,1)S(1)} %shard_map.102.rest_0_), channel_id=1, source_target_pairs={{0,8},{4,12},{8,0},{12,4},{1,9},{5,13},{9,1},{13,5},{2,10},{6,14},... | collective-permute-start | bytes 1228808 | tf_op jit(solution)/shard_map/ppermute | solution.py:521
  50.5 19.3 %collective-permute-start.1 = (bf16[320,640]{1,0:T(8,128)(2,1)S(1)}, bf16[320,640]{1,0:T(8,128)(2,1)S(1)}, u32[]{:S(2)}, u32[]{:S(2)}) collective-permute-start(bf16[320,640]{1,0:T(8,128)(2,1)S(1)} %shard_map.102.rest_0_), channel_id=1, source_target_pairs={{0,12},{4,0},{8,4},{12,8},{1,13},{5,1},{9,5},{13,9},{2,14},{6,2},{... | collective-permute-start | bytes 1228808 | tf_op jit(solution)/shard_map/ppermute | solution.py:521
  52.5 17.4 %collective-permute-start.2 = (bf16[320,640]{1,0:T(8,128)(2,1)S(1)}, bf16[320,640]{1,0:T(8,128)(2,1)S(1)}, u32[]{:S(2)}, u32[]{:S(2)}) collective-permute-start(bf16[320,640]{1,0:T(8,128)(2,1)S(1)} %shard_map.102.rest_0_), channel_id=1, source_target_pairs={{0,4},{4,8},{8,12},{12,0},{1,5},{5,9},{9,13},{13,1},{2,6},{6,10},{... | collective-permute-start | bytes 1228808 | tf_op jit(solution)/shard_map/ppermute | solution.py:521
  65.6 42.2 %copy-start.1 = (f32[2,32,128,128]{3,2,1,0:T(8,128)S(1)}, f32[2,32,128,128]{3,2,1,0:T(8,128)}, u32[]{:S(2)}) copy-start(f32[2,32,128,128]{3,2,1,0:T(8,128)} %copy-done) | copy-start | bytes 12582916
  72.4 3.8 %collective-permute-start.3 = (bf16[64,8,512]{2,1,0:T(8,128)(2,1)S(1)}, bf16[64,8,512]{2,1,0:T(8,128)(2,1)S(1)}, u32[]{:S(2)}, u32[]{:S(2)}) collective-permute-start(bf16[64,8,512]{2,1,0:T(8,128)(2,1)S(1)} %slice_bitcast_fusion), channel_id=1, source_target_pairs={{0,16},{16,0},{1,17},{17,1},{2,18},{18,2},{3,19},{19,3},{4,20},{20... | collective-permute-start | bytes 1572872 | tf_op jit(solution)/shard_map/ppermute | solution.py:531
  107.8 54.9 %copy-start.8 = (bf16[2,128,128]{2,1,0:T(8,128)(2,1)S(1)}, bf16[2,128,128]{2,1,0:T(8,128)(2,1)}, u32[]{:S(2)}) copy-start(bf16[2,128,128]{2,1,0:T(8,128)(2,1)} %gate_ref.3) | copy-start | bytes 196612
  107.8 54.9 %copy-start.13 = (s32[1280]{0:T(1024)S(1)}, s32[1280]{0:T(1024)}, u32[]{:S(2)}) copy-start(s32[1280]{0:T(1024)} %chain_ref.3) | copy-start | bytes 15364
  111.6 32.1 %copy-start.5 = (bf16[80,40,128]{2,1,0:T(8,128)(2,1)}, bf16[80,40,128]{2,1,0:T(8,128)(2,1)S(1)}, u32[]{:S(2)}) copy-start(bf16[80,40,128]{2,1,0:T(8,128)(2,1)S(1)} %get-tuple-element.13.pair_ref) | copy-start | bytes 2457604
  145.2 15.6 %all-to-all-start.4 = ((bf16[4,160,320]{2,1,0:T(8,128)(2,1)}), bf16[4,160,320]{2,1,0:T(8,128)(2,1)S(1)}, u32[]{:S(2)}, u32[]{:S(2)}) async-start(bf16[4,160,320]{2,1,0:T(8,128)(2,1)} %bitcast.6), calls=%async_computation.4 | async-start | bytes 983040 | tf_op jit(solution)/shard_map/all_to_all | solution.py:527
  150.3 16.8 %collective-permute-start.5 = (bf16[320,640]{1,0:T(8,128)(2,1)S(1)}, bf16[320,640]{1,0:T(8,128)(2,1)S(1)}, u32[]{:S(2)}, u32[]{:S(2)}) collective-permute-start(bf16[320,640]{1,0:T(8,128)(2,1)S(1)} %shard_map.107.rest_0_), channel_id=1, source_target_pairs={{0,8},{4,12},{8,0},{12,4},{1,9},{5,13},{9,1},{13,5},{2,10},{6,14},... | collective-permute-start | bytes 1228808 | tf_op jit(solution)/shard_map/ppermute | solution.py:521
  153.7 18.8 %collective-permute-start.6 = (bf16[320,640]{1,0:T(8,128)(2,1)S(1)}, bf16[320,640]{1,0:T(8,128)(2,1)S(1)}, u32[]{:S(2)}, u32[]{:S(2)}) collective-permute-start(bf16[320,640]{1,0:T(8,128)(2,1)S(1)} %shard_map.107.rest_0_), channel_id=1, source_target_pairs={{0,12},{4,0},{8,4},{12,8},{1,13},{5,1},{9,5},{13,9},{2,14},{6,2},{... | collective-permute-start | bytes 1228808 | tf_op jit(solution)/shard_map/ppermute | solution.py:521
  155.6 16.9 %collective-permute-start.7 = (bf16[320,640]{1,0:T(8,128)(2,1)S(1)}, bf16[320,640]{1,0:T(8,128)(2,1)S(1)}, u32[]{:S(2)}, u32[]{:S(2)}) collective-permute-start(bf16[320,640]{1,0:T(8,128)(2,1)S(1)} %shard_map.107.rest_0_), channel_id=1, source_target_pairs={{0,4},{4,8},{8,12},{12,0},{1,5},{5,9},{9,13},{13,1},{2,6},{6,10},{... | collective-permute-start | bytes 1228808 | tf_op jit(solution)/shard_map/ppermute | solution.py:521
  160.8 11.7 %collective-permute-start.4 = (bf16[4,160,320]{2,1,0:T(8,128)(2,1)S(1)}, bf16[4,160,320]{2,1,0:T(8,128)(2,1)S(1)}, u32[]{:S(2)}, u32[]{:S(2)}) collective-permute-start(bf16[4,160,320]{2,1,0:T(8,128)(2,1)S(1)} %all-to-all-done.4.own_ref), channel_id=1, source_target_pairs={{0,16},{16,0},{1,17},{17,1},{2,18},{18,2},{3,19},{19,3},{4,20},{20... | collective-permute-start | bytes 1228808 | tf_op jit(solution)/shard_map/ppermute | solution.py:531
  162.7 1.1 copy-start.6
  (4 other events, 2.8 us)

commit v9 on v8

--- a/solution.py
+++ b/solution.py
@@ -30,7 +30,6 @@
 BATCH = 8
 CHUNKS = jax.ShapeDtypeStruct((HIDDEN, SUB, DEPTH // SUB * LANES), jnp.bfloat16)
 BOTH_CHUNKS = jax.ShapeDtypeStruct((HIDDEN, SUB, BOTH // SUB * LANES), jnp.bfloat16)
-NORMED = jax.ShapeDtypeStruct((DEPTH, LANES, WIDTH), jnp.bfloat16)
 GATES = jax.ShapeDtypeStruct((2, DEPTH, LANES, WIDTH), jnp.float32)
 VMEM = pl.BlockSpec(memory_space=pltpu.VMEM)
 ANY = pl.BlockSpec(memory_space=pl.ANY)
@@ -131,26 +130,45 @@
         scratch[place, :] = factor[:, n * LANES : (n + 1) * LANES]
 
 
-def put_chunks(scratch, out_ref, stride, depth, channels=range(HIDDEN)):
+def put_chunks(scratch, out_ref, channels):
     for channel in channels:
-        rows = scratch[pl.ds(channel * stride, depth), :]
-        tiles = [rows[n : n + SUB] for n in range(0, depth, SUB)]
+        rows = scratch[pl.ds(channel * BOTH, BOTH), :]
+        tiles = [rows[n : n + SUB] for n in range(0, BOTH, SUB)]
         out_ref[channel] = jnp.concatenate(tiles, axis=1).astype(jnp.bfloat16)
 
 
+def factor_rows(first, count, normed, weights, mask_at, both_s):
+    left_weight, right_weight = weights
+    if count == 3:
+        rows = jnp.concatenate(pad_rows(normed, count), axis=0)
+        mask = mask_at(first, count, 0)
+        keep_rows(factor_of(rows, left_weight, mask), both_s, first, BOTH)
+        keep_rows(factor_of(rows, right_weight, mask), both_s, first + WHOLE * SUB, BOTH)
+        return
+    pieces = []
+    for n in range(BATCH):
+        piece = normed[n * COLUMNS : (n + 1) * COLUMNS]
+        pieces += [piece, piece, jnp.zeros((LANES - 2 * COLUMNS, WIDTH), jnp.float32)]
+    rows = jnp.concatenate(pieces, axis=0).astype(jnp.bfloat16)
+    factor = factor_of(rows, left_weight, mask_at(first, count, 0))
+    factor = factor + factor_of(rows, right_weight, mask_at(first, count, 1))
+    keep_rows(factor, both_s, 2 * WHOLE * SUB, BOTH)
+
+
 SCRATCH = pltpu.VMEM(((HIDDEN + 1) * STRIDE, LANES), jnp.float32)
-
-
-def right_kernel(
+BOTH_SCRATCH = pltpu.VMEM(((HIDDEN + 1) * BOTH, LANES), jnp.float32)
+
+
+def project_kernel(
     place_ref,
     valid_ref,
     pair_any,
     gain_any,
     bias_any,
     weight_any,
-    right_any,
-    right_s,
-    right_ref,
+    both_any,
+    both_s,
+    both_ref,
     pair_ref,
     gain_ref,
     bias_ref,
@@ -171,52 +189,51 @@
     columns = spread_columns(place_ref, valid_ref)
     for copy in copies[: parts[0]]:
         copy.wait()
-    weight = weight_of(weight_ref, 0, 2 * HIDDEN)
+    weights = [weight_of(weight_ref, 0, start) for start in (0, 2 * HIDDEN)]
+
+    def mask_at(first, count, shift):
+        return mask_of(first, count, place_ref, valid_ref, columns, shift)
 
     def work(first, count):
         for part in parts[first // BATCH * 3 :][:count]:
             copies[part].wait()
         values = load_pairs(pair_ref, first, count)
-        pieces = pad_rows(normalize(values, gain_ref[0:1], bias_ref[0:1]), count)
-        mask = mask_of(first, count, place_ref, valid_ref, columns)
-        factor = factor_of(jnp.concatenate(pieces, axis=0), weight, mask)
-        keep_rows(factor, right_s, first, STRIDE)
+        normed = normalize(values, gain_ref[0:1], bias_ref[0:1])
+        factor_rows(first, count, normed, weights, mask_at, both_s)
 
     batches(work)
     for part in range(0, HIDDEN, 16):
-        put_chunks(right_s, right_ref, STRIDE, DEPTH, range(part, part + 16))
+        put_chunks(both_s, both_ref, range(part, part + 16))
         span = pl.ds(part, 16)
-        pltpu.make_async_copy(right_ref.at[span], right_any.at[span], out_sem).start()
-    pltpu.make_async_copy(right_ref, right_any, out_sem).wait()
-
-
-def project_right(place, valid, *operands):
-    scratch = [pltpu.VMEM(each.shape, each.dtype) for each in (CHUNKS,) + operands]
+        pltpu.make_async_copy(both_ref.at[span], both_any.at[span], out_sem).start()
+    pltpu.make_async_copy(both_ref, both_any, out_sem).wait()
+
+
+def project(place, valid, *operands):
+    scratch = [pltpu.VMEM(each.shape, each.dtype) for each in (BOTH_CHUNKS,) + operands]
     sems = [pltpu.SemaphoreType.DMA((13,)), pltpu.SemaphoreType.DMA]
     return call(
-        right_kernel,
-        CHUNKS,
+        project_kernel,
+        BOTH_CHUNKS,
         [SMEM, SMEM] + [ANY] * 4,
-        [SCRATCH] + scratch + sems,
+        [BOTH_SCRATCH] + scratch + sems,
         outs=ANY,
         grant=60,
     )(place, valid, *operands)
 
 
-def load_normed(normed_ref, first):
-    return normed_ref[pl.ds(first, BATCH)].reshape(BATCH * LANES, WIDTH)
-
-
-def gate_work(which, place_ref, chain_ref, normed_of, gate_ref, vectors_ref, pair_ref, out_ref):
+def gate_kernel(which, place_ref, chain_ref, gate_ref, vectors_ref, pair_ref, _, out_ref):
     row = lax.broadcasted_iota(jnp.int32, (COLUMNS, WIDTH), 0)
     chain_columns = jnp.full((COLUMNS, WIDTH), -1, jnp.int32)
     for column in range(COLUMNS):
         chain_columns = jnp.where(row == column, chain_ref[place_ref[1] + column], chain_columns)
-    offset = vectors_ref[4 + which : 5 + which]
+    gain, bias, offset = [vectors_ref[n + which : n + which + 1] for n in (0, 2, 4)]
 
     def work(first, count):
+        values = load_pairs(pair_ref, first, count)
+        pieces = pad_rows(normalize(values, gain, bias), count)
         logit = jnp.dot(
-            normed_of(first, count), gate_ref[which], preferred_element_type=jnp.float32
+            jnp.concatenate(pieces, axis=0), gate_ref[which], preferred_element_type=jnp.float32
         )
         for n, rows in enumerate(block_rows(first, count)):
             for group, row in enumerate(rows):
@@ -226,75 +243,30 @@
                 out_ref[0, first + n, place] = jax.nn.sigmoid(
                     logit[start : start + COLUMNS] + jnp.where(same, offset, 0.0)
                 )
-                out_ref[1, first + n, place] = pair_ref[row].astype(jnp.float32)
-
-    return work
-
-
-def gate_kernel(
-    which, place_ref, chain_ref, normed_ref, gate_ref, vectors_ref, pair_ref, out_ref
-):
-    def normed_of(first, count):
-        return load_normed(normed_ref, first)
-
-    batches(
-        gate_work(which, place_ref, chain_ref, normed_of, gate_ref, vectors_ref, pair_ref, out_ref)
-    )
-
-
-def gates(which, place, chain, normed, gate, vectors, pair):
+                old = (n * count + group) * COLUMNS
+                out_ref[1, first + n, place] = values[old : old + COLUMNS]
+
+    batches(work)
+
+
+def gates(which, place, chain, gate, vectors, pair, after):
     kernel = functools.partial(gate_kernel, which)
-    return call(kernel, GATES, [SMEM, SMEM, VMEM, VMEM, VMEM, VMEM])(
-        place, chain, normed, gate, vectors, pair
-    )
-
-
-def left_and_gate_kernel(
-    place_ref,
-    valid_ref,
-    chain_ref,
-    weight_ref,
-    gate_ref,
-    vectors_ref,
-    pair_ref,
-    left_ref,
-    out_ref,
-    left_s,
-):
-    columns = spread_columns(place_ref, valid_ref)
-    weight = weight_of(weight_ref, 0, 0)
-
-    def work(first, count):
-        values = load_pairs(pair_ref, first, count)
-        pieces = pad_rows(normalize(values, vectors_ref[0:1], vectors_ref[2:3]), count)
-        normed = jnp.concatenate(pieces, axis=0)
-        mask = mask_of(first, count, place_ref, valid_ref, columns)
-        keep_rows(factor_of(normed, weight, mask), left_s, first, STRIDE)
-        gate(lambda *_: normed, first, count)
-
-    def gate(normed_of, first, count):
-        gate_work(
-            0, place_ref, chain_ref, normed_of, gate_ref, vectors_ref, pair_ref, out_ref
-        )(first, count)
-
-    batches(work)
-    put_chunks(left_s, left_ref, STRIDE, DEPTH)
-
-
-def left_and_gates(place, valid, chain, weight, gate, vectors, pair):
-    return call(left_and_gate_kernel, [CHUNKS, GATES], [SMEM] * 3 + [VMEM] * 4, [SCRATCH])(
-        place, valid, chain, weight, gate, vectors, pair
+    return call(kernel, GATES, [SMEM, SMEM, VMEM, VMEM, VMEM, ANY])(
+        place, chain, gate, vectors, pair, after
     )
 
 
 def finish_kernel(which, place_ref, valid_ref, out_gain_ref, gates_ref, product_ref, out_weight_ref, *rest):
     then = which == 0
     if then:
-        vectors_ref, weight_ref, out_ref, normed_ref, both_ref, hidden_s, both_s = rest
+        vectors_ref, weight_ref, out_ref, both_ref, hidden_s, both_s = rest
         new_s = out_ref
         columns = spread_columns(place_ref, valid_ref)
-        left_weight = weight_of(weight_ref, 1, 0)
-        right_weight = weight_of(weight_ref, 1, 2 * HIDDEN)
+        weights = [weight_of(weight_ref, 1, start) for start in (0, 2 * HIDDEN)]
+
+        def mask_at(first, count, shift):
+            return mask_of(first, count, place_ref, valid_ref, columns, shift)
+
     else:
         out_ref, hidden_s, new_s, out_sem = rest
 
@@ -344,34 +316,12 @@
                 pltpu.make_async_copy(new_s.at[span], out_ref.at[span], out_sem).start()
             return
         new = new.astype(jnp.bfloat16).astype(jnp.float32)
-        values = normalize(new, vectors_ref[1:2], vectors_ref[3:4])
-        pieces = pad_rows(values, count)
-        for n in range(BATCH):
-            normed_ref[first + n] = pieces[n]
-        mask = mask_of(first, count, place_ref, valid_ref, columns)
-        if count == 3:
-            normed = jnp.concatenate(pieces, axis=0)
-            keep_rows(factor_of(normed, left_weight, mask), both_s, first, BOTH)
-            right_first = first + WHOLE * SUB
-            keep_rows(factor_of(normed, right_weight, mask), both_s, right_first, BOTH)
-        else:
-            twice = [values[n * size : (n + 1) * size] for n in range(BATCH) for _ in range(2)]
-            normed = jnp.concatenate(
-                [
-                    each
-                    for n in range(BATCH)
-                    for each in twice[2 * n : 2 * n + 2]
-                    + [jnp.zeros((LANES - 2 * size, WIDTH), jnp.float32)]
-                ],
-                axis=0,
-            ).astype(jnp.bfloat16)
-            other = mask_of(first, count, place_ref, valid_ref, columns, 1)
-            factor = factor_of(normed, left_weight, mask) + factor_of(normed, right_weight, other)
-            keep_rows(factor, both_s, 2 * WHOLE * SUB, BOTH)
+        normed = normalize(new, vectors_ref[1:2], vectors_ref[3:4])
+        factor_rows(first, count, normed, weights, mask_at, both_s)
 
     batches(work)
     if then:
-        put_chunks(both_s, both_ref, BOTH, BOTH)
+        put_chunks(both_s, both_ref, range(HIDDEN))
     else:
         pltpu.make_async_copy(new_s, out_ref, out_sem).wait()
 
@@ -379,18 +329,16 @@
 def finish(which, place, valid, out_gain, gate, product, out_weight, *then):
     shape = (ROWS, COLUMNS, WIDTH)
     out = jax.ShapeDtypeStruct(shape, jnp.bfloat16)
-    both = [pltpu.VMEM(((HIDDEN + 1) * BOTH, LANES), jnp.float32)]
     last = [pltpu.VMEM(shape, jnp.bfloat16), pltpu.SemaphoreType.DMA]
     return call(
         functools.partial(finish_kernel, which),
-        [out, NORMED, BOTH_CHUNKS] if then else [out],
+        [out, BOTH_CHUNKS] if then else [out],
         [SMEM] * 3 + [VMEM] * (3 + len(then)),
-        [SCRATCH] + (both if then else last),
+        [SCRATCH] + ([BOTH_SCRATCH] if then else last),
         outs=None if then else [ANY],
     )(place, valid, out_gain, gate, product, out_weight, *then)
 
 
-ALONE = (0, 3, 0)
 LEFT = (0, 6, 0)
 RIGHT = (3, 6, COLUMNS)
 
@@ -459,11 +407,10 @@
 
 
 def outgoing_kernel(core_ref, left_ref, *rest):
-    rights, (out_ref, left_s, total) = rest[:X], rest[X:]
-    assemble_kernel(ALONE, left_ref, left_s)
+    rights, (_, out_ref, total) = rest[:X], rest[X:]
     for n, right_ref in enumerate(rights):
         total[:, n * ZH * ROWS : (n + 1) * ZH * ROWS] = lax.dot_general(
-            left_s[...],
+            left_ref[...],
             right_ref[...],
             (((1,), (1,)), ((), ())),
             preferred_element_type=jnp.float32,
@@ -479,15 +426,11 @@
                     out_ref[slot, span + zh * 2] = chunk_of(total, zh, start)
 
 
-def outgoing(core, left, rights):
+def outgoing(core, left, rights, gate):
     out = jax.ShapeDtypeStruct((2,) + CHUNKS.shape, jnp.bfloat16)
-    scratch = [
-        pltpu.VMEM((ZH * ROWS, SPAN * COLUMNS), jnp.bfloat16),
-        pltpu.VMEM((ZH * ROWS, X * ZH * ROWS), jnp.float32),
-    ]
-    return call(outgoing_kernel, out, [SMEM] + [VMEM] * (1 + X), scratch, 6 * 10**8)(
-        core, left, *rights
-    )
+    scratch = [pltpu.VMEM((ZH * ROWS, X * ZH * ROWS), jnp.float32)]
+    specs = [SMEM] + [VMEM] * (1 + X) + [ANY]
+    return call(outgoing_kernel, out, specs, scratch, 6 * 10**8)(core, left, *rights, gate)
 
 
 def incoming_kernel(core_ref, own_ref, other_ref, *rest):
@@ -550,21 +493,21 @@
     core = jnp.stack([core_index, lax.axis_index("x")]).astype(jnp.int32)
 
     vectors = jnp.concatenate([norm_gain, norm_bias, chain_bias], axis=0)
-    right = project_right(place, residue_valid, pair_acts, norm_gain, norm_bias, projection)
-    rights = gather_x(assemble(exchange(right, PLANE), ALONE))
-    left, gate = left_and_gates(
-        place, residue_valid, chain_index, projection, gate_weight, vectors, pair_acts
-    )
-    halves = outgoing(core, exchange(left, PLANE), rights)
+    both = project(place, residue_valid, pair_acts, norm_gain, norm_bias, projection)
+    both = exchange(both, PLANE)
+    rights = gather_x(assemble(both, RIGHT))
+    left = assemble(both, LEFT)
+    gate = gates(0, place, chain_index, gate_weight, vectors, pair_acts, left)
+    halves = outgoing(core, left, rights, gate)
     total = halves[0].astype(jnp.float32) + swap_cores(halves[1]).astype(jnp.float32)
     product = exchange(total.astype(jnp.bfloat16), PLANE)
-    middle, normed, both = finish(
+    middle, both = finish(
         0, place, residue_valid, out_gain, gate, product, out_weight, vectors, projection
     )
     both = exchange(both, PLANE)
     rights = gather_x(assemble(both, RIGHT))
-    gate = gates(1, place, chain_index, normed, gate_weight, vectors, middle)
     left = assemble_turned(both, LEFT).reshape(X, ZH * COLUMNS, ZH * ROWS)
+    gate = gates(1, place, chain_index, gate_weight, vectors, middle, left)
     left = exchange(left, "x")
     product = exchange(incoming(core, left, swap_cores(left), rights, gate), PLANE)
     return finish(1, place, residue_valid, out_gain, gate, product, out_weight)[0]

time: 207 us -> 203 us (0.981)
  blocking collectives: 90.8 us -> 131 us
  starting transfers between devices: 51.5 us -> 29.4 us
  waiting for transfers between devices: 29.9 us -> 17.4 us
  local copies, waits for them, and re-layouts: 8.05 us -> 0.09 us
    all_to_all x3 -> x4, blocking collectives: 90.8 us -> 131 us  [exchange(): return lax.all_to_all(values, axes, split_axis=0, concat_axis=0, tiled=True)]
    all_to_all x3 -> x1, starting transfers between devices: 26.9 us -> 4.76 us  [exchange(): return lax.all_to_all(values, axes, split_axis=0, concat_axis=0, tiled=True)]
    all_to_all x3 -> x1, waiting for transfers between devices: 16.2 us -> 0.01 us  [exchange(): return lax.all_to_all(values, axes, split_axis=0, concat_axis=0, tiled=True)]
    unnamed x34 -> x22, local copies, waits for them, and re-layouts: 8.02 us -> 0.05 us
    ppermute x6, waiting for transfers between devices: 11.8 us -> 15.5 us  [shift(): return lax.ppermute(block, 'x', [(x, (x - ahead) % X) for x in range(X)])]
  transfers between devices with their start and end apart: 11 -> 9, of which waited for: 6 -> 5; matrix products, arithmetic and copies ran while one was open for 0% -> 0% of each run, Pallas kernels for 3% -> 2%
where the time goes in v9:
time: 203 us; the launch traced here: 201 us
  blocking collectives  131 us (65%)
  starting transfers between devices  29.4 us (14%)
  Pallas kernels  21.9 us (11%)
  waiting for transfers between devices  17.4 us (9%)
    all_to_all x4, blocking collectives, exchange(): return lax.all_to_all(values, axes, split_axis=0, concat_axis=0, tiled=True)  131 us
    ppermute x6, starting transfers between devices, shift(): return lax.ppermute(block, 'x', [(x, (x - ahead) % X) for x in range(X)])  20.8 us
    ppermute x6, waiting for transfers between devices, shift(): return lax.ppermute(block, 'x', [(x, (x - ahead) % X) for x in range(X)])  15.5 us
    pallas_call x2, Pallas kernels, finish(): call(functools.partial(finish_kernel, which), [out, BOTH_CHUNKS] if then...  6.09 us
    pallas_call x1, Pallas kernels, project(): call(project_kernel, BOTH_CHUNKS, [SMEM, SMEM] + [ANY] * 4, [BOTH_SCRATCH...  5.51 us
    all_to_all x1, starting transfers between devices, exchange(): return lax.all_to_all(values, axes, split_axis=0, concat_axis=0, tiled=True)  4.76 us
  transfers between devices with their start and end apart: 9, of which 5 were waited for; matrix products, arithmetic and copies ran while one was open for 0% of the time, Pallas kernels for 2%

profile of v9, /device:TPU:6, one launch (start us, length us, event | category | flops | bytes accessed | tf_op | source)
XLA Modules:
  0.0 201.1 jit_solution(5839307689830822357)
XLA Ops:
  0.7 5.5 %shard_map.100 = bf16[64,8,896]{2,1,0:T(8,128)(2,1)} custom-call(s32[2]{0:T(128)} %pad_add_fusion.place_ref, s32[1280]{0:T(1024)} %valid_ref.5, bf16[80,40,128]{2,1,0:T(8,128)(2,1)} %pair_ref.1, f32[2,128]{1,0:T(2,128)} %gain_any.1, f32[2,128]{1,0:T(2,128)} %bias_any.1, bf16[2,128,256]{2,1,0:T(8,128)(2,1)} %rest_1_.1), custom_call_target="tpu_custom_call" | custom-call | flops 100000000 | bytes 4000000 | tf_op jit(solution)/shard_map/pallas_call | solution.py:215
  6.2 43.5 %all_to_all.25.chunks_ref = bf16[64,8,896]{2,1,0:T(8,128)(2,1)S(1)} all-to-all(bf16[64,8,896]{2,1,0:T(8,128)(2,1)} %shard_map.100), channel_id=1, replica_groups=mesh['zl'=2,'y'=8,'core'=2,'x'=4,'zh'=4] {'y','zh','zl'}, dimensions={0} | all-to-all | bytes 1835008 | tf_op jit(solution)/shard_map/all_to_all | solution.py:470
  50.1 3.3 %collective-permute-start = (bf16[320,640]{1,0:T(8,128)(2,1)S(1)}, bf16[320,640]{1,0:T(8,128)(2,1)S(1)}, u32[]{:S(2)}, u32[]{:S(2)}) collective-permute-start(bf16[320,640]{1,0:T(8,128)(2,1)S(1)} %shard_map.103.rest_0_), channel_id=1, source_target_pairs={{0,8},{4,12},{8,0},{12,4},{1,9},{5,13},{9,1},{13,5},{2,10},{6,14},... | collective-permute-start | bytes 1228808 | tf_op jit(solution)/shard_map/ppermute | solution.py:464
  53.4 1.9 collective-permute-start.1
  55.3 5.1 %collective-permute-start.2 = (bf16[320,640]{1,0:T(8,128)(2,1)S(1)}, bf16[320,640]{1,0:T(8,128)(2,1)S(1)}, u32[]{:S(2)}, u32[]{:S(2)}) collective-permute-start(bf16[320,640]{1,0:T(8,128)(2,1)S(1)} %shard_map.103.rest_0_), channel_id=1, source_target_pairs={{0,4},{4,8},{8,12},{12,0},{1,5},{5,9},{9,13},{13,1},{2,6},{6,10},{... | collective-permute-start | bytes 1228808 | tf_op jit(solution)/shard_map/ppermute | solution.py:464
  62.9 3.1 %collective-permute-done.rest_1_ = bf16[320,640]{1,0:T(8,128)(2,1)S(1)} collective-permute-done((bf16[320,640]{1,0:T(8,128)(2,1)S(1)}, bf16[320,640]{1,0:T(8,128)(2,1)S(1)}, u32[]{:S(2)}, u32[]{:S(2)}) %collective-permute-start) | collective-permute-done | bytes 409632 | tf_op jit(solution)/shard_map/ppermute | solution.py:464
  65.9 4.5 %collective-permute-done.1.rest_2_ = bf16[320,640]{1,0:T(8,128)(2,1)S(1)} collective-permute-done((bf16[320,640]{1,0:T(8,128)(2,1)S(1)}, bf16[320,640]{1,0:T(8,128)(2,1)S(1)}, u32[]{:S(2)}, u32[]{:S(2)}) %collective-permute-start.1) | collective-permute-done | bytes 409632 | tf_op jit(solution)/shard_map/ppermute | solution.py:464
  70.4 2.1 %shard_map.104 = bf16[2,64,8,512]{3,2,1,0:T(8,128)(2,1)S(1)} custom-call(s32[2]{0:T(128)S(1)} %pad_add_fusion.1.core_ref, bf16[320,640]{1,0:T(8,128)(2,1)S(1)} %shard_map.101._.left_ref, bf16[320,640]{1,0:T(8,128)(2,1)S(1)} %shard_map.103.rest_0_, bf16[320,640]{1,0:T(8,128)(2,1)S(1)} %collective-permute-done.rest_1_, ...), custom_call_target="tpu_custom_call" | custom-call | flops 600000000 | bytes 4000000 | tf_op jit(solution)/shard_map/pallas_call | solution.py:433
  72.6 1.9 collective-permute-start.3
  74.5 1.9 collective-permute-done.3
  76.5 28.1 %all_to_all.26.product_ref = bf16[64,8,512]{2,1,0:T(8,128)(2,1)S(1)} all-to-all(bf16[64,8,512]{2,1,0:T(8,128)(2,1)S(1)} %fusion), channel_id=1, replica_groups=mesh['zl'=2,'y'=8,'core'=2,'x'=4,'zh'=4] {'y','zh','zl'}, dimensions={0} | all-to-all | bytes 1048576 | tf_op jit(solution)/shard_map/all_to_all | solution.py:470
  104.7 3.8 %shard_map.105 = (bf16[80,40,128]{2,1,0:T(8,128)(2,1)S(1)}, bf16[64,8,896]{2,1,0:T(8,128)(2,1)S(1)}) custom-call(s32[2]{0:T(128)S(1)} %copy-done.6, s32[1280]{0:T(1024)S(1)} %copy-done.4, f32[2,64]{1,0:T(2,128)S(1)} %copy-done.7, f32[2,32,128,128]{3,2,1,0:T(8,128)S(1)} %shard_map.102.rest_4_.gates_ref, bf16[64,8,512]{2,1,0:T(8,128)(2,1)S(1)} %all_to_all.26.product_ref, ...), custom_call_target="tpu_custom_call" | custom-call | flops 100000000 | bytes 4000000 | tf_op jit(solution)/shard_map/pallas_call | solution.py:333
  108.5 32.1 %all_to_all.27.chunks_ref = bf16[64,8,896]{2,1,0:T(8,128)(2,1)S(1)} all-to-all(bf16[64,8,896]{2,1,0:T(8,128)(2,1)S(1)} %get-tuple-element.8), channel_id=1, replica_groups=mesh['zl'=2,'y'=8,'core'=2,'x'=4,'zh'=4] {'y','zh','zl'}, dimensions={0} | all-to-all | bytes 1835008 | tf_op jit(solution)/shard_map/all_to_all | solution.py:470
  142.0 4.8 %all-to-all-start.3 = ((bf16[4,160,320]{2,1,0:T(8,128)(2,1)}), bf16[4,160,320]{2,1,0:T(8,128)(2,1)S(1)}, u32[]{:S(2)}, u32[]{:S(2)}) async-start(bf16[4,160,320]{2,1,0:T(8,128)(2,1)} %bitcast.6._), calls=%async_computation.3 | async-start | bytes 983040 | tf_op jit(solution)/shard_map/all_to_all | solution.py:470
  147.1 3.4 %collective-permute-start.5 = (bf16[320,640]{1,0:T(8,128)(2,1)S(1)}, bf16[320,640]{1,0:T(8,128)(2,1)S(1)}, u32[]{:S(2)}, u32[]{:S(2)}) collective-permute-start(bf16[320,640]{1,0:T(8,128)(2,1)S(1)} %shard_map.108.rest_0_), channel_id=1, source_target_pairs={{0,8},{4,12},{8,0},{12,4},{1,9},{5,13},{9,1},{13,5},{2,10},{6,14},... | collective-permute-start | bytes 1228808 | tf_op jit(solution)/shard_map/ppermute | solution.py:464
  150.5 1.9 collective-permute-start.6
  152.4 5.1 %collective-permute-start.7 = (bf16[320,640]{1,0:T(8,128)(2,1)S(1)}, bf16[320,640]{1,0:T(8,128)(2,1)S(1)}, u32[]{:S(2)}, u32[]{:S(2)}) collective-permute-start(bf16[320,640]{1,0:T(8,128)(2,1)S(1)} %shard_map.108.rest_0_), channel_id=1, source_target_pairs={{0,4},{4,8},{8,12},{12,0},{1,5},{5,9},{9,13},{13,1},{2,6},{6,10},{... | collective-permute-start | bytes 1228808 | tf_op jit(solution)/shard_map/ppermute | solution.py:464
  157.6 1.9 collective-permute-start.4
  159.5 1.8 shard_map.107.rest_4_.gates_ref
  161.3 2.6 %collective-permute-done.5.rest_1_ = bf16[320,640]{1,0:T(8,128)(2,1)S(1)} collective-permute-done((bf16[320,640]{1,0:T(8,128)(2,1)S(1)}, bf16[320,640]{1,0:T(8,128)(2,1)S(1)}, u32[]{:S(2)}, u32[]{:S(2)}) %collective-permute-start.5) | collective-permute-done | bytes 409632 | tf_op jit(solution)/shard_map/ppermute | solution.py:464
  163.9 5.3 %collective-permute-done.6.rest_2_ = bf16[320,640]{1,0:T(8,128)(2,1)S(1)} collective-permute-done((bf16[320,640]{1,0:T(8,128)(2,1)S(1)}, bf16[320,640]{1,0:T(8,128)(2,1)S(1)}, u32[]{:S(2)}, u32[]{:S(2)}) %collective-permute-start.6) | collective-permute-done | bytes 409632 | tf_op jit(solution)/shard_map/ppermute | solution.py:464
  169.2 2.1 %shard_map.109 = bf16[64,8,512]{2,1,0:T(8,128)(2,1)S(1)} custom-call(s32[2]{0:T(128)S(1)} %pad_add_fusion.1.core_ref, bf16[4,160,320]{2,1,0:T(8,128)(2,1)S(1)} %all-to-all-done.3.own_ref, bf16[4,160,320]{2,1,0:T(8,128)(2,1)S(1)} %collective-permute-done.4.other_ref, bf16[320,640]{1,0:T(8,128)(2,1)S(1)} %shard_map.108.rest_0_, ...), custom_call_target="tpu_custom_call" | custom-call | flops 600000000 | bytes 4000000 | tf_op jit(solution)/shard_map/pallas_call | solution.py:457
  171.4 27.3 %all_to_all.28.product_ref = bf16[64,8,512]{2,1,0:T(8,128)(2,1)S(1)} all-to-all(bf16[64,8,512]{2,1,0:T(8,128)(2,1)S(1)} %shard_map.109), channel_id=1, replica_groups=mesh['zl'=2,'y'=8,'core'=2,'x'=4,'zh'=4] {'y','zh','zl'}, dimensions={0} | all-to-all | bytes 1048576 | tf_op jit(solution)/shard_map/all_to_all | solution.py:470
  198.7 2.3 %shard_map.110 = bf16[80,40,128]{2,1,0:T(8,128)(2,1)} custom-call(s32[2]{0:T(128)S(1)} %copy-done.6, s32[1280]{0:T(1024)S(1)} %copy-done.4, f32[2,64]{1,0:T(2,128)S(1)} %copy-done.7, f32[2,32,128,128]{3,2,1,0:T(8,128)S(1)} %shard_map.107.rest_4_.gates_ref, bf16[64,8,512]{2,1,0:T(8,128)(2,1)S(1)} %all_to_all.28.product_ref, bf16[2,64,128]{2,1,0:T(8,128)(2,1)S(1)} %copy-done.3), custom_call_target="tpu_custom_call" | custom-call | flops 100000000 | bytes 4000000 | tf_op jit(solution)/shard_map/pallas_call | solution.py:333
  (36 shorter events, 5.3 us)
Async XLA Ops:
  0.0 61.0 %copy-start = (bf16[80,40,128]{2,1,0:T(8,128)(2,1)S(1)}, bf16[80,40,128]{2,1,0:T(8,128)(2,1)}, u32[]{:S(2)}) copy-start(bf16[80,40,128]{2,1,0:T(8,128)(2,1)} %pair_ref.1) | copy-start | bytes 2457604
  0.0 60.6 %copy-start.9 = (f32[2,128]{1,0:T(2,128)S(1)}, f32[2,128]{1,0:T(2,128)}, u32[]{:S(2)}) copy-start(f32[2,128]{1,0:T(2,128)} %gain_any.1) | copy-start | bytes 3076
  0.0 60.6 %copy-start.8 = (f32[2,128]{1,0:T(2,128)S(1)}, f32[2,128]{1,0:T(2,128)}, u32[]{:S(2)}) copy-start(f32[2,128]{1,0:T(2,128)} %bias_any.1) | copy-start | bytes 3076
  0.0 60.6 %copy-start.10 = (f32[2,128]{1,0:T(2,128)S(1)}, f32[2,128]{1,0:T(2,128)}, u32[]{:S(2)}) copy-start(f32[2,128]{1,0:T(2,128)} %param.17) | copy-start | bytes 3076
  0.0 61.0 %copy-start.5 = (s32[1280]{0:T(1024)S(1)}, s32[1280]{0:T(1024)}, u32[]{:S(2)}) copy-start(s32[1280]{0:T(1024)} %chain_ref.3) | copy-start | bytes 15364
  0.0 61.0 %copy-start.2 = (bf16[2,128,128]{2,1,0:T(8,128)(2,1)S(1)}, bf16[2,128,128]{2,1,0:T(8,128)(2,1)}, u32[]{:S(2)}) copy-start(bf16[2,128,128]{2,1,0:T(8,128)(2,1)} %gate_ref.3) | copy-start | bytes 196612
  0.7 60.3 %copy-start.6 = (s32[2]{0:T(128)S(1)}, s32[2]{0:T(128)}, u32[]{:S(2)}) copy-start(s32[2]{0:T(128)} %pad_add_fusion.place_ref) | copy-start | bytes 28
  50.1 15.8 %collective-permute-start = (bf16[320,640]{1,0:T(8,128)(2,1)S(1)}, bf16[320,640]{1,0:T(8,128)(2,1)S(1)}, u32[]{:S(2)}, u32[]{:S(2)}) collective-permute-start(bf16[320,640]{1,0:T(8,128)(2,1)S(1)} %shard_map.103.rest_0_), channel_id=1, source_target_pairs={{0,8},{4,12},{8,0},{12,4},{1,9},{5,13},{9,1},{13,5},{2,10},{6,14},... | collective-permute-start | bytes 1228808 | tf_op jit(solution)/shard_map/ppermute | solution.py:464
  53.4 17.0 %collective-permute-start.1 = (bf16[320,640]{1,0:T(8,128)(2,1)S(1)}, bf16[320,640]{1,0:T(8,128)(2,1)S(1)}, u32[]{:S(2)}, u32[]{:S(2)}) collective-permute-start(bf16[320,640]{1,0:T(8,128)(2,1)S(1)} %shard_map.103.rest_0_), channel_id=1, source_target_pairs={{0,12},{4,0},{8,4},{12,8},{1,13},{5,1},{9,5},{13,9},{2,14},{6,2},{... | collective-permute-start | bytes 1228808 | tf_op jit(solution)/shard_map/ppermute | solution.py:464
  55.3 15.1 %collective-permute-start.2 = (bf16[320,640]{1,0:T(8,128)(2,1)S(1)}, bf16[320,640]{1,0:T(8,128)(2,1)S(1)}, u32[]{:S(2)}, u32[]{:S(2)}) collective-permute-start(bf16[320,640]{1,0:T(8,128)(2,1)S(1)} %shard_map.103.rest_0_), channel_id=1, source_target_pairs={{0,4},{4,8},{8,12},{12,0},{1,5},{5,9},{9,13},{13,1},{2,6},{6,10},{... | collective-permute-start | bytes 1228808 | tf_op jit(solution)/shard_map/ppermute | solution.py:464
  62.8 41.9 %copy-start.1 = (bf16[2,128,256]{2,1,0:T(8,128)(2,1)S(1)}, bf16[2,128,256]{2,1,0:T(8,128)(2,1)}, u32[]{:S(2)}) copy-start(bf16[2,128,256]{2,1,0:T(8,128)(2,1)} %rest_1_.1) | copy-start | bytes 393220
  62.8 41.8 %copy-start.3 = (bf16[2,64,128]{2,1,0:T(8,128)(2,1)S(1)}, bf16[2,64,128]{2,1,0:T(8,128)(2,1)}, u32[]{:S(2)}) copy-start(bf16[2,64,128]{2,1,0:T(8,128)(2,1)} %out_weight_ref.3) | copy-start | bytes 98308
  62.8 41.8 %copy-start.4 = (s32[1280]{0:T(1024)S(1)}, s32[1280]{0:T(1024)}, u32[]{:S(2)}) copy-start(s32[1280]{0:T(1024)} %valid_ref.5) | copy-start | bytes 15364
  62.8 41.8 %copy-start.7 = (f32[2,64]{1,0:T(2,128)S(1)}, f32[2,64]{1,0:T(2,128)}, u32[]{:S(2)}) copy-start(f32[2,64]{1,0:T(2,128)} %out_gain_ref.3) | copy-start | bytes 1540
  72.6 3.8 %collective-permute-start.3 = (bf16[64,8,512]{2,1,0:T(8,128)(2,1)S(1)}, bf16[64,8,512]{2,1,0:T(8,128)(2,1)S(1)}, u32[]{:S(2)}, u32[]{:S(2)}) collective-permute-start(bf16[64,8,512]{2,1,0:T(8,128)(2,1)S(1)} %slice_bitcast_fusion), channel_id=1, source_target_pairs={{0,16},{16,0},{1,17},{17,1},{2,18},{18,2},{3,19},{19,3},{4,20},{20... | collective-permute-start | bytes 1572872 | tf_op jit(solution)/shard_map/ppermute | solution.py:474
  142.0 15.6 %all-to-all-start.3 = ((bf16[4,160,320]{2,1,0:T(8,128)(2,1)}), bf16[4,160,320]{2,1,0:T(8,128)(2,1)S(1)}, u32[]{:S(2)}, u32[]{:S(2)}) async-start(bf16[4,160,320]{2,1,0:T(8,128)(2,1)} %bitcast.6._), calls=%async_computation.3 | async-start | bytes 983040 | tf_op jit(solution)/shard_map/all_to_all | solution.py:470
  147.1 16.8 %collective-permute-start.5 = (bf16[320,640]{1,0:T(8,128)(2,1)S(1)}, bf16[320,640]{1,0:T(8,128)(2,1)S(1)}, u32[]{:S(2)}, u32[]{:S(2)}) collective-permute-start(bf16[320,640]{1,0:T(8,128)(2,1)S(1)} %shard_map.108.rest_0_), channel_id=1, source_target_pairs={{0,8},{4,12},{8,0},{12,4},{1,9},{5,13},{9,1},{13,5},{2,10},{6,14},... | collective-permute-start | bytes 1228808 | tf_op jit(solution)/shard_map/ppermute | solution.py:464
  150.5 18.7 %collective-permute-start.6 = (bf16[320,640]{1,0:T(8,128)(2,1)S(1)}, bf16[320,640]{1,0:T(8,128)(2,1)S(1)}, u32[]{:S(2)}, u32[]{:S(2)}) collective-permute-start(bf16[320,640]{1,0:T(8,128)(2,1)S(1)} %shard_map.108.rest_0_), channel_id=1, source_target_pairs={{0,12},{4,0},{8,4},{12,8},{1,13},{5,1},{9,5},{13,9},{2,14},{6,2},{... | collective-permute-start | bytes 1228808 | tf_op jit(solution)/shard_map/ppermute | solution.py:464
  152.4 16.8 %collective-permute-start.7 = (bf16[320,640]{1,0:T(8,128)(2,1)S(1)}, bf16[320,640]{1,0:T(8,128)(2,1)S(1)}, u32[]{:S(2)}, u32[]{:S(2)}) collective-permute-start(bf16[320,640]{1,0:T(8,128)(2,1)S(1)} %shard_map.108.rest_0_), channel_id=1, source_target_pairs={{0,4},{4,8},{8,12},{12,0},{1,5},{5,9},{9,13},{13,1},{2,6},{6,10},{... | collective-permute-start | bytes 1228808 | tf_op jit(solution)/shard_map/ppermute | solution.py:464
  157.6 11.7 %collective-permute-start.4 = (bf16[4,160,320]{2,1,0:T(8,128)(2,1)S(1)}, bf16[4,160,320]{2,1,0:T(8,128)(2,1)S(1)}, u32[]{:S(2)}, u32[]{:S(2)}) collective-permute-start(bf16[4,160,320]{2,1,0:T(8,128)(2,1)S(1)} %all-to-all-done.3.own_ref), channel_id=1, source_target_pairs={{0,16},{16,0},{1,17},{17,1},{2,18},{18,2},{3,19},{19,3},{4,20},{20... | collective-permute-start | bytes 1228808 | tf_op jit(solution)/shard_map/ppermute | solution.py:474

commit v10 on v9

--- a/solution.py
+++ b/solution.py
@@ -159,9 +159,14 @@
 BOTH_SCRATCH = pltpu.VMEM(((HIDDEN + 1) * BOTH, LANES), jnp.float32)
 
 
+def place_of():
+    row = (lax.axis_index("x") * ZH + lax.axis_index("zh")) * ROWS
+    block = (lax.axis_index("zl") * 8 + lax.axis_index("y")) * 2 + lax.axis_index("core")
+    return row, block * COLUMNS
+
+
 def project_kernel(
-    place_ref,
-    valid_ref,
+    valid_any,
     pair_any,
     gain_any,
     bias_any,
@@ -169,6 +174,7 @@
     both_any,
     both_s,
     both_ref,
+    valid_ref,
     pair_ref,
     gain_ref,
     bias_ref,
@@ -176,7 +182,9 @@
     sems,
     out_sem,
 ):
-    moves = [(gain_any, gain_ref), (bias_any, bias_ref), (weight_any, weight_ref)]
+    place = place_of()
+    moves = [(valid_any, valid_ref), (gain_any, gain_ref), (bias_any, bias_ref)]
+    moves.append((weight_any, weight_ref))
     parts = []
     for first in range(0, DEPTH, BATCH):
         for row in block_rows(first, 3 if first < WHOLE * BATCH else 1)[0]:
@@ -186,13 +194,13 @@
     copies = [pltpu.make_async_copy(a, b, sems.at[n]) for n, (a, b) in enumerate(moves)]
     for copy in copies:
         copy.start()
-    columns = spread_columns(place_ref, valid_ref)
     for copy in copies[: parts[0]]:
         copy.wait()
+    columns = spread_columns(place, valid_ref)
     weights = [weight_of(weight_ref, 0, start) for start in (0, 2 * HIDDEN)]
 
     def mask_at(first, count, shift):
-        return mask_of(first, count, place_ref, valid_ref, columns, shift)
+        return mask_of(first, count, place, valid_ref, columns, shift)
 
     def work(first, count):
         for part in parts[first // BATCH * 3 :][:count]:
@@ -209,17 +217,18 @@
     pltpu.make_async_copy(both_ref, both_any, out_sem).wait()
 
 
-def project(place, valid, *operands):
+def project(valid, *operands):
     scratch = [pltpu.VMEM(each.shape, each.dtype) for each in (BOTH_CHUNKS,) + operands]
-    sems = [pltpu.SemaphoreType.DMA((13,)), pltpu.SemaphoreType.DMA]
+    scratch.insert(1, pltpu.SMEM(valid.shape, valid.dtype))
+    sems = [pltpu.SemaphoreType.DMA((14,)), pltpu.SemaphoreType.DMA]
     return call(
         project_kernel,
         BOTH_CHUNKS,
-        [SMEM, SMEM] + [ANY] * 4,
+        [ANY] * 5,
         [BOTH_SCRATCH] + scratch + sems,
         outs=ANY,
         grant=60,
-    )(place, valid, *operands)
+    )(valid, *operands)
 
 
 def gate_kernel(which, place_ref, chain_ref, gate_ref, vectors_ref, pair_ref, _, out_ref):
@@ -486,14 +495,11 @@
     out_gain,
     out_weight,
 ):
-    row_start = (lax.axis_index("x") * ZH + lax.axis_index("zh")) * ROWS
-    core_index = lax.axis_index("core")
-    column_block = (lax.axis_index("zl") * 8 + lax.axis_index("y")) * 2 + core_index
-    place = jnp.stack([row_start, column_block * COLUMNS]).astype(jnp.int32)
-    core = jnp.stack([core_index, lax.axis_index("x")]).astype(jnp.int32)
+    place = jnp.stack(place_of()).astype(jnp.int32)
+    core = jnp.stack([lax.axis_index("core"), lax.axis_index("x")]).astype(jnp.int32)
 
     vectors = jnp.concatenate([norm_gain, norm_bias, chain_bias], axis=0)
-    both = project(place, residue_valid, pair_acts, norm_gain, norm_bias, projection)
+    both = project(residue_valid, pair_acts, norm_gain, norm_bias, projection)
     both = exchange(both, PLANE)
     rights = gather_x(assemble(both, RIGHT))
     left = assemble(both, LEFT)

time: 203 us -> 202 us (level)
  no operation moved by 1% of the time
where the time goes in v10:
time: 202 us; the launch traced here: 200 us
  blocking collectives  131 us (65%)
  starting transfers between devices  29.4 us (15%)
  Pallas kernels  21.3 us (11%)
  waiting for transfers between devices  17.4 us (9%)
    all_to_all x4, blocking collectives, exchange(): return lax.all_to_all(values, axes, split_axis=0, concat_axis=0, tiled=True)  131 us
    ppermute x6, starting transfers between devices, shift(): return lax.ppermute(block, 'x', [(x, (x - ahead) % X) for x in range(X)])  20.8 us
    ppermute x6, waiting for transfers between devices, shift(): return lax.ppermute(block, 'x', [(x, (x - ahead) % X) for x in range(X)])  15.5 us
    pallas_call x2, Pallas kernels, finish(): call(functools.partial(finish_kernel, which), [out, BOTH_CHUNKS] if then...  6.14 us
    all_to_all x1, starting transfers between devices, exchange(): return lax.all_to_all(values, axes, split_axis=0, concat_axis=0, tiled=True)  4.78 us
    pallas_call x1, Pallas kernels, project(): call(project_kernel, BOTH_CHUNKS, [ANY] * 5, [BOTH_SCRATCH] + scratch + s...  4.73 us
  transfers between devices with their start and end apart: 9, of which 5 were waited for; matrix products, arithmetic and copies ran while one was open for 0% of the time, Pallas kernels for 2%

profile of v10, /device:TPU:6, one launch (start us, length us, event | category | flops | bytes accessed | tf_op | source)
XLA Modules:
  0.0 199.8 jit_solution(14462612226689528635)
XLA Ops:
  0.0 4.7 %shard_map.100 = bf16[64,8,896]{2,1,0:T(8,128)(2,1)} custom-call(s32[1280]{0:T(1024)} %valid_ref.3, bf16[80,40,128]{2,1,0:T(8,128)(2,1)} %pair_ref.1, f32[2,128]{1,0:T(2,128)} %gain_any.1, f32[2,128]{1,0:T(2,128)} %bias_any.1, bf16[2,128,256]{2,1,0:T(8,128)(2,1)} %rest_1_.1), custom_call_target="tpu_custom_call" | custom-call | flops 100000000 | bytes 4000000 | tf_op jit(solution)/shard_map/pallas_call | solution.py:224
  4.8 43.5 %all_to_all.25.chunks_ref = bf16[64,8,896]{2,1,0:T(8,128)(2,1)S(1)} all-to-all(bf16[64,8,896]{2,1,0:T(8,128)(2,1)} %shard_map.100), channel_id=1, replica_groups=mesh['zl'=2,'y'=8,'core'=2,'x'=4,'zh'=4] {'y','zh','zl'}, dimensions={0} | all-to-all | bytes 1835008 | tf_op jit(solution)/shard_map/all_to_all | solution.py:479
  48.6 3.3 %collective-permute-start = (bf16[320,640]{1,0:T(8,128)(2,1)S(1)}, bf16[320,640]{1,0:T(8,128)(2,1)S(1)}, u32[]{:S(2)}, u32[]{:S(2)}) collective-permute-start(bf16[320,640]{1,0:T(8,128)(2,1)S(1)} %shard_map.103.rest_0_), channel_id=1, source_target_pairs={{0,8},{4,12},{8,0},{12,4},{1,9},{5,13},{9,1},{13,5},{2,10},{6,14},... | collective-permute-start | bytes 1228808 | tf_op jit(solution)/shard_map/ppermute | solution.py:473
  52.0 1.9 collective-permute-start.1
  53.9 5.1 %collective-permute-start.2 = (bf16[320,640]{1,0:T(8,128)(2,1)S(1)}, bf16[320,640]{1,0:T(8,128)(2,1)S(1)}, u32[]{:S(2)}, u32[]{:S(2)}) collective-permute-start(bf16[320,640]{1,0:T(8,128)(2,1)S(1)} %shard_map.103.rest_0_), channel_id=1, source_target_pairs={{0,4},{4,8},{8,12},{12,0},{1,5},{5,9},{9,13},{13,1},{2,6},{6,10},{... | collective-permute-start | bytes 1228808 | tf_op jit(solution)/shard_map/ppermute | solution.py:473
  59.6 1.8 shard_map.102.rest_4_.gates_ref
  61.5 3.0 %collective-permute-done.rest_1_ = bf16[320,640]{1,0:T(8,128)(2,1)S(1)} collective-permute-done((bf16[320,640]{1,0:T(8,128)(2,1)S(1)}, bf16[320,640]{1,0:T(8,128)(2,1)S(1)}, u32[]{:S(2)}, u32[]{:S(2)}) %collective-permute-start) | collective-permute-done | bytes 409632 | tf_op jit(solution)/shard_map/ppermute | solution.py:473
  64.5 4.5 %collective-permute-done.1.rest_2_ = bf16[320,640]{1,0:T(8,128)(2,1)S(1)} collective-permute-done((bf16[320,640]{1,0:T(8,128)(2,1)S(1)}, bf16[320,640]{1,0:T(8,128)(2,1)S(1)}, u32[]{:S(2)}, u32[]{:S(2)}) %collective-permute-start.1) | collective-permute-done | bytes 409632 | tf_op jit(solution)/shard_map/ppermute | solution.py:473
  69.0 2.1 %shard_map.104 = bf16[2,64,8,512]{3,2,1,0:T(8,128)(2,1)S(1)} custom-call(s32[2]{0:T(128)S(1)} %pad_add_fusion.1.core_ref, bf16[320,640]{1,0:T(8,128)(2,1)S(1)} %shard_map.101._.left_ref, bf16[320,640]{1,0:T(8,128)(2,1)S(1)} %shard_map.103.rest_0_, bf16[320,640]{1,0:T(8,128)(2,1)S(1)} %collective-permute-done.rest_1_, ...), custom_call_target="tpu_custom_call" | custom-call | flops 600000000 | bytes 4000000 | tf_op jit(solution)/shard_map/pallas_call | solution.py:442
  71.2 1.9 collective-permute-start.3
  73.1 1.9 collective-permute-done.3
  75.1 28.1 %all_to_all.26.product_ref = bf16[64,8,512]{2,1,0:T(8,128)(2,1)S(1)} all-to-all(bf16[64,8,512]{2,1,0:T(8,128)(2,1)S(1)} %fusion), channel_id=1, replica_groups=mesh['zl'=2,'y'=8,'core'=2,'x'=4,'zh'=4] {'y','zh','zl'}, dimensions={0} | all-to-all | bytes 1048576 | tf_op jit(solution)/shard_map/all_to_all | solution.py:479
  103.3 3.8 %shard_map.105 = (bf16[80,40,128]{2,1,0:T(8,128)(2,1)S(1)}, bf16[64,8,896]{2,1,0:T(8,128)(2,1)S(1)}) custom-call(s32[2]{0:T(128)S(1)} %pad_add_fusion.place_ref, s32[1280]{0:T(1024)S(1)} %copy-done.4, f32[2,64]{1,0:T(2,128)S(1)} %copy-done.6, f32[2,32,128,128]{3,2,1,0:T(8,128)S(1)} %shard_map.102.rest_4_.gates_ref, ...), custom_call_target="tpu_custom_call" | custom-call | flops 100000000 | bytes 4000000 | tf_op jit(solution)/shard_map/pallas_call | solution.py:342
  107.1 32.1 %all_to_all.27.chunks_ref = bf16[64,8,896]{2,1,0:T(8,128)(2,1)S(1)} all-to-all(bf16[64,8,896]{2,1,0:T(8,128)(2,1)S(1)} %get-tuple-element.8), channel_id=1, replica_groups=mesh['zl'=2,'y'=8,'core'=2,'x'=4,'zh'=4] {'y','zh','zl'}, dimensions={0} | all-to-all | bytes 1835008 | tf_op jit(solution)/shard_map/all_to_all | solution.py:479
  140.6 4.8 %all-to-all-start.3 = ((bf16[4,160,320]{2,1,0:T(8,128)(2,1)}), bf16[4,160,320]{2,1,0:T(8,128)(2,1)S(1)}, u32[]{:S(2)}, u32[]{:S(2)}) async-start(bf16[4,160,320]{2,1,0:T(8,128)(2,1)} %bitcast.6._), calls=%async_computation.3 | async-start | bytes 983040 | tf_op jit(solution)/shard_map/all_to_all | solution.py:479
  145.7 3.4 %collective-permute-start.5 = (bf16[320,640]{1,0:T(8,128)(2,1)S(1)}, bf16[320,640]{1,0:T(8,128)(2,1)S(1)}, u32[]{:S(2)}, u32[]{:S(2)}) collective-permute-start(bf16[320,640]{1,0:T(8,128)(2,1)S(1)} %shard_map.108.rest_0_), channel_id=1, source_target_pairs={{0,8},{4,12},{8,0},{12,4},{1,9},{5,13},{9,1},{13,5},{2,10},{6,14},... | collective-permute-start | bytes 1228808 | tf_op jit(solution)/shard_map/ppermute | solution.py:473
  149.1 1.9 collective-permute-start.6
  151.0 5.1 %collective-permute-start.7 = (bf16[320,640]{1,0:T(8,128)(2,1)S(1)}, bf16[320,640]{1,0:T(8,128)(2,1)S(1)}, u32[]{:S(2)}, u32[]{:S(2)}) collective-permute-start(bf16[320,640]{1,0:T(8,128)(2,1)S(1)} %shard_map.108.rest_0_), channel_id=1, source_target_pairs={{0,4},{4,8},{8,12},{12,0},{1,5},{5,9},{9,13},{13,1},{2,6},{6,10},{... | collective-permute-start | bytes 1228808 | tf_op jit(solution)/shard_map/ppermute | solution.py:473
  156.2 1.9 collective-permute-start.4
  159.9 2.6 %collective-permute-done.5.rest_1_ = bf16[320,640]{1,0:T(8,128)(2,1)S(1)} collective-permute-done((bf16[320,640]{1,0:T(8,128)(2,1)S(1)}, bf16[320,640]{1,0:T(8,128)(2,1)S(1)}, u32[]{:S(2)}, u32[]{:S(2)}) %collective-permute-start.5) | collective-permute-done | bytes 409632 | tf_op jit(solution)/shard_map/ppermute | solution.py:473
  162.5 5.4 %collective-permute-done.6.rest_2_ = bf16[320,640]{1,0:T(8,128)(2,1)S(1)} collective-permute-done((bf16[320,640]{1,0:T(8,128)(2,1)S(1)}, bf16[320,640]{1,0:T(8,128)(2,1)S(1)}, u32[]{:S(2)}, u32[]{:S(2)}) %collective-permute-start.6) | collective-permute-done | bytes 409632 | tf_op jit(solution)/shard_map/ppermute | solution.py:473
  167.9 2.1 %shard_map.109 = bf16[64,8,512]{2,1,0:T(8,128)(2,1)S(1)} custom-call(s32[2]{0:T(128)S(1)} %pad_add_fusion.1.core_ref, bf16[4,160,320]{2,1,0:T(8,128)(2,1)S(1)} %all-to-all-done.3.own_ref, bf16[4,160,320]{2,1,0:T(8,128)(2,1)S(1)} %collective-permute-done.4.other_ref, bf16[320,640]{1,0:T(8,128)(2,1)S(1)} %shard_map.108.rest_0_, ...), custom_call_target="tpu_custom_call" | custom-call | flops 600000000 | bytes 4000000 | tf_op jit(solution)/shard_map/pallas_call | solution.py:466
  170.1 27.2 %all_to_all.28.product_ref = bf16[64,8,512]{2,1,0:T(8,128)(2,1)S(1)} all-to-all(bf16[64,8,512]{2,1,0:T(8,128)(2,1)S(1)} %shard_map.109), channel_id=1, replica_groups=mesh['zl'=2,'y'=8,'core'=2,'x'=4,'zh'=4] {'y','zh','zl'}, dimensions={0} | all-to-all | bytes 1048576 | tf_op jit(solution)/shard_map/all_to_all | solution.py:479
  197.3 2.3 %shard_map.110 = bf16[80,40,128]{2,1,0:T(8,128)(2,1)} custom-call(s32[2]{0:T(128)S(1)} %pad_add_fusion.place_ref, s32[1280]{0:T(1024)S(1)} %copy-done.4, f32[2,64]{1,0:T(2,128)S(1)} %copy-done.6, f32[2,32,128,128]{3,2,1,0:T(8,128)S(1)} %shard_map.107.rest_4_.gates_ref, bf16[64,8,512]{2,1,0:T(8,128)(2,1)S(1)} %all_to_all.28.product_ref, ...), custom_call_target="tpu_custom_call" | custom-call | flops 100000000 | bytes 4000000 | tf_op jit(solution)/shard_map/pallas_call | solution.py:342
  (34 shorter events, 4.7 us)
Async XLA Ops:
  0.0 59.6 %copy-start = (bf16[80,40,128]{2,1,0:T(8,128)(2,1)S(1)}, bf16[80,40,128]{2,1,0:T(8,128)(2,1)}, u32[]{:S(2)}) copy-start(bf16[80,40,128]{2,1,0:T(8,128)(2,1)} %pair_ref.1) | copy-start | bytes 2457604
  0.0 59.2 %copy-start.8 = (f32[2,128]{1,0:T(2,128)S(1)}, f32[2,128]{1,0:T(2,128)}, u32[]{:S(2)}) copy-start(f32[2,128]{1,0:T(2,128)} %gain_any.1) | copy-start | bytes 3076
  0.0 59.2 %copy-start.7 = (f32[2,128]{1,0:T(2,128)S(1)}, f32[2,128]{1,0:T(2,128)}, u32[]{:S(2)}) copy-start(f32[2,128]{1,0:T(2,128)} %bias_any.1) | copy-start | bytes 3076
  0.0 59.2 %copy-start.9 = (f32[2,128]{1,0:T(2,128)S(1)}, f32[2,128]{1,0:T(2,128)}, u32[]{:S(2)}) copy-start(f32[2,128]{1,0:T(2,128)} %param.17) | copy-start | bytes 3076
  0.0 59.6 %copy-start.5 = (s32[1280]{0:T(1024)S(1)}, s32[1280]{0:T(1024)}, u32[]{:S(2)}) copy-start(s32[1280]{0:T(1024)} %chain_ref.3) | copy-start | bytes 15364
  0.0 59.6 %copy-start.2 = (bf16[2,128,128]{2,1,0:T(8,128)(2,1)S(1)}, bf16[2,128,128]{2,1,0:T(8,128)(2,1)}, u32[]{:S(2)}) copy-start(bf16[2,128,128]{2,1,0:T(8,128)(2,1)} %gate_ref.3) | copy-start | bytes 196612
  48.6 15.8 %collective-permute-start = (bf16[320,640]{1,0:T(8,128)(2,1)S(1)}, bf16[320,640]{1,0:T(8,128)(2,1)S(1)}, u32[]{:S(2)}, u32[]{:S(2)}) collective-permute-start(bf16[320,640]{1,0:T(8,128)(2,1)S(1)} %shard_map.103.rest_0_), channel_id=1, source_target_pairs={{0,8},{4,12},{8,0},{12,4},{1,9},{5,13},{9,1},{13,5},{2,10},{6,14},... | collective-permute-start | bytes 1228808 | tf_op jit(solution)/shard_map/ppermute | solution.py:473
  52.0 17.0 %collective-permute-start.1 = (bf16[320,640]{1,0:T(8,128)(2,1)S(1)}, bf16[320,640]{1,0:T(8,128)(2,1)S(1)}, u32[]{:S(2)}, u32[]{:S(2)}) collective-permute-start(bf16[320,640]{1,0:T(8,128)(2,1)S(1)} %shard_map.103.rest_0_), channel_id=1, source_target_pairs={{0,12},{4,0},{8,4},{12,8},{1,13},{5,1},{9,5},{13,9},{2,14},{6,2},{... | collective-permute-start | bytes 1228808 | tf_op jit(solution)/shard_map/ppermute | solution.py:473
  53.9 15.1 %collective-permute-start.2 = (bf16[320,640]{1,0:T(8,128)(2,1)S(1)}, bf16[320,640]{1,0:T(8,128)(2,1)S(1)}, u32[]{:S(2)}, u32[]{:S(2)}) collective-permute-start(bf16[320,640]{1,0:T(8,128)(2,1)S(1)} %shard_map.103.rest_0_), channel_id=1, source_target_pairs={{0,4},{4,8},{8,12},{12,0},{1,5},{5,9},{9,13},{13,1},{2,6},{6,10},{... | collective-permute-start | bytes 1228808 | tf_op jit(solution)/shard_map/ppermute | solution.py:473
  61.4 41.8 %copy-start.1 = (bf16[2,128,256]{2,1,0:T(8,128)(2,1)S(1)}, bf16[2,128,256]{2,1,0:T(8,128)(2,1)}, u32[]{:S(2)}) copy-start(bf16[2,128,256]{2,1,0:T(8,128)(2,1)} %rest_1_.1) | copy-start | bytes 393220
  61.4 41.8 %copy-start.3 = (bf16[2,64,128]{2,1,0:T(8,128)(2,1)S(1)}, bf16[2,64,128]{2,1,0:T(8,128)(2,1)}, u32[]{:S(2)}) copy-start(bf16[2,64,128]{2,1,0:T(8,128)(2,1)} %out_weight_ref.3) | copy-start | bytes 98308
  61.5 41.8 %copy-start.4 = (s32[1280]{0:T(1024)S(1)}, s32[1280]{0:T(1024)}, u32[]{:S(2)}) copy-start(s32[1280]{0:T(1024)} %valid_ref.3) | copy-start | bytes 15364
  61.5 41.8 %copy-start.6 = (f32[2,64]{1,0:T(2,128)S(1)}, f32[2,64]{1,0:T(2,128)}, u32[]{:S(2)}) copy-start(f32[2,64]{1,0:T(2,128)} %out_gain_ref.3) | copy-start | bytes 1540
  71.2 3.8 %collective-permute-start.3 = (bf16[64,8,512]{2,1,0:T(8,128)(2,1)S(1)}, bf16[64,8,512]{2,1,0:T(8,128)(2,1)S(1)}, u32[]{:S(2)}, u32[]{:S(2)}) collective-permute-start(bf16[64,8,512]{2,1,0:T(8,128)(2,1)S(1)} %slice_bitcast_fusion), channel_id=1, source_target_pairs={{0,16},{16,0},{1,17},{17,1},{2,18},{18,2},{3,19},{19,3},{4,20},{20... | collective-permute-start | bytes 1572872 | tf_op jit(solution)/shard_map/ppermute | solution.py:483
  140.6 15.6 %all-to-all-start.3 = ((bf16[4,160,320]{2,1,0:T(8,128)(2,1)}), bf16[4,160,320]{2,1,0:T(8,128)(2,1)S(1)}, u32[]{:S(2)}, u32[]{:S(2)}) async-start(bf16[4,160,320]{2,1,0:T(8,128)(2,1)} %bitcast.6._), calls=%async_computation.3 | async-start | bytes 983040 | tf_op jit(solution)/shard_map/all_to_all | solution.py:479
  145.7 16.8 %collective-permute-start.5 = (bf16[320,640]{1,0:T(8,128)(2,1)S(1)}, bf16[320,640]{1,0:T(8,128)(2,1)S(1)}, u32[]{:S(2)}, u32[]{:S(2)}) collective-permute-start(bf16[320,640]{1,0:T(8,128)(2,1)S(1)} %shard_map.108.rest_0_), channel_id=1, source_target_pairs={{0,8},{4,12},{8,0},{12,4},{1,9},{5,13},{9,1},{13,5},{2,10},{6,14},... | collective-permute-start | bytes 1228808 | tf_op jit(solution)/shard_map/ppermute | solution.py:473
  149.1 18.8 %collective-permute-start.6 = (bf16[320,640]{1,0:T(8,128)(2,1)S(1)}, bf16[320,640]{1,0:T(8,128)(2,1)S(1)}, u32[]{:S(2)}, u32[]{:S(2)}) collective-permute-start(bf16[320,640]{1,0:T(8,128)(2,1)S(1)} %shard_map.108.rest_0_), channel_id=1, source_target_pairs={{0,12},{4,0},{8,4},{12,8},{1,13},{5,1},{9,5},{13,9},{2,14},{6,2},{... | collective-permute-start | bytes 1228808 | tf_op jit(solution)/shard_map/ppermute | solution.py:473
  151.0 16.9 %collective-permute-start.7 = (bf16[320,640]{1,0:T(8,128)(2,1)S(1)}, bf16[320,640]{1,0:T(8,128)(2,1)S(1)}, u32[]{:S(2)}, u32[]{:S(2)}) collective-permute-start(bf16[320,640]{1,0:T(8,128)(2,1)S(1)} %shard_map.108.rest_0_), channel_id=1, source_target_pairs={{0,4},{4,8},{8,12},{12,0},{1,5},{5,9},{9,13},{13,1},{2,6},{6,10},{... | collective-permute-start | bytes 1228808 | tf_op jit(solution)/shard_map/ppermute | solution.py:473
  156.2 11.7 %collective-permute-start.4 = (bf16[4,160,320]{2,1,0:T(8,128)(2,1)S(1)}, bf16[4,160,320]{2,1,0:T(8,128)(2,1)S(1)}, u32[]{:S(2)}, u32[]{:S(2)}) collective-permute-start(bf16[4,160,320]{2,1,0:T(8,128)(2,1)S(1)} %all-to-all-done.3.own_ref), channel_id=1, source_target_pairs={{0,16},{16,0},{1,17},{17,1},{2,18},{18,2},{3,19},{19,3},{4,20},{20... | collective-permute-start | bytes 1228808 | tf_op jit(solution)/shard_map/ppermute | solution.py:483

commit v11 on v10

--- a/solution.py
+++ b/solution.py
@@ -25,6 +25,7 @@
 WHOLE = 3
 TAIL = 8 * 9
 ORDER = (0, 2, 1, 3)
+HALF = 32
 STRIDE = 40
 BOTH = 56
 BATCH = 8
@@ -415,8 +416,7 @@
     return jnp.concatenate(lanes, axis=1).astype(jnp.bfloat16)
 
 
-def outgoing_kernel(core_ref, left_ref, *rest):
-    rights, (_, out_ref, total) = rest[:X], rest[X:]
+def outgoing_part(core_ref, left_ref, rights, aheads, base, out_ref, total):
     for n, right_ref in enumerate(rights):
         total[:, n * ZH * ROWS : (n + 1) * ZH * ROWS] = lax.dot_general(
             left_ref[...],
@@ -426,20 +426,37 @@
         )
     for half in range(2):
         slot = lax.rem(core_ref[0] + half, 2)
-        for n, ahead in enumerate(ORDER):
-            x = lax.rem(core_ref[1] + ahead, X)
+        for n, ahead in enumerate(aheads):
+            zl = lax.rem(core_ref[1] + ahead, X) // 2
             for low in range(ZH):
-                span = ((lax.rem(x, 2) * ZH + low) * ZH) * 2 + x // 2
+                start = ((n * ZH + low) * 2 + half) * COLUMNS
                 for zh in range(ZH):
-                    start = ((n * ZH + low) * 2 + half) * COLUMNS
-                    out_ref[slot, span + zh * 2] = chunk_of(total, zh, start)
+                    place = base + (low * ZH + zh) * 2 + zl
+                    out_ref[slot, place] = chunk_of(total, zh, start)
+
+
+def outgoing_first_kernel(core_ref, left_ref, own_ref, across_ref, out_ref, total):
+    outgoing_part(core_ref, left_ref, (own_ref, across_ref), ORDER[:2], 0, out_ref, total)
+
+
+def outgoing_last_kernel(core_ref, left_ref, next_ref, last_ref, first_ref, _, out_ref, total):
+    parity = lax.rem(core_ref[1], 2)
+    for slot in range(2):
+        out_ref[slot, pl.ds(parity * HALF, HALF)] = first_ref[slot]
+    base = (1 - parity) * HALF
+    outgoing_part(core_ref, left_ref, (next_ref, last_ref), ORDER[2:], base, out_ref, total)
 
 
 def outgoing(core, left, rights, gate):
+    half = jax.ShapeDtypeStruct((2, HALF) + CHUNKS.shape[1:], jnp.bfloat16)
     out = jax.ShapeDtypeStruct((2,) + CHUNKS.shape, jnp.bfloat16)
-    scratch = [pltpu.VMEM((ZH * ROWS, X * ZH * ROWS), jnp.float32)]
-    specs = [SMEM] + [VMEM] * (1 + X) + [ANY]
-    return call(outgoing_kernel, out, specs, scratch, 6 * 10**8)(core, left, *rights, gate)
+    scratch = [pltpu.VMEM((ZH * ROWS, 2 * ZH * ROWS), jnp.float32)]
+    first = call(outgoing_first_kernel, half, [SMEM] + [VMEM] * 3, scratch, 3 * 10**8)(
+        core, left, *rights[:2]
+    )
+    return call(outgoing_last_kernel, out, [SMEM] + [VMEM] * 4 + [ANY], scratch, 3 * 10**8)(
+        core, left, *rights[2:], first, gate
+    )
 
 
 def incoming_kernel(core_ref, own_ref, other_ref, *rest):

time: 202 us -> 202 us (level)
  transfers between devices with their start and end apart: 9 -> 9, of which waited for: 5 -> 5; matrix products, arithmetic and copies ran while one was open for 0% -> 0% of each run, Pallas kernels for 2% -> 3%
where the time goes in v11:
time: 202 us; the launch traced here: 199 us
  blocking collectives  131 us (65%)
  starting transfers between devices  29.4 us (15%)
  Pallas kernels  22.3 us (11%)
  waiting for transfers between devices  15.8 us (8%)
    all_to_all x4, blocking collectives, exchange(): return lax.all_to_all(values, axes, split_axis=0, concat_axis=0, tiled=True)  131 us
    ppermute x6, starting transfers between devices, shift(): return lax.ppermute(block, 'x', [(x, (x - ahead) % X) for x in range(X)])  20.8 us
    ppermute x6, waiting for transfers between devices, shift(): return lax.ppermute(block, 'x', [(x, (x - ahead) % X) for x in range(X)])  13.9 us
    pallas_call x2, Pallas kernels, finish(): call(functools.partial(finish_kernel, which), [out, BOTH_CHUNKS] if then...  6.14 us
    all_to_all x1, starting transfers between devices, exchange(): return lax.all_to_all(values, axes, split_axis=0, concat_axis=0, tiled=True)  4.78 us
    pallas_call x1, Pallas kernels, project(): call(project_kernel, BOTH_CHUNKS, [ANY] * 5, [BOTH_SCRATCH] + scratch + s...  4.73 us
  transfers between devices with their start and end apart: 9, of which 5 were waited for; matrix products, arithmetic and copies ran while one was open for 0% of the time, Pallas kernels for 3%

profile of v11, /device:TPU:6, one launch (start us, length us, event | category | flops | bytes accessed | tf_op | source)
XLA Modules:
  0.0 199.4 jit_solution(4005373561995383338)
XLA Ops:
  0.0 4.7 %shard_map.100 = bf16[64,8,896]{2,1,0:T(8,128)(2,1)} custom-call(s32[1280]{0:T(1024)} %valid_ref.3, bf16[80,40,128]{2,1,0:T(8,128)(2,1)} %pair_ref.1, f32[2,128]{1,0:T(2,128)} %gain_any.1, f32[2,128]{1,0:T(2,128)} %bias_any.1, bf16[2,128,256]{2,1,0:T(8,128)(2,1)} %rest_1_.1), custom_call_target="tpu_custom_call" | custom-call | flops 100000000 | bytes 4000000 | tf_op jit(solution)/shard_map/pallas_call | solution.py:225
  4.8 43.5 %all_to_all.25.chunks_ref = bf16[64,8,896]{2,1,0:T(8,128)(2,1)S(1)} all-to-all(bf16[64,8,896]{2,1,0:T(8,128)(2,1)} %shard_map.100), channel_id=1, replica_groups=mesh['zl'=2,'y'=8,'core'=2,'x'=4,'zh'=4] {'y','zh','zl'}, dimensions={0} | all-to-all | bytes 1835008 | tf_op jit(solution)/shard_map/all_to_all | solution.py:496
  48.6 3.3 %collective-permute-start.2 = (bf16[320,640]{1,0:T(8,128)(2,1)S(1)}, bf16[320,640]{1,0:T(8,128)(2,1)S(1)}, u32[]{:S(2)}, u32[]{:S(2)}) collective-permute-start(bf16[320,640]{1,0:T(8,128)(2,1)S(1)} %shard_map.103.own_ref), channel_id=1, source_target_pairs={{0,8},{4,12},{8,0},{12,4},{1,9},{5,13},{9,1},{13,5},{2,10},{6,14},... | collective-permute-start | bytes 1228808 | tf_op jit(solution)/shard_map/ppermute | solution.py:490
  52.0 1.9 collective-permute-start
  53.9 5.1 %collective-permute-start.1 = (bf16[320,640]{1,0:T(8,128)(2,1)S(1)}, bf16[320,640]{1,0:T(8,128)(2,1)S(1)}, u32[]{:S(2)}, u32[]{:S(2)}) collective-permute-start(bf16[320,640]{1,0:T(8,128)(2,1)S(1)} %shard_map.103.own_ref), channel_id=1, source_target_pairs={{0,4},{4,8},{8,12},{12,0},{1,5},{5,9},{9,13},{13,1},{2,6},{6,10},{... | collective-permute-start | bytes 1228808 | tf_op jit(solution)/shard_map/ppermute | solution.py:490
  59.6 1.8 shard_map.102._.gates_ref
  61.4 3.0 %collective-permute-done.2.across_ref = bf16[320,640]{1,0:T(8,128)(2,1)S(1)} collective-permute-done((bf16[320,640]{1,0:T(8,128)(2,1)S(1)}, bf16[320,640]{1,0:T(8,128)(2,1)S(1)}, u32[]{:S(2)}, u32[]{:S(2)}) %collective-permute-start.2) | collective-permute-done | bytes 409632 | tf_op jit(solution)/shard_map/ppermute | solution.py:490
  66.1 2.9 %collective-permute-done.next_ref = bf16[320,640]{1,0:T(8,128)(2,1)S(1)} collective-permute-done((bf16[320,640]{1,0:T(8,128)(2,1)S(1)}, bf16[320,640]{1,0:T(8,128)(2,1)S(1)}, u32[]{:S(2)}, u32[]{:S(2)}) %collective-permute-start) | collective-permute-done | bytes 409632 | tf_op jit(solution)/shard_map/ppermute | solution.py:490
  70.6 1.9 collective-permute-start.3
  72.6 1.9 collective-permute-done.3
  74.6 28.1 %all_to_all.26.product_ref = bf16[64,8,512]{2,1,0:T(8,128)(2,1)S(1)} all-to-all(bf16[64,8,512]{2,1,0:T(8,128)(2,1)S(1)} %fusion), channel_id=1, replica_groups=mesh['zl'=2,'y'=8,'core'=2,'x'=4,'zh'=4] {'y','zh','zl'}, dimensions={0} | all-to-all | bytes 1048576 | tf_op jit(solution)/shard_map/all_to_all | solution.py:496
  102.7 3.8 %shard_map.106 = (bf16[80,40,128]{2,1,0:T(8,128)(2,1)S(1)}, bf16[64,8,896]{2,1,0:T(8,128)(2,1)S(1)}) custom-call(s32[2]{0:T(128)S(1)} %pad_add_fusion.place_ref, s32[1280]{0:T(1024)S(1)} %copy-done.4, f32[2,64]{1,0:T(2,128)S(1)} %copy-done.6, f32[2,32,128,128]{3,2,1,0:T(8,128)S(1)} %shard_map.102._.gates_ref, ...), custom_call_target="tpu_custom_call" | custom-call | flops 100000000 | bytes 4000000 | tf_op jit(solution)/shard_map/pallas_call | solution.py:343
  106.5 32.3 %all_to_all.27.chunks_ref = bf16[64,8,896]{2,1,0:T(8,128)(2,1)S(1)} all-to-all(bf16[64,8,896]{2,1,0:T(8,128)(2,1)S(1)} %get-tuple-element.8), channel_id=1, replica_groups=mesh['zl'=2,'y'=8,'core'=2,'x'=4,'zh'=4] {'y','zh','zl'}, dimensions={0} | all-to-all | bytes 1835008 | tf_op jit(solution)/shard_map/all_to_all | solution.py:496
  140.2 4.8 %all-to-all-start.3 = ((bf16[4,160,320]{2,1,0:T(8,128)(2,1)}), bf16[4,160,320]{2,1,0:T(8,128)(2,1)S(1)}, u32[]{:S(2)}, u32[]{:S(2)}) async-start(bf16[4,160,320]{2,1,0:T(8,128)(2,1)} %bitcast.6._), calls=%async_computation.3 | async-start | bytes 983040 | tf_op jit(solution)/shard_map/all_to_all | solution.py:496
  145.4 3.4 %collective-permute-start.5 = (bf16[320,640]{1,0:T(8,128)(2,1)S(1)}, bf16[320,640]{1,0:T(8,128)(2,1)S(1)}, u32[]{:S(2)}, u32[]{:S(2)}) collective-permute-start(bf16[320,640]{1,0:T(8,128)(2,1)S(1)} %shard_map.109.rest_0_), channel_id=1, source_target_pairs={{0,8},{4,12},{8,0},{12,4},{1,9},{5,13},{9,1},{13,5},{2,10},{6,14},... | collective-permute-start | bytes 1228808 | tf_op jit(solution)/shard_map/ppermute | solution.py:490
  148.8 1.9 collective-permute-start.6
  150.7 5.1 %collective-permute-start.7 = (bf16[320,640]{1,0:T(8,128)(2,1)S(1)}, bf16[320,640]{1,0:T(8,128)(2,1)S(1)}, u32[]{:S(2)}, u32[]{:S(2)}) collective-permute-start(bf16[320,640]{1,0:T(8,128)(2,1)S(1)} %shard_map.109.rest_0_), channel_id=1, source_target_pairs={{0,4},{4,8},{8,12},{12,0},{1,5},{5,9},{9,13},{13,1},{2,6},{6,10},{... | collective-permute-start | bytes 1228808 | tf_op jit(solution)/shard_map/ppermute | solution.py:490
  155.8 1.9 collective-permute-start.4
  157.8 1.8 shard_map.108.rest_4_.gates_ref
  159.6 2.6 %collective-permute-done.5.rest_1_ = bf16[320,640]{1,0:T(8,128)(2,1)S(1)} collective-permute-done((bf16[320,640]{1,0:T(8,128)(2,1)S(1)}, bf16[320,640]{1,0:T(8,128)(2,1)S(1)}, u32[]{:S(2)}, u32[]{:S(2)}) %collective-permute-start.5) | collective-permute-done | bytes 409632 | tf_op jit(solution)/shard_map/ppermute | solution.py:490
  162.2 5.4 %collective-permute-done.6.rest_2_ = bf16[320,640]{1,0:T(8,128)(2,1)S(1)} collective-permute-done((bf16[320,640]{1,0:T(8,128)(2,1)S(1)}, bf16[320,640]{1,0:T(8,128)(2,1)S(1)}, u32[]{:S(2)}, u32[]{:S(2)}) %collective-permute-start.6) | collective-permute-done | bytes 409632 | tf_op jit(solution)/shard_map/ppermute | solution.py:490
  167.6 2.2 %shard_map.110 = bf16[64,8,512]{2,1,0:T(8,128)(2,1)S(1)} custom-call(s32[2]{0:T(128)S(1)} %pad_add_fusion.1.core_ref, bf16[4,160,320]{2,1,0:T(8,128)(2,1)S(1)} %all-to-all-done.3.own_ref, bf16[4,160,320]{2,1,0:T(8,128)(2,1)S(1)} %collective-permute-done.4.other_ref, bf16[320,640]{1,0:T(8,128)(2,1)S(1)} %shard_map.109.rest_0_, ...), custom_call_target="tpu_custom_call" | custom-call | flops 600000000 | bytes 4000000 | tf_op jit(solution)/shard_map/pallas_call | solution.py:483
  169.7 27.2 %all_to_all.28.product_ref = bf16[64,8,512]{2,1,0:T(8,128)(2,1)S(1)} all-to-all(bf16[64,8,512]{2,1,0:T(8,128)(2,1)S(1)} %shard_map.110), channel_id=1, replica_groups=mesh['zl'=2,'y'=8,'core'=2,'x'=4,'zh'=4] {'y','zh','zl'}, dimensions={0} | all-to-all | bytes 1048576 | tf_op jit(solution)/shard_map/all_to_all | solution.py:496
  196.9 2.3 %shard_map.111 = bf16[80,40,128]{2,1,0:T(8,128)(2,1)} custom-call(s32[2]{0:T(128)S(1)} %pad_add_fusion.place_ref, s32[1280]{0:T(1024)S(1)} %copy-done.4, f32[2,64]{1,0:T(2,128)S(1)} %copy-done.6, f32[2,32,128,128]{3,2,1,0:T(8,128)S(1)} %shard_map.108.rest_4_.gates_ref, bf16[64,8,512]{2,1,0:T(8,128)(2,1)S(1)} %all_to_all.28.product_ref, ...), custom_call_target="tpu_custom_call" | custom-call | flops 100000000 | bytes 4000000 | tf_op jit(solution)/shard_map/pallas_call | solution.py:343
  (35 shorter events, 6.1 us)
Async XLA Ops:
  0.0 59.6 %copy-start = (bf16[80,40,128]{2,1,0:T(8,128)(2,1)S(1)}, bf16[80,40,128]{2,1,0:T(8,128)(2,1)}, u32[]{:S(2)}) copy-start(bf16[80,40,128]{2,1,0:T(8,128)(2,1)} %pair_ref.1) | copy-start | bytes 2457604
  0.0 59.2 %copy-start.8 = (f32[2,128]{1,0:T(2,128)S(1)}, f32[2,128]{1,0:T(2,128)}, u32[]{:S(2)}) copy-start(f32[2,128]{1,0:T(2,128)} %gain_any.1) | copy-start | bytes 3076
  0.0 59.2 %copy-start.7 = (f32[2,128]{1,0:T(2,128)S(1)}, f32[2,128]{1,0:T(2,128)}, u32[]{:S(2)}) copy-start(f32[2,128]{1,0:T(2,128)} %bias_any.1) | copy-start | bytes 3076
  0.0 59.2 %copy-start.9 = (f32[2,128]{1,0:T(2,128)S(1)}, f32[2,128]{1,0:T(2,128)}, u32[]{:S(2)}) copy-start(f32[2,128]{1,0:T(2,128)} %param.17) | copy-start | bytes 3076
  0.0 59.6 %copy-start.5 = (s32[1280]{0:T(1024)S(1)}, s32[1280]{0:T(1024)}, u32[]{:S(2)}) copy-start(s32[1280]{0:T(1024)} %chain_ref.3) | copy-start | bytes 15364
  0.0 59.6 %copy-start.2 = (bf16[2,128,128]{2,1,0:T(8,128)(2,1)S(1)}, bf16[2,128,128]{2,1,0:T(8,128)(2,1)}, u32[]{:S(2)}) copy-start(bf16[2,128,128]{2,1,0:T(8,128)(2,1)} %gate_ref.3) | copy-start | bytes 196612
  48.6 15.8 %collective-permute-start.2 = (bf16[320,640]{1,0:T(8,128)(2,1)S(1)}, bf16[320,640]{1,0:T(8,128)(2,1)S(1)}, u32[]{:S(2)}, u32[]{:S(2)}) collective-permute-start(bf16[320,640]{1,0:T(8,128)(2,1)S(1)} %shard_map.103.own_ref), channel_id=1, source_target_pairs={{0,8},{4,12},{8,0},{12,4},{1,9},{5,13},{9,1},{13,5},{2,10},{6,14},... | collective-permute-start | bytes 1228808 | tf_op jit(solution)/shard_map/ppermute | solution.py:490
  52.0 17.0 %collective-permute-start = (bf16[320,640]{1,0:T(8,128)(2,1)S(1)}, bf16[320,640]{1,0:T(8,128)(2,1)S(1)}, u32[]{:S(2)}, u32[]{:S(2)}) collective-permute-start(bf16[320,640]{1,0:T(8,128)(2,1)S(1)} %shard_map.103.own_ref), channel_id=1, source_target_pairs={{0,12},{4,0},{8,4},{12,8},{1,13},{5,1},{9,5},{13,9},{2,14},{6,2},{... | collective-permute-start | bytes 1228808 | tf_op jit(solution)/shard_map/ppermute | solution.py:490
  53.9 15.1 %collective-permute-start.1 = (bf16[320,640]{1,0:T(8,128)(2,1)S(1)}, bf16[320,640]{1,0:T(8,128)(2,1)S(1)}, u32[]{:S(2)}, u32[]{:S(2)}) collective-permute-start(bf16[320,640]{1,0:T(8,128)(2,1)S(1)} %shard_map.103.own_ref), channel_id=1, source_target_pairs={{0,4},{4,8},{8,12},{12,0},{1,5},{5,9},{9,13},{13,1},{2,6},{6,10},{... | collective-permute-start | bytes 1228808 | tf_op jit(solution)/shard_map/ppermute | solution.py:490
  66.1 36.7 %copy-start.1 = (bf16[2,128,256]{2,1,0:T(8,128)(2,1)S(1)}, bf16[2,128,256]{2,1,0:T(8,128)(2,1)}, u32[]{:S(2)}) copy-start(bf16[2,128,256]{2,1,0:T(8,128)(2,1)} %rest_1_.1) | copy-start | bytes 393220
  66.1 36.6 %copy-start.3 = (bf16[2,64,128]{2,1,0:T(8,128)(2,1)S(1)}, bf16[2,64,128]{2,1,0:T(8,128)(2,1)}, u32[]{:S(2)}) copy-start(bf16[2,64,128]{2,1,0:T(8,128)(2,1)} %out_weight_ref.3) | copy-start | bytes 98308
  66.1 36.6 %copy-start.4 = (s32[1280]{0:T(1024)S(1)}, s32[1280]{0:T(1024)}, u32[]{:S(2)}) copy-start(s32[1280]{0:T(1024)} %valid_ref.3) | copy-start | bytes 15364
  66.1 36.6 %copy-start.6 = (f32[2,64]{1,0:T(2,128)S(1)}, f32[2,64]{1,0:T(2,128)}, u32[]{:S(2)}) copy-start(f32[2,64]{1,0:T(2,128)} %out_gain_ref.3) | copy-start | bytes 1540
  70.6 3.8 %collective-permute-start.3 = (bf16[64,8,512]{2,1,0:T(8,128)(2,1)S(1)}, bf16[64,8,512]{2,1,0:T(8,128)(2,1)S(1)}, u32[]{:S(2)}, u32[]{:S(2)}) collective-permute-start(bf16[64,8,512]{2,1,0:T(8,128)(2,1)S(1)} %slice_bitcast_fusion), channel_id=1, source_target_pairs={{0,16},{16,0},{1,17},{17,1},{2,18},{18,2},{3,19},{19,3},{4,20},{20... | collective-permute-start | bytes 1572872 | tf_op jit(solution)/shard_map/ppermute | solution.py:500
  140.2 15.6 %all-to-all-start.3 = ((bf16[4,160,320]{2,1,0:T(8,128)(2,1)}), bf16[4,160,320]{2,1,0:T(8,128)(2,1)S(1)}, u32[]{:S(2)}, u32[]{:S(2)}) async-start(bf16[4,160,320]{2,1,0:T(8,128)(2,1)} %bitcast.6._), calls=%async_computation.3 | async-start | bytes 983040 | tf_op jit(solution)/shard_map/all_to_all | solution.py:496
  145.4 16.8 %collective-permute-start.5 = (bf16[320,640]{1,0:T(8,128)(2,1)S(1)}, bf16[320,640]{1,0:T(8,128)(2,1)S(1)}, u32[]{:S(2)}, u32[]{:S(2)}) collective-permute-start(bf16[320,640]{1,0:T(8,128)(2,1)S(1)} %shard_map.109.rest_0_), channel_id=1, source_target_pairs={{0,8},{4,12},{8,0},{12,4},{1,9},{5,13},{9,1},{13,5},{2,10},{6,14},... | collective-permute-start | bytes 1228808 | tf_op jit(solution)/shard_map/ppermute | solution.py:490
  148.8 18.8 %collective-permute-start.6 = (bf16[320,640]{1,0:T(8,128)(2,1)S(1)}, bf16[320,640]{1,0:T(8,128)(2,1)S(1)}, u32[]{:S(2)}, u32[]{:S(2)}) collective-permute-start(bf16[320,640]{1,0:T(8,128)(2,1)S(1)} %shard_map.109.rest_0_), channel_id=1, source_target_pairs={{0,12},{4,0},{8,4},{12,8},{1,13},{5,1},{9,5},{13,9},{2,14},{6,2},{... | collective-permute-start | bytes 1228808 | tf_op jit(solution)/shard_map/ppermute | solution.py:490
  150.7 16.9 %collective-permute-start.7 = (bf16[320,640]{1,0:T(8,128)(2,1)S(1)}, bf16[320,640]{1,0:T(8,128)(2,1)S(1)}, u32[]{:S(2)}, u32[]{:S(2)}) collective-permute-start(bf16[320,640]{1,0:T(8,128)(2,1)S(1)} %shard_map.109.rest_0_), channel_id=1, source_target_pairs={{0,4},{4,8},{8,12},{12,0},{1,5},{5,9},{9,13},{13,1},{2,6},{6,10},{... | collective-permute-start | bytes 1228808 | tf_op jit(solution)/shard_map/ppermute | solution.py:490
  155.8 11.7 %collective-permute-start.4 = (bf16[4,160,320]{2,1,0:T(8,128)(2,1)S(1)}, bf16[4,160,320]{2,1,0:T(8,128)(2,1)S(1)}, u32[]{:S(2)}, u32[]{:S(2)}) collective-permute-start(bf16[4,160,320]{2,1,0:T(8,128)(2,1)S(1)} %all-to-all-done.3.own_ref), channel_id=1, source_target_pairs={{0,16},{16,0},{1,17},{17,1},{2,18},{18,2},{3,19},{19,3},{4,20},{20... | collective-permute-start | bytes 1228808 | tf_op jit(solution)/shard_map/ppermute | solution.py:500

commit v12 on v11

--- a/solution.py
+++ b/solution.py
@@ -386,7 +386,7 @@
     return call(functools.partial(assemble_kernel, layout), out, [VMEM])(chunks)
 
 
-def assemble_turned_kernel(layout, chunks_ref, out_ref, whole):
+def assemble_turned_kernel(layout, chunks_ref, out_ref, whole, turned_s, sem):
     def put(start, values):
         whole[pl.ds(start, 2 * SUB), :] = values
 
@@ -394,14 +394,21 @@
     whole[pl.ds(ZH * ROWS, 64), :] = jnp.zeros((64, SPAN * COLUMNS), jnp.float32)
     for part in range(SPAN * COLUMNS // 128):
         turned = whole[:, part * 128 : (part + 1) * 128].T
-        out_ref[pl.ds(part * 128, 128), :] = turned[:, : ZH * ROWS].astype(jnp.bfloat16)
+        rows = pl.ds(part * 128, 128)
+        turned_s[rows, :] = turned[:, : ZH * ROWS].astype(jnp.bfloat16)
+        pltpu.make_async_copy(turned_s.at[rows], out_ref.at[rows], sem).start()
+    pltpu.make_async_copy(turned_s, out_ref, sem).wait()
 
 
 def assemble_turned(chunks, layout):
     out = jax.ShapeDtypeStruct((SPAN * COLUMNS, ZH * ROWS), jnp.bfloat16)
-    scratch = [pltpu.VMEM((ZH * ROWS + 64, SPAN * COLUMNS), jnp.float32)]
+    scratch = [
+        pltpu.VMEM((ZH * ROWS + 64, SPAN * COLUMNS), jnp.float32),
+        pltpu.VMEM(out.shape, out.dtype),
+        pltpu.SemaphoreType.DMA,
+    ]
     kernel = functools.partial(assemble_turned_kernel, layout)
-    return call(kernel, out, [VMEM], scratch)(chunks)
+    return call(kernel, out, [VMEM], scratch, outs=ANY)(chunks)
 
 
 def chunk_of(total, zh, start):

time: 202 us -> 202 us (level)
  no operation moved by 1% of the time
where the time goes in v12:
time: 202 us; the launch traced here: 199 us
  blocking collectives  131 us (65%)
  starting transfers between devices  29.4 us (15%)
  Pallas kernels  22.2 us (11%)
  waiting for transfers between devices  15.8 us (8%)
    all_to_all x4, blocking collectives, exchange(): return lax.all_to_all(values, axes, split_axis=0, concat_axis=0, tiled=True)  131 us
    ppermute x6, starting transfers between devices, shift(): return lax.ppermute(block, 'x', [(x, (x - ahead) % X) for x in range(X)])  20.8 us
    ppermute x6, waiting for transfers between devices, shift(): return lax.ppermute(block, 'x', [(x, (x - ahead) % X) for x in range(X)])  13.9 us
    pallas_call x2, Pallas kernels, finish(): call(functools.partial(finish_kernel, which), [out, BOTH_CHUNKS] if then...  6.14 us
    all_to_all x1, starting transfers between devices, exchange(): return lax.all_to_all(values, axes, split_axis=0, concat_axis=0, tiled=True)  4.79 us
    pallas_call x1, Pallas kernels, project(): call(project_kernel, BOTH_CHUNKS, [ANY] * 5, [BOTH_SCRATCH] + scratch + s...  4.73 us
  transfers between devices with their start and end apart: 9, of which 5 were waited for; matrix products, arithmetic and copies ran while one was open for 0% of the time, Pallas kernels for 3%

profile of v12, /device:TPU:6, one launch (start us, length us, event | category | flops | bytes accessed | tf_op | source)
XLA Modules:
  0.0 199.3 jit_solution(1917992772569277230)
XLA Ops:
  0.0 4.7 %shard_map.100 = bf16[64,8,896]{2,1,0:T(8,128)(2,1)} custom-call(s32[1280]{0:T(1024)} %valid_ref.3, bf16[80,40,128]{2,1,0:T(8,128)(2,1)} %pair_ref.1, f32[2,128]{1,0:T(2,128)} %gain_any.1, f32[2,128]{1,0:T(2,128)} %bias_any.1, bf16[2,128,256]{2,1,0:T(8,128)(2,1)} %rest_1_.1), custom_call_target="tpu_custom_call" | custom-call | flops 100000000 | bytes 4000000 | tf_op jit(solution)/shard_map/pallas_call | solution.py:225
  4.8 43.5 %all_to_all.25.chunks_ref = bf16[64,8,896]{2,1,0:T(8,128)(2,1)S(1)} all-to-all(bf16[64,8,896]{2,1,0:T(8,128)(2,1)} %shard_map.100), channel_id=1, replica_groups=mesh['zl'=2,'y'=8,'core'=2,'x'=4,'zh'=4] {'y','zh','zl'}, dimensions={0} | all-to-all | bytes 1835008 | tf_op jit(solution)/shard_map/all_to_all | solution.py:503
  48.6 3.3 %collective-permute-start.2 = (bf16[320,640]{1,0:T(8,128)(2,1)S(1)}, bf16[320,640]{1,0:T(8,128)(2,1)S(1)}, u32[]{:S(2)}, u32[]{:S(2)}) collective-permute-start(bf16[320,640]{1,0:T(8,128)(2,1)S(1)} %shard_map.103.own_ref), channel_id=1, source_target_pairs={{0,8},{4,12},{8,0},{12,4},{1,9},{5,13},{9,1},{13,5},{2,10},{6,14},... | collective-permute-start | bytes 1228808 | tf_op jit(solution)/shard_map/ppermute | solution.py:497
  52.0 1.9 collective-permute-start
  53.9 5.1 %collective-permute-start.1 = (bf16[320,640]{1,0:T(8,128)(2,1)S(1)}, bf16[320,640]{1,0:T(8,128)(2,1)S(1)}, u32[]{:S(2)}, u32[]{:S(2)}) collective-permute-start(bf16[320,640]{1,0:T(8,128)(2,1)S(1)} %shard_map.103.own_ref), channel_id=1, source_target_pairs={{0,4},{4,8},{8,12},{12,0},{1,5},{5,9},{9,13},{13,1},{2,6},{6,10},{... | collective-permute-start | bytes 1228808 | tf_op jit(solution)/shard_map/ppermute | solution.py:497
  59.6 1.8 shard_map.102._.gates_ref
  61.4 3.0 %collective-permute-done.2.across_ref = bf16[320,640]{1,0:T(8,128)(2,1)S(1)} collective-permute-done((bf16[320,640]{1,0:T(8,128)(2,1)S(1)}, bf16[320,640]{1,0:T(8,128)(2,1)S(1)}, u32[]{:S(2)}, u32[]{:S(2)}) %collective-permute-start.2) | collective-permute-done | bytes 409632 | tf_op jit(solution)/shard_map/ppermute | solution.py:497
  66.1 2.9 %collective-permute-done.next_ref = bf16[320,640]{1,0:T(8,128)(2,1)S(1)} collective-permute-done((bf16[320,640]{1,0:T(8,128)(2,1)S(1)}, bf16[320,640]{1,0:T(8,128)(2,1)S(1)}, u32[]{:S(2)}, u32[]{:S(2)}) %collective-permute-start) | collective-permute-done | bytes 409632 | tf_op jit(solution)/shard_map/ppermute | solution.py:497
  70.6 1.9 collective-permute-start.3
  72.6 1.9 collective-permute-done.3
  74.6 28.1 %all_to_all.26.product_ref = bf16[64,8,512]{2,1,0:T(8,128)(2,1)S(1)} all-to-all(bf16[64,8,512]{2,1,0:T(8,128)(2,1)S(1)} %fusion), channel_id=1, replica_groups=mesh['zl'=2,'y'=8,'core'=2,'x'=4,'zh'=4] {'y','zh','zl'}, dimensions={0} | all-to-all | bytes 1048576 | tf_op jit(solution)/shard_map/all_to_all | solution.py:503
  102.7 3.8 %shard_map.106 = (bf16[80,40,128]{2,1,0:T(8,128)(2,1)S(1)}, bf16[64,8,896]{2,1,0:T(8,128)(2,1)S(1)}) custom-call(s32[2]{0:T(128)S(1)} %pad_add_fusion.place_ref, s32[1280]{0:T(1024)S(1)} %copy-done.4, f32[2,64]{1,0:T(2,128)S(1)} %copy-done.6, f32[2,32,128,128]{3,2,1,0:T(8,128)S(1)} %shard_map.102._.gates_ref, ...), custom_call_target="tpu_custom_call" | custom-call | flops 100000000 | bytes 4000000 | tf_op jit(solution)/shard_map/pallas_call | solution.py:343
  106.5 32.3 %all_to_all.27.chunks_ref = bf16[64,8,896]{2,1,0:T(8,128)(2,1)S(1)} all-to-all(bf16[64,8,896]{2,1,0:T(8,128)(2,1)S(1)} %get-tuple-element.8), channel_id=1, replica_groups=mesh['zl'=2,'y'=8,'core'=2,'x'=4,'zh'=4] {'y','zh','zl'}, dimensions={0} | all-to-all | bytes 1835008 | tf_op jit(solution)/shard_map/all_to_all | solution.py:503
  140.1 4.8 %all-to-all-start.3 = ((bf16[4,160,320]{2,1,0:T(8,128)(2,1)}), bf16[4,160,320]{2,1,0:T(8,128)(2,1)S(1)}, u32[]{:S(2)}, u32[]{:S(2)}) async-start(bf16[4,160,320]{2,1,0:T(8,128)(2,1)} %bitcast.6._), calls=%async_computation.3 | async-start | bytes 983040 | tf_op jit(solution)/shard_map/all_to_all | solution.py:503
  145.3 3.4 %collective-permute-start.5 = (bf16[320,640]{1,0:T(8,128)(2,1)S(1)}, bf16[320,640]{1,0:T(8,128)(2,1)S(1)}, u32[]{:S(2)}, u32[]{:S(2)}) collective-permute-start(bf16[320,640]{1,0:T(8,128)(2,1)S(1)} %shard_map.109.rest_0_), channel_id=1, source_target_pairs={{0,8},{4,12},{8,0},{12,4},{1,9},{5,13},{9,1},{13,5},{2,10},{6,14},... | collective-permute-start | bytes 1228808 | tf_op jit(solution)/shard_map/ppermute | solution.py:497
  148.7 1.9 collective-permute-start.6
  150.6 5.1 %collective-permute-start.7 = (bf16[320,640]{1,0:T(8,128)(2,1)S(1)}, bf16[320,640]{1,0:T(8,128)(2,1)S(1)}, u32[]{:S(2)}, u32[]{:S(2)}) collective-permute-start(bf16[320,640]{1,0:T(8,128)(2,1)S(1)} %shard_map.109.rest_0_), channel_id=1, source_target_pairs={{0,4},{4,8},{8,12},{12,0},{1,5},{5,9},{9,13},{13,1},{2,6},{6,10},{... | collective-permute-start | bytes 1228808 | tf_op jit(solution)/shard_map/ppermute | solution.py:497
  155.8 1.9 collective-permute-start.4
  157.7 1.8 shard_map.108.rest_4_.gates_ref
  159.5 2.6 %collective-permute-done.5.rest_1_ = bf16[320,640]{1,0:T(8,128)(2,1)S(1)} collective-permute-done((bf16[320,640]{1,0:T(8,128)(2,1)S(1)}, bf16[320,640]{1,0:T(8,128)(2,1)S(1)}, u32[]{:S(2)}, u32[]{:S(2)}) %collective-permute-start.5) | collective-permute-done | bytes 409632 | tf_op jit(solution)/shard_map/ppermute | solution.py:497
  162.1 5.4 %collective-permute-done.6.rest_2_ = bf16[320,640]{1,0:T(8,128)(2,1)S(1)} collective-permute-done((bf16[320,640]{1,0:T(8,128)(2,1)S(1)}, bf16[320,640]{1,0:T(8,128)(2,1)S(1)}, u32[]{:S(2)}, u32[]{:S(2)}) %collective-permute-start.6) | collective-permute-done | bytes 409632 | tf_op jit(solution)/shard_map/ppermute | solution.py:497
  167.5 2.1 %shard_map.110 = bf16[64,8,512]{2,1,0:T(8,128)(2,1)S(1)} custom-call(s32[2]{0:T(128)S(1)} %pad_add_fusion.1.core_ref, bf16[4,160,320]{2,1,0:T(8,128)(2,1)S(1)} %all-to-all-done.3.own_ref, bf16[4,160,320]{2,1,0:T(8,128)(2,1)S(1)} %collective-permute-done.4.other_ref, bf16[320,640]{1,0:T(8,128)(2,1)S(1)} %shard_map.109.rest_0_, ...), custom_call_target="tpu_custom_call" | custom-call | flops 600000000 | bytes 4000000 | tf_op jit(solution)/shard_map/pallas_call | solution.py:490
  169.6 27.2 %all_to_all.28.product_ref = bf16[64,8,512]{2,1,0:T(8,128)(2,1)S(1)} all-to-all(bf16[64,8,512]{2,1,0:T(8,128)(2,1)S(1)} %shard_map.110), channel_id=1, replica_groups=mesh['zl'=2,'y'=8,'core'=2,'x'=4,'zh'=4] {'y','zh','zl'}, dimensions={0} | all-to-all | bytes 1048576 | tf_op jit(solution)/shard_map/all_to_all | solution.py:503
  196.9 2.3 %shard_map.111 = bf16[80,40,128]{2,1,0:T(8,128)(2,1)} custom-call(s32[2]{0:T(128)S(1)} %pad_add_fusion.place_ref, s32[1280]{0:T(1024)S(1)} %copy-done.4, f32[2,64]{1,0:T(2,128)S(1)} %copy-done.6, f32[2,32,128,128]{3,2,1,0:T(8,128)S(1)} %shard_map.108.rest_4_.gates_ref, bf16[64,8,512]{2,1,0:T(8,128)(2,1)S(1)} %all_to_all.28.product_ref, ...), custom_call_target="tpu_custom_call" | custom-call | flops 100000000 | bytes 4000000 | tf_op jit(solution)/shard_map/pallas_call | solution.py:343
  (35 shorter events, 6.0 us)
Async XLA Ops:
  0.0 59.6 %copy-start = (bf16[80,40,128]{2,1,0:T(8,128)(2,1)S(1)}, bf16[80,40,128]{2,1,0:T(8,128)(2,1)}, u32[]{:S(2)}) copy-start(bf16[80,40,128]{2,1,0:T(8,128)(2,1)} %pair_ref.1) | copy-start | bytes 2457604
  0.0 59.2 %copy-start.8 = (f32[2,128]{1,0:T(2,128)S(1)}, f32[2,128]{1,0:T(2,128)}, u32[]{:S(2)}) copy-start(f32[2,128]{1,0:T(2,128)} %gain_any.1) | copy-start | bytes 3076
  0.0 59.2 %copy-start.7 = (f32[2,128]{1,0:T(2,128)S(1)}, f32[2,128]{1,0:T(2,128)}, u32[]{:S(2)}) copy-start(f32[2,128]{1,0:T(2,128)} %bias_any.1) | copy-start | bytes 3076
  0.0 59.2 %copy-start.9 = (f32[2,128]{1,0:T(2,128)S(1)}, f32[2,128]{1,0:T(2,128)}, u32[]{:S(2)}) copy-start(f32[2,128]{1,0:T(2,128)} %param.17) | copy-start | bytes 3076
  0.0 59.6 %copy-start.5 = (s32[1280]{0:T(1024)S(1)}, s32[1280]{0:T(1024)}, u32[]{:S(2)}) copy-start(s32[1280]{0:T(1024)} %chain_ref.3) | copy-start | bytes 15364
  0.0 59.6 %copy-start.2 = (bf16[2,128,128]{2,1,0:T(8,128)(2,1)S(1)}, bf16[2,128,128]{2,1,0:T(8,128)(2,1)}, u32[]{:S(2)}) copy-start(bf16[2,128,128]{2,1,0:T(8,128)(2,1)} %gate_ref.3) | copy-start | bytes 196612
  48.6 15.8 %collective-permute-start.2 = (bf16[320,640]{1,0:T(8,128)(2,1)S(1)}, bf16[320,640]{1,0:T(8,128)(2,1)S(1)}, u32[]{:S(2)}, u32[]{:S(2)}) collective-permute-start(bf16[320,640]{1,0:T(8,128)(2,1)S(1)} %shard_map.103.own_ref), channel_id=1, source_target_pairs={{0,8},{4,12},{8,0},{12,4},{1,9},{5,13},{9,1},{13,5},{2,10},{6,14},... | collective-permute-start | bytes 1228808 | tf_op jit(solution)/shard_map/ppermute | solution.py:497
  52.0 17.0 %collective-permute-start = (bf16[320,640]{1,0:T(8,128)(2,1)S(1)}, bf16[320,640]{1,0:T(8,128)(2,1)S(1)}, u32[]{:S(2)}, u32[]{:S(2)}) collective-permute-start(bf16[320,640]{1,0:T(8,128)(2,1)S(1)} %shard_map.103.own_ref), channel_id=1, source_target_pairs={{0,12},{4,0},{8,4},{12,8},{1,13},{5,1},{9,5},{13,9},{2,14},{6,2},{... | collective-permute-start | bytes 1228808 | tf_op jit(solution)/shard_map/ppermute | solution.py:497
  53.9 15.1 %collective-permute-start.1 = (bf16[320,640]{1,0:T(8,128)(2,1)S(1)}, bf16[320,640]{1,0:T(8,128)(2,1)S(1)}, u32[]{:S(2)}, u32[]{:S(2)}) collective-permute-start(bf16[320,640]{1,0:T(8,128)(2,1)S(1)} %shard_map.103.own_ref), channel_id=1, source_target_pairs={{0,4},{4,8},{8,12},{12,0},{1,5},{5,9},{9,13},{13,1},{2,6},{6,10},{... | collective-permute-start | bytes 1228808 | tf_op jit(solution)/shard_map/ppermute | solution.py:497
  66.1 36.7 %copy-start.1 = (bf16[2,128,256]{2,1,0:T(8,128)(2,1)S(1)}, bf16[2,128,256]{2,1,0:T(8,128)(2,1)}, u32[]{:S(2)}) copy-start(bf16[2,128,256]{2,1,0:T(8,128)(2,1)} %rest_1_.1) | copy-start | bytes 393220
  66.1 36.6 %copy-start.3 = (bf16[2,64,128]{2,1,0:T(8,128)(2,1)S(1)}, bf16[2,64,128]{2,1,0:T(8,128)(2,1)}, u32[]{:S(2)}) copy-start(bf16[2,64,128]{2,1,0:T(8,128)(2,1)} %out_weight_ref.3) | copy-start | bytes 98308
  66.1 36.6 %copy-start.4 = (s32[1280]{0:T(1024)S(1)}, s32[1280]{0:T(1024)}, u32[]{:S(2)}) copy-start(s32[1280]{0:T(1024)} %valid_ref.3) | copy-start | bytes 15364
  66.1 36.6 %copy-start.6 = (f32[2,64]{1,0:T(2,128)S(1)}, f32[2,64]{1,0:T(2,128)}, u32[]{:S(2)}) copy-start(f32[2,64]{1,0:T(2,128)} %out_gain_ref.3) | copy-start | bytes 1540
  70.6 3.8 %collective-permute-start.3 = (bf16[64,8,512]{2,1,0:T(8,128)(2,1)S(1)}, bf16[64,8,512]{2,1,0:T(8,128)(2,1)S(1)}, u32[]{:S(2)}, u32[]{:S(2)}) collective-permute-start(bf16[64,8,512]{2,1,0:T(8,128)(2,1)S(1)} %slice_bitcast_fusion), channel_id=1, source_target_pairs={{0,16},{16,0},{1,17},{17,1},{2,18},{18,2},{3,19},{19,3},{4,20},{20... | collective-permute-start | bytes 1572872 | tf_op jit(solution)/shard_map/ppermute | solution.py:507
  140.1 15.6 %all-to-all-start.3 = ((bf16[4,160,320]{2,1,0:T(8,128)(2,1)}), bf16[4,160,320]{2,1,0:T(8,128)(2,1)S(1)}, u32[]{:S(2)}, u32[]{:S(2)}) async-start(bf16[4,160,320]{2,1,0:T(8,128)(2,1)} %bitcast.6._), calls=%async_computation.3 | async-start | bytes 983040 | tf_op jit(solution)/shard_map/all_to_all | solution.py:503
  145.3 16.8 %collective-permute-start.5 = (bf16[320,640]{1,0:T(8,128)(2,1)S(1)}, bf16[320,640]{1,0:T(8,128)(2,1)S(1)}, u32[]{:S(2)}, u32[]{:S(2)}) collective-permute-start(bf16[320,640]{1,0:T(8,128)(2,1)S(1)} %shard_map.109.rest_0_), channel_id=1, source_target_pairs={{0,8},{4,12},{8,0},{12,4},{1,9},{5,13},{9,1},{13,5},{2,10},{6,14},... | collective-permute-start | bytes 1228808 | tf_op jit(solution)/shard_map/ppermute | solution.py:497
  148.7 18.8 %collective-permute-start.6 = (bf16[320,640]{1,0:T(8,128)(2,1)S(1)}, bf16[320,640]{1,0:T(8,128)(2,1)S(1)}, u32[]{:S(2)}, u32[]{:S(2)}) collective-permute-start(bf16[320,640]{1,0:T(8,128)(2,1)S(1)} %shard_map.109.rest_0_), channel_id=1, source_target_pairs={{0,12},{4,0},{8,4},{12,8},{1,13},{5,1},{9,5},{13,9},{2,14},{6,2},{... | collective-permute-start | bytes 1228808 | tf_op jit(solution)/shard_map/ppermute | solution.py:497
  150.6 16.9 %collective-permute-start.7 = (bf16[320,640]{1,0:T(8,128)(2,1)S(1)}, bf16[320,640]{1,0:T(8,128)(2,1)S(1)}, u32[]{:S(2)}, u32[]{:S(2)}) collective-permute-start(bf16[320,640]{1,0:T(8,128)(2,1)S(1)} %shard_map.109.rest_0_), channel_id=1, source_target_pairs={{0,4},{4,8},{8,12},{12,0},{1,5},{5,9},{9,13},{13,1},{2,6},{6,10},{... | collective-permute-start | bytes 1228808 | tf_op jit(solution)/shard_map/ppermute | solution.py:497
  155.8 11.7 %collective-permute-start.4 = (bf16[4,160,320]{2,1,0:T(8,128)(2,1)S(1)}, bf16[4,160,320]{2,1,0:T(8,128)(2,1)S(1)}, u32[]{:S(2)}, u32[]{:S(2)}) collective-permute-start(bf16[4,160,320]{2,1,0:T(8,128)(2,1)S(1)} %all-to-all-done.3.own_ref), channel_id=1, source_target_pairs={{0,16},{16,0},{1,17},{17,1},{2,18},{18,2},{3,19},{19,3},{4,20},{20... | collective-permute-start | bytes 1228808 | tf_op jit(solution)/shard_map/ppermute | solution.py:507

commit v13 on v12

--- a/solution.py
+++ b/solution.py
@@ -466,30 +466,47 @@
     )
 
 
-def incoming_kernel(core_ref, own_ref, other_ref, *rest):
-    rights, (_, out_ref, total) = rest[:X], rest[X:]
-    for n, left_ref in enumerate((own_ref, other_ref)):
+def incoming_part(core_ref, lefts, rights, aheads, total, before=None):
+    for n, left_ref in enumerate(lefts):
         side = lax.rem(core_ref[0] + n, 2)
         product = jnp.zeros((ZH * COLUMNS, SPAN * COLUMNS), jnp.float32)
-        for ahead, right_ref in zip(ORDER, rights):
+        for ahead, right_ref in zip(aheads, rights):
             product = product + jnp.dot(
                 left_ref[lax.rem(core_ref[1] + ahead, X)],
                 right_ref[...],
                 preferred_element_type=jnp.float32,
             )
         for zh in range(ZH):
-            start = pl.multiple_of(zh * ROWS + side * COLUMNS, 8)
-            total[pl.ds(start, COLUMNS), :] = product[zh * COLUMNS : (zh + 1) * COLUMNS]
+            place = pl.ds(pl.multiple_of(zh * ROWS + side * COLUMNS, 8), COLUMNS)
+            part = product[zh * COLUMNS : (zh + 1) * COLUMNS]
+            total[place, :] = part if before is None else part + before[place, :]
+
+
+def incoming_first_kernel(core_ref, own_ref, other_ref, here_ref, across_ref, out_ref):
+    incoming_part(core_ref, (own_ref, other_ref), (here_ref, across_ref), ORDER[:2], out_ref)
+
+
+def incoming_last_kernel(
+    core_ref, own_ref, other_ref, next_ref, last_ref, before_ref, _, out_ref, total
+):
+    rights = (next_ref, last_ref)
+    incoming_part(core_ref, (own_ref, other_ref), rights, ORDER[2:], total, before_ref)
     for span in range(SPAN):
         for zh in range(ZH):
             out_ref[spot(span, zh)] = chunk_of(total, zh, span * COLUMNS)
 
 
 def incoming(core, own, other, rights, gate):
-    scratch = [pltpu.VMEM((ZH * ROWS, SPAN * COLUMNS), jnp.float32)]
-    return call(
-        incoming_kernel, CHUNKS, [SMEM] + [VMEM] * (2 + X) + [ANY], scratch, 6 * 10**8
-    )(core, own, other, *rights, gate)
+    size = (ZH * ROWS, SPAN * COLUMNS)
+    half = jax.ShapeDtypeStruct(size, jnp.float32)
+    first = call(incoming_first_kernel, half, [SMEM] + [VMEM] * 4, (), 3 * 10**8)(
+        core, own, other, *rights[:2]
+    )
+    specs = [SMEM] + [VMEM] * 5 + [ANY]
+    scratch = [pltpu.VMEM(size, jnp.float32)]
+    return call(incoming_last_kernel, CHUNKS, specs, scratch, 3 * 10**8)(
+        core, own, other, *rights[2:], first, gate
+    )
 
 
 def gather_x(block):

time: 202 us -> 209 us (1.035)
  waiting for transfers between devices: 15.8 us -> 21 us
  starting transfers between devices: 29.4 us -> 32.3 us
    all_to_all x1, waiting for transfers between devices: 0.01 us -> 4.65 us  [exchange(): return lax.all_to_all(values, axes, split_axis=0, concat_axis=0, tiled=True)]
    ppermute x6, starting transfers between devices: 20.8 us -> 23.7 us  [shift(): return lax.ppermute(block, 'x', [(x, (x - ahead) % X) for x in range(X)])]
  transfers between devices with their start and end apart: 9 -> 9, of which waited for: 5 -> 6; matrix products, arithmetic and copies ran while one was open for 0% -> 0% of each run, Pallas kernels for 3% -> 3%
where the time goes in v13:
time: 209 us; the launch traced here: 207 us
  blocking collectives  130 us (62%)
  starting transfers between devices  32.3 us (15%)
  Pallas kernels  23 us (11%)
  waiting for transfers between devices  21 us (10%)
    all_to_all x4, blocking collectives, exchange(): return lax.all_to_all(values, axes, split_axis=0, concat_axis=0, tiled=True)  130 us
    ppermute x6, starting transfers between devices, shift(): return lax.ppermute(block, 'x', [(x, (x - ahead) % X) for x in range(X)])  23.7 us
    ppermute x6, waiting for transfers between devices, shift(): return lax.ppermute(block, 'x', [(x, (x - ahead) % X) for x in range(X)])  14.4 us
    pallas_call x2, Pallas kernels, finish(): call(functools.partial(finish_kernel, which), [out, BOTH_CHUNKS] if then...  6.14 us
    all_to_all x1, starting transfers between devices, exchange(): return lax.all_to_all(values, axes, split_axis=0, concat_axis=0, tiled=True)  4.76 us
    pallas_call x1, Pallas kernels, project(): call(project_kernel, BOTH_CHUNKS, [ANY] * 5, [BOTH_SCRATCH] + scratch + s...  4.73 us
    all_to_all x1, waiting for transfers between devices, exchange(): return lax.all_to_all(values, axes, split_axis=0, concat_axis=0, tiled=True)  4.65 us
  transfers between devices with their start and end apart: 9, of which 6 were waited for; matrix products, arithmetic and copies ran while one was open for 0% of the time, Pallas kernels for 3%

profile of v13, /device:TPU:6, one launch (start us, length us, event | category | flops | bytes accessed | tf_op | source)
XLA Modules:
  0.0 206.8 jit_solution(1166689826766257318)
XLA Ops:
  0.0 4.7 %shard_map.100 = bf16[64,8,896]{2,1,0:T(8,128)(2,1)} custom-call(s32[1280]{0:T(1024)} %valid_ref.3, bf16[80,40,128]{2,1,0:T(8,128)(2,1)} %pair_ref.1, f32[2,128]{1,0:T(2,128)} %gain_any.1, f32[2,128]{1,0:T(2,128)} %bias_any.1, bf16[2,128,256]{2,1,0:T(8,128)(2,1)} %rest_1_.1), custom_call_target="tpu_custom_call" | custom-call | flops 100000000 | bytes 4000000 | tf_op jit(solution)/shard_map/pallas_call | solution.py:225
  4.8 43.5 %all_to_all.25.chunks_ref = bf16[64,8,896]{2,1,0:T(8,128)(2,1)S(1)} all-to-all(bf16[64,8,896]{2,1,0:T(8,128)(2,1)} %shard_map.100), channel_id=1, replica_groups=mesh['zl'=2,'y'=8,'core'=2,'x'=4,'zh'=4] {'y','zh','zl'}, dimensions={0} | all-to-all | bytes 1835008 | tf_op jit(solution)/shard_map/all_to_all | solution.py:520
  48.6 3.3 %collective-permute-start.2 = (bf16[320,640]{1,0:T(8,128)(2,1)S(1)}, bf16[320,640]{1,0:T(8,128)(2,1)S(1)}, u32[]{:S(2)}, u32[]{:S(2)}) collective-permute-start(bf16[320,640]{1,0:T(8,128)(2,1)S(1)} %shard_map.103.own_ref), channel_id=1, source_target_pairs={{0,8},{4,12},{8,0},{12,4},{1,9},{5,13},{9,1},{13,5},{2,10},{6,14},... | collective-permute-start | bytes 1228808 | tf_op jit(solution)/shard_map/ppermute | solution.py:514
  52.0 1.9 collective-permute-start
  53.9 5.1 %collective-permute-start.1 = (bf16[320,640]{1,0:T(8,128)(2,1)S(1)}, bf16[320,640]{1,0:T(8,128)(2,1)S(1)}, u32[]{:S(2)}, u32[]{:S(2)}) collective-permute-start(bf16[320,640]{1,0:T(8,128)(2,1)S(1)} %shard_map.103.own_ref), channel_id=1, source_target_pairs={{0,4},{4,8},{8,12},{12,0},{1,5},{5,9},{9,13},{13,1},{2,6},{6,10},{... | collective-permute-start | bytes 1228808 | tf_op jit(solution)/shard_map/ppermute | solution.py:514
  59.6 1.8 shard_map.102._.gates_ref
  61.4 3.0 %collective-permute-done.2.across_ref = bf16[320,640]{1,0:T(8,128)(2,1)S(1)} collective-permute-done((bf16[320,640]{1,0:T(8,128)(2,1)S(1)}, bf16[320,640]{1,0:T(8,128)(2,1)S(1)}, u32[]{:S(2)}, u32[]{:S(2)}) %collective-permute-start.2) | collective-permute-done | bytes 409632 | tf_op jit(solution)/shard_map/ppermute | solution.py:514
  66.1 2.9 %collective-permute-done.next_ref = bf16[320,640]{1,0:T(8,128)(2,1)S(1)} collective-permute-done((bf16[320,640]{1,0:T(8,128)(2,1)S(1)}, bf16[320,640]{1,0:T(8,128)(2,1)S(1)}, u32[]{:S(2)}, u32[]{:S(2)}) %collective-permute-start) | collective-permute-done | bytes 409632 | tf_op jit(solution)/shard_map/ppermute | solution.py:514
  70.6 1.9 collective-permute-start.3
  72.6 1.9 collective-permute-done.3
  74.6 28.1 %all_to_all.26.product_ref = bf16[64,8,512]{2,1,0:T(8,128)(2,1)S(1)} all-to-all(bf16[64,8,512]{2,1,0:T(8,128)(2,1)S(1)} %fusion), channel_id=1, replica_groups=mesh['zl'=2,'y'=8,'core'=2,'x'=4,'zh'=4] {'y','zh','zl'}, dimensions={0} | all-to-all | bytes 1048576 | tf_op jit(solution)/shard_map/all_to_all | solution.py:520
  102.7 3.8 %shard_map.106 = (bf16[80,40,128]{2,1,0:T(8,128)(2,1)S(1)}, bf16[64,8,896]{2,1,0:T(8,128)(2,1)S(1)}) custom-call(s32[2]{0:T(128)S(1)} %pad_add_fusion.place_ref, s32[1280]{0:T(1024)S(1)} %copy-done.4, f32[2,64]{1,0:T(2,128)S(1)} %copy-done.6, f32[2,32,128,128]{3,2,1,0:T(8,128)S(1)} %shard_map.102._.gates_ref, ...), custom_call_target="tpu_custom_call" | custom-call | flops 100000000 | bytes 4000000 | tf_op jit(solution)/shard_map/pallas_call | solution.py:343
  106.6 32.3 %all_to_all.27.chunks_ref = bf16[64,8,896]{2,1,0:T(8,128)(2,1)S(1)} all-to-all(bf16[64,8,896]{2,1,0:T(8,128)(2,1)S(1)} %get-tuple-element.8), channel_id=1, replica_groups=mesh['zl'=2,'y'=8,'core'=2,'x'=4,'zh'=4] {'y','zh','zl'}, dimensions={0} | all-to-all | bytes 1835008 | tf_op jit(solution)/shard_map/all_to_all | solution.py:520
  140.1 4.8 %all-to-all-start.3 = ((bf16[4,160,320]{2,1,0:T(8,128)(2,1)}), bf16[4,160,320]{2,1,0:T(8,128)(2,1)S(1)}, u32[]{:S(2)}, u32[]{:S(2)}) async-start(bf16[4,160,320]{2,1,0:T(8,128)(2,1)} %bitcast.6._), calls=%async_computation.3 | async-start | bytes 983040 | tf_op jit(solution)/shard_map/all_to_all | solution.py:520
  145.3 3.4 %collective-permute-start.7 = (bf16[320,640]{1,0:T(8,128)(2,1)S(1)}, bf16[320,640]{1,0:T(8,128)(2,1)S(1)}, u32[]{:S(2)}, u32[]{:S(2)}) collective-permute-start(bf16[320,640]{1,0:T(8,128)(2,1)S(1)} %shard_map.109.here_ref), channel_id=1, source_target_pairs={{0,8},{4,12},{8,0},{12,4},{1,9},{5,13},{9,1},{13,5},{2,10},{6,14},... | collective-permute-start | bytes 1228808 | tf_op jit(solution)/shard_map/ppermute | solution.py:514
  148.7 4.7 %all-to-all-done.3.own_ref = bf16[4,160,320]{2,1,0:T(8,128)(2,1)S(1)} async-done(((bf16[4,160,320]{2,1,0:T(8,128)(2,1)}), bf16[4,160,320]{2,1,0:T(8,128)(2,1)S(1)}, u32[]{:S(2)}, u32[]{:S(2)}) %all-to-all-start.3) | async-done | bytes 409632 | tf_op jit(solution)/shard_map/all_to_all | solution.py:520
  153.3 1.9 collective-permute-start.4
  155.2 8.1 %collective-permute-start.5 = (bf16[320,640]{1,0:T(8,128)(2,1)S(1)}, bf16[320,640]{1,0:T(8,128)(2,1)S(1)}, u32[]{:S(2)}, u32[]{:S(2)}) collective-permute-start(bf16[320,640]{1,0:T(8,128)(2,1)S(1)} %shard_map.109.here_ref), channel_id=1, source_target_pairs={{0,12},{4,0},{8,4},{12,8},{1,13},{5,1},{9,5},{13,9},{2,14},{6,2},{... | collective-permute-start | bytes 1228808 | tf_op jit(solution)/shard_map/ppermute | solution.py:514
  163.3 1.9 collective-permute-start.6
  165.2 1.8 shard_map.108._.gates_ref
  168.3 4.4 %collective-permute-done.5.next_ref = bf16[320,640]{1,0:T(8,128)(2,1)S(1)} collective-permute-done((bf16[320,640]{1,0:T(8,128)(2,1)S(1)}, bf16[320,640]{1,0:T(8,128)(2,1)S(1)}, u32[]{:S(2)}, u32[]{:S(2)}) %collective-permute-start.5) | collective-permute-done | bytes 409632 | tf_op jit(solution)/shard_map/ppermute | solution.py:514
  172.7 4.1 %collective-permute-done.6.last_ref = bf16[320,640]{1,0:T(8,128)(2,1)S(1)} collective-permute-done((bf16[320,640]{1,0:T(8,128)(2,1)S(1)}, bf16[320,640]{1,0:T(8,128)(2,1)S(1)}, u32[]{:S(2)}, u32[]{:S(2)}) %collective-permute-start.6) | collective-permute-done | bytes 409632 | tf_op jit(solution)/shard_map/ppermute | solution.py:514
  178.5 25.8 %all_to_all.28.product_ref = bf16[64,8,512]{2,1,0:T(8,128)(2,1)S(1)} all-to-all(bf16[64,8,512]{2,1,0:T(8,128)(2,1)S(1)} %shard_map.111), channel_id=1, replica_groups=mesh['zl'=2,'y'=8,'core'=2,'x'=4,'zh'=4] {'y','zh','zl'}, dimensions={0} | all-to-all | bytes 1048576 | tf_op jit(solution)/shard_map/all_to_all | solution.py:520
  204.3 2.3 %shard_map.112 = bf16[80,40,128]{2,1,0:T(8,128)(2,1)} custom-call(s32[2]{0:T(128)S(1)} %pad_add_fusion.place_ref, s32[1280]{0:T(1024)S(1)} %copy-done.4, f32[2,64]{1,0:T(2,128)S(1)} %copy-done.6, f32[2,32,128,128]{3,2,1,0:T(8,128)S(1)} %shard_map.108._.gates_ref, bf16[64,8,512]{2,1,0:T(8,128)(2,1)S(1)} %all_to_all.28.product_ref, ...), custom_call_target="tpu_custom_call" | custom-call | flops 100000000 | bytes 4000000 | tf_op jit(solution)/shard_map/pallas_call | solution.py:343
  (36 shorter events, 8.9 us)
Async XLA Ops:
  0.0 59.2 %copy-start.7 = (f32[2,128]{1,0:T(2,128)S(1)}, f32[2,128]{1,0:T(2,128)}, u32[]{:S(2)}) copy-start(f32[2,128]{1,0:T(2,128)} %bias_any.1) | copy-start | bytes 3076
  0.0 59.2 %copy-start.8 = (f32[2,128]{1,0:T(2,128)S(1)}, f32[2,128]{1,0:T(2,128)}, u32[]{:S(2)}) copy-start(f32[2,128]{1,0:T(2,128)} %gain_any.1) | copy-start | bytes 3076
  0.0 59.6 %copy-start = (bf16[80,40,128]{2,1,0:T(8,128)(2,1)S(1)}, bf16[80,40,128]{2,1,0:T(8,128)(2,1)}, u32[]{:S(2)}) copy-start(bf16[80,40,128]{2,1,0:T(8,128)(2,1)} %pair_ref.1) | copy-start | bytes 2457604
  0.0 59.2 %copy-start.9 = (f32[2,128]{1,0:T(2,128)S(1)}, f32[2,128]{1,0:T(2,128)}, u32[]{:S(2)}) copy-start(f32[2,128]{1,0:T(2,128)} %param.17) | copy-start | bytes 3076
  0.0 59.6 %copy-start.5 = (s32[1280]{0:T(1024)S(1)}, s32[1280]{0:T(1024)}, u32[]{:S(2)}) copy-start(s32[1280]{0:T(1024)} %chain_ref.3) | copy-start | bytes 15364
  0.0 59.6 %copy-start.2 = (bf16[2,128,128]{2,1,0:T(8,128)(2,1)S(1)}, bf16[2,128,128]{2,1,0:T(8,128)(2,1)}, u32[]{:S(2)}) copy-start(bf16[2,128,128]{2,1,0:T(8,128)(2,1)} %gate_ref.3) | copy-start | bytes 196612
  48.6 15.8 %collective-permute-start.2 = (bf16[320,640]{1,0:T(8,128)(2,1)S(1)}, bf16[320,640]{1,0:T(8,128)(2,1)S(1)}, u32[]{:S(2)}, u32[]{:S(2)}) collective-permute-start(bf16[320,640]{1,0:T(8,128)(2,1)S(1)} %shard_map.103.own_ref), channel_id=1, source_target_pairs={{0,8},{4,12},{8,0},{12,4},{1,9},{5,13},{9,1},{13,5},{2,10},{6,14},... | collective-permute-start | bytes 1228808 | tf_op jit(solution)/shard_map/ppermute | solution.py:514
  52.0 17.0 %collective-permute-start = (bf16[320,640]{1,0:T(8,128)(2,1)S(1)}, bf16[320,640]{1,0:T(8,128)(2,1)S(1)}, u32[]{:S(2)}, u32[]{:S(2)}) collective-permute-start(bf16[320,640]{1,0:T(8,128)(2,1)S(1)} %shard_map.103.own_ref), channel_id=1, source_target_pairs={{0,12},{4,0},{8,4},{12,8},{1,13},{5,1},{9,5},{13,9},{2,14},{6,2},{... | collective-permute-start | bytes 1228808 | tf_op jit(solution)/shard_map/ppermute | solution.py:514
  53.9 15.1 %collective-permute-start.1 = (bf16[320,640]{1,0:T(8,128)(2,1)S(1)}, bf16[320,640]{1,0:T(8,128)(2,1)S(1)}, u32[]{:S(2)}, u32[]{:S(2)}) collective-permute-start(bf16[320,640]{1,0:T(8,128)(2,1)S(1)} %shard_map.103.own_ref), channel_id=1, source_target_pairs={{0,4},{4,8},{8,12},{12,0},{1,5},{5,9},{9,13},{13,1},{2,6},{6,10},{... | collective-permute-start | bytes 1228808 | tf_op jit(solution)/shard_map/ppermute | solution.py:514
  66.1 36.7 %copy-start.1 = (bf16[2,128,256]{2,1,0:T(8,128)(2,1)S(1)}, bf16[2,128,256]{2,1,0:T(8,128)(2,1)}, u32[]{:S(2)}) copy-start(bf16[2,128,256]{2,1,0:T(8,128)(2,1)} %rest_1_.1) | copy-start | bytes 393220
  66.1 36.7 %copy-start.3 = (bf16[2,64,128]{2,1,0:T(8,128)(2,1)S(1)}, bf16[2,64,128]{2,1,0:T(8,128)(2,1)}, u32[]{:S(2)}) copy-start(bf16[2,64,128]{2,1,0:T(8,128)(2,1)} %out_weight_ref.3) | copy-start | bytes 98308
  66.1 36.6 %copy-start.4 = (s32[1280]{0:T(1024)S(1)}, s32[1280]{0:T(1024)}, u32[]{:S(2)}) copy-start(s32[1280]{0:T(1024)} %valid_ref.3) | copy-start | bytes 15364
  66.1 36.6 %copy-start.6 = (f32[2,64]{1,0:T(2,128)S(1)}, f32[2,64]{1,0:T(2,128)}, u32[]{:S(2)}) copy-start(f32[2,64]{1,0:T(2,128)} %out_gain_ref.3) | copy-start | bytes 1540
  70.6 3.8 %collective-permute-start.3 = (bf16[64,8,512]{2,1,0:T(8,128)(2,1)S(1)}, bf16[64,8,512]{2,1,0:T(8,128)(2,1)S(1)}, u32[]{:S(2)}, u32[]{:S(2)}) collective-permute-start(bf16[64,8,512]{2,1,0:T(8,128)(2,1)S(1)} %slice_bitcast_fusion), channel_id=1, source_target_pairs={{0,16},{16,0},{1,17},{17,1},{2,18},{18,2},{3,19},{19,3},{4,20},{20... | collective-permute-start | bytes 1572872 | tf_op jit(solution)/shard_map/ppermute | solution.py:524
  140.1 13.2 %all-to-all-start.3 = ((bf16[4,160,320]{2,1,0:T(8,128)(2,1)}), bf16[4,160,320]{2,1,0:T(8,128)(2,1)S(1)}, u32[]{:S(2)}, u32[]{:S(2)}) async-start(bf16[4,160,320]{2,1,0:T(8,128)(2,1)} %bitcast.6._), calls=%async_computation.3 | async-start | bytes 983040 | tf_op jit(solution)/shard_map/all_to_all | solution.py:520
  145.3 21.8 %collective-permute-start.7 = (bf16[320,640]{1,0:T(8,128)(2,1)S(1)}, bf16[320,640]{1,0:T(8,128)(2,1)S(1)}, u32[]{:S(2)}, u32[]{:S(2)}) collective-permute-start(bf16[320,640]{1,0:T(8,128)(2,1)S(1)} %shard_map.109.here_ref), channel_id=1, source_target_pairs={{0,8},{4,12},{8,0},{12,4},{1,9},{5,13},{9,1},{13,5},{2,10},{6,14},... | collective-permute-start | bytes 1228808 | tf_op jit(solution)/shard_map/ppermute | solution.py:514
  153.3 13.7 %collective-permute-start.4 = (bf16[4,160,320]{2,1,0:T(8,128)(2,1)S(1)}, bf16[4,160,320]{2,1,0:T(8,128)(2,1)S(1)}, u32[]{:S(2)}, u32[]{:S(2)}) collective-permute-start(bf16[4,160,320]{2,1,0:T(8,128)(2,1)S(1)} %all-to-all-done.3.own_ref), channel_id=1, source_target_pairs={{0,16},{16,0},{1,17},{17,1},{2,18},{18,2},{3,19},{19,3},{4,20},{20... | collective-permute-start | bytes 1228808 | tf_op jit(solution)/shard_map/ppermute | solution.py:524
  155.2 17.4 %collective-permute-start.5 = (bf16[320,640]{1,0:T(8,128)(2,1)S(1)}, bf16[320,640]{1,0:T(8,128)(2,1)S(1)}, u32[]{:S(2)}, u32[]{:S(2)}) collective-permute-start(bf16[320,640]{1,0:T(8,128)(2,1)S(1)} %shard_map.109.here_ref), channel_id=1, source_target_pairs={{0,12},{4,0},{8,4},{12,8},{1,13},{5,1},{9,5},{13,9},{2,14},{6,2},{... | collective-permute-start | bytes 1228808 | tf_op jit(solution)/shard_map/ppermute | solution.py:514
  163.3 13.5 %collective-permute-start.6 = (bf16[320,640]{1,0:T(8,128)(2,1)S(1)}, bf16[320,640]{1,0:T(8,128)(2,1)S(1)}, u32[]{:S(2)}, u32[]{:S(2)}) collective-permute-start(bf16[320,640]{1,0:T(8,128)(2,1)S(1)} %shard_map.109.here_ref), channel_id=1, source_target_pairs={{0,4},{4,8},{8,12},{12,0},{1,5},{5,9},{9,13},{13,1},{2,6},{6,10},{... | collective-permute-start | bytes 1228808 | tf_op jit(solution)/shard_map/ppermute | solution.py:514
